TPU v7x, 32 devices: a whole 2x2x4 slice. The times are simulated.
32 devices in a mesh: dp: 8 (over z, y), ctx: 4 (over x, core).
Axes of the slice: x: 2, y: 2, z: 4, core: 2. Of those that a mesh axis runs over, the one named last changes fastest.
Arguments:
- tokens_in: bfloat16 [2, 8, 512, 576], P(None, 'dp', 'ctx'), may hold values from -6 to 6
- places: int32 [2, 8, 512], P(None, 'dp', 'ctx'), may hold values from 0 to 511, as said below
- out_grad: bfloat16 [2, 8, 512, 576], P(None, 'dp', 'ctx')
- weights: float32 [3538944], P(('dp', 'ctx'))
- first_moment: float32 [3538944], P(('dp', 'ctx'))
- second_moment: float32 [3538944], P(('dp', 'ctx')), as said below
- vectors: float32 [2112], replicated
- vector_first: float32 [2112], replicated
- vector_second: float32 [2112], replicated, as said below
Outputs:
- block_out: bfloat16 [2, 8, 512, 576], P(None, 'dp', 'ctx')
- input_grad: bfloat16 [2, 8, 512, 576], P(None, 'dp', 'ctx')
- new_weights: float32 [3538944], P(('dp', 'ctx'))
- new_first: float32 [3538944], P(('dp', 'ctx'))
- new_second: float32 [3538944], P(('dp', 'ctx'))
- new_vectors: float32 [2112], replicated
- new_vector_first: float32 [2112], replicated
- new_vector_second: float32 [2112], replicated
Inputs may be any that keep to these rules, and one draw needn't show every extreme that they name: `places`: each sequence holds every position 0 to 511 once; the tokens of one index of ctx are two blocks of 64 consecutive positions in rising order, block p and block 7 - p, with p differing between the indices of ctx of one sequence. `second_moment`: every entry is positive. `vector_second`: every entry is positive.
All inputs are finite; a program needn't handle non-finite values.
Results may differ from a plain program's by a relative error of at most 0.014.
The roundings to bfloat16 on the way count: a program that leaves them out, or rounds other values in their place, can miss the bound.
Values may be sent and summed in bfloat16 or wider, within the bound.
No kernel may reach another device: no remote copies, remote signals or barrier semaphores. Data moves between devices by JAX's collectives and lax.ppermute only.
A program may use at most 128 MiB of HBM per device.

v0:
```python
import jax
import jax.numpy as jnp
from jax import lax
from jax.sharding import PartitionSpec as P

MODEL_WIDTH = 576
QUERY_HEADS = 9
KEY_VALUE_HEADS = 3
HEAD_SIZE = 64
FF = 1536
STEP = 10


EPS_NORM = 1e-05
THETA = 100000.0
BETA_ONE = 0.9
BETA_TWO = 0.95
EPS_ADAM = 1e-08
RATE_MATRIX = 0.06
RATE_VECTOR = 0.3
DECAY = 0.1
MASKED = -1e30


def split_matrices(flat):
    query_width = QUERY_HEADS * HEAD_SIZE
    paired_width = KEY_VALUE_HEADS * HEAD_SIZE
    shapes = (
        (MODEL_WIDTH, query_width),
        (MODEL_WIDTH, paired_width),
        (MODEL_WIDTH, paired_width),
        (query_width, MODEL_WIDTH),
        (MODEL_WIDTH, FF),
        (MODEL_WIDTH, FF),
        (FF, MODEL_WIDTH),
    )
    pieces = []
    offset = 0
    for rows_count, cols_count in shapes:
        pieces.append(
            flat[offset : offset + rows_count * cols_count].reshape(rows_count, cols_count)
        )
        offset += rows_count * cols_count
    return pieces


def split_vectors(flat):
    width_list = (
        MODEL_WIDTH,
        MODEL_WIDTH,
        QUERY_HEADS * HEAD_SIZE,
        KEY_VALUE_HEADS * HEAD_SIZE,
        KEY_VALUE_HEADS * HEAD_SIZE,
    )
    pieces = []
    offset = 0
    for size_one in width_list:
        pieces.append(flat[offset : offset + size_one])
        offset += size_one
    return pieces


def rope_tables(place_rows):
    half_dim = HEAD_SIZE // 2
    frequency = THETA ** (-2.0 * jnp.arange(half_dim, dtype=jnp.float32) / HEAD_SIZE)
    angles = place_rows.astype(jnp.float32)[:, None] * frequency[None, :]
    return (jnp.cos(angles), jnp.sin(angles))


def apply_rotation(entries, cosine_table, sine_table, sign):
    half_dim = HEAD_SIZE // 2
    front_half = entries[..., :half_dim]
    back_half = entries[..., half_dim:]
    cos_rows = cosine_table[:, None, :]
    sin_rows = sine_table[:, None, :] * sign
    return jnp.concatenate(
        [
            front_half * cos_rows - back_half * sin_rows,
            back_half * cos_rows + front_half * sin_rows,
        ],
        axis=-1,
    )


def times_transposed(left, right):
    return lax.dot_general(
        left, right, (((1,), (1,)), ((), ())), preferred_element_type=jnp.float32
    )


def rows_product(left, right):
    return lax.dot_general(
        left, right, (((0,), (0,)), ((), ())), preferred_element_type=jnp.float32
    )


def scores_of(grouped_queries, gathered_pairs, places_own, places_keys):
    sequence_count, total_length, pair_twice = gathered_pairs.shape
    paired_width = pair_twice // 2
    keys_gathered = gathered_pairs[..., :paired_width].reshape(
        sequence_count, total_length, KEY_VALUE_HEADS, HEAD_SIZE
    )
    scaled = jnp.einsum(
        "sqhgd,skhd->shgqk", grouped_queries, keys_gathered, preferred_element_type=jnp.float32
    ) * HEAD_SIZE ** (-0.5)
    allowed = places_own[:, None, None, :, None] >= places_keys[:, None, None, None, :]
    return jnp.where(allowed, scaled, MASKED)


def forward(whole, vectors, tokens, places_own, places_keys, cosine_table, sine_table):
    w_query, w_key, w_value, w_out, w_gate, w_up, w_down = split_matrices(whole)
    gain_one, gain_two, bias_query, bias_key, bias_value = split_vectors(vectors)
    sequence_count, rows_per_shard, width = tokens.shape
    row_number = sequence_count * rows_per_shard
    paired_width = KEY_VALUE_HEADS * HEAD_SIZE
    resid_in = tokens.astype(jnp.float32).reshape(row_number, width)
    scale_one = lax.rsqrt(jnp.mean(resid_in * resid_in, axis=-1, keepdims=True) + EPS_NORM)
    normed_one = resid_in * scale_one
    hidden_one = (normed_one * gain_one).astype(jnp.bfloat16)
    queries = jnp.dot(hidden_one, w_query, preferred_element_type=jnp.float32) + bias_query
    keys_local = jnp.dot(hidden_one, w_key, preferred_element_type=jnp.float32) + bias_key
    values_own = jnp.dot(hidden_one, w_value, preferred_element_type=jnp.float32) + bias_value
    rotated_queries = apply_rotation(
        queries.reshape(row_number, QUERY_HEADS, HEAD_SIZE), cosine_table, sine_table, 1.0
    ).astype(jnp.bfloat16)
    rotated_keys = apply_rotation(
        keys_local.reshape(row_number, KEY_VALUE_HEADS, HEAD_SIZE), cosine_table, sine_table, 1.0
    ).astype(jnp.bfloat16)
    pairs = jnp.concatenate(
        [
            rotated_keys.reshape(sequence_count, rows_per_shard, paired_width),
            values_own.astype(jnp.bfloat16).reshape(sequence_count, rows_per_shard, paired_width),
        ],
        axis=-1,
    )
    gathered_pairs = lax.all_gather(pairs, "ctx", axis=1, tiled=True)
    grouped_queries = rotated_queries.reshape(
        sequence_count, rows_per_shard, KEY_VALUE_HEADS, QUERY_HEADS // KEY_VALUE_HEADS, HEAD_SIZE
    )
    scores = scores_of(grouped_queries, gathered_pairs, places_own, places_keys)
    row_top = jnp.max(scores, axis=-1, keepdims=True)
    log_total = row_top + jnp.log(jnp.sum(jnp.exp(scores - row_top), axis=-1, keepdims=True))
    probs_low = jnp.exp(scores - log_total).astype(jnp.bfloat16)
    values_gathered = gathered_pairs[..., paired_width:].reshape(
        sequence_count, -1, KEY_VALUE_HEADS, HEAD_SIZE
    )
    attended = jnp.einsum(
        "shgqk,skhd->sqhgd", probs_low, values_gathered, preferred_element_type=jnp.float32
    )
    attended = attended.reshape(row_number, QUERY_HEADS * HEAD_SIZE).astype(jnp.bfloat16)
    resid_mid = resid_in + jnp.dot(attended, w_out, preferred_element_type=jnp.float32)
    scale_two = lax.rsqrt(jnp.mean(resid_mid * resid_mid, axis=-1, keepdims=True) + EPS_NORM)
    normed_two = resid_mid * scale_two
    hidden_two = (normed_two * gain_two).astype(jnp.bfloat16)
    gate_pre = jnp.dot(hidden_two, w_gate, preferred_element_type=jnp.float32)
    up_pre = jnp.dot(hidden_two, w_up, preferred_element_type=jnp.float32)
    act_low = (gate_pre * jax.nn.sigmoid(gate_pre) * up_pre).astype(jnp.bfloat16)
    result = resid_mid + jnp.dot(act_low, w_down, preferred_element_type=jnp.float32)
    block_out = result.astype(jnp.bfloat16).reshape(sequence_count, rows_per_shard, width)
    kept = (
        normed_one,
        scale_one,
        hidden_one,
        grouped_queries,
        pairs,
        gathered_pairs,
        log_total,
        attended,
        normed_two,
        scale_two,
        hidden_two,
        gate_pre,
        up_pre,
        act_low,
    )
    return (block_out, kept)


def backward(whole, vectors, grad_out, kept, places_own, places_keys, cosine_table, sine_table):
    w_query, w_key, w_value, w_out, w_gate, w_up, w_down = split_matrices(whole)
    gain_one, gain_two, bias_query, bias_key, bias_value = split_vectors(vectors)
    (
        normed_one,
        scale_one,
        hidden_one,
        grouped_queries,
        pairs,
        gathered_pairs,
        log_total,
        attended,
        normed_two,
        scale_two,
        hidden_two,
        gate_pre,
        up_pre,
        act_low,
    ) = kept
    sequence_count, rows_per_shard, width = grad_out.shape
    row_number = sequence_count * rows_per_shard
    paired_width = KEY_VALUE_HEADS * HEAD_SIZE
    score_scale = HEAD_SIZE ** (-0.5)
    grad_rows = grad_out.reshape(row_number, width)
    d_act = times_transposed(grad_rows, w_down)
    sigma = jax.nn.sigmoid(gate_pre)
    d_up = (d_act * gate_pre * sigma).astype(jnp.bfloat16)
    d_gate = (d_act * up_pre * sigma * (1.0 + gate_pre * (1.0 - sigma))).astype(jnp.bfloat16)
    d_hidden_two = times_transposed(d_gate, w_gate) + times_transposed(d_up, w_up)
    grad_gain_two = jnp.sum(d_hidden_two * normed_two, axis=0)
    d_norm_two = d_hidden_two * gain_two
    d_mid = grad_rows.astype(jnp.float32) + scale_two * (
        d_norm_two - normed_two * jnp.mean(d_norm_two * normed_two, axis=-1, keepdims=True)
    )
    d_branch = d_mid.astype(jnp.bfloat16)
    grad_attended = times_transposed(d_branch, w_out).astype(jnp.bfloat16)
    total_length = gathered_pairs.shape[1]
    keys_gathered = gathered_pairs[..., :paired_width].reshape(
        sequence_count, total_length, KEY_VALUE_HEADS, HEAD_SIZE
    )
    values_gathered = gathered_pairs[..., paired_width:].reshape(
        sequence_count, total_length, KEY_VALUE_HEADS, HEAD_SIZE
    )
    scores = scores_of(grouped_queries, gathered_pairs, places_own, places_keys)
    probs = jnp.exp(scores - log_total)
    probs_low = probs.astype(jnp.bfloat16)
    grad_attended_group = grad_attended.reshape(
        sequence_count, rows_per_shard, KEY_VALUE_HEADS, QUERY_HEADS // KEY_VALUE_HEADS, HEAD_SIZE
    )
    d_probs = jnp.einsum(
        "sqhgd,skhd->shgqk",
        grad_attended_group,
        values_gathered,
        preferred_element_type=jnp.float32,
    )
    row_delta = jnp.sum(probs * d_probs, axis=-1, keepdims=True)
    d_scores = (probs * (d_probs - row_delta)).astype(jnp.bfloat16)
    d_query_rot = (
        jnp.einsum("shgqk,skhd->sqhgd", d_scores, keys_gathered, preferred_element_type=jnp.float32)
        * score_scale
    )
    d_key_rot = (
        jnp.einsum(
            "shgqk,sqhgd->skhd", d_scores, grouped_queries, preferred_element_type=jnp.float32
        )
        * score_scale
    )
    d_value_all = jnp.einsum(
        "shgqk,sqhgd->skhd", probs_low, grad_attended_group, preferred_element_type=jnp.float32
    )
    joined = jnp.concatenate(
        [
            d_key_rot.reshape(sequence_count, total_length, paired_width),
            d_value_all.reshape(sequence_count, total_length, paired_width),
        ],
        axis=-1,
    )
    local_portion = lax.psum_scatter(joined, "ctx", scatter_dimension=1, tiled=True)
    d_key = (
        apply_rotation(
            local_portion[..., :paired_width].reshape(row_number, KEY_VALUE_HEADS, HEAD_SIZE),
            cosine_table,
            sine_table,
            -1.0,
        )
        .reshape(row_number, paired_width)
        .astype(jnp.bfloat16)
    )
    d_value = (
        local_portion[..., paired_width:].reshape(row_number, paired_width).astype(jnp.bfloat16)
    )
    d_query = (
        apply_rotation(
            d_query_rot.reshape(row_number, QUERY_HEADS, HEAD_SIZE), cosine_table, sine_table, -1.0
        )
        .reshape(row_number, QUERY_HEADS * HEAD_SIZE)
        .astype(jnp.bfloat16)
    )
    d_hidden_one = times_transposed(d_query, w_query)
    d_hidden_one = d_hidden_one + times_transposed(d_key, w_key)
    d_hidden_one = d_hidden_one + times_transposed(d_value, w_value)
    grad_gain_one = jnp.sum(d_hidden_one * normed_one, axis=0)
    d_norm_one = d_hidden_one * gain_one
    d_input = d_mid + scale_one * (
        d_norm_one - normed_one * jnp.mean(d_norm_one * normed_one, axis=-1, keepdims=True)
    )
    vector_part = jnp.concatenate(
        [
            grad_gain_one,
            grad_gain_two,
            jnp.sum(d_query.astype(jnp.float32), axis=0),
            jnp.sum(d_key.astype(jnp.float32), axis=0),
            jnp.sum(d_value.astype(jnp.float32), axis=0),
        ]
    )
    row_terms = (
        hidden_one,
        d_query,
        d_key,
        d_value,
        attended,
        d_branch,
        hidden_two,
        d_gate,
        d_up,
        act_low,
        grad_rows,
    )
    return (
        d_input.astype(jnp.bfloat16).reshape(sequence_count, rows_per_shard, width),
        vector_part,
        row_terms,
    )


def adamw(param, grad, mom_one, mom_two, rate, decay):
    new_one = BETA_ONE * mom_one + (1.0 - BETA_ONE) * grad
    new_two = BETA_TWO * mom_two + (1.0 - BETA_TWO) * grad * grad
    fixed_one = new_one / (1.0 - BETA_ONE**STEP)
    fixed_two = new_two / (1.0 - BETA_TWO**STEP)
    new_param = param - rate * (fixed_one / (jnp.sqrt(fixed_two) + EPS_ADAM) + decay * param)
    return (new_param, new_one, new_two)


def local(
    tokens_in,
    places,
    out_grad,
    weights,
    first_moment,
    second_moment,
    vectors,
    vector_first,
    vector_second,
):
    micro_count = tokens_in.shape[0]
    places_keys_all = lax.all_gather(places, "ctx", axis=2, tiled=True)
    low_weights = weights.astype(jnp.bfloat16)
    fetch_forward = lambda: lax.all_gather(low_weights, ("dp", "ctx"), axis=0, tiled=True)
    fetch_backward = lambda: lax.all_gather(low_weights, ("dp", "ctx"), axis=0, tiled=True)
    outputs = []
    input_grads = []
    row_lists = []
    grad_vectors = jnp.zeros(vectors.shape, jnp.float32)
    for index_mb in range(micro_count):
        places_own = places[index_mb]
        places_keys = places_keys_all[index_mb]
        cosine_table, sine_table = rope_tables(places_own.reshape(-1))
        whole = fetch_forward()
        block_out, kept = forward(
            whole, vectors, tokens_in[index_mb], places_own, places_keys, cosine_table, sine_table
        )
        whole_back = fetch_backward()
        input_grad, vector_part, row_terms = backward(
            whole_back,
            vectors,
            out_grad[index_mb],
            kept,
            places_own,
            places_keys,
            cosine_table,
            sine_table,
        )
        outputs.append(block_out)
        input_grads.append(input_grad)
        row_lists.append(row_terms)
        grad_vectors = grad_vectors + vector_part
    stacked = [
        jnp.concatenate([terms[position] for terms in row_lists], axis=0)
        for position in range(len(row_lists[0]))
    ]
    (
        hidden_one,
        d_query,
        d_key,
        d_value,
        attended,
        d_branch,
        hidden_two,
        d_gate,
        d_up,
        act_low,
        grad_rows,
    ) = stacked
    grad_list = (
        rows_product(hidden_one, d_query),
        rows_product(hidden_one, d_key),
        rows_product(hidden_one, d_value),
        rows_product(attended, d_branch),
        rows_product(hidden_two, d_gate),
        rows_product(hidden_two, d_up),
        rows_product(act_low, grad_rows),
    )
    grad_flat = jnp.concatenate([matrix.reshape(-1) for matrix in grad_list])
    data_count = lax.axis_size("dp")
    ctx_count = lax.axis_size("ctx")
    grad_grid = grad_flat.reshape(data_count * ctx_count, -1)
    grad_own = lax.psum_scatter(grad_grid, ("dp", "ctx"), scatter_dimension=0, tiled=True).reshape(
        -1
    )
    grad_vector_all = lax.psum(grad_vectors, ("dp", "ctx"))
    new_weights, new_first, new_second = adamw(
        weights, grad_own, first_moment, second_moment, RATE_MATRIX, DECAY
    )
    new_vectors, new_vector_first, new_vector_second = adamw(
        vectors, grad_vector_all, vector_first, vector_second, RATE_VECTOR, 0.0
    )
    return (
        jnp.stack(outputs),
        jnp.stack(input_grads),
        new_weights,
        new_first,
        new_second,
        new_vectors,
        new_vector_first,
        new_vector_second,
    )


def solution(mesh):
    in_specs = (
        P(None, "dp", "ctx", None),
        P(None, "dp", "ctx"),
        P(None, "dp", "ctx", None),
        P(("dp", "ctx")),
        P(("dp", "ctx")),
        P(("dp", "ctx")),
        P(),
        P(),
        P(),
    )
    out_specs = (
        P(None, "dp", "ctx", None),
        P(None, "dp", "ctx", None),
        P(("dp", "ctx")),
        P(("dp", "ctx")),
        P(("dp", "ctx")),
        P(),
        P(),
        P(),
    )
    return jax.shard_map(local, mesh=mesh, in_specs=in_specs, out_specs=out_specs, check_vma=False)
```

profile of v0, /device:TPU:0, one launch (start us, length us, event | category | flops | bytes accessed | tf_op | source)
XLA Modules:
  0.0 502.0 jit_solution(8564529870978651050)
XLA Ops:
  9.0 6.3 %all_gather.17 = s32[2,1,512]{2,1,0:T(1,128)S(1)} all-gather(s32[2,1,128]{2,1,0:T(1,128)} %param.10), channel_id=1, replica_groups=mesh['dp'=8,'ctx'=4] {'ctx'}, dimensions={2}, use_global_device_ids=true | all-gather | bytes 5120 | tf_op jit(solution)/shard_map/all_gather | solution.py:335
  23.3 63.4 %all-gather.2.cloned.1.call-done = bf16[3538944]{0:T(1024)(128)(2,1)} async-done(((bf16[110592]{0:T(1024)(128)(2,1)}), bf16[3538944]{0:T(1024)(128)(2,1)}) %all-gather.2.cloned.1.call-update) | async-done | bytes 7077904 | tf_op jit(solution)/shard_map/all_gather | solution.py:337
  93.8 6.5 %all_gather.18 = bf16[1,512,384]{1,2,0:T(8,128)(2,1)S(1)} all-gather(bf16[1,128,384]{1,2,0:T(8,128)(2,1)S(1)} %pad_maximum_fusion.11), channel_id=1, replica_groups=mesh['dp'=8,'ctx'=4] {'ctx'}, dimensions={1}, use_global_device_ids=true | all-gather | bytes 491520 | tf_op jit(solution)/shard_map/all_gather | solution.py:136
  103.5 6.6 %all_gather.16 = bf16[1,512,384]{1,2,0:T(8,128)(2,1)S(1)} all-gather(bf16[1,128,384]{1,2,0:T(8,128)(2,1)S(1)} %pad_maximum_fusion.10), channel_id=1, replica_groups=mesh['dp'=8,'ctx'=4] {'ctx'}, dimensions={1}, use_global_device_ids=true | all-gather | bytes 491520 | tf_op jit(solution)/shard_map/all_gather | solution.py:136
  115.2 5.0 fusion.113
  120.2 4.4 slice.263
  124.6 4.4 slice.265
  129.2 3.0 fusion.123
  133.6 4.3 slice.267
  138.0 3.8 multiply_convert_fusion.2
  162.6 2.8 reshape.709
  173.1 1.9 fusion.22
  175.0 2.1 reshape.713
  177.1 1.9 fusion.26
  179.0 2.1 reshape.714
  181.1 3.9 fusion.30
  185.0 3.7 reshape.715
  191.0 13.3 %reduce-scatter.3.cloned.1.call-done = f32[1,128,384]{1,2,0:T(8,128)} async-done(((f32[1,512,384]{1,2,0:T(8,128)}), f32[1,128,384]{1,2,0:T(8,128)}) %reduce-scatter.3.cloned.1.call-update) | async-done | bytes 196624 | tf_op jit(solution)/shard_map/reduce_scatter | solution.py:256
  207.5 2.1 fusion.81
  209.6 2.1 reshape.710
  214.4 2.0 fusion.85
  216.4 2.1 reshape.711
  218.5 2.0 constant_dynamic-update-slice_fusion.5
  222.3 2.5 constant_dynamic-update-slice_fusion.3
  224.8 2.0 constant_dynamic-update-slice_fusion.2
  228.1 2.0 constant_dynamic-update-slice_fusion.1
  230.1 2.1 constant_dynamic-update-slice_fusion
  232.2 10.7 %reshape.716 = f32[32,110592]{1,0:T(8,128)} reshape(f32[3538944]{0:T(1024)} %constant_dynamic-update-slice_fusion) | data formatting | bytes 28311552 | tf_op jit(solution)/shard_map/reshape | solution.py:395
  250.4 41.4 %psum.7 = f32[2112]{0:T(1024)S(1)} all-reduce(f32[2112]{0:T(1024)S(1)} %add.257), channel_id=1, replica_groups=mesh['dp'=8,'ctx'=4] {'dp','ctx'}, use_global_device_ids=true, to_apply=%region_27.28 | all-reduce | flops 2112 | bytes 16896 | tf_op jit(solution)/shard_map/psum | solution.py:399
  293.7 197.1 %all-reduce.3.cloned.1.call-done = f32[32,110592]{1,0:T(8,128)} async-done(((f32[32,110592]{1,0:T(8,128)}), f32[32,110592]{1,0:T(8,128)}) %all-reduce.3.cloned.1.call-update) | async-done | bytes 14155792
  490.8 2.3 constant_dynamic-slice_fusion
  493.1 2.4 multiply_subtract_fusion
  (346 shorter events, 74.4 us)
Async XLA Ops:
  7.2 79.5 %all-gather.2.cloned.1.call-start = ((), (), s32[]{:S(2)}) async-start(), calls=%async_computation.2 | async-start | bytes 7299072 | tf_op jit(solution)/shard_map/all_gather | solution.py:337
  9.0 179.7 %reduce-scatter.5.cloned.1.call-start = ((), (), s32[]{:S(2)}) async-start(), calls=%async_computation.4 | async-start | bytes 983040 | tf_op jit(solution)/shard_map/reduce_scatter | solution.py:256
  16.4 73.3 %copy-start.105 = (f32[128]{0:T(128)}, f32[128]{0:T(128)S(1)}, u32[]{:S(2)}) copy-start(f32[128]{0:T(128)S(1)} %get-tuple-element.114) | copy-start | bytes 1540
  16.4 73.3 %copy-start.107 = (f32[128]{0:T(128)}, f32[128]{0:T(128)S(1)}, u32[]{:S(2)}) copy-start(f32[128]{0:T(128)S(1)} %get-tuple-element.113) | copy-start | bytes 1540
  18.8 71.0 %copy-start.91 = (f32[576]{0:T(1024)}, f32[576]{0:T(1024)S(1)}, u32[]{:S(2)}) copy-start(f32[576]{0:T(1024)S(1)} %get-tuple-element.79) | copy-start | bytes 6916
  18.8 130.2 %copy-start.78 = (f32[576]{0:T(1024)}, f32[576]{0:T(1024)S(1)}, u32[]{:S(2)}) copy-start(f32[576]{0:T(1024)S(1)} %get-tuple-element.77) | copy-start | bytes 6916
  19.6 80.8 %copy-start.76 = (f32[128,32]{0,1:T(8,128)}, f32[128,32]{0,1:T(8,128)S(1)}, u32[]{:S(2)}) copy-start(f32[128,32]{0,1:T(8,128)S(1)} %get-tuple-element.96) | copy-start | bytes 49156
  23.2 68.8 %copy-start.20 = (bf16[128,576]{0,1:T(8,128)(2,1)}, bf16[128,576]{0,1:T(8,128)(2,1)S(1)}, u32[]{:S(2)}) copy-start(bf16[128,576]{0,1:T(8,128)(2,1)S(1)} %get-tuple-element.66) | copy-start | bytes 442372
  23.3 69.3 %copy-start.18 = (bf16[128,576]{0,1:T(8,128)(2,1)}, bf16[128,576]{0,1:T(8,128)(2,1)S(1)}, u32[]{:S(2)}) copy-start(bf16[128,576]{0,1:T(8,128)(2,1)S(1)} %get-tuple-element.65) | copy-start | bytes 442372
  92.0 9.0 %copy-start.6 = (bf16[576,576]{1,0:T(8,128)(2,1)}, bf16[576,576]{1,0:T(8,128)(2,1)S(1)}, u32[]{:S(2)}) copy-start(bf16[576,576]{1,0:T(8,128)(2,1)S(1)} %slice.255) | copy-start | bytes 1990660
  100.3 11.9 %copy-start.35 = (bf16[1,512,192]{1,2,0:T(8,128)(2,1)}, bf16[1,512,192]{1,2,0:T(8,128)(2,1)S(1)}, u32[]{:S(2)}) copy-start(bf16[1,512,192]{1,2,0:T(8,128)(2,1)S(1)} %get-tuple-element.54) | copy-start | bytes 589828
  102.5 7.7 %copy-start.63 = (f32[128,576]{0,1:T(8,128)S(1)}, f32[128,576]{0,1:T(8,128)}, u32[]{:S(2)}) copy-start(f32[128,576]{0,1:T(8,128)} %convolution_add_fusion.11) | copy-start | bytes 884740
  102.8 9.4 %copy-start.86 = (f32[3,3,128]{2,1,0:T(4,128)}, f32[3,3,128]{2,1,0:T(4,128)S(1)}, u32[]{:S(2)}) copy-start(f32[3,3,128]{2,1,0:T(4,128)S(1)} %log_add_fusion) | copy-start | bytes 13828
  115.0 35.3 %copy-start.12 = (f32[128,576]{0,1:T(8,128)}, f32[128,576]{0,1:T(8,128)S(1)}, u32[]{:S(2)}) copy-start(f32[128,576]{0,1:T(8,128)S(1)} %get-tuple-element.103) | copy-start | bytes 884740
  115.2 27.2 %copy-start.100 = (f32[128]{0:T(128)}, f32[128]{0:T(128)S(1)}, u32[]{:S(2)}) copy-start(f32[128]{0:T(128)S(1)} %add_rsqrt_fusion.2) | copy-start | bytes 1540
  115.2 33.8 %copy-start.103 = (f32[128]{0:T(128)}, f32[128]{0:T(128)S(1)}, u32[]{:S(2)}) copy-start(f32[128]{0:T(128)S(1)} %add_rsqrt_fusion) | copy-start | bytes 1540
  144.8 5.5 %copy-start.31 = (f32[128,576]{0,1:T(8,128)}, f32[128,576]{0,1:T(8,128)S(1)}, u32[]{:S(2)}) copy-start(f32[128,576]{0,1:T(8,128)S(1)} %get-tuple-element.106) | copy-start | bytes 884740
  156.3 48.0 %reduce-scatter.3.cloned.1.call-start = ((), (), s32[]{:S(2)}) async-start(), calls=%async_computation.3 | async-start | bytes 983040 | tf_op jit(solution)/shard_map/reduce_scatter | solution.py:256
  169.3 321.5 %all-reduce.3.cloned.1.call-start = ((), (), s32[]{:S(2)}) async-start(), calls=%async_computation.5 | async-start | bytes 28311552
  218.5 6.3 %copy-start.10 = (f32[884736]{0:T(1024)S(1)}, f32[884736]{0:T(1024)}, u32[]{:S(2)}) copy-start(f32[884736]{0:T(1024)} %reshape.713) | copy-start | bytes 10616836
  248.7 43.1 %copy-start.30 = (bf16[2,1,128,576]{2,3,1,0:T(8,128)(2,1)S(1)}, bf16[2,1,128,576]{2,3,1,0:T(8,128)(2,1)}, u32[]{:S(2)}) copy-start(bf16[2,1,128,576]{2,3,1,0:T(8,128)(2,1)} %param.11) | copy-start | bytes 884740
  248.8 43.0 %copy-start.34 = (f32[128,576]{0,1:T(8,128)S(1)}, f32[128,576]{0,1:T(8,128)}, u32[]{:S(2)}) copy-start(f32[128,576]{0,1:T(8,128)} %copy-done.33) | copy-start | bytes 884740
  248.8 43.0 %copy-start.79 = (f32[576]{0:T(1024)S(1)}, f32[576]{0:T(1024)}, u32[]{:S(2)}) copy-start(f32[576]{0:T(1024)} %copy-done.78) | copy-start | bytes 6916
  248.8 43.0 %copy-start.104 = (f32[128]{0:T(128)S(1)}, f32[128]{0:T(128)}, u32[]{:S(2)}) copy-start(f32[128]{0:T(128)} %copy-done.103) | copy-start | bytes 1540
  248.8 43.0 %copy-start.112 = (f32[128]{0:T(128)S(1)}, f32[128]{0:T(128)}, u32[]{:S(2)}) copy-start(f32[128]{0:T(128)} %copy-done.111) | copy-start | bytes 1540
  249.2 42.9 %copy-start.32 = (f32[128,576]{0,1:T(8,128)S(1)}, f32[128,576]{0,1:T(8,128)}, u32[]{:S(2)}) copy-start(f32[128,576]{0,1:T(8,128)} %copy-done.31) | copy-start | bytes 884740
  249.2 42.9 %copy-start.102 = (f32[128]{0:T(128)S(1)}, f32[128]{0:T(128)}, u32[]{:S(2)}) copy-start(f32[128]{0:T(128)} %copy-done.100) | copy-start | bytes 1540
  249.2 42.9 %copy-start.110 = (f32[128]{0:T(128)S(1)}, f32[128]{0:T(128)}, u32[]{:S(2)}) copy-start(f32[128]{0:T(128)} %copy-done.109) | copy-start | bytes 1540
  249.8 43.3 %copy-start.93 = (f32[2112]{0:T(1024)S(1)}, f32[2112]{0:T(1024)}, u32[]{:S(2)}) copy-start(f32[2112]{0:T(1024)} %param.15) | copy-start | bytes 25348
  249.8 43.3 %copy-start.98 = (f32[2112]{0:T(1024)S(1)}, f32[2112]{0:T(1024)}, u32[]{:S(2)}) copy-start(f32[2112]{0:T(1024)} %param.16) | copy-start | bytes 25348
  249.8 43.3 %copy-start.99 = (f32[2112]{0:T(1024)S(1)}, f32[2112]{0:T(1024)}, u32[]{:S(2)}) copy-start(f32[2112]{0:T(1024)} %param.17) | copy-start | bytes 25348
  250.2 242.9 %copy-start.43 = (f32[110592]{0:T(1024)S(1)}, f32[110592]{0:T(1024)}, u32[]{:S(2)}) copy-start(f32[110592]{0:T(1024)} %param.12) | copy-start | bytes 1327108
  (85 other events, 170.5 us)
Sparse Core Ops, SparseCore 0:
  11.5 75.1 all-gather.1
  156.4 21.8 reduce-scatter.4
  181.0 23.2 reduce-scatter.2
  243.1 247.6 all-reduce.2
where the time goes:
time: 504 us; the launch traced here: 502 us
  waiting for transfers between devices  274 us (54%)
  local copies, waits for them, and re-layouts  80.9 us (16%)
  blocking collectives  60.8 us (12%)
  matrix products  48.1 us (10%)
  other arithmetic  22.9 us (5%)
  between operations  15.4 us (3%)
    unnamed x5, waiting for transfers between devices  197 us
    all_gather x1, waiting for transfers between devices, local(): lax.all_gather(low_weights, ('dp', 'ctx'), axis=0, tiled=True)  63.4 us
    psum x1, blocking collectives, local(): grad_vector_all = lax.psum(grad_vectors, ('dp', 'ctx'))  41.4 us
    unnamed x233, local copies, waits for them, and re-layouts  23.6 us
    slice x10, local copies, waits for them, and re-layouts, split_matrices(): flat[offset:offset + rows_count * cols_count]  22.2 us
    reshape x7, local copies, waits for them, and re-layouts, local(): grad_flat = jnp.concatenate([matrix.reshape(-1) for matrix in grad_list])  16.6 us
    dot_general x7, matrix products, rows_product(): lax.dot_general(left, right, (((0,), (0,)), ((), ())), preferred_element_...  13.7 us
    reduce_scatter x2, waiting for transfers between devices, backward(): lax.psum_scatter(joined, 'ctx', scatter_dimension=1, tiled=True)  13.3 us
  transfers between devices with their start and end apart: 4, of which 3 were waited for; matrix products, arithmetic and copies ran while one was open for 10% of the time, Pallas kernels for 0%

commit v1 on v0

v1 whole, which is shorter than its diff:
```python
import jax
import jax.numpy as jnp
from jax import lax
from jax.experimental import pallas as pl
from jax.experimental.pallas import tpu as pltpu
from jax.sharding import PartitionSpec as P

MODEL_WIDTH = 576
QUERY_HEADS = 9
KEY_VALUE_HEADS = 3
HEAD_SIZE = 64
FF = 1536
STEP = 10

EPS_NORM = 1e-05
THETA = 100000.0
BETA_ONE = 0.9
BETA_TWO = 0.95
EPS_ADAM = 1e-08
RATE_MATRIX = 0.06
RATE_VECTOR = 0.3
DECAY = 0.1
MASKED = -1e30

LANES = 128
WIDE = 640
BLOCKS = 32
BLOCK_ROWS = 864
HEAD_ROWS = 576
TAIL_ROWS = BLOCK_ROWS - HEAD_ROWS
SIZES = {"z": 4, "y": 2, "x": 2, "c": 2}
ROWS = 128
F32 = jnp.float32
BF16 = jnp.bfloat16


def coordinates(number):
    found = {}
    for name in ("c", "x", "y", "z"):
        found[name] = number % SIZES[name]
        number = number // SIZES[name]
    return found


def number_of(found):
    number = 0
    for name in ("z", "y", "x", "c"):
        number = number * SIZES[name] + found[name]
    return number


def device_number():
    return lax.axis_index("dp") * lax.axis_size("ctx") + lax.axis_index("ctx")


def inner_count():
    return lax.axis_size("dp") * lax.axis_size("ctx") // BLOCKS


def moved(buffer, name, shift):
    inner = inner_count()
    pairs = []
    for number in range(BLOCKS):
        found = coordinates(number)
        found[name] = (found[name] + shift) % SIZES[name]
        target = number_of(found)
        pairs += [(number * inner + k, target * inner + k) for k in range(inner)]
    return lax.ppermute(buffer, ("dp", "ctx"), pairs)


def across(buffer, distance):
    count = lax.axis_size("ctx")
    return lax.ppermute(buffer, "ctx", [(i, i ^ distance) for i in range(count)])


def together(*arrays):
    return lax.optimization_barrier(arrays)


def gather_blocks(head, tail):
    hz = [moved(head, "z", s) for s in (1, 2, 3)]
    tx = moved(tail, "x", 1)
    head, tail, tx, *hz = together(head, tail, tx, *hz)
    own = jnp.stack([head] + hz)
    pair = jnp.stack([tail, tx])
    ay = moved(own, "y", 1)
    ax = moved(own, "x", 1)
    ac = moved(own, "c", 1)
    tz = [moved(pair, "z", s) for s in (1, 2, 3)]
    own, pair, ay, ax, *tz = together(own, pair, ay, ax, *tz)
    eight = jnp.concatenate([pair] + tz)
    axy = moved(ay, "x", 1)
    ty = moved(eight, "y", 1)
    acy = moved(ay, "c", 1)
    acx = moved(ax, "c", 1)
    tc = moved(eight, "c", 1)
    axy, ty = together(axy, ty)
    acxy = moved(axy, "c", 1)
    tcy = moved(ty, "c", 1)
    return [own, ay, ax, axy, ac, acy, acx, acxy], [eight, ty, tc, tcy]


def fold(order, relative):
    slot = 0
    for name in order:
        slot = slot * SIZES[name] + relative[name]
    return slot


def slot_table():
    mine = coordinates(device_number() // inner_count())
    entries = []
    for order in (("c", "x", "y", "z"), ("c", "y", "z", "x")):
        for number in range(BLOCKS):
            found = coordinates(number)
            entries.append(fold(order, {n: (mine[n] - found[n]) % SIZES[n] for n in SIZES}))
    for order in (("x", "y", "z"), ("y", "z", "x")):
        for number in range(0, BLOCKS, 2):
            found = coordinates(number)
            entries.append(fold(order, {n: (found[n] - mine[n]) % SIZES[n] for n in SIZES}))
    entries.append(mine["c"])
    return jnp.stack([jnp.asarray(entry, jnp.int32) for entry in entries])


AT_HEAD, AT_TAIL, TO_HEAD, TO_TAIL, MY_CORE = 0, BLOCKS, 2 * BLOCKS, 2 * BLOCKS + 16, 2 * BLOCKS + 32


def summed(kept, received):
    return kept.astype(F32) + received.astype(F32)


def scatter_blocks(head_send, head_keep, tail_send, tail_keep, vector):
    hr = moved(head_send, "c", 1)
    tr = moved(tail_send, "c", 1)
    vr = moved(vector, "c", 1)
    hr, tr, vr = together(hr, tr, vr)
    hx = summed(head_keep[8:], hr[8:]).astype(BF16)
    ty = summed(tail_keep[8:], tr[8:]).astype(BF16)
    head = summed(head_keep[:8], hr[:8])
    tail = summed(tail_keep[:8], tr[:8])
    vector = vector + vr
    hr = moved(hx, "x", 1)
    tr = moved(ty, "y", 1)
    vr = moved(vector, "x", 1)
    hr, tr, vr = together(hr, tr, vr)
    hy = summed(head[4:], hr[4:]).astype(BF16)
    tz = [summed(tail[2 * s : 2 * s + 2], tr[2 * s : 2 * s + 2]).astype(BF16) for s in (1, 2, 3)]
    head = summed(head[:4], hr[:4])
    tail = summed(tail[:2], tr[:2])
    vector = vector + vr
    hr = moved(hy, "y", 1)
    tr = [moved(tz[s - 1], "z", s) for s in (1, 2, 3)]
    vr = moved(vector, "y", 1)
    hr, vr, *tr = together(hr, vr, *tr)
    hz = [summed(head[s], hr[s]).astype(BF16) for s in (1, 2, 3)]
    head = summed(head[0], hr[0])
    tx = summed(summed(tail[1], tr[0][1]), summed(tr[1][1], tr[2][1])).astype(BF16)
    tail = summed(summed(tail[0], tr[0][0]), summed(tr[1][0], tr[2][0]))
    vector = vector + vr
    hr = [moved(hz[s - 1], "z", s) for s in (1, 2, 3)]
    tr = moved(tx, "x", 1)
    vr = [moved(vector, "z", s) for s in (1, 2, 3)]
    head = summed(summed(head, hr[0]), summed(hr[1], hr[2]))
    place = coordinates(device_number() // inner_count())["z"]
    parts = jnp.stack([vector] + vr)
    vector = sum(
        lax.dynamic_index_in_dim(parts, (place - z) % 4, 0, keepdims=False) for z in range(4)
    )
    return head, summed(tail, tr), vector


def lower_lanes(shape):
    return lax.broadcasted_iota(jnp.int32, shape, 1) < HEAD_SIZE


def half_turn(value):
    return pltpu.roll(value, HEAD_SIZE, 1)


def side_by_side(left, right):
    return jnp.where(lower_lanes(left.shape), left, half_turn(right))


def kind_of(block):
    return jnp.where(block >= 24, 1, jnp.where(block >= 8, 0, jnp.where((block == 3) | (block == 4), 2, 1)))


def tile_kernel(kind_ref, flat_ref, head_ref, tail_ref, tiles, narrow):
    kind = kind_ref[0]

    @pl.when(kind == 0)
    def _():
        for j in range(12):
            tiles[72 * j : 72 * j + 72, :] = flat_ref[pl.ds(j, 72, stride=12), :]

    @pl.when(kind == 1)
    def _():
        lines = [flat_ref[pl.ds(t, 96, stride=9), :] for t in range(9)]
        turned = [half_turn(line) for line in lines[4:]]
        low = lower_lanes((96, LANES))
        for j in range(4):
            tiles[pl.ds(192 * j, 96, stride=2), :] = lines[j]
            tiles[pl.ds(192 * j + 1, 96, stride=2), :] = jnp.where(low, turned[j], turned[j + 1])
        narrow[pl.ds(0, 96, stride=2), :] = lines[4]
        narrow[pl.ds(1, 96, stride=2), :] = turned[4]
        tiles[768:864, :] = side_by_side(narrow[0:96, :], narrow[96:192, :])

    @pl.when(kind == 2)
    def _():
        lines = [flat_ref[pl.ds(t, 288, stride=3), :] for t in range(3)]
        first, second = half_turn(lines[1]), half_turn(lines[2])
        tiles[pl.ds(0, 288, stride=2), :] = lines[0]
        tiles[pl.ds(1, 288, stride=2), :] = jnp.where(lower_lanes((288, LANES)), first, second)
        narrow[pl.ds(0, 288, stride=2), :] = lines[1]
        narrow[pl.ds(1, 288, stride=2), :] = second
        tiles[576:864, :] = side_by_side(narrow[0:288, :], narrow[288:576, :])

    head_ref[...] = tiles[0:HEAD_ROWS, :].astype(BF16)
    tail_ref[...] = tiles[HEAD_ROWS:BLOCK_ROWS, :].astype(BF16)


def to_tiles(kind, flat):
    return pl.pallas_call(
        tile_kernel,
        out_shape=(
            jax.ShapeDtypeStruct((HEAD_ROWS, LANES), BF16),
            jax.ShapeDtypeStruct((TAIL_ROWS, LANES), BF16),
        ),
        in_specs=[
            pl.BlockSpec(memory_space=pltpu.SMEM),
            pl.BlockSpec(memory_space=pltpu.VMEM),
        ],
        out_specs=(pl.BlockSpec(memory_space=pltpu.VMEM),) * 2,
        scratch_shapes=[
            pltpu.VMEM((BLOCK_ROWS, LANES), F32),
            pltpu.VMEM((HEAD_ROWS, LANES), F32),
        ],
        name="to_tiles",
    )(kind, flat)


def flat_kernel(kind_ref, head_ref, tail_ref, flat_ref, tiles, narrow):
    kind = kind_ref[0]
    tiles[0:HEAD_ROWS, :] = head_ref[...]
    tiles[HEAD_ROWS:BLOCK_ROWS, :] = tail_ref[...]

    @pl.when(kind == 0)
    def _():
        for j in range(12):
            flat_ref[pl.ds(j, 72, stride=12), :] = tiles[72 * j : 72 * j + 72, :]

    @pl.when(kind == 1)
    def _():
        low = lower_lanes((96, LANES))
        narrow[0:96, :] = tiles[768:864, :]
        narrow[96:192, :] = half_turn(tiles[768:864, :])
        odd = [half_turn(tiles[pl.ds(192 * j + 1, 96, stride=2), :]) for j in range(4)]
        for j in range(4):
            flat_ref[pl.ds(j, 96, stride=9), :] = tiles[pl.ds(192 * j, 96, stride=2), :]
        flat_ref[pl.ds(4, 96, stride=9), :] = jnp.where(low, narrow[pl.ds(0, 96, stride=2), :], odd[0])
        for j in range(3):
            flat_ref[pl.ds(5 + j, 96, stride=9), :] = jnp.where(low, odd[j], odd[j + 1])
        last = half_turn(narrow[pl.ds(1, 96, stride=2), :])
        flat_ref[pl.ds(8, 96, stride=9), :] = jnp.where(low, odd[3], last)

    @pl.when(kind == 2)
    def _():
        low = lower_lanes((288, LANES))
        narrow[0:288, :] = tiles[576:864, :]
        narrow[288:576, :] = half_turn(tiles[576:864, :])
        odd = half_turn(tiles[pl.ds(1, 288, stride=2), :])
        flat_ref[pl.ds(0, 288, stride=3), :] = tiles[pl.ds(0, 288, stride=2), :]
        flat_ref[pl.ds(1, 288, stride=3), :] = jnp.where(low, narrow[pl.ds(0, 288, stride=2), :], odd)
        last = half_turn(narrow[pl.ds(1, 288, stride=2), :])
        flat_ref[pl.ds(2, 288, stride=3), :] = jnp.where(low, odd, last)


def to_flat(kind, head, tail):
    return pl.pallas_call(
        flat_kernel,
        out_shape=jax.ShapeDtypeStruct((BLOCK_ROWS, LANES), F32),
        in_specs=[
            pl.BlockSpec(memory_space=pltpu.SMEM),
            pl.BlockSpec(memory_space=pltpu.VMEM),
            pl.BlockSpec(memory_space=pltpu.VMEM),
        ],
        out_specs=pl.BlockSpec(memory_space=pltpu.VMEM),
        scratch_shapes=[
            pltpu.VMEM((BLOCK_ROWS, LANES), F32),
            pltpu.VMEM((HEAD_ROWS, LANES), F32),
        ],
        name="to_flat",
    )(kind, head, tail)


def product(left, right):
    return jnp.dot(left, right, preferred_element_type=F32)


def times_transposed(left, right):
    return lax.dot_general(left, right, (((1,), (1,)), ((), ())), preferred_element_type=F32)


def rows_product(left, right):
    return lax.dot_general(left, right, (((0,), (0,)), ((), ())), preferred_element_type=F32)


def swapped(value):
    lane = lax.broadcasted_iota(jnp.int32, value.shape, 1)
    return jnp.where(lane % HEAD_SIZE < HEAD_SIZE // 2, pltpu.roll(value, 96, 1), pltpu.roll(value, 32, 1))


def rope(value, cosines, sines):
    return value * cosines + swapped(value) * sines


def rope_back(value, cosines, sines):
    return value * cosines - swapped(value) * sines


def row_mean(value):
    return jnp.sum(value, axis=-1, keepdims=True) * (1.0 / MODEL_WIDTH)


def normed_rows(value):
    scale = lax.rsqrt(row_mean(value * value) + EPS_NORM)
    return value * scale, scale


def place_rows(ref, head_tile, tail_tile, first):
    for j in range(3):
        ref[first : first + 192, LANES * j : LANES * j + LANES] = head_tile[192 * j : 192 * j + 192, :]
    ref[first : first + 192, 384:512] = tail_tile[0:192, :]
    rest = tail_tile[192:288, :].astype(F32)
    low = lower_lanes(rest.shape)
    ref[first : first + 96, 512:640] = jnp.where(low, rest, 0.0).astype(BF16)
    ref[first + 96 : first + 192, 512:640] = jnp.where(low, half_turn(rest), 0.0).astype(BF16)


def tiles_of_rows(value):
    head = jnp.concatenate([value[:, LANES * j : LANES * j + LANES] for j in range(3)], axis=0)
    rest = side_by_side(value[0:96, 512:640], value[96:192, 512:640])
    return head, jnp.concatenate([value[:, 384:512], rest], axis=0)


def layer_kernel(*refs):
    slots = refs[0]
    head_parts = refs[1:9]
    tail_parts = refs[9:13]
    (tokens_ref, cos_ref, sin_ref, place_q_ref, place_k_ref, gains_ref, bias_q_ref, bias_kv_ref, grad_ref) = refs[13:22]
    (block_out_ref, head_send, head_keep, tail_send, tail_keep, vector_ref, dkv_ref, dq_wq_ref, d_mid_ref, w_kv) = refs[22:32]
    (raw_head, raw_tail, w_q, w_out, w_gate, w_up, w_down, normed_all, hidden_all, keys, values, queries, probs, attended, act_all, block_acc, d_hidden, d_attended, dkv_all, d_query, sems) = refs[32:]

    copies = []
    for k, part in enumerate(head_parts):
        copies.append(pltpu.make_async_copy(part, raw_head.at[pl.ds(4 * k, 4)], sems.at[k]))
    for k, part in enumerate(tail_parts):
        copies.append(pltpu.make_async_copy(part, raw_tail.at[pl.ds(8 * k, 8)], sems.at[8 + k]))
    for copy in copies:
        copy.start()
    for copy in copies:
        copy.wait()

    core = slots[MY_CORE]

    def head_tile(block):
        return raw_head.at[slots[AT_HEAD + block]]

    def tail_tile(block):
        return raw_tail.at[slots[AT_TAIL + block]]

    for ref in (w_q, w_out, w_gate, w_up, w_kv):
        ref[576:640, :] = jnp.zeros((64, ref.shape[1]), BF16)
    for k in range(3):
        place_rows(w_q, head_tile(k), tail_tile(k), 192 * k)
        place_rows(w_out, head_tile(5 + k), tail_tile(5 + k), 192 * k)
    for k in range(8):
        place_rows(w_down, head_tile(24 + k), tail_tile(24 + k), 192 * k)
    w_kv[0:576, 0:128] = head_tile(3)[...]
    w_kv[0:576, 128:256] = head_tile(4)[...]
    rest_key = tail_tile(3)[...].astype(F32)
    rest_value = tail_tile(4)[...].astype(F32)
    low = lower_lanes(rest_key.shape)
    w_kv[0:288, 256:384] = jnp.where(low, rest_key, half_turn(rest_value)).astype(BF16)
    w_kv[288:576, 256:384] = jnp.where(low, half_turn(rest_key), rest_value).astype(BF16)
    for ref, base in ((w_gate, 8), (w_up, 16)):
        for k in range(4):
            for i in range(6):
                if i < 4:
                    even = head_tile(base + 2 * k)[144 * i : 144 * i + 144, :].astype(F32)
                    odd = head_tile(base + 2 * k + 1)[144 * i : 144 * i + 144, :].astype(F32)
                else:
                    even = tail_tile(base + 2 * k)[144 * (i - 4) : 144 * (i - 4) + 144, :].astype(F32)
                    odd = tail_tile(base + 2 * k + 1)[144 * (i - 4) : 144 * (i - 4) + 144, :].astype(F32)
                ref[144 * k : 144 * k + 144, 256 * i : 256 * i + 128] = jnp.concatenate(
                    [even[0:72], odd[0:72]], axis=0
                ).astype(BF16)
                ref[144 * k : 144 * k + 144, 256 * i + 128 : 256 * i + 256] = jnp.concatenate(
                    [even[72:144], odd[72:144]], axis=0
                ).astype(BF16)

    gain_one = gains_ref[0:1, :]
    gain_two = gains_ref[1:2, :]
    low_rows = lower_lanes((ROWS, LANES))

    @pl.loop(0, 8)
    def _(step):
        slot, mb = step // 2, step % 2
        first = pl.multiple_of(mb * 512 + slot * ROWS, ROWS)
        lane = lax.broadcasted_iota(jnp.int32, (ROWS, WIDE), 1)
        x = jnp.where(lane < MODEL_WIDTH, tokens_ref[slot, mb].astype(F32), 0.0)
        normed, _ = normed_rows(x)
        hidden = (normed * gain_one).astype(BF16)
        normed_all[pl.ds(first, ROWS), :] = normed
        hidden_all[pl.ds(first, ROWS), :] = hidden
        pair = product(hidden, w_kv[...]) + bias_kv_ref[...]
        cosines, sines = cos_ref[slot, mb], sin_ref[slot, mb]
        key_a = rope(pair[:, 0:128], cosines, sines)
        key_b = rope(pair[:, 256:384], cosines, sines)
        value_a, value_b = pair[:, 128:256], pair[:, 256:384]
        turned = half_turn(key_a)
        rows = pl.ds(first, ROWS)
        keys[rows, 0:128] = jnp.where(low_rows, key_a, turned).astype(BF16)
        keys[rows, 128:256] = jnp.where(low_rows, turned, key_a).astype(BF16)
        keys[rows, 256:384] = jnp.where(low_rows, key_b, half_turn(key_b)).astype(BF16)
        turned = half_turn(value_a)
        values[rows, 0:128] = jnp.where(low_rows, value_a, turned).astype(BF16)
        values[rows, 128:256] = jnp.where(low_rows, turned, value_a).astype(BF16)
        values[rows, 256:384] = jnp.where(low_rows, half_turn(value_b), value_b).astype(BF16)

    def heads_of(ref, rows, group):
        stacked = []
        for k in range(3):
            number = 3 * group + k
            tile = ref[rows, LANES * (number // 2) : LANES * (number // 2) + LANES]
            keep = low_rows if number % 2 == 0 else jnp.logical_not(low_rows)
            stacked.append(jnp.where(keep, tile.astype(F32), 0.0).astype(BF16))
        return jnp.concatenate(stacked, axis=0)

    def tiles_of_heads(parts):
        found = [jnp.where(low_rows, parts[2 * k], parts[2 * k + 1]) for k in range(4)]
        return found + [jnp.where(low_rows, parts[8], 0.0)]

    @pl.loop(0, 2)
    def _(mb):
        rows = pl.ds(pl.multiple_of(mb * ROWS, ROWS), ROWS)
        key_rows = pl.ds(pl.multiple_of(mb * 512, 512), 512)
        cosines, sines = cos_ref[0, mb], sin_ref[0, mb]
        made = product(hidden_all[pl.ds(pl.multiple_of(mb * 512, 512), ROWS), :], w_q[...]) + bias_q_ref[...]
        for k in range(5):
            queries[rows, LANES * k : LANES * k + LANES] = rope(
                made[:, LANES * k : LANES * k + LANES], cosines, sines
            ).astype(BF16)
        allowed = place_q_ref[mb] >= place_k_ref[mb]
        allowed = jnp.concatenate([allowed.astype(F32)] * 3, axis=0) > 0.5
        parts = []
        for group in range(KEY_VALUE_HEADS):
            lanes = slice(LANES * group, LANES * group + LANES)
            scores = times_transposed(heads_of(queries, rows, group), keys[key_rows, lanes])
            scores = jnp.where(allowed, scores * HEAD_SIZE ** (-0.5), MASKED)
            top = jnp.max(scores, axis=-1, keepdims=True)
            powers = jnp.exp(scores - top)
            found = powers * (1.0 / jnp.sum(powers, axis=-1, keepdims=True))
            probs[mb, group] = found
            out = product(found.astype(BF16), values[key_rows, lanes])
            parts += [out[ROWS * k : ROWS * k + ROWS] for k in range(3)]
        for k, tile in enumerate(tiles_of_heads(parts)):
            attended[rows, LANES * k : LANES * k + LANES] = tile.astype(BF16)

    lane = lax.broadcasted_iota(jnp.int32, (2 * ROWS, WIDE), 1)
    x_own = tokens_ref[0].astype(F32).reshape(2 * ROWS, WIDE)
    x_own = jnp.where(lane < MODEL_WIDTH, x_own, 0.0)
    resid_mid = x_own + product(attended[...], w_out[...])
    normed_two, scale_two = normed_rows(resid_mid)
    hidden_two = (normed_two * gain_two).astype(BF16)
    grad_low = grad_ref[...]
    block_acc[...] = resid_mid
    d_hidden[...] = jnp.zeros_like(d_hidden)

    def store_pair(at, even, odd, send, keep, table, rows):
        slot = slots[table + at]
        send[slot, rows, :] = jnp.where(core == 0, odd, even).astype(BF16)
        keep[slot, rows, :] = jnp.where(core == 0, even, odd).astype(BF16)

    def feed_forward(chunk, first, send, keep, table):
        cols = pl.ds(pl.multiple_of(chunk * 256, 256), 256)
        gate = product(hidden_two, w_gate[:, cols])
        up = product(hidden_two, w_up[:, cols])
        sigma = 1.0 / (1.0 + jnp.exp(-gate))
        act = (gate * sigma * up).astype(BF16)
        act_all[:, cols] = act
        down = w_down[cols, :]
        d_act = times_transposed(grad_low, down)
        block_acc[...] += product(act, down)
        d_up = (d_act * gate * sigma).astype(BF16)
        d_gate = (d_act * up * sigma * (1.0 + gate * (1.0 - sigma))).astype(BF16)
        d_hidden[...] += times_transposed(d_gate, w_gate[:, cols]) + times_transposed(d_up, w_up[:, cols])
        rows = pl.ds(pl.multiple_of((chunk - first) * 144, 144), 144)
        for base, cotangent in ((4, d_gate), (8, d_up)):
            made = rows_product(hidden_two, cotangent)
            for k in range(4):
                part = made[144 * k : 144 * k + 144, :]
                even = jnp.concatenate([part[0:72, 0:128], part[0:72, 128:256]], axis=0)
                odd = jnp.concatenate([part[72:144, 0:128], part[72:144, 128:256]], axis=0)
                store_pair(base + k, even, odd, send, keep, table, rows)

    @pl.loop(0, 4)
    def _(chunk):
        feed_forward(chunk, 0, head_send, head_keep, TO_HEAD)

    @pl.loop(4, 6)
    def _(chunk):
        feed_forward(chunk, 4, tail_send, tail_keep, TO_TAIL)

    def store_rows(at, even, odd):
        even_head, even_tail = even
        odd_head, odd_tail = odd
        store_pair(at, even_head, odd_head, head_send, head_keep, TO_HEAD, slice(0, HEAD_ROWS))
        store_pair(at, even_tail, odd_tail, tail_send, tail_keep, TO_TAIL, slice(0, TAIL_ROWS))

    @pl.loop(0, 4)
    def _(k):
        made = rows_product(act_all[:, pl.ds(pl.multiple_of(k * 384, 128), 384)], grad_low)
        store_rows(12 + k, tiles_of_rows(made[0:192]), tiles_of_rows(made[192:384]))

    block_out_ref[...] = block_acc[...][:, 0:MODEL_WIDTH].astype(BF16).reshape(2, ROWS, MODEL_WIDTH)

    d_two = d_hidden[...]
    vector_ref[...] = jnp.zeros_like(vector_ref)
    vector_ref[1:2, :] = jnp.sum(d_two * normed_two, axis=0, keepdims=True)
    d_norm = d_two * gain_two
    d_mid = grad_low.astype(F32) + scale_two * (d_norm - normed_two * row_mean(d_norm * normed_two))
    d_mid_ref[...] = d_mid
    d_branch = d_mid.astype(BF16)
    d_attended[...] = times_transposed(d_branch, w_out[...]).astype(BF16)
    grad_out = rows_product(attended[...], d_branch)

    @pl.loop(0, 2)
    def _(mb):
        rows = pl.ds(pl.multiple_of(mb * ROWS, ROWS), ROWS)
        key_rows = pl.ds(pl.multiple_of(mb * 512, 512), 512)
        parts = []
        d_keys = []
        d_values = []
        for group in range(KEY_VALUE_HEADS):
            lanes = slice(LANES * group, LANES * group + LANES)
            query_rows = heads_of(queries, rows, group)
            cotangent = heads_of(d_attended, rows, group)
            found = probs[mb, group]
            d_probs = times_transposed(cotangent, values[key_rows, lanes])
            delta = jnp.sum(found * d_probs, axis=-1, keepdims=True)
            d_scores = (found * (d_probs - delta)).astype(BF16)
            out = product(d_scores, keys[key_rows, lanes]) * HEAD_SIZE ** (-0.5)
            parts += [out[ROWS * k : ROWS * k + ROWS] for k in range(3)]
            d_key = rows_product(d_scores, query_rows) * HEAD_SIZE ** (-0.5)
            d_value = rows_product(found.astype(BF16), cotangent)
            d_keys.append(d_key + half_turn(d_key))
            d_values.append(d_value + half_turn(d_value))
        cosines, sines = cos_ref[0, mb], sin_ref[0, mb]
        for k, tile in enumerate(tiles_of_heads(parts)):
            d_query[rows, LANES * k : LANES * k + LANES] = rope_back(tile, cosines, sines).astype(BF16)
        low_keys = lower_lanes((512, LANES))
        cosines = cos_ref[:, mb].reshape(512, LANES)
        sines = sin_ref[:, mb].reshape(512, LANES)
        key_a = rope_back(jnp.where(low_keys, d_keys[0], d_keys[1]), cosines, sines)
        key_b = rope_back(d_keys[2], cosines, sines)
        dkv_all[key_rows, 0:128] = key_a.astype(BF16)
        dkv_all[key_rows, 128:256] = jnp.where(low_keys, d_values[0], d_values[1]).astype(BF16)
        dkv_all[key_rows, 256:384] = jnp.where(low_keys, key_b, d_values[2]).astype(BF16)
        for slot in range(4):
            dkv_ref[slot, mb] = dkv_all[pl.ds(pl.multiple_of(mb * 512 + slot * ROWS, ROWS), ROWS), :]

    dkv = dkv_all[...]
    d_q = d_query[...]
    dq_wq = times_transposed(d_q, w_q[...])
    dq_wq_ref[...] = dq_wq
    vector_ref[2:3, :] = jnp.sum(d_q.astype(F32), axis=0, keepdims=True)
    vector_ref[3:4, 0:384] = jnp.sum(dkv.astype(F32), axis=0, keepdims=True)
    gain_sum = jnp.zeros((1, WIDE), F32)
    for mb in range(2):
        gain_sum += jnp.sum(dq_wq[ROWS * mb : ROWS * mb + ROWS] * normed_all[512 * mb : 512 * mb + ROWS, :], axis=0, keepdims=True)
    for k in range(4):
        part = slice(256 * k, 256 * k + 256)
        gain_sum += jnp.sum(times_transposed(dkv_all[part, :], w_kv[...]) * normed_all[part, :], axis=0, keepdims=True)
    vector_ref[0:1, :] = gain_sum

    hidden_own = jnp.concatenate([hidden_all[0:ROWS, :], hidden_all[512 : 512 + ROWS, :]], axis=0)
    grad_q = rows_product(hidden_own, d_q)
    grad_kv = rows_product(hidden_all[...], dkv)
    rest = grad_kv[0:576, 256:384]
    low = lower_lanes((288, LANES))
    key_tiles = (grad_kv[0:576, 0:128], jnp.where(low, rest[0:288], half_turn(rest[288:576])))
    value_tiles = (grad_kv[0:576, 128:256], jnp.where(low, half_turn(rest[0:288]), rest[288:576]))
    query_tiles = [tiles_of_rows(grad_q[192 * k : 192 * k + 192]) for k in range(3)]
    out_tiles = [tiles_of_rows(grad_out[192 * k : 192 * k + 192]) for k in range(3)]
    store_rows(0, query_tiles[0], query_tiles[1])
    store_rows(1, query_tiles[2], key_tiles)
    store_rows(2, value_tiles, out_tiles[0])
    store_rows(3, out_tiles[1], out_tiles[2])


def run_layer(slots, heads, tails, tokens, cosines, sines, place_q, place_k, gains, bias_q, bias_kv, grad):
    shape = jax.ShapeDtypeStruct
    vmem = pl.BlockSpec(memory_space=pltpu.VMEM)
    anywhere = pl.BlockSpec(memory_space=pl.ANY)
    scratch = [
        ((BLOCKS, HEAD_ROWS, LANES), BF16),
        ((BLOCKS, TAIL_ROWS, LANES), BF16),
        ((WIDE, WIDE), BF16),
        ((WIDE, WIDE), BF16),
        ((WIDE, FF), BF16),
        ((WIDE, FF), BF16),
        ((FF, WIDE), BF16),
        ((1024, WIDE), F32),
        ((1024, WIDE), BF16),
        ((1024, 384), BF16),
        ((1024, 384), BF16),
        ((256, WIDE), BF16),
        ((2, 3, 384, 512), F32),
        ((256, WIDE), BF16),
        ((256, FF), BF16),
        ((256, WIDE), F32),
        ((256, WIDE), F32),
        ((256, WIDE), BF16),
        ((1024, 384), BF16),
        ((256, WIDE), BF16),
    ]
    return pl.pallas_call(
        layer_kernel,
        out_shape=(
            shape((2, ROWS, MODEL_WIDTH), BF16),
            shape((16, HEAD_ROWS, LANES), BF16),
            shape((16, HEAD_ROWS, LANES), BF16),
            shape((16, TAIL_ROWS, LANES), BF16),
            shape((16, TAIL_ROWS, LANES), BF16),
            shape((8, WIDE), F32),
            shape((4, 2, ROWS, 384), BF16),
            shape((256, WIDE), F32),
            shape((256, WIDE), F32),
            shape((WIDE, 384), BF16),
        ),
        in_specs=[pl.BlockSpec(memory_space=pltpu.SMEM)] + [anywhere] * 12 + [vmem] * 9,
        out_specs=(vmem,) * 10,
        scratch_shapes=[pltpu.VMEM(dims, kind) for dims, kind in scratch]
        + [pltpu.SemaphoreType.DMA((12,))],
        compiler_params=pltpu.CompilerParams(vmem_limit_bytes=56 * 1024 * 1024),
        name="layer",
    )(slots, *heads, *tails, tokens, cosines, sines, place_q, place_k, gains, bias_q, bias_kv, grad)


def input_kernel(tokens_ref, gains_ref, w_kv_ref, dq_wq_ref, d_mid_ref, own_ref, one_ref, two_ref, three_ref, out_ref):
    lane = lax.broadcasted_iota(jnp.int32, (2 * ROWS, WIDE), 1)
    x = jnp.where(lane < MODEL_WIDTH, tokens_ref[0].astype(F32).reshape(2 * ROWS, WIDE), 0.0)
    normed, scale = normed_rows(x)
    total = (own_ref[...].astype(F32) + one_ref[...].astype(F32)) + (two_ref[...].astype(F32) + three_ref[...].astype(F32))
    total = total.reshape(2 * ROWS, 384).astype(BF16)
    d_norm = (dq_wq_ref[...] + times_transposed(total, w_kv_ref[...])) * gains_ref[0:1, :]
    d_input = d_mid_ref[...] + scale * (d_norm - normed * row_mean(d_norm * normed))
    out_ref[...] = d_input[:, 0:MODEL_WIDTH].astype(BF16).reshape(2, ROWS, MODEL_WIDTH)


def run_input(tokens, gains, w_kv, dq_wq, d_mid, parts):
    return pl.pallas_call(
        input_kernel,
        out_shape=jax.ShapeDtypeStruct((2, ROWS, MODEL_WIDTH), BF16),
        in_specs=[pl.BlockSpec(memory_space=pltpu.VMEM)] * 9,
        out_specs=pl.BlockSpec(memory_space=pltpu.VMEM),
        name="input_grad",
    )(tokens, gains, w_kv, dq_wq, d_mid, *parts)


def adamw(param, grad, mom_one, mom_two, rate, decay):
    new_one = BETA_ONE * mom_one + (1.0 - BETA_ONE) * grad
    new_two = BETA_TWO * mom_two + (1.0 - BETA_TWO) * grad * grad
    fixed_one = new_one / (1.0 - BETA_ONE**STEP)
    fixed_two = new_two / (1.0 - BETA_TWO**STEP)
    new_param = param - rate * (fixed_one / (jnp.sqrt(fixed_two) + EPS_ADAM) + decay * param)
    return (new_param, new_one, new_two)


def inner_groups():
    inner = inner_count()
    data_inner = inner // lax.axis_size("ctx")
    data_count = lax.axis_size("dp")
    return [list(range(k, k + data_inner)) for k in range(0, data_count, data_inner)]


def whole_block(flat):
    if inner_count() == 1:
        return flat
    flat = lax.all_gather(flat, "ctx", axis=0, tiled=True)
    return lax.all_gather(flat, "dp", axis=0, tiled=True, axis_index_groups=inner_groups())


def own_slice(block):
    if inner_count() == 1:
        return block
    block = lax.psum_scatter(
        block, "dp", scatter_dimension=0, tiled=True, axis_index_groups=inner_groups()
    )
    return lax.psum_scatter(block, "ctx", scatter_dimension=0, tiled=True)


def bias_tiles(bias_key, bias_value):
    return jnp.concatenate([bias_key[:128], bias_value[:128], bias_key[128:], bias_value[128:]])


def local(tokens_in, places, out_grad, weights, first_moment, second_moment, vectors, vector_first, vector_second):
    kind = kind_of(device_number() // inner_count()).astype(jnp.int32).reshape(1)
    slots = slot_table()
    block = whole_block(weights).reshape(BLOCK_ROWS, LANES)
    head, tail = to_tiles(kind, block)

    own_tokens = tokens_in.reshape(2, ROWS, MODEL_WIDTH)
    own_places = places.reshape(2, ROWS)
    marks = jnp.stack([own_places // 16, own_places % 16], axis=-1).astype(BF16)
    packed = jnp.concatenate(
        [own_tokens, marks, jnp.zeros((2, ROWS, WIDE - MODEL_WIDTH - 2), BF16)], axis=-1
    )
    tokens = jnp.stack([packed] + [across(packed, d) for d in (1, 2, 3)])
    heads, tails = gather_blocks(head, tail)

    found = tokens[..., MODEL_WIDTH : MODEL_WIDTH + 2].astype(F32)
    place_all = found[..., 0] * 16.0 + found[..., 1]
    half_dim = HEAD_SIZE // 2
    frequency = THETA ** (-2.0 * jnp.arange(half_dim, dtype=F32) / HEAD_SIZE)
    angles = place_all[..., None] * jnp.tile(frequency, 4)
    sign = jnp.where(jnp.arange(LANES) % HEAD_SIZE < half_dim, -1.0, 1.0).astype(F32)
    cosines = jnp.cos(angles)
    sines = jnp.sin(angles) * sign
    place_q = place_all[0][..., None]
    place_k = jnp.transpose(place_all, (1, 0, 2)).reshape(2, 1, 4 * ROWS)
    padding = ((0, 0), (0, WIDE - MODEL_WIDTH))
    gains = jnp.pad(vectors[: 2 * MODEL_WIDTH].reshape(2, MODEL_WIDTH), padding)
    bias_q = jnp.pad(vectors[2 * MODEL_WIDTH : 3 * MODEL_WIDTH].reshape(1, MODEL_WIDTH), padding)
    bias_kv = bias_tiles(vectors[1728:1920], vectors[1920:2112]).reshape(1, 384)
    grad = jnp.pad(out_grad.reshape(2 * ROWS, MODEL_WIDTH), padding)

    (block_out, head_send, head_keep, tail_send, tail_keep, vector, dkv, dq_wq, d_mid, w_kv) = run_layer(
        slots, heads, tails, tokens, cosines, sines, place_q, place_k, gains, bias_q, bias_kv, grad
    )
    parts = [dkv[0]] + [across(dkv[d], d) for d in (1, 2, 3)]
    input_grad = run_input(tokens, gains, w_kv, dq_wq, d_mid, parts)
    head, tail, vector = scatter_blocks(head_send, head_keep, tail_send, tail_keep, vector)
    if inner_count() > 1:
        vector = lax.psum(vector, "ctx")
        vector = lax.psum(vector, "dp", axis_index_groups=inner_groups())
    grad_own = own_slice(to_flat(kind, head, tail).reshape(-1))
    new_weights, new_first, new_second = adamw(
        weights, grad_own, first_moment, second_moment, RATE_MATRIX, DECAY
    )
    pair = vector[3]
    vector_grad = jnp.concatenate(
        [
            vector[0, :MODEL_WIDTH],
            vector[1, :MODEL_WIDTH],
            vector[2, :MODEL_WIDTH],
            pair[0:128],
            pair[256:320],
            pair[128:256],
            pair[320:384],
        ]
    )
    new_vectors, new_vector_first, new_vector_second = adamw(
        vectors, vector_grad, vector_first, vector_second, RATE_VECTOR, 0.0
    )
    shape = tokens_in.shape
    return (
        block_out.reshape(shape),
        input_grad.reshape(shape),
        new_weights,
        new_first,
        new_second,
        new_vectors,
        new_vector_first,
        new_vector_second,
    )


def solution(mesh):
    in_specs = (
        P(None, "dp", "ctx", None),
        P(None, "dp", "ctx"),
        P(None, "dp", "ctx", None),
        P(("dp", "ctx")),
        P(("dp", "ctx")),
        P(("dp", "ctx")),
        P(),
        P(),
        P(),
    )
    out_specs = (
        P(None, "dp", "ctx", None),
        P(None, "dp", "ctx", None),
        P(("dp", "ctx")),
        P(("dp", "ctx")),
        P(("dp", "ctx")),
        P(),
        P(),
        P(),
    )
    return jax.shard_map(local, mesh=mesh, in_specs=in_specs, out_specs=out_specs, check_vma=False)
```

time: 504 us -> 192 us (0.38)
  waiting for transfers between devices: 274 us -> 75.9 us
  local copies, waits for them, and re-layouts: 80.9 us -> 16 us
  blocking collectives: 60.8 us -> 0 us
  matrix products: 48.1 us -> 0 us
  Pallas kernels: 0 us -> 41.3 us
  starting transfers between devices: 0.16 us -> 40.2 us
  between operations: 15.4 us -> 1.07 us
  other arithmetic: 22.9 us -> 17 us
    unnamed x5 -> x0, waiting for transfers between devices: 197 us -> none
    ppermute x0 -> x41, waiting for transfers between devices: none -> 75.9 us  [the longest x35 65.1 us: moved(): return lax.ppermute(buffer, ('dp', 'ctx'), pairs)]
    all_gather x1 -> x0, waiting for transfers between devices: 63.4 us -> none  [local(): lax.all_gather(low_weights, ('dp', 'ctx'), axis=0, tiled=True)]
    dot_general x47 -> x0, matrix products: 48.1 us -> none  [the longest x7 13.7 us: rows_product(): lax.dot_general(left, right, (((0,), (0,)), ((), ())), preferred_element_...]
    psum x1 -> x0, blocking collectives: 41.4 us -> none  [local(): grad_vector_all = lax.psum(grad_vectors, ('dp', 'ctx'))]
    pallas_call x0 -> x4, Pallas kernels: none -> 41.3 us  [the longest x1 34.1 us: run_layer(): pl.pallas_call(layer_kernel, out_shape=(shape((2, ROWS, MODEL_WIDTH), BF1...]
    ppermute x0 -> x41, starting transfers between devices: none -> 40.2 us  [the longest x35 37.1 us: moved(): return lax.ppermute(buffer, ('dp', 'ctx'), pairs)]
    reshape x8 -> x5, local copies, waits for them, and re-layouts: 27.3 us -> 2.05 us  [the longest x1 0.8 us: local(): own_places = places.reshape(2, ROWS)]
  transfers between devices with their start and end apart: 4 -> 41, of which waited for: 3 -> 14; matrix products, arithmetic and copies ran while one was open for 10% -> 12% of each run, Pallas kernels for 0% -> 2%
where the time goes in v1:
time: 192 us; the launch traced here: 191 us
  waiting for transfers between devices  75.9 us (40%)
  Pallas kernels  41.3 us (22%)
  starting transfers between devices  40.2 us (21%)
  other arithmetic  17 us (9%)
  local copies, waits for them, and re-layouts  16 us (8%)
    ppermute x35, waiting for transfers between devices, moved(): return lax.ppermute(buffer, ('dp', 'ctx'), pairs)  65.1 us
    ppermute x35, starting transfers between devices, moved(): return lax.ppermute(buffer, ('dp', 'ctx'), pairs)  37.1 us
    pallas_call x1, Pallas kernels, run_layer(): pl.pallas_call(layer_kernel, out_shape=(shape((2, ROWS, MODEL_WIDTH), BF1...  34.1 us
    ppermute x6, waiting for transfers between devices, across(): lax.ppermute(buffer, 'ctx', [(i, i ^ distance) for i in range(count)])  10.8 us
    unnamed x61, local copies, waits for them, and re-layouts  7.81 us
    add x4, other arithmetic, summed(): return kept.astype(F32) + received.astype(F32)  4.56 us
  transfers between devices with their start and end apart: 41, of which 14 were waited for; matrix products, arithmetic and copies ran while one was open for 12% of the time, Pallas kernels for 2%

profile of v1, /device:TPU:0, one launch (start us, length us, event | category | flops | bytes accessed | tf_op | source)
XLA Modules:
  0.0 191.4 jit_solution(2456591144935257404)
XLA Ops:
  0.7 1.9 to_tiles.1
  2.5 5.0 %collective-permute-start.3 = (bf16[576,128]{1,0:T(8,128)(2,1)}, bf16[576,128]{1,0:T(8,128)(2,1)S(1)}, u32[]{:S(2)}, u32[]{:S(2)}) collective-permute-start(bf16[576,128]{1,0:T(8,128)(2,1)} %get-tuple-element.48), channel_id=1, source_target_pairs={{0,24},{1,25},{2,26},{3,27},{4,28},{5,29},{6,30},{7,31},{8,0},{9,1... | collective-permute-start | bytes 442376 | tf_op jit(solution)/shard_map/ppermute | solution.py:68
  13.9 6.3 %collective-permute-done.2 = bf16[576,128]{1,0:T(8,128)(2,1)S(1)} collective-permute-done((bf16[576,128]{1,0:T(8,128)(2,1)}, bf16[576,128]{1,0:T(8,128)(2,1)S(1)}, u32[]{:S(2)}, u32[]{:S(2)}) %collective-permute-start.2) | collective-permute-done | bytes 147488 | tf_op jit(solution)/shard_map/ppermute | solution.py:68
  21.2 1.6 collective-permute-start.5
  24.4 1.6 collective-permute-start.8
  27.3 1.9 %collective-permute-start.6 = (bf16[2,288,128]{2,1,0:T(8,128)(2,1)S(1)}, bf16[2,288,128]{2,1,0:T(8,128)(2,1)}, u32[]{:S(2)}, u32[]{:S(2)}) collective-permute-start(bf16[2,288,128]{2,1,0:T(8,128)(2,1)S(1)} %pad_maximum_fusion.2), channel_id=1, source_target_pairs={{0,8},{1,9},{2,10},{3,11},{4,12},{5,13},{6,14},{7,15},{8,16},{9,17... | collective-permute-start | bytes 442376 | tf_op jit(solution)/shard_map/ppermute | solution.py:68
  33.5 5.9 %collective-permute-done.7 = bf16[2,288,128]{2,1,0:T(8,128)(2,1)} collective-permute-done((bf16[2,288,128]{2,1,0:T(8,128)(2,1)S(1)}, bf16[2,288,128]{2,1,0:T(8,128)(2,1)}, u32[]{:S(2)}, u32[]{:S(2)}) %collective-permute-start.7) | collective-permute-done | bytes 147488 | tf_op jit(solution)/shard_map/ppermute | solution.py:68
  43.3 2.4 %collective-permute-start.9 = (bf16[4,576,128]{2,1,0:T(8,128)(2,1)S(1)}, bf16[4,576,128]{2,1,0:T(8,128)(2,1)S(1)}, u32[]{:S(2)}, u32[]{:S(2)}) collective-permute-start(bf16[4,576,128]{2,1,0:T(8,128)(2,1)S(1)} %collective-permute-done.4.refs_2_), channel_id=1, source_target_pairs={{0,2},{1,3},{2,0},{3,1},{4,6},{5,7},{6,4},{7,5},{8,10},{9,11},{10,... | collective-permute-start | bytes 1769480 | tf_op jit(solution)/shard_map/ppermute | solution.py:68
  45.9 4.4 %collective-permute-done.19 = bf16[2,128,640]{2,1,0:T(8,128)(2,1)S(1)} collective-permute-done((bf16[2,128,640]{2,1,0:T(8,128)(2,1)S(1)}, bf16[2,128,640]{2,1,0:T(8,128)(2,1)S(1)}, u32[]{:S(2)}, u32[]{:S(2)}) %collective-permute-start.19) | collective-permute-done | bytes 327712 | tf_op jit(solution)/shard_map/ppermute | solution.py:73
  51.2 6.8 %collective-permute-done.10.refs_10_ = bf16[8,288,128]{2,1,0:T(8,128)(2,1)S(1)} collective-permute-done((bf16[8,288,128]{2,1,0:T(8,128)(2,1)S(1)}, bf16[8,288,128]{2,1,0:T(8,128)(2,1)S(1)}, u32[]{:S(2)}, u32[]{:S(2)}) %collective-permute-start.10) | collective-permute-done | bytes 589856 | tf_op jit(solution)/shard_map/ppermute | solution.py:68
  58.1 4.5 %collective-permute-done.9.refs_4_ = bf16[4,576,128]{2,1,0:T(8,128)(2,1)S(1)} collective-permute-done((bf16[4,576,128]{2,1,0:T(8,128)(2,1)S(1)}, bf16[4,576,128]{2,1,0:T(8,128)(2,1)S(1)}, u32[]{:S(2)}, u32[]{:S(2)}) %collective-permute-start.9) | collective-permute-done | bytes 589856 | tf_op jit(solution)/shard_map/ppermute | solution.py:68
  64.7 3.0 %fusion.1 = (f32[4,2,128,128]{3,2,1,0:T(8,128)}, f32[4,2,128,128]{3,2,1,0:T(8,128)}) fusion(f32[128]{0:T(128)S(1)} %compare_select_fusion, f32[128]{0:T(128)S(1)} %mul.226, f32[4,2,128]{2,1,0:T(2,128)S(1)} %get-tuple-element.109), kind=kLoop, calls=%fused_computation.12 | loop fusion | flops 262144 | bytes 1053696 | tf_op jit(solution)/shard_map/mul | solution.py:730
  69.4 34.1 %layer.1 = (bf16[2,128,576]{2,1,0:T(8,128)(2,1)}, bf16[16,576,128]{2,1,0:T(8,128)(2,1)}, bf16[16,576,128]{2,1,0:T(8,128)(2,1)}, bf16[16,288,128]{2,1,0:T(8,128)(...) custom-call(s32[97]{0:T(128)} %stack.449.refs_0_, ...), custom_call_target="tpu_custom_call" | custom-call | tf_op jit(solution)/shard_map/layer/pallas_call | solution.py:628
  104.1 5.9 %collective-permute-done.25 = f32[8,640]{1,0:T(8,128)S(1)} collective-permute-done((f32[8,640]{1,0:T(8,128)}, f32[8,640]{1,0:T(8,128)S(1)}, u32[]{:S(2)}, u32[]{:S(2)}) %collective-permute-start.25) | collective-permute-done | bytes 20512 | tf_op jit(solution)/shard_map/ppermute | solution.py:68
  110.0 2.3 %add_convert_fusion = (bf16[8,576,128]{2,1,0:T(8,128)(2,1)S(1)}, f32[8,576,128]{2,1,0:T(8,128)S(1)}) fusion(bf16[16,576,128]{2,1,0:T(8,128)(2,1)S(1)} %collective-permute-done.23, bf16[16,576,128]{2,1,0:T(8,128)(2,1)} %get-tuple-element.68), kind=kLoop, calls=%fused_computation | loop fusion | flops 4128768 | bytes 8257536 | tf_op jit(solution)/shard_map/convert_element_type | solution.py:137
  114.1 1.6 collective-permute-start.27
  116.2 24.6 %collective-permute-done.28 = f32[8,640]{1,0:T(8,128)S(1)} collective-permute-done((f32[8,640]{1,0:T(8,128)S(1)}, f32[8,640]{1,0:T(8,128)S(1)}, u32[]{:S(2)}, u32[]{:S(2)}) %collective-permute-start.28) | collective-permute-done | bytes 20512 | tf_op jit(solution)/shard_map/ppermute | solution.py:68
  141.0 1.6 collective-permute-start.29
  146.4 4.2 %collective-permute-done.22.three_ref = bf16[2,128,384]{2,1,0:T(8,128)(2,1)S(1)} collective-permute-done((bf16[2,128,384]{2,1,0:T(8,128)(2,1)S(1)}, bf16[2,128,384]{2,1,0:T(8,128)(2,1)S(1)}, u32[]{:S(2)}, u32[]{:S(2)}) %collective-permute-start.22) | collective-permute-done | bytes 196640 | tf_op jit(solution)/shard_map/ppermute | solution.py:73
  150.5 2.5 %collective-permute-start.32 = (bf16[2,288,128]{2,1,0:T(8,128)(2,1)}, bf16[2,288,128]{2,1,0:T(8,128)(2,1)}, u32[]{:S(2)}, u32[]{:S(2)}) collective-permute-start(bf16[2,288,128]{2,1,0:T(8,128)(2,1)} %get-tuple-element.119), channel_id=1, source_target_pairs={{0,16},{1,17},{2,18},{3,19},{4,20},{5,21},{6,22},{7,23},{8,24},{9,... | collective-permute-start | bytes 442376 | tf_op jit(solution)/shard_map/ppermute | solution.py:68
  153.0 1.8 collective-permute-done.21.two_ref
  157.2 3.3 %input_grad.1 = bf16[2,128,576]{2,1,0:T(8,128)(2,1)} custom-call(bf16[4,2,128,640]{3,2,1,0:T(8,128)(2,1)} %copy-done, f32[2,640]{1,0:T(2,128)} %pad.12.refs_18_.gains_ref, bf16[640,384]{1,0:T(8,128)(2,1)} %get-tuple-element.64.w_kv_ref, f32[256,640]{1,0:T(8,128)} %get-tuple-element.65.dq_wq_ref, f32[256,640]{1,0:T(8,128)} %get-tuple-element.66.d_mid_ref, ...), custom_call_target="tpu_custom_call" | custom-call | tf_op jit(solution)/shard_map/input_grad/pallas_call | solution.py:663
  160.5 1.9 copy.31
  162.4 1.7 collective-permute-done.32
  164.1 1.6 collective-permute-start.40
  169.3 2.4 %collective-permute-start.34 = (bf16[576,128]{1,0:T(8,128)(2,1)}, bf16[576,128]{1,0:T(8,128)(2,1)S(1)}, u32[]{:S(2)}, u32[]{:S(2)}) collective-permute-start(bf16[576,128]{1,0:T(8,128)(2,1)} %get-tuple-element.121), channel_id=1, source_target_pairs={{0,8},{1,9},{2,10},{3,11},{4,12},{5,13},{6,14},{7,15},{8,16},{9,17... | collective-permute-start | bytes 442376 | tf_op jit(solution)/shard_map/ppermute | solution.py:68
  174.3 1.7 fusion.20.tail_ref
  176.0 2.2 %collective-permute-done.34 = bf16[576,128]{1,0:T(8,128)(2,1)S(1)} collective-permute-done((bf16[576,128]{1,0:T(8,128)(2,1)}, bf16[576,128]{1,0:T(8,128)(2,1)S(1)}, u32[]{:S(2)}, u32[]{:S(2)}) %collective-permute-start.34) | collective-permute-done | bytes 147488 | tf_op jit(solution)/shard_map/ppermute | solution.py:68
  179.1 6.3 %collective-permute-done.35 = bf16[576,128]{1,0:T(8,128)(2,1)} collective-permute-done((bf16[576,128]{1,0:T(8,128)(2,1)S(1)}, bf16[576,128]{1,0:T(8,128)(2,1)}, u32[]{:S(2)}, u32[]{:S(2)}) %collective-permute-start.35) | collective-permute-done | bytes 147488 | tf_op jit(solution)/shard_map/ppermute | solution.py:68
  185.4 1.8 fusion.12.head_ref
  187.2 2.0 %to_flat.1 = f32[864,128]{1,0:T(8,128)} custom-call(s32[1]{0:T(128)} %bitcast.97.kind_ref, f32[576,128]{1,0:T(8,128)} %fusion.12.head_ref, f32[288,128]{1,0:T(8,128)} %fusion.20.tail_ref), custom_call_target="tpu_custom_call" | custom-call | tf_op jit(solution)/shard_map/to_flat/pallas_call | solution.py:279
  189.2 2.3 %multiply_subtract_fusion = (f32[110592]{0:T(1024)}, f32[110592]{0:T(1024)}, f32[110592]{0:T(1024)}) fusion(f32[110592]{0:T(1024)S(1)} %copy-done.2, f32[864,128]{1,0:T(8,128)} %to_flat.1, f32[110592]{0:T(1024)S(1)} %copy-done.16, f32[110592]{0:T(1024)S(1)} %copy-done.17), kind=kLoop, calls=%fused_computation.18 | loop fusion | flops 1658880 | bytes 3096576 | tf_op jit(solution)/shard_map/sub | solution.py:677
  (167 shorter events, 39.5 us)
Async XLA Ops:
  2.5 11.4 %collective-permute-start.3 = (bf16[576,128]{1,0:T(8,128)(2,1)}, bf16[576,128]{1,0:T(8,128)(2,1)S(1)}, u32[]{:S(2)}, u32[]{:S(2)}) collective-permute-start(bf16[576,128]{1,0:T(8,128)(2,1)} %get-tuple-element.48), channel_id=1, source_target_pairs={{0,24},{1,25},{2,26},{3,27},{4,28},{5,29},{6,30},{7,31},{8,0},{9,1... | collective-permute-start | bytes 442376 | tf_op jit(solution)/shard_map/ppermute | solution.py:68
  7.6 12.6 %collective-permute-start.2 = (bf16[576,128]{1,0:T(8,128)(2,1)}, bf16[576,128]{1,0:T(8,128)(2,1)S(1)}, u32[]{:S(2)}, u32[]{:S(2)}) collective-permute-start(bf16[576,128]{1,0:T(8,128)(2,1)} %get-tuple-element.48), channel_id=1, source_target_pairs={{0,16},{1,17},{2,18},{3,19},{4,20},{5,21},{6,22},{7,23},{8,24},{9,... | collective-permute-start | bytes 442376 | tf_op jit(solution)/shard_map/ppermute | solution.py:68
  7.6 12.6 %collective-permute-start.1 = (bf16[576,128]{1,0:T(8,128)(2,1)}, bf16[576,128]{1,0:T(8,128)(2,1)S(1)}, u32[]{:S(2)}, u32[]{:S(2)}) collective-permute-start(bf16[576,128]{1,0:T(8,128)(2,1)} %get-tuple-element.48), channel_id=1, source_target_pairs={{0,8},{1,9},{2,10},{3,11},{4,12},{5,13},{6,14},{7,15},{8,16},{9,17... | collective-permute-start | bytes 442376 | tf_op jit(solution)/shard_map/ppermute | solution.py:68
  21.2 18.9 %collective-permute-start.5 = (bf16[4,576,128]{2,1,0:T(8,128)(2,1)S(1)}, bf16[4,576,128]{2,1,0:T(8,128)(2,1)S(1)}, u32[]{:S(2)}, u32[]{:S(2)}) collective-permute-start(bf16[4,576,128]{2,1,0:T(8,128)(2,1)S(1)} %pad_maximum_fusion.1.refs_1_), channel_id=1, source_target_pairs={{0,2},{1,3},{2,0},{3,1},{4,6},{5,7},{6,4},{7,5},{8,10},{9,11},{10,... | collective-permute-start | bytes 1769480 | tf_op jit(solution)/shard_map/ppermute | solution.py:68
  22.8 17.4 %collective-permute-start.4 = (bf16[4,576,128]{2,1,0:T(8,128)(2,1)S(1)}, bf16[4,576,128]{2,1,0:T(8,128)(2,1)S(1)}, u32[]{:S(2)}, u32[]{:S(2)}) collective-permute-start(bf16[4,576,128]{2,1,0:T(8,128)(2,1)S(1)} %pad_maximum_fusion.1.refs_1_), channel_id=1, source_target_pairs={{0,4},{1,5},{2,6},{3,7},{4,0},{5,1},{6,2},{7,3},{8,12},{9,13},{10,... | collective-permute-start | bytes 1769480 | tf_op jit(solution)/shard_map/ppermute | solution.py:68
  24.4 8.5 %collective-permute-start.8 = (bf16[2,288,128]{2,1,0:T(8,128)(2,1)S(1)}, bf16[2,288,128]{2,1,0:T(8,128)(2,1)S(1)}, u32[]{:S(2)}, u32[]{:S(2)}) collective-permute-start(bf16[2,288,128]{2,1,0:T(8,128)(2,1)S(1)} %pad_maximum_fusion.2), channel_id=1, source_target_pairs={{0,24},{1,25},{2,26},{3,27},{4,28},{5,29},{6,30},{7,31},{8,0},{9,1... | collective-permute-start | bytes 442376 | tf_op jit(solution)/shard_map/ppermute | solution.py:68
  26.0 13.4 %collective-permute-start.7 = (bf16[2,288,128]{2,1,0:T(8,128)(2,1)S(1)}, bf16[2,288,128]{2,1,0:T(8,128)(2,1)}, u32[]{:S(2)}, u32[]{:S(2)}) collective-permute-start(bf16[2,288,128]{2,1,0:T(8,128)(2,1)S(1)} %pad_maximum_fusion.2), channel_id=1, source_target_pairs={{0,16},{1,17},{2,18},{3,19},{4,20},{5,21},{6,22},{7,23},{8,24},{9,... | collective-permute-start | bytes 442376 | tf_op jit(solution)/shard_map/ppermute | solution.py:68
  27.3 12.1 %collective-permute-start.6 = (bf16[2,288,128]{2,1,0:T(8,128)(2,1)S(1)}, bf16[2,288,128]{2,1,0:T(8,128)(2,1)}, u32[]{:S(2)}, u32[]{:S(2)}) collective-permute-start(bf16[2,288,128]{2,1,0:T(8,128)(2,1)S(1)} %pad_maximum_fusion.2), channel_id=1, source_target_pairs={{0,8},{1,9},{2,10},{3,11},{4,12},{5,13},{6,14},{7,15},{8,16},{9,17... | collective-permute-start | bytes 442376 | tf_op jit(solution)/shard_map/ppermute | solution.py:68
  33.0 10.3 %collective-permute-start.18 = (bf16[2,128,640]{2,1,0:T(8,128)(2,1)S(1)}, bf16[2,128,640]{2,1,0:T(8,128)(2,1)S(1)}, u32[]{:S(2)}, u32[]{:S(2)}) collective-permute-start(bf16[2,128,640]{2,1,0:T(8,128)(2,1)S(1)} %maximum_maximum_fusion), channel_id=1, source_target_pairs={{0,2},{1,3},{2,0},{3,1},{4,6},{5,7},{6,4},{7,5},{8,10},{9,11},{10,... | collective-permute-start | bytes 983048 | tf_op jit(solution)/shard_map/ppermute | solution.py:73
  39.4 10.9 %collective-permute-start.19 = (bf16[2,128,640]{2,1,0:T(8,128)(2,1)S(1)}, bf16[2,128,640]{2,1,0:T(8,128)(2,1)S(1)}, u32[]{:S(2)}, u32[]{:S(2)}) collective-permute-start(bf16[2,128,640]{2,1,0:T(8,128)(2,1)S(1)} %maximum_maximum_fusion), channel_id=1, source_target_pairs={{0,3},{1,2},{2,1},{3,0},{4,7},{5,6},{6,5},{7,4},{8,11},{9,10},{10,... | collective-permute-start | bytes 983048 | tf_op jit(solution)/shard_map/ppermute | solution.py:73
  40.1 22.5 %collective-permute-start.11 = (bf16[4,576,128]{2,1,0:T(8,128)(2,1)S(1)}, bf16[4,576,128]{2,1,0:T(8,128)(2,1)S(1)}, u32[]{:S(2)}, u32[]{:S(2)}) collective-permute-start(bf16[4,576,128]{2,1,0:T(8,128)(2,1)S(1)} %pad_maximum_fusion.1.refs_1_), channel_id=1, source_target_pairs={{0,1},{1,0},{2,3},{3,2},{4,5},{5,4},{6,7},{7,6},{8,9},{9,8},{10,11... | collective-permute-start | bytes 1769480 | tf_op jit(solution)/shard_map/ppermute | solution.py:68
  42.3 15.8 %collective-permute-start.10 = (bf16[8,288,128]{2,1,0:T(8,128)(2,1)S(1)}, bf16[8,288,128]{2,1,0:T(8,128)(2,1)S(1)}, u32[]{:S(2)}, u32[]{:S(2)}) collective-permute-start(bf16[8,288,128]{2,1,0:T(8,128)(2,1)S(1)} %constant_dynamic-update-slice_fusion.refs_9_), channel_id=1, source_target_pairs={{0,4},{1,5},{2,6},{3,7},{4,0},{5,1},{6,2},{7,3},{8,12},{9,13},{10,... | collective-permute-start | bytes 1769480 | tf_op jit(solution)/shard_map/ppermute | solution.py:68
  43.3 19.2 %collective-permute-start.9 = (bf16[4,576,128]{2,1,0:T(8,128)(2,1)S(1)}, bf16[4,576,128]{2,1,0:T(8,128)(2,1)S(1)}, u32[]{:S(2)}, u32[]{:S(2)}) collective-permute-start(bf16[4,576,128]{2,1,0:T(8,128)(2,1)S(1)} %collective-permute-done.4.refs_2_), channel_id=1, source_target_pairs={{0,2},{1,3},{2,0},{3,1},{4,6},{5,7},{6,4},{7,5},{8,10},{9,11},{10,... | collective-permute-start | bytes 1769480 | tf_op jit(solution)/shard_map/ppermute | solution.py:68
  50.6 17.1 %collective-permute-start.15 = (bf16[8,288,128]{2,1,0:T(8,128)(2,1)S(1)}, bf16[8,288,128]{2,1,0:T(8,128)(2,1)S(1)}, u32[]{:S(2)}, u32[]{:S(2)}) collective-permute-start(bf16[8,288,128]{2,1,0:T(8,128)(2,1)S(1)} %constant_dynamic-update-slice_fusion.refs_9_), channel_id=1, source_target_pairs={{0,1},{1,0},{2,3},{3,2},{4,5},{5,4},{6,7},{7,6},{8,9},{9,8},{10,11... | collective-permute-start | bytes 1769480 | tf_op jit(solution)/shard_map/ppermute | solution.py:68
  50.8 16.9 %collective-permute-start.12 = (bf16[4,576,128]{2,1,0:T(8,128)(2,1)S(1)}, bf16[4,576,128]{2,1,0:T(8,128)(2,1)S(1)}, u32[]{:S(2)}, u32[]{:S(2)}) collective-permute-start(bf16[4,576,128]{2,1,0:T(8,128)(2,1)S(1)} %collective-permute-done.4.refs_2_), channel_id=1, source_target_pairs={{0,1},{1,0},{2,3},{3,2},{4,5},{5,4},{6,7},{7,6},{8,9},{9,8},{10,11... | collective-permute-start | bytes 1769480 | tf_op jit(solution)/shard_map/ppermute | solution.py:68
  58.0 9.7 %collective-permute-start.13 = (bf16[4,576,128]{2,1,0:T(8,128)(2,1)S(1)}, bf16[4,576,128]{2,1,0:T(8,128)(2,1)S(1)}, u32[]{:S(2)}, u32[]{:S(2)}) collective-permute-start(bf16[4,576,128]{2,1,0:T(8,128)(2,1)S(1)} %collective-permute-done.5.refs_3_), channel_id=1, source_target_pairs={{0,1},{1,0},{2,3},{3,2},{4,5},{5,4},{6,7},{7,6},{8,9},{9,8},{10,11... | collective-permute-start | bytes 1769480 | tf_op jit(solution)/shard_map/ppermute | solution.py:68
  112.3 28.5 %collective-permute-start.26 = (bf16[8,576,128]{2,1,0:T(8,128)(2,1)S(1)}, bf16[8,576,128]{2,1,0:T(8,128)(2,1)S(1)}, u32[]{:S(2)}, u32[]{:S(2)}) collective-permute-start(bf16[8,576,128]{2,1,0:T(8,128)(2,1)S(1)} %get-tuple-element.111), channel_id=1, source_target_pairs={{0,2},{1,3},{2,0},{3,1},{4,6},{5,7},{6,4},{7,5},{8,10},{9,11},{10,... | collective-permute-start | bytes 3538952 | tf_op jit(solution)/shard_map/ppermute | solution.py:68
  114.1 26.7 %collective-permute-start.27 = (bf16[8,288,128]{2,1,0:T(8,128)(2,1)S(1)}, bf16[8,288,128]{2,1,0:T(8,128)(2,1)S(1)}, u32[]{:S(2)}, u32[]{:S(2)}) collective-permute-start(bf16[8,288,128]{2,1,0:T(8,128)(2,1)S(1)} %get-tuple-element.116), channel_id=1, source_target_pairs={{0,4},{1,5},{2,6},{3,7},{4,0},{5,1},{6,2},{7,3},{8,12},{9,13},{10,... | collective-permute-start | bytes 1769480 | tf_op jit(solution)/shard_map/ppermute | solution.py:68
  115.7 25.1 %collective-permute-start.28 = (f32[8,640]{1,0:T(8,128)S(1)}, f32[8,640]{1,0:T(8,128)S(1)}, u32[]{:S(2)}, u32[]{:S(2)}) collective-permute-start(f32[8,640]{1,0:T(8,128)S(1)} %add.1320), channel_id=1, source_target_pairs={{0,2},{1,3},{2,0},{3,1},{4,6},{5,7},{6,4},{7,5},{8,10},{9,11},{10,... | collective-permute-start | bytes 61448 | tf_op jit(solution)/shard_map/ppermute | solution.py:68
  141.0 23.1 %collective-permute-start.29 = (bf16[4,576,128]{2,1,0:T(8,128)(2,1)S(1)}, bf16[4,576,128]{2,1,0:T(8,128)(2,1)S(1)}, u32[]{:S(2)}, u32[]{:S(2)}) collective-permute-start(bf16[4,576,128]{2,1,0:T(8,128)(2,1)S(1)} %get-tuple-element.113), channel_id=1, source_target_pairs={{0,4},{1,5},{2,6},{3,7},{4,0},{5,1},{6,2},{7,3},{8,12},{9,13},{10,... | collective-permute-start | bytes 1769480 | tf_op jit(solution)/shard_map/ppermute | solution.py:68
  143.4 7.2 %collective-permute-start.22 = (bf16[2,128,384]{2,1,0:T(8,128)(2,1)S(1)}, bf16[2,128,384]{2,1,0:T(8,128)(2,1)S(1)}, u32[]{:S(2)}, u32[]{:S(2)}) collective-permute-start(bf16[2,128,384]{2,1,0:T(8,128)(2,1)S(1)} %get-tuple-element.124), channel_id=1, source_target_pairs={{0,3},{1,2},{2,1},{3,0},{4,7},{5,6},{6,5},{7,4},{8,11},{9,10},{10,... | collective-permute-start | bytes 589832 | tf_op jit(solution)/shard_map/ppermute | solution.py:73
  143.5 11.3 %collective-permute-start.21 = (bf16[2,128,384]{2,1,0:T(8,128)(2,1)S(1)}, bf16[2,128,384]{2,1,0:T(8,128)(2,1)S(1)}, u32[]{:S(2)}, u32[]{:S(2)}) collective-permute-start(bf16[2,128,384]{2,1,0:T(8,128)(2,1)S(1)} %get-tuple-element.125), channel_id=1, source_target_pairs={{0,2},{1,3},{2,0},{3,1},{4,6},{5,7},{6,4},{7,5},{8,10},{9,11},{10,... | collective-permute-start | bytes 589832 | tf_op jit(solution)/shard_map/ppermute | solution.py:73
  144.9 10.7 %collective-permute-start.20 = (bf16[2,128,384]{2,1,0:T(8,128)(2,1)S(1)}, bf16[2,128,384]{2,1,0:T(8,128)(2,1)}, u32[]{:S(2)}, u32[]{:S(2)}) collective-permute-start(bf16[2,128,384]{2,1,0:T(8,128)(2,1)S(1)} %get-tuple-element.126), channel_id=1, source_target_pairs={{0,1},{1,0},{2,3},{3,2},{4,5},{5,4},{6,7},{7,6},{8,9},{9,8},{10,11... | collective-permute-start | bytes 589832 | tf_op jit(solution)/shard_map/ppermute | solution.py:73
  146.1 16.3 %collective-permute-start.33 = (bf16[2,288,128]{2,1,0:T(8,128)(2,1)}, bf16[2,288,128]{2,1,0:T(8,128)(2,1)}, u32[]{:S(2)}, u32[]{:S(2)}) collective-permute-start(bf16[2,288,128]{2,1,0:T(8,128)(2,1)} %get-tuple-element.118), channel_id=1, source_target_pairs={{0,24},{1,25},{2,26},{3,27},{4,28},{5,29},{6,30},{7,31},{8,0},{9,1... | collective-permute-start | bytes 442376 | tf_op jit(solution)/shard_map/ppermute | solution.py:68
  150.5 13.6 %collective-permute-start.32 = (bf16[2,288,128]{2,1,0:T(8,128)(2,1)}, bf16[2,288,128]{2,1,0:T(8,128)(2,1)}, u32[]{:S(2)}, u32[]{:S(2)}) collective-permute-start(bf16[2,288,128]{2,1,0:T(8,128)(2,1)} %get-tuple-element.119), channel_id=1, source_target_pairs={{0,16},{1,17},{2,18},{3,19},{4,20},{5,21},{6,22},{7,23},{8,24},{9,... | collective-permute-start | bytes 442376 | tf_op jit(solution)/shard_map/ppermute | solution.py:68
  154.8 9.3 %collective-permute-start.31 = (bf16[2,288,128]{2,1,0:T(8,128)(2,1)}, bf16[2,288,128]{2,1,0:T(8,128)(2,1)}, u32[]{:S(2)}, u32[]{:S(2)}) collective-permute-start(bf16[2,288,128]{2,1,0:T(8,128)(2,1)} %get-tuple-element.120), channel_id=1, source_target_pairs={{0,8},{1,9},{2,10},{3,11},{4,12},{5,13},{6,14},{7,15},{8,16},{9,17... | collective-permute-start | bytes 442376 | tf_op jit(solution)/shard_map/ppermute | solution.py:68
  164.1 7.5 %collective-permute-start.40 = (f32[8,640]{1,0:T(8,128)S(1)}, f32[8,640]{1,0:T(8,128)S(1)}, u32[]{:S(2)}, u32[]{:S(2)}) collective-permute-start(f32[8,640]{1,0:T(8,128)S(1)} %add.1350), channel_id=1, source_target_pairs={{0,24},{1,25},{2,26},{3,27},{4,28},{5,29},{6,30},{7,31},{8,0},{9,1... | collective-permute-start | bytes 61448 | tf_op jit(solution)/shard_map/ppermute | solution.py:68
  165.7 7.4 %collective-permute-start.39 = (f32[8,640]{1,0:T(8,128)S(1)}, f32[8,640]{1,0:T(8,128)S(1)}, u32[]{:S(2)}, u32[]{:S(2)}) collective-permute-start(f32[8,640]{1,0:T(8,128)S(1)} %add.1350), channel_id=1, source_target_pairs={{0,16},{1,17},{2,18},{3,19},{4,20},{5,21},{6,22},{7,23},{8,24},{9,... | collective-permute-start | bytes 61448 | tf_op jit(solution)/shard_map/ppermute | solution.py:68
  166.5 7.0 %collective-permute-start.38 = (f32[8,640]{1,0:T(8,128)S(1)}, f32[8,640]{1,0:T(8,128)S(1)}, u32[]{:S(2)}, u32[]{:S(2)}) collective-permute-start(f32[8,640]{1,0:T(8,128)S(1)} %add.1350), channel_id=1, source_target_pairs={{0,8},{1,9},{2,10},{3,11},{4,12},{5,13},{6,14},{7,15},{8,16},{9,17... | collective-permute-start | bytes 61448 | tf_op jit(solution)/shard_map/ppermute | solution.py:68
  169.3 8.9 %collective-permute-start.34 = (bf16[576,128]{1,0:T(8,128)(2,1)}, bf16[576,128]{1,0:T(8,128)(2,1)S(1)}, u32[]{:S(2)}, u32[]{:S(2)}) collective-permute-start(bf16[576,128]{1,0:T(8,128)(2,1)} %get-tuple-element.121), channel_id=1, source_target_pairs={{0,8},{1,9},{2,10},{3,11},{4,12},{5,13},{6,14},{7,15},{8,16},{9,17... | collective-permute-start | bytes 442376 | tf_op jit(solution)/shard_map/ppermute | solution.py:68
  171.6 7.5 %collective-permute-start.36 = (bf16[576,128]{1,0:T(8,128)(2,1)}, bf16[576,128]{1,0:T(8,128)(2,1)}, u32[]{:S(2)}, u32[]{:S(2)}) collective-permute-start(bf16[576,128]{1,0:T(8,128)(2,1)} %get-tuple-element.122), channel_id=1, source_target_pairs={{0,24},{1,25},{2,26},{3,27},{4,28},{5,29},{6,30},{7,31},{8,0},{9,1... | collective-permute-start | bytes 442376 | tf_op jit(solution)/shard_map/ppermute | solution.py:68
  173.1 12.3 %collective-permute-start.35 = (bf16[576,128]{1,0:T(8,128)(2,1)S(1)}, bf16[576,128]{1,0:T(8,128)(2,1)}, u32[]{:S(2)}, u32[]{:S(2)}) collective-permute-start(bf16[576,128]{1,0:T(8,128)(2,1)S(1)} %get-tuple-element.123), channel_id=1, source_target_pairs={{0,16},{1,17},{2,18},{3,19},{4,20},{5,21},{6,22},{7,23},{8,24},{9,... | collective-permute-start | bytes 442376 | tf_op jit(solution)/shard_map/ppermute | solution.py:68
  (37 other events, 270.2 us)

commit v2 on v1

--- a/solution.py
+++ b/solution.py
@@ -77,27 +77,44 @@
     return lax.optimization_barrier(arrays)
 
 
-def gather_blocks(head, tail):
+def gather_all(head, tail, packed):
     hz = [moved(head, "z", s) for s in (1, 2, 3)]
     tx = moved(tail, "x", 1)
-    head, tail, tx, *hz = together(head, tail, tx, *hz)
+    two = across(packed, 2)
+    one = across(packed, 1)
+    head, tail, tx, one, two, *hz = together(head, tail, tx, one, two, *hz)
     own = jnp.stack([head] + hz)
     pair = jnp.stack([tail, tx])
     ay = moved(own, "y", 1)
     ax = moved(own, "x", 1)
     ac = moved(own, "c", 1)
     tz = [moved(pair, "z", s) for s in (1, 2, 3)]
-    own, pair, ay, ax, *tz = together(own, pair, ay, ax, *tz)
+    three = across(two, 1)
+    own, pair, ay, ax, three, *tz = together(own, pair, ay, ax, three, *tz)
+    tokens = jnp.stack([packed, one, two, three])
+    tables = place_tables(tokens)
     eight = jnp.concatenate([pair] + tz)
     axy = moved(ay, "x", 1)
     ty = moved(eight, "y", 1)
     acy = moved(ay, "c", 1)
     acx = moved(ax, "c", 1)
     tc = moved(eight, "c", 1)
-    axy, ty = together(axy, ty)
+    axy, ty, tokens, *tables = together(axy, ty, tokens, *tables)
     acxy = moved(axy, "c", 1)
     tcy = moved(ty, "c", 1)
-    return [own, ay, ax, axy, ac, acy, acx, acxy], [eight, ty, tc, tcy]
+    return [own, ay, ax, axy, ac, acy, acx, acxy], [eight, ty, tc, tcy], tokens, tables
+
+
+def place_tables(tokens):
+    found = tokens[..., MODEL_WIDTH : MODEL_WIDTH + 2].astype(F32)
+    place_all = found[..., 0] * 16.0 + found[..., 1]
+    half_dim = HEAD_SIZE // 2
+    frequency = THETA ** (-2.0 * jnp.arange(half_dim, dtype=F32) / HEAD_SIZE)
+    angles = place_all[..., None] * jnp.tile(frequency, 4)
+    sign = jnp.where(jnp.arange(LANES) % HEAD_SIZE < half_dim, -1.0, 1.0).astype(F32)
+    place_q = place_all[0][..., None]
+    place_k = jnp.transpose(place_all, (1, 0, 2)).reshape(2, 1, 4 * ROWS)
+    return jnp.cos(angles), jnp.sin(angles) * sign, place_q, place_k
 
 
 def fold(order, relative):
@@ -129,44 +146,49 @@
     return kept.astype(F32) + received.astype(F32)
 
 
-def scatter_blocks(head_send, head_keep, tail_send, tail_keep, vector):
-    hr = moved(head_send, "c", 1)
-    tr = moved(tail_send, "c", 1)
+def scatter_blocks(head_sends, head_keep, tail_sends, tail_keep, vector, pairs):
+    head_first, head_rest = head_sends
+    tail_first, tail_rest = tail_sends
+    h1 = moved(head_first, "c", 1)
+    t1 = moved(tail_first, "c", 1)
+    hr = moved(head_rest, "c", 1)
+    tr = moved(tail_rest, "c", 1)
     vr = moved(vector, "c", 1)
-    hr, tr, vr = together(hr, tr, vr)
-    hx = summed(head_keep[8:], hr[8:]).astype(BF16)
-    ty = summed(tail_keep[8:], tr[8:]).astype(BF16)
-    head = summed(head_keep[:8], hr[:8])
-    tail = summed(tail_keep[:8], tr[:8])
+    h1, t1 = together(h1, t1)
+    hx = summed(head_keep[12:], h1).astype(BF16)
+    ty = summed(tail_keep[8:], t1).astype(BF16)
+    hx1 = moved(hx, "x", 1)
+    tr1 = moved(ty, "y", 1)
+    hx = summed(head_keep[8:12], hr[8:]).astype(BF16)
+    hy = summed(head_keep[4:8], hr[4:8])
+    hz = summed(head_keep[:4], hr[:4])
+    tail = summed(tail_keep[:8], tr)
     vector = vector + vr
-    hr = moved(hx, "x", 1)
-    tr = moved(ty, "y", 1)
     vr = moved(vector, "x", 1)
-    hr, tr, vr = together(hr, tr, vr)
-    hy = summed(head[4:], hr[4:]).astype(BF16)
-    tz = [summed(tail[2 * s : 2 * s + 2], tr[2 * s : 2 * s + 2]).astype(BF16) for s in (1, 2, 3)]
-    head = summed(head[:4], hr[:4])
-    tail = summed(tail[:2], tr[:2])
+    hx1, tr1, vr, hx, hy, hz, tail = together(hx1, tr1, vr, hx, hy, hz, tail)
+    hy = summed(hy, hx1).astype(BF16)
+    tz = [summed(tail[2 * s : 2 * s + 2], tr1[2 * s : 2 * s + 2]).astype(BF16) for s in (1, 2, 3)]
     vector = vector + vr
-    hr = moved(hy, "y", 1)
-    tr = [moved(tz[s - 1], "z", s) for s in (1, 2, 3)]
+    hy1 = moved(hy, "y", 1)
+    hx1 = moved(hx, "x", 1)
+    tzr = [moved(tz[s - 1], "z", s) for s in (1, 2, 3)]
     vr = moved(vector, "y", 1)
-    hr, vr, *tr = together(hr, vr, *tr)
-    hz = [summed(head[s], hr[s]).astype(BF16) for s in (1, 2, 3)]
-    head = summed(head[0], hr[0])
-    tx = summed(summed(tail[1], tr[0][1]), summed(tr[1][1], tr[2][1])).astype(BF16)
-    tail = summed(summed(tail[0], tr[0][0]), summed(tr[1][0], tr[2][0]))
+    tail = summed(tail[:2], tr1[:2])
+    hy1, hx1, vr, tail, pairs, *tzr = together(hy1, hx1, vr, tail, pairs, *tzr)
+    head = [summed(summed(hz[s], hx1[s]), hy1[s]) for s in range(4)]
+    tx = summed(summed(tail[1], tzr[0][1]), summed(tzr[1][1], tzr[2][1])).astype(BF16)
+    tail = summed(summed(tail[0], tzr[0][0]), summed(tzr[1][0], tzr[2][0]))
     vector = vector + vr
-    hr = [moved(hz[s - 1], "z", s) for s in (1, 2, 3)]
-    tr = moved(tx, "x", 1)
+    hzr = [moved(head[s].astype(BF16), "z", s) for s in (1, 2, 3)]
+    txr = moved(tx, "x", 1)
+    pairs = [pairs[0]] + [across(pairs[d], d) for d in (1, 2, 3)]
     vr = [moved(vector, "z", s) for s in (1, 2, 3)]
-    head = summed(summed(head, hr[0]), summed(hr[1], hr[2]))
     place = coordinates(device_number() // inner_count())["z"]
     parts = jnp.stack([vector] + vr)
     vector = sum(
         lax.dynamic_index_in_dim(parts, (place - z) % 4, 0, keepdims=False) for z in range(4)
     )
-    return head, summed(tail, tr), vector
+    return head[0], hzr, tail, txr, vector, pairs
 
 
 def lower_lanes(shape):
@@ -239,10 +261,13 @@
     )(kind, flat)
 
 
-def flat_kernel(kind_ref, head_ref, tail_ref, flat_ref, tiles, narrow):
+def flat_kernel(kind_ref, head_ref, one_ref, two_ref, three_ref, tail_ref, other_ref, *refs):
     kind = kind_ref[0]
-    tiles[0:HEAD_ROWS, :] = head_ref[...]
-    tiles[HEAD_ROWS:BLOCK_ROWS, :] = tail_ref[...]
+    tiles, narrow, flat_ref = refs[-3:]
+    tiles[0:HEAD_ROWS, :] = (head_ref[...] + one_ref[...].astype(F32)) + (
+        two_ref[...].astype(F32) + three_ref[...].astype(F32)
+    )
+    tiles[HEAD_ROWS:BLOCK_ROWS, :] = tail_ref[...] + other_ref[...].astype(F32)
 
     @pl.when(kind == 0)
     def _():
@@ -275,22 +300,35 @@
         flat_ref[pl.ds(2, 288, stride=3), :] = jnp.where(low, odd, last)
 
 
-def to_flat(kind, head, tail):
+    if len(refs) == 4:
+        refs[0][...] = flat_ref[...]
+        return
+    weight_ref, first_ref, second_ref, new_weight, new_first, new_second = refs[:6]
+
+    @pl.loop(0, 6)
+    def _(k):
+        rows = pl.ds(pl.multiple_of(k * 144, 8), 144)
+        new_weight[rows, :], new_first[rows, :], new_second[rows, :] = adamw(
+            weight_ref[rows, :], flat_ref[rows, :], first_ref[rows, :], second_ref[rows, :], RATE_MATRIX, DECAY
+        )
+
+
+def finish(kind, parts, state):
+    vmem = pl.BlockSpec(memory_space=pltpu.VMEM)
+    flat = jax.ShapeDtypeStruct((BLOCK_ROWS, LANES), F32)
+    count = max(1, len(state))
     return pl.pallas_call(
         flat_kernel,
-        out_shape=jax.ShapeDtypeStruct((BLOCK_ROWS, LANES), F32),
-        in_specs=[
-            pl.BlockSpec(memory_space=pltpu.SMEM),
-            pl.BlockSpec(memory_space=pltpu.VMEM),
-            pl.BlockSpec(memory_space=pltpu.VMEM),
-        ],
-        out_specs=pl.BlockSpec(memory_space=pltpu.VMEM),
+        out_shape=(flat,) * count,
+        in_specs=[pl.BlockSpec(memory_space=pltpu.SMEM)] + [vmem] * (6 + len(state)),
+        out_specs=(vmem,) * count,
         scratch_shapes=[
             pltpu.VMEM((BLOCK_ROWS, LANES), F32),
             pltpu.VMEM((HEAD_ROWS, LANES), F32),
+            pltpu.VMEM((BLOCK_ROWS, LANES), F32),
         ],
-        name="to_flat",
-    )(kind, head, tail)
+        name="finish",
+    )(kind, *parts, *state)
 
 
 def product(left, right):
@@ -348,8 +386,8 @@
     head_parts = refs[1:9]
     tail_parts = refs[9:13]
     (tokens_ref, cos_ref, sin_ref, place_q_ref, place_k_ref, gains_ref, bias_q_ref, bias_kv_ref, grad_ref) = refs[13:22]
-    (block_out_ref, head_send, head_keep, tail_send, tail_keep, vector_ref, dkv_ref, dq_wq_ref, d_mid_ref, w_kv) = refs[22:32]
-    (raw_head, raw_tail, w_q, w_out, w_gate, w_up, w_down, normed_all, hidden_all, keys, values, queries, probs, attended, act_all, block_acc, d_hidden, d_attended, dkv_all, d_query, sems) = refs[32:]
+    (block_out_ref, head_first, head_rest, head_keep_out, tail_first, tail_rest, tail_keep_out, vector_ref, dkv_ref, dq_wq_ref, d_mid_ref, w_kv) = refs[22:34]
+    (raw_head, raw_tail, w_q, w_out, w_gate, w_up, w_down, normed_all, hidden_all, keys, values, queries, probs, attended, act_all, block_acc, d_hidden, d_attended, dkv_all, d_query, head_send, head_keep, tail_send, tail_keep, sems) = refs[34:]
 
     copies = []
     for k, part in enumerate(head_parts):
@@ -523,7 +561,8 @@
         made = rows_product(act_all[:, pl.ds(pl.multiple_of(k * 384, 128), 384)], grad_low)
         store_rows(12 + k, tiles_of_rows(made[0:192]), tiles_of_rows(made[192:384]))
 
-    block_out_ref[...] = block_acc[...][:, 0:MODEL_WIDTH].astype(BF16).reshape(2, ROWS, MODEL_WIDTH)
+    for mb in range(2):
+        block_out_ref[mb] = block_acc[ROWS * mb : ROWS * mb + ROWS, :].T[0:MODEL_WIDTH].astype(BF16)
 
     d_two = d_hidden[...]
     vector_ref[...] = jnp.zeros_like(vector_ref)
@@ -597,6 +636,18 @@
     store_rows(1, query_tiles[2], key_tiles)
     store_rows(2, value_tiles, out_tiles[0])
     store_rows(3, out_tiles[1], out_tiles[2])
+    copies = [
+        pltpu.make_async_copy(head_send.at[pl.ds(12, 4)], head_first, sems.at[0]),
+        pltpu.make_async_copy(tail_send.at[pl.ds(8, 8)], tail_first, sems.at[1]),
+        pltpu.make_async_copy(head_send.at[pl.ds(0, 12)], head_rest, sems.at[2]),
+        pltpu.make_async_copy(tail_send.at[pl.ds(0, 8)], tail_rest, sems.at[3]),
+        pltpu.make_async_copy(head_keep, head_keep_out, sems.at[4]),
+        pltpu.make_async_copy(tail_keep, tail_keep_out, sems.at[5]),
+    ]
+    for copy in copies:
+        copy.start()
+    for copy in copies:
+        copy.wait()
 
 
 def run_layer(slots, heads, tails, tokens, cosines, sines, place_q, place_k, gains, bias_q, bias_kv, grad):
@@ -624,14 +675,20 @@
         ((256, WIDE), BF16),
         ((1024, 384), BF16),
         ((256, WIDE), BF16),
+        ((16, HEAD_ROWS, LANES), BF16),
+        ((16, HEAD_ROWS, LANES), BF16),
+        ((16, TAIL_ROWS, LANES), BF16),
+        ((16, TAIL_ROWS, LANES), BF16),
     ]
     return pl.pallas_call(
         layer_kernel,
         out_shape=(
-            shape((2, ROWS, MODEL_WIDTH), BF16),
+            shape((2, MODEL_WIDTH, ROWS), BF16),
+            shape((4, HEAD_ROWS, LANES), BF16),
+            shape((12, HEAD_ROWS, LANES), BF16),
             shape((16, HEAD_ROWS, LANES), BF16),
-            shape((16, HEAD_ROWS, LANES), BF16),
-            shape((16, TAIL_ROWS, LANES), BF16),
+            shape((8, TAIL_ROWS, LANES), BF16),
+            shape((8, TAIL_ROWS, LANES), BF16),
             shape((16, TAIL_ROWS, LANES), BF16),
             shape((8, WIDE), F32),
             shape((4, 2, ROWS, 384), BF16),
@@ -640,7 +697,7 @@
             shape((WIDE, 384), BF16),
         ),
         in_specs=[pl.BlockSpec(memory_space=pltpu.SMEM)] + [anywhere] * 12 + [vmem] * 9,
-        out_specs=(vmem,) * 10,
+        out_specs=(vmem,) + (anywhere,) * 6 + (vmem,) * 5,
         scratch_shapes=[pltpu.VMEM(dims, kind) for dims, kind in scratch]
         + [pltpu.SemaphoreType.DMA((12,))],
         compiler_params=pltpu.CompilerParams(vmem_limit_bytes=56 * 1024 * 1024),
@@ -656,13 +713,14 @@
     total = total.reshape(2 * ROWS, 384).astype(BF16)
     d_norm = (dq_wq_ref[...] + times_transposed(total, w_kv_ref[...])) * gains_ref[0:1, :]
     d_input = d_mid_ref[...] + scale * (d_norm - normed * row_mean(d_norm * normed))
-    out_ref[...] = d_input[:, 0:MODEL_WIDTH].astype(BF16).reshape(2, ROWS, MODEL_WIDTH)
+    for mb in range(2):
+        out_ref[mb] = d_input[ROWS * mb : ROWS * mb + ROWS].T[0:MODEL_WIDTH].astype(BF16)
 
 
 def run_input(tokens, gains, w_kv, dq_wq, d_mid, parts):
     return pl.pallas_call(
         input_kernel,
-        out_shape=jax.ShapeDtypeStruct((2, ROWS, MODEL_WIDTH), BF16),
+        out_shape=jax.ShapeDtypeStruct((2, MODEL_WIDTH, ROWS), BF16),
         in_specs=[pl.BlockSpec(memory_space=pltpu.VMEM)] * 9,
         out_specs=pl.BlockSpec(memory_space=pltpu.VMEM),
         name="input_grad",
@@ -717,38 +775,33 @@
     packed = jnp.concatenate(
         [own_tokens, marks, jnp.zeros((2, ROWS, WIDE - MODEL_WIDTH - 2), BF16)], axis=-1
     )
-    tokens = jnp.stack([packed] + [across(packed, d) for d in (1, 2, 3)])
-    heads, tails = gather_blocks(head, tail)
-
-    found = tokens[..., MODEL_WIDTH : MODEL_WIDTH + 2].astype(F32)
-    place_all = found[..., 0] * 16.0 + found[..., 1]
-    half_dim = HEAD_SIZE // 2
-    frequency = THETA ** (-2.0 * jnp.arange(half_dim, dtype=F32) / HEAD_SIZE)
-    angles = place_all[..., None] * jnp.tile(frequency, 4)
-    sign = jnp.where(jnp.arange(LANES) % HEAD_SIZE < half_dim, -1.0, 1.0).astype(F32)
-    cosines = jnp.cos(angles)
-    sines = jnp.sin(angles) * sign
-    place_q = place_all[0][..., None]
-    place_k = jnp.transpose(place_all, (1, 0, 2)).reshape(2, 1, 4 * ROWS)
+    heads, tails, tokens, tables = gather_all(head, tail, packed)
     padding = ((0, 0), (0, WIDE - MODEL_WIDTH))
     gains = jnp.pad(vectors[: 2 * MODEL_WIDTH].reshape(2, MODEL_WIDTH), padding)
     bias_q = jnp.pad(vectors[2 * MODEL_WIDTH : 3 * MODEL_WIDTH].reshape(1, MODEL_WIDTH), padding)
     bias_kv = bias_tiles(vectors[1728:1920], vectors[1920:2112]).reshape(1, 384)
     grad = jnp.pad(out_grad.reshape(2 * ROWS, MODEL_WIDTH), padding)
 
-    (block_out, head_send, head_keep, tail_send, tail_keep, vector, dkv, dq_wq, d_mid, w_kv) = run_layer(
-        slots, heads, tails, tokens, cosines, sines, place_q, place_k, gains, bias_q, bias_kv, grad
-    )
-    parts = [dkv[0]] + [across(dkv[d], d) for d in (1, 2, 3)]
-    input_grad = run_input(tokens, gains, w_kv, dq_wq, d_mid, parts)
-    head, tail, vector = scatter_blocks(head_send, head_keep, tail_send, tail_keep, vector)
-    if inner_count() > 1:
+    (block_out, head_first, head_rest, head_keep, tail_first, tail_rest, tail_keep, vector, dkv, dq_wq, d_mid, w_kv) = run_layer(
+        slots, heads, tails, tokens, *tables, gains, bias_q, bias_kv, grad
+    )
+    head, hzr, tail, txr, vector, pairs = scatter_blocks(
+        (head_first, head_rest), head_keep, (tail_first, tail_rest), tail_keep, vector, dkv
+    )
+    input_grad = run_input(tokens, gains, w_kv, dq_wq, d_mid, pairs)
+    state = (weights, first_moment, second_moment)
+    parts = (head, *hzr, tail, txr)
+    if inner_count() == 1:
+        updated = finish(kind, parts, [array.reshape(BLOCK_ROWS, LANES) for array in state])
+        new_weights, new_first, new_second = [array.reshape(-1) for array in updated]
+    else:
         vector = lax.psum(vector, "ctx")
         vector = lax.psum(vector, "dp", axis_index_groups=inner_groups())
-    grad_own = own_slice(to_flat(kind, head, tail).reshape(-1))
-    new_weights, new_first, new_second = adamw(
-        weights, grad_own, first_moment, second_moment, RATE_MATRIX, DECAY
-    )
+        (block_grad,) = finish(kind, parts, [])
+        grad_own = own_slice(block_grad.reshape(-1))
+        new_weights, new_first, new_second = adamw(
+            weights, grad_own, first_moment, second_moment, RATE_MATRIX, DECAY
+        )
     pair = vector[3]
     vector_grad = jnp.concatenate(
         [
@@ -766,8 +819,8 @@
     )
     shape = tokens_in.shape
     return (
-        block_out.reshape(shape),
-        input_grad.reshape(shape),
+        jnp.transpose(block_out, (0, 2, 1)).reshape(shape),
+        jnp.transpose(input_grad, (0, 2, 1)).reshape(shape),
         new_weights,
         new_first,
         new_second,

time: 192 us -> 186 us (0.969)
  starting transfers between devices: 40.2 us -> 36.9 us
  Pallas kernels: 41.3 us -> 43.9 us
  local copies, waits for them, and re-layouts: 16 us -> 13.6 us
    ppermute x6, waiting for transfers between devices: 10.8 us -> 0.43 us  [across(): lax.ppermute(buffer, 'ctx', [(i, i ^ distance) for i in range(count)])]
    ppermute x35 -> x38, waiting for transfers between devices: 65.1 us -> 74.7 us  [moved(): return lax.ppermute(buffer, ('dp', 'ctx'), pairs)]
    ppermute x35 -> x38, starting transfers between devices: 37.1 us -> 31.6 us  [moved(): return lax.ppermute(buffer, ('dp', 'ctx'), pairs)]
    pallas_call x3, Pallas kernels: 39.4 us -> 42.1 us  [the longest x1 35.3 us: run_layer(): pl.pallas_call(layer_kernel, out_shape=(shape((2, MODEL_WIDTH, ROWS), BF1...]
    add x4 -> x2, other arithmetic: 4.56 us -> 2.21 us  [summed(): return kept.astype(F32) + received.astype(F32)]
    ppermute x6, starting transfers between devices: 3.05 us -> 5.35 us  [across(): lax.ppermute(buffer, 'ctx', [(i, i ^ distance) for i in range(count)])]
    sub x2 -> x1, other arithmetic: 2.9 us -> 0.66 us  [adamw(): param - rate * (fixed_one / (jnp.sqrt(fixed_two) + EPS_ADAM) + decay * pa...]
    unnamed x61 -> x57, local copies, waits for them, and re-layouts: 7.81 us -> 6.67 us
  transfers between devices with their start and end apart: 41 -> 44, of which waited for: 14 -> 15; matrix products, arithmetic and copies ran while one was open for 12% -> 10% of each run, Pallas kernels for 2% -> 3%
where the time goes in v2:
time: 186 us
  waiting for transfers between devices  75.2 us (40%)
  Pallas kernels  43.9 us (24%)
  starting transfers between devices  36.9 us (20%)
  other arithmetic  15.1 us (8%)
  local copies, waits for them, and re-layouts  13.6 us (7%)
    ppermute x38, waiting for transfers between devices, moved(): return lax.ppermute(buffer, ('dp', 'ctx'), pairs)  74.7 us
    pallas_call x1, Pallas kernels, run_layer(): pl.pallas_call(layer_kernel, out_shape=(shape((2, MODEL_WIDTH, ROWS), BF1...  35.3 us
    ppermute x38, starting transfers between devices, moved(): return lax.ppermute(buffer, ('dp', 'ctx'), pairs)  31.6 us
    unnamed x57, local copies, waits for them, and re-layouts  6.67 us
    ppermute x6, starting transfers between devices, across(): lax.ppermute(buffer, 'ctx', [(i, i ^ distance) for i in range(count)])  5.35 us
  transfers between devices with their start and end apart: 44, of which 15 were waited for; matrix products, arithmetic and copies ran while one was open for 10% of the time, Pallas kernels for 3%

profile of v2, /device:TPU:0, one launch (start us, length us, event | category | flops | bytes accessed | tf_op | source)
XLA Modules:
  0.0 185.7 jit_solution(9261242781699934101)
XLA Ops:
  3.0 3.0 %collective-permute-start.2 = (bf16[2,128,640]{2,1,0:T(8,128)(2,1)S(1)}, bf16[2,128,640]{2,1,0:T(8,128)(2,1)S(1)}, u32[]{:S(2)}, u32[]{:S(2)}) collective-permute-start(bf16[2,128,640]{2,1,0:T(8,128)(2,1)S(1)} %maximum_maximum_fusion), channel_id=1, source_target_pairs={{0,2},{1,3},{2,0},{3,1},{4,6},{5,7},{6,4},{7,5},{8,10},{9,11},{10,... | collective-permute-start | bytes 983048 | tf_op jit(solution)/shard_map/ppermute | solution.py:73
  6.0 1.9 %to_tiles.1 = (bf16[576,128]{1,0:T(8,128)(2,1)}, bf16[288,128]{1,0:T(8,128)(2,1)}) custom-call(s32[1]{0:T(128)} %bitcast.97.kind_ref, f32[864,128]{1,0:T(8,128)} %bitcast.168), custom_call_target="tpu_custom_call" | custom-call | tf_op jit(solution)/shard_map/to_tiles/pallas_call | solution.py:245
  7.9 4.0 %collective-permute-start.5 = (bf16[576,128]{1,0:T(8,128)(2,1)}, bf16[576,128]{1,0:T(8,128)(2,1)S(1)}, u32[]{:S(2)}, u32[]{:S(2)}) collective-permute-start(bf16[576,128]{1,0:T(8,128)(2,1)} %get-tuple-element.67), channel_id=1, source_target_pairs={{0,24},{1,25},{2,26},{3,27},{4,28},{5,29},{6,30},{7,31},{8,0},{9,1... | collective-permute-start | bytes 442376 | tf_op jit(solution)/shard_map/ppermute | solution.py:68
  12.0 3.3 %collective-permute-done = bf16[288,128]{1,0:T(8,128)(2,1)S(1)} collective-permute-done((bf16[288,128]{1,0:T(8,128)(2,1)}, bf16[288,128]{1,0:T(8,128)(2,1)S(1)}, u32[]{:S(2)}, u32[]{:S(2)}) %collective-permute-start) | collective-permute-done | bytes 73760 | tf_op jit(solution)/shard_map/ppermute | solution.py:68
  15.2 1.8 collective-permute-start.3
  17.1 8.0 %collective-permute-done.4 = bf16[576,128]{1,0:T(8,128)(2,1)S(1)} collective-permute-done((bf16[576,128]{1,0:T(8,128)(2,1)}, bf16[576,128]{1,0:T(8,128)(2,1)S(1)}, u32[]{:S(2)}, u32[]{:S(2)}) %collective-permute-start.4) | collective-permute-done | bytes 147488 | tf_op jit(solution)/shard_map/ppermute | solution.py:68
  26.3 1.6 collective-permute-start.7
  27.9 1.5 collective-permute-start.6
  29.4 1.5 collective-permute-start.11
  31.0 1.3 collective-permute-start.10
  32.3 2.3 %collective-permute-done.11 = bf16[2,288,128]{2,1,0:T(8,128)(2,1)S(1)} collective-permute-done((bf16[2,288,128]{2,1,0:T(8,128)(2,1)S(1)}, bf16[2,288,128]{2,1,0:T(8,128)(2,1)S(1)}, u32[]{:S(2)}, u32[]{:S(2)}) %collective-permute-start.11) | collective-permute-done | bytes 147488 | tf_op jit(solution)/shard_map/ppermute | solution.py:68
  36.0 8.6 %collective-permute-done.10 = bf16[2,288,128]{2,1,0:T(8,128)(2,1)S(1)} collective-permute-done((bf16[2,288,128]{2,1,0:T(8,128)(2,1)S(1)}, bf16[2,288,128]{2,1,0:T(8,128)(2,1)S(1)}, u32[]{:S(2)}, u32[]{:S(2)}) %collective-permute-start.10) | collective-permute-done | bytes 147488 | tf_op jit(solution)/shard_map/ppermute | solution.py:68
  49.6 3.2 %fusion = (f32[4,2,128,128]{3,2,1,0:T(8,128)}, f32[4,2,128,128]{3,2,1,0:T(8,128)}) fusion(f32[128]{0:T(128)S(1)} %compare_select_fusion, f32[128]{0:T(128)S(1)} %mul.204, f32[4,2,128]{2,1,0:T(2,128)S(1)} %get-tuple-element.144), kind=kLoop, calls=%fused_computation.11 | loop fusion | flops 262144 | bytes 1053696 | tf_op jit(solution)/shard_map/mul | solution.py:117
  52.9 8.6 %collective-permute-done.13.refs_10_ = bf16[8,288,128]{2,1,0:T(8,128)(2,1)} collective-permute-done((bf16[8,288,128]{2,1,0:T(8,128)(2,1)S(1)}, bf16[8,288,128]{2,1,0:T(8,128)(2,1)}, u32[]{:S(2)}, u32[]{:S(2)}) %collective-permute-start.13) | collective-permute-done | bytes 589856 | tf_op jit(solution)/shard_map/ppermute | solution.py:68
  70.9 35.3 %layer.1 = (bf16[2,576,128]{2,1,0:T(8,128)(2,1)}, bf16[4,576,128]{2,1,0:T(8,128)(2,1)}, bf16[12,576,128]{2,1,0:T(8,128)(2,1)}, bf16[16,576,128]{2,1,0:T(8,128)(2...) custom-call(s32[97]{0:T(128)} %stack.449.refs_0_, ...), custom_call_target="tpu_custom_call" | custom-call | tf_op jit(solution)/shard_map/layer/pallas_call | solution.py:683
  107.3 3.7 %collective-permute-done.20 = bf16[4,576,128]{2,1,0:T(8,128)(2,1)S(1)} collective-permute-done((bf16[4,576,128]{2,1,0:T(8,128)(2,1)}, bf16[4,576,128]{2,1,0:T(8,128)(2,1)S(1)}, u32[]{:S(2)}, u32[]{:S(2)}) %collective-permute-start.20) | collective-permute-done | bytes 589856 | tf_op jit(solution)/shard_map/ppermute | solution.py:68
  112.7 1.7 convert_add_fusion
  114.4 1.6 collective-permute-start.23
  118.3 1.5 collective-permute-start.25
  119.8 12.3 %collective-permute-done.25 = f32[8,640]{1,0:T(8,128)S(1)} collective-permute-done((f32[8,640]{1,0:T(8,128)S(1)}, f32[8,640]{1,0:T(8,128)S(1)}, u32[]{:S(2)}, u32[]{:S(2)}) %collective-permute-start.25) | collective-permute-done | bytes 20512 | tf_op jit(solution)/shard_map/ppermute | solution.py:68
  134.1 1.5 collective-permute-start.30
  137.8 10.1 %collective-permute-done.30 = f32[8,640]{1,0:T(8,128)S(1)} collective-permute-done((f32[8,640]{1,0:T(8,128)S(1)}, f32[8,640]{1,0:T(8,128)S(1)}, u32[]{:S(2)}, u32[]{:S(2)}) %collective-permute-start.30) | collective-permute-done | bytes 20512 | tf_op jit(solution)/shard_map/ppermute | solution.py:68
  147.9 7.5 %collective-permute-done.31 = bf16[2,288,128]{2,1,0:T(8,128)(2,1)} collective-permute-done((bf16[2,288,128]{2,1,0:T(8,128)(2,1)}, bf16[2,288,128]{2,1,0:T(8,128)(2,1)}, u32[]{:S(2)}, u32[]{:S(2)}) %collective-permute-start.31) | collective-permute-done | bytes 147488 | tf_op jit(solution)/shard_map/ppermute | solution.py:68
  155.6 1.9 %collective-permute-start.41 = (f32[8,640]{1,0:T(8,128)S(1)}, f32[8,640]{1,0:T(8,128)S(1)}, u32[]{:S(2)}, u32[]{:S(2)}) collective-permute-start(f32[8,640]{1,0:T(8,128)S(1)} %add.1336), channel_id=1, source_target_pairs={{0,8},{1,9},{2,10},{3,11},{4,12},{5,13},{6,14},{7,15},{8,16},{9,17... | collective-permute-start | bytes 61448 | tf_op jit(solution)/shard_map/ppermute | solution.py:68
  158.3 2.0 %fusion.3 = (bf16[576,128]{1,0:T(8,128)(2,1)S(1)}, bf16[576,128]{1,0:T(8,128)(2,1)S(1)}, bf16[576,128]{1,0:T(8,128)(2,1)S(1)}, f32[576,128]{1,0:T(8,128)}) fusion(f32[4,576,128]{2,1,0:T(8,128)S(1)} %get-tuple-element.111, bf16[4,576,128]{2,1,0:T(8,128)(2,1)S(1)} %collective-permute-done.28, bf16[4,576,128]{2,1,0:T(8,128)(2,1)} %collective-permute-done.29), kind=kLoop, calls=%fused_computation.35 | loop fusion | flops 1400832 | bytes 3096576 | tf_op jit(solution)/shard_map/convert_element_type | solution.py:182
  160.3 2.4 %collective-permute-start.39 = (bf16[576,128]{1,0:T(8,128)(2,1)S(1)}, bf16[576,128]{1,0:T(8,128)(2,1)S(1)}, u32[]{:S(2)}, u32[]{:S(2)}) collective-permute-start(bf16[576,128]{1,0:T(8,128)(2,1)S(1)} %get-tuple-element.149), channel_id=1, source_target_pairs={{0,24},{1,25},{2,26},{3,27},{4,28},{5,29},{6,30},{7,31},{8,0},{9,1... | collective-permute-start | bytes 442376 | tf_op jit(solution)/shard_map/ppermute | solution.py:68
  163.3 1.8 fusion.8
  165.1 1.9 %collective-permute-start.37 = (bf16[576,128]{1,0:T(8,128)(2,1)S(1)}, bf16[576,128]{1,0:T(8,128)(2,1)S(1)}, u32[]{:S(2)}, u32[]{:S(2)}) collective-permute-start(bf16[576,128]{1,0:T(8,128)(2,1)S(1)} %get-tuple-element.151), channel_id=1, source_target_pairs={{0,8},{1,9},{2,10},{3,11},{4,12},{5,13},{6,14},{7,15},{8,16},{9,17... | collective-permute-start | bytes 442376 | tf_op jit(solution)/shard_map/ppermute | solution.py:68
  167.9 6.2 %collective-permute-done.40.other_ref = bf16[288,128]{1,0:T(8,128)(2,1)S(1)} collective-permute-done((bf16[288,128]{1,0:T(8,128)(2,1)S(1)}, bf16[288,128]{1,0:T(8,128)(2,1)S(1)}, u32[]{:S(2)}, u32[]{:S(2)}) %collective-permute-start.40) | collective-permute-done | bytes 73760 | tf_op jit(solution)/shard_map/ppermute | solution.py:68
  174.1 2.3 %collective-permute-start.35 = (bf16[2,128,384]{2,1,0:T(8,128)(2,1)S(1)}, bf16[2,128,384]{2,1,0:T(8,128)(2,1)S(1)}, u32[]{:S(2)}, u32[]{:S(2)}) collective-permute-start(bf16[2,128,384]{2,1,0:T(8,128)(2,1)S(1)} %get-tuple-element.161), channel_id=1, source_target_pairs={{0,2},{1,3},{2,0},{3,1},{4,6},{5,7},{6,4},{7,5},{8,10},{9,11},{10,... | collective-permute-start | bytes 589832 | tf_op jit(solution)/shard_map/ppermute | solution.py:73
  177.8 3.3 %finish.1 = (f32[864,128]{1,0:T(8,128)}, f32[864,128]{1,0:T(8,128)}, f32[864,128]{1,0:T(8,128)}) custom-call(s32[1]{0:T(128)} %bitcast.97.kind_ref, f32[576,128]{1,0:T(8,128)} %get-tuple-element.152.head_ref, bf16[576,128]{1,0:T(8,128)(2,1)} %copy-done.19, bf16[576,128]{1,0:T(8,128)(2,1)} %copy-done.18, bf16[576,128]{1,0:T(8,128)(2,1)} %copy-done.17, ...), custom_call_target="tpu_custom_call" | custom-call | tf_op jit(solution)/shard_map/finish/pallas_call | solution.py:320
  182.3 3.4 %input_grad.1 = bf16[2,576,128]{2,1,0:T(8,128)(2,1)} custom-call(bf16[4,2,128,640]{3,2,1,0:T(8,128)(2,1)} %copy-done, f32[2,640]{1,0:T(2,128)} %pad.12.refs_18_.gains_ref, bf16[640,384]{1,0:T(8,128)(2,1)} %get-tuple-element.91.w_kv_ref, f32[256,640]{1,0:T(8,128)} %get-tuple-element.92.dq_wq_ref, f32[256,640]{1,0:T(8,128)} %get-tuple-element.93.d_mid_ref, ...), custom_call_target="tpu_custom_call" | custom-call | tf_op jit(solution)/shard_map/input_grad/pallas_call | solution.py:721
  (167 shorter events, 33.6 us)
Async XLA Ops:
  3.0 22.2 %collective-permute-start.2 = (bf16[2,128,640]{2,1,0:T(8,128)(2,1)S(1)}, bf16[2,128,640]{2,1,0:T(8,128)(2,1)S(1)}, u32[]{:S(2)}, u32[]{:S(2)}) collective-permute-start(bf16[2,128,640]{2,1,0:T(8,128)(2,1)S(1)} %maximum_maximum_fusion), channel_id=1, source_target_pairs={{0,2},{1,3},{2,0},{3,1},{4,6},{5,7},{6,4},{7,5},{8,10},{9,11},{10,... | collective-permute-start | bytes 983048 | tf_op jit(solution)/shard_map/ppermute | solution.py:73
  6.0 19.2 %collective-permute-start.1 = (bf16[2,128,640]{2,1,0:T(8,128)(2,1)S(1)}, bf16[2,128,640]{2,1,0:T(8,128)(2,1)S(1)}, u32[]{:S(2)}, u32[]{:S(2)}) collective-permute-start(bf16[2,128,640]{2,1,0:T(8,128)(2,1)S(1)} %maximum_maximum_fusion), channel_id=1, source_target_pairs={{0,1},{1,0},{2,3},{3,2},{4,5},{5,4},{6,7},{7,6},{8,9},{9,8},{10,11... | collective-permute-start | bytes 983048 | tf_op jit(solution)/shard_map/ppermute | solution.py:73
  7.9 9.1 %collective-permute-start.5 = (bf16[576,128]{1,0:T(8,128)(2,1)}, bf16[576,128]{1,0:T(8,128)(2,1)S(1)}, u32[]{:S(2)}, u32[]{:S(2)}) collective-permute-start(bf16[576,128]{1,0:T(8,128)(2,1)} %get-tuple-element.67), channel_id=1, source_target_pairs={{0,24},{1,25},{2,26},{3,27},{4,28},{5,29},{6,30},{7,31},{8,0},{9,1... | collective-permute-start | bytes 442376 | tf_op jit(solution)/shard_map/ppermute | solution.py:68
  12.0 13.1 %collective-permute-start.4 = (bf16[576,128]{1,0:T(8,128)(2,1)}, bf16[576,128]{1,0:T(8,128)(2,1)S(1)}, u32[]{:S(2)}, u32[]{:S(2)}) collective-permute-start(bf16[576,128]{1,0:T(8,128)(2,1)} %get-tuple-element.67), channel_id=1, source_target_pairs={{0,16},{1,17},{2,18},{3,19},{4,20},{5,21},{6,22},{7,23},{8,24},{9,... | collective-permute-start | bytes 442376 | tf_op jit(solution)/shard_map/ppermute | solution.py:68
  15.2 9.9 %collective-permute-start.3 = (bf16[576,128]{1,0:T(8,128)(2,1)}, bf16[576,128]{1,0:T(8,128)(2,1)S(1)}, u32[]{:S(2)}, u32[]{:S(2)}) collective-permute-start(bf16[576,128]{1,0:T(8,128)(2,1)} %get-tuple-element.67), channel_id=1, source_target_pairs={{0,8},{1,9},{2,10},{3,11},{4,12},{5,13},{6,14},{7,15},{8,16},{9,17... | collective-permute-start | bytes 442376 | tf_op jit(solution)/shard_map/ppermute | solution.py:68
  26.3 18.4 %collective-permute-start.7 = (bf16[4,576,128]{2,1,0:T(8,128)(2,1)S(1)}, bf16[4,576,128]{2,1,0:T(8,128)(2,1)S(1)}, u32[]{:S(2)}, u32[]{:S(2)}) collective-permute-start(bf16[4,576,128]{2,1,0:T(8,128)(2,1)S(1)} %pad_maximum_fusion.1.refs_1_), channel_id=1, source_target_pairs={{0,2},{1,3},{2,0},{3,1},{4,6},{5,7},{6,4},{7,5},{8,10},{9,11},{10,... | collective-permute-start | bytes 1769480 | tf_op jit(solution)/shard_map/ppermute | solution.py:68
  27.9 17.5 %collective-permute-start.6 = (bf16[4,576,128]{2,1,0:T(8,128)(2,1)S(1)}, bf16[4,576,128]{2,1,0:T(8,128)(2,1)}, u32[]{:S(2)}, u32[]{:S(2)}) collective-permute-start(bf16[4,576,128]{2,1,0:T(8,128)(2,1)S(1)} %pad_maximum_fusion.1.refs_1_), channel_id=1, source_target_pairs={{0,4},{1,5},{2,6},{3,7},{4,0},{5,1},{6,2},{7,3},{8,12},{9,13},{10,... | collective-permute-start | bytes 1769480 | tf_op jit(solution)/shard_map/ppermute | solution.py:68
  30.9 13.8 %collective-permute-start.8 = (bf16[2,128,640]{2,1,0:T(8,128)(2,1)S(1)}, bf16[2,128,640]{2,1,0:T(8,128)(2,1)S(1)}, u32[]{:S(2)}, u32[]{:S(2)}) collective-permute-start(bf16[2,128,640]{2,1,0:T(8,128)(2,1)S(1)} %collective-permute-done.2), channel_id=1, source_target_pairs={{0,1},{1,0},{2,3},{3,2},{4,5},{5,4},{6,7},{7,6},{8,9},{9,8},{10,11... | collective-permute-start | bytes 983048 | tf_op jit(solution)/shard_map/ppermute | solution.py:73
  31.0 13.7 %collective-permute-start.10 = (bf16[2,288,128]{2,1,0:T(8,128)(2,1)S(1)}, bf16[2,288,128]{2,1,0:T(8,128)(2,1)S(1)}, u32[]{:S(2)}, u32[]{:S(2)}) collective-permute-start(bf16[2,288,128]{2,1,0:T(8,128)(2,1)S(1)} %pad_maximum_fusion.2), channel_id=1, source_target_pairs={{0,16},{1,17},{2,18},{3,19},{4,20},{5,21},{6,22},{7,23},{8,24},{9,... | collective-permute-start | bytes 442376 | tf_op jit(solution)/shard_map/ppermute | solution.py:68
  34.6 10.1 %collective-permute-start.9 = (bf16[2,288,128]{2,1,0:T(8,128)(2,1)S(1)}, bf16[2,288,128]{2,1,0:T(8,128)(2,1)S(1)}, u32[]{:S(2)}, u32[]{:S(2)}) collective-permute-start(bf16[2,288,128]{2,1,0:T(8,128)(2,1)S(1)} %pad_maximum_fusion.2), channel_id=1, source_target_pairs={{0,8},{1,9},{2,10},{3,11},{4,12},{5,13},{6,14},{7,15},{8,16},{9,17... | collective-permute-start | bytes 442376 | tf_op jit(solution)/shard_map/ppermute | solution.py:68
  44.7 18.0 %collective-permute-start.14 = (bf16[4,576,128]{2,1,0:T(8,128)(2,1)S(1)}, bf16[4,576,128]{2,1,0:T(8,128)(2,1)S(1)}, u32[]{:S(2)}, u32[]{:S(2)}) collective-permute-start(bf16[4,576,128]{2,1,0:T(8,128)(2,1)S(1)} %pad_maximum_fusion.1.refs_1_), channel_id=1, source_target_pairs={{0,1},{1,0},{2,3},{3,2},{4,5},{5,4},{6,7},{7,6},{8,9},{9,8},{10,11... | collective-permute-start | bytes 1769480 | tf_op jit(solution)/shard_map/ppermute | solution.py:68
  45.5 23.7 %collective-permute-start.18 = (bf16[8,288,128]{2,1,0:T(8,128)(2,1)S(1)}, bf16[8,288,128]{2,1,0:T(8,128)(2,1)}, u32[]{:S(2)}, u32[]{:S(2)}) collective-permute-start(bf16[8,288,128]{2,1,0:T(8,128)(2,1)S(1)} %constant_dynamic-update-slice_fusion.refs_9_), channel_id=1, source_target_pairs={{0,1},{1,0},{2,3},{3,2},{4,5},{5,4},{6,7},{7,6},{8,9},{9,8},{10,11... | collective-permute-start | bytes 1769480 | tf_op jit(solution)/shard_map/ppermute | solution.py:68
  46.1 15.4 %collective-permute-start.13 = (bf16[8,288,128]{2,1,0:T(8,128)(2,1)S(1)}, bf16[8,288,128]{2,1,0:T(8,128)(2,1)}, u32[]{:S(2)}, u32[]{:S(2)}) collective-permute-start(bf16[8,288,128]{2,1,0:T(8,128)(2,1)S(1)} %constant_dynamic-update-slice_fusion.refs_9_), channel_id=1, source_target_pairs={{0,4},{1,5},{2,6},{3,7},{4,0},{5,1},{6,2},{7,3},{8,12},{9,13},{10,... | collective-permute-start | bytes 1769480 | tf_op jit(solution)/shard_map/ppermute | solution.py:68
  46.6 22.6 %collective-permute-start.15 = (bf16[4,576,128]{2,1,0:T(8,128)(2,1)}, bf16[4,576,128]{2,1,0:T(8,128)(2,1)}, u32[]{:S(2)}, u32[]{:S(2)}) collective-permute-start(bf16[4,576,128]{2,1,0:T(8,128)(2,1)} %collective-permute-done.6.refs_2_), channel_id=1, source_target_pairs={{0,1},{1,0},{2,3},{3,2},{4,5},{5,4},{6,7},{7,6},{8,9},{9,8},{10,11... | collective-permute-start | bytes 1769480 | tf_op jit(solution)/shard_map/ppermute | solution.py:68
  46.6 16.1 %collective-permute-start.12 = (bf16[4,576,128]{2,1,0:T(8,128)(2,1)}, bf16[4,576,128]{2,1,0:T(8,128)(2,1)}, u32[]{:S(2)}, u32[]{:S(2)}) collective-permute-start(bf16[4,576,128]{2,1,0:T(8,128)(2,1)} %collective-permute-done.6.refs_2_), channel_id=1, source_target_pairs={{0,2},{1,3},{2,0},{3,1},{4,6},{5,7},{6,4},{7,5},{8,10},{9,11},{10,... | collective-permute-start | bytes 1769480 | tf_op jit(solution)/shard_map/ppermute | solution.py:68
  61.5 7.7 %collective-permute-start.16 = (bf16[4,576,128]{2,1,0:T(8,128)(2,1)S(1)}, bf16[4,576,128]{2,1,0:T(8,128)(2,1)S(1)}, u32[]{:S(2)}, u32[]{:S(2)}) collective-permute-start(bf16[4,576,128]{2,1,0:T(8,128)(2,1)S(1)} %collective-permute-done.7.refs_3_), channel_id=1, source_target_pairs={{0,1},{1,0},{2,3},{3,2},{4,5},{5,4},{6,7},{7,6},{8,9},{9,8},{10,11... | collective-permute-start | bytes 1769480 | tf_op jit(solution)/shard_map/ppermute | solution.py:68
  106.2 9.8 %collective-permute-start.26 = (bf16[12,576,128]{2,1,0:T(8,128)(2,1)}, bf16[12,576,128]{2,1,0:T(8,128)(2,1)S(1)}, u32[]{:S(2)}, u32[]{:S(2)}) collective-permute-start(bf16[12,576,128]{2,1,0:T(8,128)(2,1)} %get-tuple-element.101), channel_id=1, source_target_pairs={{0,1},{1,0},{2,3},{3,2},{4,5},{5,4},{6,7},{7,6},{8,9},{9,8},{10,11... | collective-permute-start | bytes 5308424 | tf_op jit(solution)/shard_map/ppermute | solution.py:68
  114.4 17.7 %collective-permute-start.23 = (bf16[8,288,128]{2,1,0:T(8,128)(2,1)S(1)}, bf16[8,288,128]{2,1,0:T(8,128)(2,1)S(1)}, u32[]{:S(2)}, u32[]{:S(2)}) collective-permute-start(bf16[8,288,128]{2,1,0:T(8,128)(2,1)S(1)} %get-tuple-element.159), channel_id=1, source_target_pairs={{0,4},{1,5},{2,6},{3,7},{4,0},{5,1},{6,2},{7,3},{8,12},{9,13},{10,... | collective-permute-start | bytes 1769480 | tf_op jit(solution)/shard_map/ppermute | solution.py:68
  116.5 15.6 %collective-permute-start.22 = (bf16[4,576,128]{2,1,0:T(8,128)(2,1)S(1)}, bf16[4,576,128]{2,1,0:T(8,128)(2,1)S(1)}, u32[]{:S(2)}, u32[]{:S(2)}) collective-permute-start(bf16[4,576,128]{2,1,0:T(8,128)(2,1)S(1)} %get-tuple-element.153), channel_id=1, source_target_pairs={{0,2},{1,3},{2,0},{3,1},{4,6},{5,7},{6,4},{7,5},{8,10},{9,11},{10,... | collective-permute-start | bytes 1769480 | tf_op jit(solution)/shard_map/ppermute | solution.py:68
  118.3 13.8 %collective-permute-start.25 = (f32[8,640]{1,0:T(8,128)S(1)}, f32[8,640]{1,0:T(8,128)S(1)}, u32[]{:S(2)}, u32[]{:S(2)}) collective-permute-start(f32[8,640]{1,0:T(8,128)S(1)} %add.1309), channel_id=1, source_target_pairs={{0,2},{1,3},{2,0},{3,1},{4,6},{5,7},{6,4},{7,5},{8,10},{9,11},{10,... | collective-permute-start | bytes 61448 | tf_op jit(solution)/shard_map/ppermute | solution.py:68
  133.0 22.4 %collective-permute-start.28 = (bf16[4,576,128]{2,1,0:T(8,128)(2,1)}, bf16[4,576,128]{2,1,0:T(8,128)(2,1)S(1)}, u32[]{:S(2)}, u32[]{:S(2)}) collective-permute-start(bf16[4,576,128]{2,1,0:T(8,128)(2,1)} %add_convert_fusion), channel_id=1, source_target_pairs={{0,4},{1,5},{2,6},{3,7},{4,0},{5,1},{6,2},{7,3},{8,12},{9,13},{10,... | collective-permute-start | bytes 1769480 | tf_op jit(solution)/shard_map/ppermute | solution.py:68
  133.6 21.8 %collective-permute-start.29 = (bf16[4,576,128]{2,1,0:T(8,128)(2,1)S(1)}, bf16[4,576,128]{2,1,0:T(8,128)(2,1)}, u32[]{:S(2)}, u32[]{:S(2)}) collective-permute-start(bf16[4,576,128]{2,1,0:T(8,128)(2,1)S(1)} %get-tuple-element.105), channel_id=1, source_target_pairs={{0,2},{1,3},{2,0},{3,1},{4,6},{5,7},{6,4},{7,5},{8,10},{9,11},{10,... | collective-permute-start | bytes 1769480 | tf_op jit(solution)/shard_map/ppermute | solution.py:68
  134.1 13.8 %collective-permute-start.30 = (f32[8,640]{1,0:T(8,128)S(1)}, f32[8,640]{1,0:T(8,128)S(1)}, u32[]{:S(2)}, u32[]{:S(2)}) collective-permute-start(f32[8,640]{1,0:T(8,128)S(1)} %add.1315), channel_id=1, source_target_pairs={{0,4},{1,5},{2,6},{3,7},{4,0},{5,1},{6,2},{7,3},{8,12},{9,13},{10,... | collective-permute-start | bytes 61448 | tf_op jit(solution)/shard_map/ppermute | solution.py:68
  136.4 11.5 %collective-permute-start.33 = (bf16[2,288,128]{2,1,0:T(8,128)(2,1)}, bf16[2,288,128]{2,1,0:T(8,128)(2,1)}, u32[]{:S(2)}, u32[]{:S(2)}) collective-permute-start(bf16[2,288,128]{2,1,0:T(8,128)(2,1)} %get-tuple-element.154), channel_id=1, source_target_pairs={{0,24},{1,25},{2,26},{3,27},{4,28},{5,29},{6,30},{7,31},{8,0},{9,1... | collective-permute-start | bytes 442376 | tf_op jit(solution)/shard_map/ppermute | solution.py:68
  137.0 10.9 %collective-permute-start.32 = (bf16[2,288,128]{2,1,0:T(8,128)(2,1)}, bf16[2,288,128]{2,1,0:T(8,128)(2,1)}, u32[]{:S(2)}, u32[]{:S(2)}) collective-permute-start(bf16[2,288,128]{2,1,0:T(8,128)(2,1)} %get-tuple-element.155), channel_id=1, source_target_pairs={{0,16},{1,17},{2,18},{3,19},{4,20},{5,21},{6,22},{7,23},{8,24},{9,... | collective-permute-start | bytes 442376 | tf_op jit(solution)/shard_map/ppermute | solution.py:68
  155.4 9.7 %collective-permute-start.43 = (f32[8,640]{1,0:T(8,128)S(1)}, f32[8,640]{1,0:T(8,128)S(1)}, u32[]{:S(2)}, u32[]{:S(2)}) collective-permute-start(f32[8,640]{1,0:T(8,128)S(1)} %add.1336), channel_id=1, source_target_pairs={{0,24},{1,25},{2,26},{3,27},{4,28},{5,29},{6,30},{7,31},{8,0},{9,1... | collective-permute-start | bytes 61448 | tf_op jit(solution)/shard_map/ppermute | solution.py:68
  155.5 11.6 %collective-permute-start.42 = (f32[8,640]{1,0:T(8,128)S(1)}, f32[8,640]{1,0:T(8,128)S(1)}, u32[]{:S(2)}, u32[]{:S(2)}) collective-permute-start(f32[8,640]{1,0:T(8,128)S(1)} %add.1336), channel_id=1, source_target_pairs={{0,16},{1,17},{2,18},{3,19},{4,20},{5,21},{6,22},{7,23},{8,24},{9,... | collective-permute-start | bytes 61448 | tf_op jit(solution)/shard_map/ppermute | solution.py:68
  155.6 11.5 %collective-permute-start.41 = (f32[8,640]{1,0:T(8,128)S(1)}, f32[8,640]{1,0:T(8,128)S(1)}, u32[]{:S(2)}, u32[]{:S(2)}) collective-permute-start(f32[8,640]{1,0:T(8,128)S(1)} %add.1336), channel_id=1, source_target_pairs={{0,8},{1,9},{2,10},{3,11},{4,12},{5,13},{6,14},{7,15},{8,16},{9,17... | collective-permute-start | bytes 61448 | tf_op jit(solution)/shard_map/ppermute | solution.py:68
  160.3 16.1 %collective-permute-start.39 = (bf16[576,128]{1,0:T(8,128)(2,1)S(1)}, bf16[576,128]{1,0:T(8,128)(2,1)S(1)}, u32[]{:S(2)}, u32[]{:S(2)}) collective-permute-start(bf16[576,128]{1,0:T(8,128)(2,1)S(1)} %get-tuple-element.149), channel_id=1, source_target_pairs={{0,24},{1,25},{2,26},{3,27},{4,28},{5,29},{6,30},{7,31},{8,0},{9,1... | collective-permute-start | bytes 442376 | tf_op jit(solution)/shard_map/ppermute | solution.py:68
  162.7 14.4 %collective-permute-start.38 = (bf16[576,128]{1,0:T(8,128)(2,1)S(1)}, bf16[576,128]{1,0:T(8,128)(2,1)S(1)}, u32[]{:S(2)}, u32[]{:S(2)}) collective-permute-start(bf16[576,128]{1,0:T(8,128)(2,1)S(1)} %get-tuple-element.150), channel_id=1, source_target_pairs={{0,16},{1,17},{2,18},{3,19},{4,20},{5,21},{6,22},{7,23},{8,24},{9,... | collective-permute-start | bytes 442376 | tf_op jit(solution)/shard_map/ppermute | solution.py:68
  165.1 12.0 %collective-permute-start.37 = (bf16[576,128]{1,0:T(8,128)(2,1)S(1)}, bf16[576,128]{1,0:T(8,128)(2,1)S(1)}, u32[]{:S(2)}, u32[]{:S(2)}) collective-permute-start(bf16[576,128]{1,0:T(8,128)(2,1)S(1)} %get-tuple-element.151), channel_id=1, source_target_pairs={{0,8},{1,9},{2,10},{3,11},{4,12},{5,13},{6,14},{7,15},{8,16},{9,17... | collective-permute-start | bytes 442376 | tf_op jit(solution)/shard_map/ppermute | solution.py:68
  167.1 14.1 %collective-permute-start.36 = (bf16[2,128,384]{2,1,0:T(8,128)(2,1)S(1)}, bf16[2,128,384]{2,1,0:T(8,128)(2,1)S(1)}, u32[]{:S(2)}, u32[]{:S(2)}) collective-permute-start(bf16[2,128,384]{2,1,0:T(8,128)(2,1)S(1)} %get-tuple-element.160), channel_id=1, source_target_pairs={{0,3},{1,2},{2,1},{3,0},{4,7},{5,6},{6,5},{7,4},{8,11},{9,10},{10,... | collective-permute-start | bytes 589832 | tf_op jit(solution)/shard_map/ppermute | solution.py:73
  (39 other events, 295.3 us)

commit v3 on v2

--- a/solution.py
+++ b/solution.py
@@ -26,6 +26,7 @@
 WIDE = 640
 BLOCKS = 32
 BLOCK_ROWS = 864
+VECTOR_ROWS = 48
 HEAD_ROWS = 576
 TAIL_ROWS = BLOCK_ROWS - HEAD_ROWS
 SIZES = {"z": 4, "y": 2, "x": 2, "c": 2}
@@ -77,32 +78,33 @@
     return lax.optimization_barrier(arrays)
 
 
-def gather_all(head, tail, packed):
+def gather_all(head, tail, packed, others):
     hz = [moved(head, "z", s) for s in (1, 2, 3)]
     tx = moved(tail, "x", 1)
     two = across(packed, 2)
-    one = across(packed, 1)
-    head, tail, tx, one, two, *hz = together(head, tail, tx, one, two, *hz)
+    head, tail, tx, two, *hz = together(head, tail, tx, two, *hz)
+    near = jnp.stack([packed, two])
     own = jnp.stack([head] + hz)
     pair = jnp.stack([tail, tx])
+    far = across(near, 1)
     ay = moved(own, "y", 1)
     ax = moved(own, "x", 1)
-    ac = moved(own, "c", 1)
     tz = [moved(pair, "z", s) for s in (1, 2, 3)]
-    three = across(two, 1)
-    own, pair, ay, ax, three, *tz = together(own, pair, ay, ax, three, *tz)
-    tokens = jnp.stack([packed, one, two, three])
+    own, pair, ay, ax, near, far, others, *tz = together(own, pair, ay, ax, near, far, others, *tz)
+    tokens = jnp.stack([near[0], far[0], near[1], far[1]])
     tables = place_tables(tokens)
     eight = jnp.concatenate([pair] + tz)
     axy = moved(ay, "x", 1)
     ty = moved(eight, "y", 1)
+    ac = moved(own, "c", 1)
     acy = moved(ay, "c", 1)
     acx = moved(ax, "c", 1)
     tc = moved(eight, "c", 1)
-    axy, ty, tokens, *tables = together(axy, ty, tokens, *tables)
+    axy, ty, ac, acy, acx, tc, tokens, *tables = together(axy, ty, ac, acy, acx, tc, tokens, *tables)
     acxy = moved(axy, "c", 1)
     tcy = moved(ty, "c", 1)
-    return [own, ay, ax, axy, ac, acy, acx, acxy], [eight, ty, tc, tcy], tokens, tables
+    heads = [own, ay, ax, axy, ac, acy, acx, acxy]
+    return heads, [eight, ty, tc, tcy], tokens, tables, others
 
 
 def place_tables(tokens):
@@ -146,49 +148,60 @@
     return kept.astype(F32) + received.astype(F32)
 
 
-def scatter_blocks(head_sends, head_keep, tail_sends, tail_keep, vector, pairs):
+def packed_vector(vector):
+    high = lax.reduce_precision(vector, 8, 7)
+    return jnp.concatenate([high.astype(BF16), (vector - high).astype(BF16)])
+
+
+def unpacked_vector(rows):
+    return rows[:VECTOR_ROWS].astype(F32) + rows[VECTOR_ROWS:].astype(F32)
+
+
+def scatter_blocks(head_sends, head_keep, tail_sends, tail_keep, vector, dkv_send, dkv_keep):
     head_first, head_rest = head_sends
     tail_first, tail_rest = tail_sends
     h1 = moved(head_first, "c", 1)
     t1 = moved(tail_first, "c", 1)
     hr = moved(head_rest, "c", 1)
     tr = moved(tail_rest, "c", 1)
-    vr = moved(vector, "c", 1)
+    dr = across(dkv_send, 1)
     h1, t1 = together(h1, t1)
-    hx = summed(head_keep[12:], h1).astype(BF16)
+    cut = 4 * HEAD_ROWS
+    hx = summed(head_keep[12:].reshape(cut, LANES), h1[:cut]).astype(BF16)
+    vector = unpacked_vector(vector) + unpacked_vector(h1[cut:])
+    vector = packed_vector(vector)
     ty = summed(tail_keep[8:], t1).astype(BF16)
-    hx1 = moved(hx, "x", 1)
+    hx1 = moved(jnp.concatenate([hx, vector]), "x", 1)
     tr1 = moved(ty, "y", 1)
     hx = summed(head_keep[8:12], hr[8:]).astype(BF16)
-    hy = summed(head_keep[4:8], hr[4:8])
+    hy = summed(head_keep[4:8], hr[4:8]).reshape(cut, LANES)
     hz = summed(head_keep[:4], hr[:4])
     tail = summed(tail_keep[:8], tr)
-    vector = vector + vr
-    vr = moved(vector, "x", 1)
-    hx1, tr1, vr, hx, hy, hz, tail = together(hx1, tr1, vr, hx, hy, hz, tail)
-    hy = summed(hy, hx1).astype(BF16)
+    dkv = summed(dkv_keep, dr).astype(BF16)
+    hx1, tr1, hx, hy, hz, tail, dkv, vector = together(hx1, tr1, hx, hy, hz, tail, dkv, vector)
+    hy = summed(hy, hx1[:cut]).astype(BF16)
+    vector = packed_vector(unpacked_vector(vector) + unpacked_vector(hx1[cut:]))
     tz = [summed(tail[2 * s : 2 * s + 2], tr1[2 * s : 2 * s + 2]).astype(BF16) for s in (1, 2, 3)]
-    vector = vector + vr
-    hy1 = moved(hy, "y", 1)
+    hy1 = moved(jnp.concatenate([hy, vector]), "y", 1)
     hx1 = moved(hx, "x", 1)
     tzr = [moved(tz[s - 1], "z", s) for s in (1, 2, 3)]
-    vr = moved(vector, "y", 1)
     tail = summed(tail[:2], tr1[:2])
-    hy1, hx1, vr, tail, pairs, *tzr = together(hy1, hx1, vr, tail, pairs, *tzr)
+    hy1, hx1, tail, dkv, vector, *tzr = together(hy1, hx1, tail, dkv, vector, *tzr)
+    vector = packed_vector(unpacked_vector(vector) + unpacked_vector(hy1[cut:]))
+    hy1 = hy1[:cut].reshape(4, HEAD_ROWS, LANES)
     head = [summed(summed(hz[s], hx1[s]), hy1[s]) for s in range(4)]
     tx = summed(summed(tail[1], tzr[0][1]), summed(tzr[1][1], tzr[2][1])).astype(BF16)
     tail = summed(summed(tail[0], tzr[0][0]), summed(tzr[1][0], tzr[2][0]))
-    vector = vector + vr
-    hzr = [moved(head[s].astype(BF16), "z", s) for s in (1, 2, 3)]
+    hzr = [moved(jnp.concatenate([head[s].astype(BF16), vector]), "z", s) for s in (1, 2, 3)]
+    dr = across(dkv[1], 2)
     txr = moved(tx, "x", 1)
-    pairs = [pairs[0]] + [across(pairs[d], d) for d in (1, 2, 3)]
-    vr = [moved(vector, "z", s) for s in (1, 2, 3)]
     place = coordinates(device_number() // inner_count())["z"]
-    parts = jnp.stack([vector] + vr)
+    parts = jnp.stack([vector] + [part[HEAD_ROWS:] for part in hzr])
     vector = sum(
-        lax.dynamic_index_in_dim(parts, (place - z) % 4, 0, keepdims=False) for z in range(4)
-    )
-    return head[0], hzr, tail, txr, vector, pairs
+        unpacked_vector(lax.dynamic_index_in_dim(parts, (place - z) % 4, 0, keepdims=False))
+        for z in range(4)
+    )
+    return head[0], hzr, tail, txr, vector, (dkv[0], dr)
 
 
 def lower_lanes(shape):
@@ -264,8 +277,8 @@
 def flat_kernel(kind_ref, head_ref, one_ref, two_ref, three_ref, tail_ref, other_ref, *refs):
     kind = kind_ref[0]
     tiles, narrow, flat_ref = refs[-3:]
-    tiles[0:HEAD_ROWS, :] = (head_ref[...] + one_ref[...].astype(F32)) + (
-        two_ref[...].astype(F32) + three_ref[...].astype(F32)
+    tiles[0:HEAD_ROWS, :] = (head_ref[...] + one_ref[0:HEAD_ROWS, :].astype(F32)) + (
+        two_ref[0:HEAD_ROWS, :].astype(F32) + three_ref[0:HEAD_ROWS, :].astype(F32)
     )
     tiles[HEAD_ROWS:BLOCK_ROWS, :] = tail_ref[...] + other_ref[...].astype(F32)
 
@@ -386,8 +399,8 @@
     head_parts = refs[1:9]
     tail_parts = refs[9:13]
     (tokens_ref, cos_ref, sin_ref, place_q_ref, place_k_ref, gains_ref, bias_q_ref, bias_kv_ref, grad_ref) = refs[13:22]
-    (block_out_ref, head_first, head_rest, head_keep_out, tail_first, tail_rest, tail_keep_out, vector_ref, dkv_ref, dq_wq_ref, d_mid_ref, w_kv) = refs[22:34]
-    (raw_head, raw_tail, w_q, w_out, w_gate, w_up, w_down, normed_all, hidden_all, keys, values, queries, probs, attended, act_all, block_acc, d_hidden, d_attended, dkv_all, d_query, head_send, head_keep, tail_send, tail_keep, sems) = refs[34:]
+    (block_out_ref, head_first, head_rest, head_keep_out, tail_first, tail_rest, tail_keep_out, vector_out, dkv_send, dkv_keep, dq_wq_ref, d_mid_ref, w_kv) = refs[22:35]
+    (raw_head, raw_tail, w_q, w_out, w_gate, w_up, w_down, normed_all, hidden_all, keys, values, queries, probs, attended, act_all, block_acc, d_hidden, d_attended, dkv_all, d_query, head_send, head_keep, tail_send, tail_keep, vector_ref, sems) = refs[35:]
 
     copies = []
     for k, part in enumerate(head_parts):
@@ -521,7 +534,7 @@
         keep[slot, rows, :] = jnp.where(core == 0, even, odd).astype(BF16)
 
     def feed_forward(chunk, first, send, keep, table):
-        cols = pl.ds(pl.multiple_of(chunk * 256, 256), 256)
+        cols = pl.ds(pl.multiple_of(chunk * 512, 512), 512)
         gate = product(hidden_two, w_gate[:, cols])
         up = product(hidden_two, w_up[:, cols])
         sigma = 1.0 / (1.0 + jnp.exp(-gate))
@@ -533,22 +546,20 @@
         d_up = (d_act * gate * sigma).astype(BF16)
         d_gate = (d_act * up * sigma * (1.0 + gate * (1.0 - sigma))).astype(BF16)
         d_hidden[...] += times_transposed(d_gate, w_gate[:, cols]) + times_transposed(d_up, w_up[:, cols])
-        rows = pl.ds(pl.multiple_of((chunk - first) * 144, 144), 144)
+        rows = pl.ds(pl.multiple_of((chunk - first) * 288, 288), 288)
         for base, cotangent in ((4, d_gate), (8, d_up)):
             made = rows_product(hidden_two, cotangent)
             for k in range(4):
                 part = made[144 * k : 144 * k + 144, :]
-                even = jnp.concatenate([part[0:72, 0:128], part[0:72, 128:256]], axis=0)
-                odd = jnp.concatenate([part[72:144, 0:128], part[72:144, 128:256]], axis=0)
+                even = jnp.concatenate([part[0:72, LANES * j : LANES * j + LANES] for j in range(4)], axis=0)
+                odd = jnp.concatenate([part[72:144, LANES * j : LANES * j + LANES] for j in range(4)], axis=0)
                 store_pair(base + k, even, odd, send, keep, table, rows)
 
-    @pl.loop(0, 4)
+    @pl.loop(0, 2)
     def _(chunk):
         feed_forward(chunk, 0, head_send, head_keep, TO_HEAD)
 
-    @pl.loop(4, 6)
-    def _(chunk):
-        feed_forward(chunk, 4, tail_send, tail_keep, TO_TAIL)
+    feed_forward(2, 2, tail_send, tail_keep, TO_TAIL)
 
     def store_rows(at, even, odd):
         even_head, even_tail = even
@@ -607,7 +618,8 @@
         dkv_all[key_rows, 128:256] = jnp.where(low_keys, d_values[0], d_values[1]).astype(BF16)
         dkv_all[key_rows, 256:384] = jnp.where(low_keys, key_b, d_values[2]).astype(BF16)
         for slot in range(4):
-            dkv_ref[slot, mb] = dkv_all[pl.ds(pl.multiple_of(mb * 512 + slot * ROWS, ROWS), ROWS), :]
+            target = dkv_send if slot % 2 else dkv_keep
+            target[slot // 2, mb] = dkv_all[pl.ds(pl.multiple_of(mb * 512 + slot * ROWS, ROWS), ROWS), :]
 
     dkv = dkv_all[...]
     d_q = d_query[...]
@@ -636,8 +648,18 @@
     store_rows(1, query_tiles[2], key_tiles)
     store_rows(2, value_tiles, out_tiles[0])
     store_rows(3, out_tiles[1], out_tiles[2])
+    vector = jnp.concatenate(
+        [vector_ref[:, LANES * k : LANES * k + LANES] for k in range(5)] + [jnp.zeros((8, LANES), F32)], axis=0
+    )
+    high = vector.astype(BF16)
+    vector_out[0:VECTOR_ROWS, :] = high
+    vector_out[VECTOR_ROWS:, :] = (vector - high.astype(F32)).astype(BF16)
     copies = [
-        pltpu.make_async_copy(head_send.at[pl.ds(12, 4)], head_first, sems.at[0]),
+        pltpu.make_async_copy(head_send.at[12 + k], head_first.at[pl.ds(HEAD_ROWS * k, HEAD_ROWS)], sems.at[6 + k])
+        for k in range(4)
+    ]
+    copies += [
+        pltpu.make_async_copy(vector_out, head_first.at[pl.ds(4 * HEAD_ROWS, 2 * VECTOR_ROWS)], sems.at[0]),
         pltpu.make_async_copy(tail_send.at[pl.ds(8, 8)], tail_first, sems.at[1]),
         pltpu.make_async_copy(head_send.at[pl.ds(0, 12)], head_rest, sems.at[2]),
         pltpu.make_async_copy(tail_send.at[pl.ds(0, 8)], tail_rest, sems.at[3]),
@@ -679,37 +701,39 @@
         ((16, HEAD_ROWS, LANES), BF16),
         ((16, TAIL_ROWS, LANES), BF16),
         ((16, TAIL_ROWS, LANES), BF16),
+        ((8, WIDE), F32),
     ]
     return pl.pallas_call(
         layer_kernel,
         out_shape=(
             shape((2, MODEL_WIDTH, ROWS), BF16),
-            shape((4, HEAD_ROWS, LANES), BF16),
+            shape((4 * HEAD_ROWS + 2 * VECTOR_ROWS, LANES), BF16),
             shape((12, HEAD_ROWS, LANES), BF16),
             shape((16, HEAD_ROWS, LANES), BF16),
             shape((8, TAIL_ROWS, LANES), BF16),
             shape((8, TAIL_ROWS, LANES), BF16),
             shape((16, TAIL_ROWS, LANES), BF16),
-            shape((8, WIDE), F32),
-            shape((4, 2, ROWS, 384), BF16),
+            shape((2 * VECTOR_ROWS, LANES), BF16),
+            shape((2, 2, ROWS, 384), BF16),
+            shape((2, 2, ROWS, 384), BF16),
             shape((256, WIDE), F32),
             shape((256, WIDE), F32),
             shape((WIDE, 384), BF16),
         ),
         in_specs=[pl.BlockSpec(memory_space=pltpu.SMEM)] + [anywhere] * 12 + [vmem] * 9,
-        out_specs=(vmem,) + (anywhere,) * 6 + (vmem,) * 5,
+        out_specs=(vmem,) + (anywhere,) * 6 + (vmem,) * 6,
         scratch_shapes=[pltpu.VMEM(dims, kind) for dims, kind in scratch]
         + [pltpu.SemaphoreType.DMA((12,))],
-        compiler_params=pltpu.CompilerParams(vmem_limit_bytes=56 * 1024 * 1024),
+        compiler_params=pltpu.CompilerParams(vmem_limit_bytes=50 * 1024 * 1024),
         name="layer",
     )(slots, *heads, *tails, tokens, cosines, sines, place_q, place_k, gains, bias_q, bias_kv, grad)
 
 
-def input_kernel(tokens_ref, gains_ref, w_kv_ref, dq_wq_ref, d_mid_ref, own_ref, one_ref, two_ref, three_ref, out_ref):
+def input_kernel(tokens_ref, gains_ref, w_kv_ref, dq_wq_ref, d_mid_ref, own_ref, other_ref, out_ref):
     lane = lax.broadcasted_iota(jnp.int32, (2 * ROWS, WIDE), 1)
     x = jnp.where(lane < MODEL_WIDTH, tokens_ref[0].astype(F32).reshape(2 * ROWS, WIDE), 0.0)
     normed, scale = normed_rows(x)
-    total = (own_ref[...].astype(F32) + one_ref[...].astype(F32)) + (two_ref[...].astype(F32) + three_ref[...].astype(F32))
+    total = own_ref[...].astype(F32) + other_ref[...].astype(F32)
     total = total.reshape(2 * ROWS, 384).astype(BF16)
     d_norm = (dq_wq_ref[...] + times_transposed(total, w_kv_ref[...])) * gains_ref[0:1, :]
     d_input = d_mid_ref[...] + scale * (d_norm - normed * row_mean(d_norm * normed))
@@ -721,7 +745,7 @@
     return pl.pallas_call(
         input_kernel,
         out_shape=jax.ShapeDtypeStruct((2, MODEL_WIDTH, ROWS), BF16),
-        in_specs=[pl.BlockSpec(memory_space=pltpu.VMEM)] * 9,
+        in_specs=[pl.BlockSpec(memory_space=pltpu.VMEM)] * 7,
         out_specs=pl.BlockSpec(memory_space=pltpu.VMEM),
         name="input_grad",
     )(tokens, gains, w_kv, dq_wq, d_mid, *parts)
@@ -765,30 +789,33 @@
 
 def local(tokens_in, places, out_grad, weights, first_moment, second_moment, vectors, vector_first, vector_second):
     kind = kind_of(device_number() // inner_count()).astype(jnp.int32).reshape(1)
-    slots = slot_table()
     block = whole_block(weights).reshape(BLOCK_ROWS, LANES)
     head, tail = to_tiles(kind, block)
 
+    head, tail, tokens_in, places = together(head, tail, tokens_in, places)
     own_tokens = tokens_in.reshape(2, ROWS, MODEL_WIDTH)
     own_places = places.reshape(2, ROWS)
     marks = jnp.stack([own_places // 16, own_places % 16], axis=-1).astype(BF16)
     packed = jnp.concatenate(
         [own_tokens, marks, jnp.zeros((2, ROWS, WIDE - MODEL_WIDTH - 2), BF16)], axis=-1
     )
-    heads, tails, tokens, tables = gather_all(head, tail, packed)
     padding = ((0, 0), (0, WIDE - MODEL_WIDTH))
     gains = jnp.pad(vectors[: 2 * MODEL_WIDTH].reshape(2, MODEL_WIDTH), padding)
     bias_q = jnp.pad(vectors[2 * MODEL_WIDTH : 3 * MODEL_WIDTH].reshape(1, MODEL_WIDTH), padding)
     bias_kv = bias_tiles(vectors[1728:1920], vectors[1920:2112]).reshape(1, 384)
     grad = jnp.pad(out_grad.reshape(2 * ROWS, MODEL_WIDTH), padding)
-
-    (block_out, head_first, head_rest, head_keep, tail_first, tail_rest, tail_keep, vector, dkv, dq_wq, d_mid, w_kv) = run_layer(
+    others = (slot_table(), gains, bias_q, bias_kv, grad)
+    heads, tails, tokens, tables, others = gather_all(head, tail, packed, others)
+    slots, gains, bias_q, bias_kv, grad = others
+
+    (block_out, head_first, head_rest, head_keep, tail_first, tail_rest, tail_keep, vector, dkv_send, dkv_keep, dq_wq, d_mid, w_kv) = run_layer(
         slots, heads, tails, tokens, *tables, gains, bias_q, bias_kv, grad
     )
     head, hzr, tail, txr, vector, pairs = scatter_blocks(
-        (head_first, head_rest), head_keep, (tail_first, tail_rest), tail_keep, vector, dkv
+        (head_first, head_rest), head_keep, (tail_first, tail_rest), tail_keep, vector, dkv_send, dkv_keep
     )
     input_grad = run_input(tokens, gains, w_kv, dq_wq, d_mid, pairs)
+    head, input_grad = together(head, input_grad)
     state = (weights, first_moment, second_moment)
     parts = (head, *hzr, tail, txr)
     if inner_count() == 1:
@@ -802,6 +829,7 @@
         new_weights, new_first, new_second = adamw(
             weights, grad_own, first_moment, second_moment, RATE_MATRIX, DECAY
         )
+    vector = jnp.transpose(vector.reshape(6, 8, LANES), (1, 0, 2)).reshape(8, 6 * LANES)
     pair = vector[3]
     vector_grad = jnp.concatenate(
         [

time: 186 us -> 168 us (0.903)
  waiting for transfers between devices: 75.2 us -> 67.8 us
  starting transfers between devices: 36.9 us -> 32.8 us
  other arithmetic: 15.1 us -> 11.4 us
  Pallas kernels: 43.9 us -> 41.6 us
    ppermute x38 -> x32, waiting for transfers between devices: 74.7 us -> 67.8 us  [moved(): return lax.ppermute(buffer, ('dp', 'ctx'), pairs)]
    ppermute x6 -> x4, starting transfers between devices: 5.35 us -> 2.54 us  [across(): lax.ppermute(buffer, 'ctx', [(i, i ^ distance) for i in range(count)])]
    pallas_call x1, Pallas kernels: 35.3 us -> 33.1 us  [run_layer(): pl.pallas_call(layer_kernel, out_shape=(shape((2, MODEL_WIDTH, ROWS), BF1...]
    ppermute x38 -> x32, starting transfers between devices: 31.6 us -> 30.3 us  [moved(): return lax.ppermute(buffer, ('dp', 'ctx'), pairs)]
    unnamed x57 -> x64, local copies, waits for them, and re-layouts: 6.67 us -> 7.36 us
  transfers between devices with their start and end apart: 44 -> 36, of which waited for: 15 -> 15; matrix products, arithmetic and copies ran while one was open for 10% -> 8% of each run, Pallas kernels for 3% -> 2%
where the time goes in v3:
time: 168 us; the launch traced here: 167 us
  waiting for transfers between devices  67.8 us (40%)
  Pallas kernels  41.6 us (25%)
  starting transfers between devices  32.8 us (20%)
  local copies, waits for them, and re-layouts  12.4 us (7%)
  other arithmetic  11.4 us (7%)
    ppermute x32, waiting for transfers between devices, moved(): return lax.ppermute(buffer, ('dp', 'ctx'), pairs)  67.8 us
    pallas_call x1, Pallas kernels, run_layer(): pl.pallas_call(layer_kernel, out_shape=(shape((2, MODEL_WIDTH, ROWS), BF1...  33.1 us
    ppermute x32, starting transfers between devices, moved(): return lax.ppermute(buffer, ('dp', 'ctx'), pairs)  30.3 us
    unnamed x64, local copies, waits for them, and re-layouts  7.36 us
  transfers between devices with their start and end apart: 36, of which 15 were waited for; matrix products, arithmetic and copies ran while one was open for 8% of the time, Pallas kernels for 2%

profile of v3, /device:TPU:0, one launch (start us, length us, event | category | flops | bytes accessed | tf_op | source)
XLA Modules:
  0.0 167.3 jit_solution(10173888971406093057)
XLA Ops:
  0.7 1.9 %to_tiles.1 = (bf16[576,128]{1,0:T(8,128)(2,1)}, bf16[288,128]{1,0:T(8,128)(2,1)}) custom-call(s32[1]{0:T(128)} %bitcast.kind_ref, f32[864,128]{1,0:T(8,128)} %bitcast.179), custom_call_target="tpu_custom_call" | custom-call | tf_op jit(solution)/shard_map/to_tiles/pallas_call | solution.py:258
  2.5 2.9 %collective-permute-start.2 = (bf16[576,128]{1,0:T(8,128)(2,1)}, bf16[576,128]{1,0:T(8,128)(2,1)S(1)}, u32[]{:S(2)}, u32[]{:S(2)}) collective-permute-start(bf16[576,128]{1,0:T(8,128)(2,1)} %get-tuple-element.88), channel_id=1, source_target_pairs={{0,8},{1,9},{2,10},{3,11},{4,12},{5,13},{6,14},{7,15},{8,16},{9,17... | collective-permute-start | bytes 442376 | tf_op jit(solution)/shard_map/ppermute | solution.py:69
  5.4 2.7 %collective-permute-start.3 = (bf16[576,128]{1,0:T(8,128)(2,1)}, bf16[576,128]{1,0:T(8,128)(2,1)S(1)}, u32[]{:S(2)}, u32[]{:S(2)}) collective-permute-start(bf16[576,128]{1,0:T(8,128)(2,1)} %get-tuple-element.88), channel_id=1, source_target_pairs={{0,16},{1,17},{2,18},{3,19},{4,20},{5,21},{6,22},{7,23},{8,24},{9,... | collective-permute-start | bytes 442376 | tf_op jit(solution)/shard_map/ppermute | solution.py:69
  8.1 1.2 collective-permute-start.4
  10.3 1.2 copy.23
  11.7 1.6 collective-permute-start.1
  14.0 8.0 %collective-permute-done = bf16[288,128]{1,0:T(8,128)(2,1)S(1)} collective-permute-done((bf16[288,128]{1,0:T(8,128)(2,1)S(1)}, bf16[288,128]{1,0:T(8,128)(2,1)S(1)}, u32[]{:S(2)}, u32[]{:S(2)}) %collective-permute-start) | collective-permute-done | bytes 73760 | tf_op jit(solution)/shard_map/ppermute | solution.py:69
  22.1 1.6 collective-permute-start.5
  23.7 1.5 collective-permute-start.6
  26.8 1.4 collective-permute-start.8
  28.2 4.7 %collective-permute-done.10 = bf16[2,288,128]{2,1,0:T(8,128)(2,1)S(1)} collective-permute-done((bf16[2,288,128]{2,1,0:T(8,128)(2,1)}, bf16[2,288,128]{2,1,0:T(8,128)(2,1)S(1)}, u32[]{:S(2)}, u32[]{:S(2)}) %collective-permute-start.10) | collective-permute-done | bytes 147488 | tf_op jit(solution)/shard_map/ppermute | solution.py:69
  32.9 2.7 %collective-permute-start.9 = (bf16[2,288,128]{2,1,0:T(8,128)(2,1)}, bf16[2,288,128]{2,1,0:T(8,128)(2,1)}, u32[]{:S(2)}, u32[]{:S(2)}) collective-permute-start(bf16[2,288,128]{2,1,0:T(8,128)(2,1)} %pad_maximum_fusion.11), channel_id=1, source_target_pairs={{0,16},{1,17},{2,18},{3,19},{4,20},{5,21},{6,22},{7,23},{8,24},{9,... | collective-permute-start | bytes 442376 | tf_op jit(solution)/shard_map/ppermute | solution.py:69
  36.3 6.2 %collective-permute-done.9 = bf16[2,288,128]{2,1,0:T(8,128)(2,1)} collective-permute-done((bf16[2,288,128]{2,1,0:T(8,128)(2,1)}, bf16[2,288,128]{2,1,0:T(8,128)(2,1)}, u32[]{:S(2)}, u32[]{:S(2)}) %collective-permute-start.9) | collective-permute-done | bytes 147488 | tf_op jit(solution)/shard_map/ppermute | solution.py:69
  47.6 11.2 %collective-permute-done.12.refs_10_ = bf16[8,288,128]{2,1,0:T(8,128)(2,1)} collective-permute-done((bf16[8,288,128]{2,1,0:T(8,128)(2,1)S(1)}, bf16[8,288,128]{2,1,0:T(8,128)(2,1)}, u32[]{:S(2)}, u32[]{:S(2)}) %collective-permute-start.12) | collective-permute-done | bytes 589856 | tf_op jit(solution)/shard_map/ppermute | solution.py:69
  59.3 1.9 %fusion.1 = (f32[4,2,128,128]{3,2,1,0:T(8,128)S(1)}, f32[4,2,128,128]{3,2,1,0:T(8,128)S(1)}) fusion(f32[128]{0:T(128)S(1)} %compare_select_fusion, f32[128]{0:T(128)S(1)} %mul.204, f32[4,2,128]{2,1,0:T(2,128)S(1)} %get-tuple-element.178), kind=kLoop, calls=%fused_computation.16 | loop fusion | flops 262144 | bytes 1053696 | tf_op jit(solution)/shard_map/mul | solution.py:119
  64.4 1.1 collective-permute-done.18.refs_12_
  66.4 33.1 %layer.1 = (bf16[2,576,128]{2,1,0:T(8,128)(2,1)}, bf16[2400,128]{1,0:T(8,128)(2,1)}, bf16[12,576,128]{2,1,0:T(8,128)(2,1)}, bf16[16,576,128]{2,1,0:T(8,128)(2,1)...) custom-call(s32[97]{0:T(128)S(1)} %stack.457.refs_0_, ...), custom_call_target="tpu_custom_call" | custom-call | tf_op jit(solution)/shard_map/layer/pallas_call | solution.py:706
  102.5 1.7 %collective-permute-done.24 = bf16[8,288,128]{2,1,0:T(8,128)(2,1)S(1)} collective-permute-done((bf16[8,288,128]{2,1,0:T(8,128)(2,1)S(1)}, bf16[8,288,128]{2,1,0:T(8,128)(2,1)S(1)}, u32[]{:S(2)}, u32[]{:S(2)}) %collective-permute-start.24) | collective-permute-done | bytes 589856 | tf_op jit(solution)/shard_map/ppermute | solution.py:69
  104.4 1.6 collective-permute-start.22
  107.9 1.2 convert_add_fusion.2
  109.1 10.8 %collective-permute-done.22 = bf16[8,288,128]{2,1,0:T(8,128)(2,1)S(1)} collective-permute-done((bf16[8,288,128]{2,1,0:T(8,128)(2,1)S(1)}, bf16[8,288,128]{2,1,0:T(8,128)(2,1)S(1)}, u32[]{:S(2)}, u32[]{:S(2)}) %collective-permute-start.22) | collective-permute-done | bytes 589856 | tf_op jit(solution)/shard_map/ppermute | solution.py:69
  119.9 2.1 %collective-permute-done.21 = bf16[2400,128]{1,0:T(8,128)(2,1)S(1)} collective-permute-done((bf16[2400,128]{1,0:T(8,128)(2,1)S(1)}, bf16[2400,128]{1,0:T(8,128)(2,1)S(1)}, u32[]{:S(2)}, u32[]{:S(2)}) %collective-permute-start.21) | collective-permute-done | bytes 614432 | tf_op jit(solution)/shard_map/ppermute | solution.py:69
  124.0 3.0 %collective-permute-start.29 = (bf16[2,288,128]{2,1,0:T(8,128)(2,1)S(1)}, bf16[2,288,128]{2,1,0:T(8,128)(2,1)}, u32[]{:S(2)}, u32[]{:S(2)}) collective-permute-start(bf16[2,288,128]{2,1,0:T(8,128)(2,1)S(1)} %get-tuple-element.188), channel_id=1, source_target_pairs={{0,16},{1,17},{2,18},{3,19},{4,20},{5,21},{6,22},{7,23},{8,24},{9,... | collective-permute-start | bytes 442376 | tf_op jit(solution)/shard_map/ppermute | solution.py:69
  128.1 4.2 %collective-permute-done.28 = bf16[2,288,128]{2,1,0:T(8,128)(2,1)} collective-permute-done((bf16[2,288,128]{2,1,0:T(8,128)(2,1)S(1)}, bf16[2,288,128]{2,1,0:T(8,128)(2,1)}, u32[]{:S(2)}, u32[]{:S(2)}) %collective-permute-start.28) | collective-permute-done | bytes 147488 | tf_op jit(solution)/shard_map/ppermute | solution.py:69
  132.3 3.8 %collective-permute-done.29 = bf16[2,288,128]{2,1,0:T(8,128)(2,1)} collective-permute-done((bf16[2,288,128]{2,1,0:T(8,128)(2,1)S(1)}, bf16[2,288,128]{2,1,0:T(8,128)(2,1)}, u32[]{:S(2)}, u32[]{:S(2)}) %collective-permute-start.29) | collective-permute-done | bytes 147488 | tf_op jit(solution)/shard_map/ppermute | solution.py:69
  137.2 2.1 %fusion.2 = (bf16[576,128]{1,0:T(8,128)(2,1)S(1)}, bf16[576,128]{1,0:T(8,128)(2,1)S(1)}, bf16[576,128]{1,0:T(8,128)(2,1)S(1)}, f32[576,128]{1,0:T(8,128)}) fusion(f32[4,576,128]{2,1,0:T(8,128)S(1)} %get-tuple-element.132, bf16[2400,128]{1,0:T(8,128)(2,1)S(1)} %collective-permute-done.26, bf16[4,576,128]{2,1,0:T(8,128)(2,1)} %collective-permute-done.27), kind=kLoop, calls=%fused_computation.21 | loop fusion | flops 1400832 | bytes 3096576 | tf_op jit(solution)/shard_map/convert_element_type | solution.py:195
  139.3 3.1 %collective-permute-start.34 = (bf16[672,128]{1,0:T(8,128)(2,1)S(1)}, bf16[672,128]{1,0:T(8,128)(2,1)S(1)}, u32[]{:S(2)}, u32[]{:S(2)}) collective-permute-start(bf16[672,128]{1,0:T(8,128)(2,1)S(1)} %get-tuple-element.211), channel_id=1, source_target_pairs={{0,24},{1,25},{2,26},{3,27},{4,28},{5,29},{6,30},{7,31},{8,0},{9,1... | collective-permute-start | bytes 516104 | tf_op jit(solution)/shard_map/ppermute | solution.py:69
  143.2 1.8 %fusion.9 = (bf16[288,128]{1,0:T(8,128)(2,1)S(1)}, f32[288,128]{1,0:T(8,128)}) fusion(f32[2,288,128]{2,1,0:T(8,128)S(1)} %get-tuple-element.149, bf16[2,288,128]{2,1,0:T(8,128)(2,1)} %collective-permute-done.30, bf16[2,288,128]{2,1,0:T(8,128)(2,1)} %collective-permute-done.29, bf16[2,288,128]{2,1,0:T(8,128)(2,1)} %collective-permute-done.28), kind=kLoop, calls=%fused_computation.55 | loop fusion | flops 479232 | bytes 958464 | tf_op jit(solution)/shard_map/convert_element_type | solution.py:193
  145.0 1.5 collective-permute-start.35
  147.8 10.6 %collective-permute-done.33.two_ref = bf16[672,128]{1,0:T(8,128)(2,1)S(1)} collective-permute-done((bf16[672,128]{1,0:T(8,128)(2,1)S(1)}, bf16[672,128]{1,0:T(8,128)(2,1)S(1)}, u32[]{:S(2)}, u32[]{:S(2)}) %collective-permute-start.33) | collective-permute-done | bytes 172064 | tf_op jit(solution)/shard_map/ppermute | solution.py:69
  160.0 3.3 %input_grad.1 = bf16[2,576,128]{2,1,0:T(8,128)(2,1)} custom-call(bf16[4,2,128,640]{3,2,1,0:T(8,128)(2,1)} %copy-done.2, f32[2,640]{1,0:T(2,128)} %copy-done.1, bf16[640,384]{1,0:T(8,128)(2,1)} %copy-done, f32[256,640]{1,0:T(8,128)} %get-tuple-element.143.dq_wq_ref, f32[256,640]{1,0:T(8,128)} %get-tuple-element.144.d_mid_ref, ...), custom_call_target="tpu_custom_call" | custom-call | tf_op jit(solution)/shard_map/input_grad/pallas_call | solution.py:745
  164.0 3.4 %finish.1 = (f32[864,128]{1,0:T(8,128)}, f32[864,128]{1,0:T(8,128)}, f32[864,128]{1,0:T(8,128)}) custom-call(s32[1]{0:T(128)} %bitcast.kind_ref, f32[576,128]{1,0:T(8,128)} %get-tuple-element.147.head_ref, bf16[672,128]{1,0:T(8,128)(2,1)} %copy-done.18, bf16[672,128]{1,0:T(8,128)(2,1)} %copy-done.17, bf16[672,128]{1,0:T(8,128)(2,1)} %copy-done.16, ...), custom_call_target="tpu_custom_call" | custom-call | tf_op jit(solution)/shard_map/finish/pallas_call | solution.py:333
  (175 shorter events, 27.2 us)
Async XLA Ops:
  2.5 19.4 %collective-permute-start.2 = (bf16[576,128]{1,0:T(8,128)(2,1)}, bf16[576,128]{1,0:T(8,128)(2,1)S(1)}, u32[]{:S(2)}, u32[]{:S(2)}) collective-permute-start(bf16[576,128]{1,0:T(8,128)(2,1)} %get-tuple-element.88), channel_id=1, source_target_pairs={{0,8},{1,9},{2,10},{3,11},{4,12},{5,13},{6,14},{7,15},{8,16},{9,17... | collective-permute-start | bytes 442376 | tf_op jit(solution)/shard_map/ppermute | solution.py:69
  5.4 16.5 %collective-permute-start.3 = (bf16[576,128]{1,0:T(8,128)(2,1)}, bf16[576,128]{1,0:T(8,128)(2,1)S(1)}, u32[]{:S(2)}, u32[]{:S(2)}) collective-permute-start(bf16[576,128]{1,0:T(8,128)(2,1)} %get-tuple-element.88), channel_id=1, source_target_pairs={{0,16},{1,17},{2,18},{3,19},{4,20},{5,21},{6,22},{7,23},{8,24},{9,... | collective-permute-start | bytes 442376 | tf_op jit(solution)/shard_map/ppermute | solution.py:69
  8.1 13.8 %collective-permute-start.4 = (bf16[576,128]{1,0:T(8,128)(2,1)}, bf16[576,128]{1,0:T(8,128)(2,1)S(1)}, u32[]{:S(2)}, u32[]{:S(2)}) collective-permute-start(bf16[576,128]{1,0:T(8,128)(2,1)} %get-tuple-element.88), channel_id=1, source_target_pairs={{0,24},{1,25},{2,26},{3,27},{4,28},{5,29},{6,30},{7,31},{8,0},{9,1... | collective-permute-start | bytes 442376 | tf_op jit(solution)/shard_map/ppermute | solution.py:69
  11.7 10.3 %collective-permute-start.1 = (bf16[2,128,640]{2,1,0:T(8,128)(2,1)S(1)}, bf16[2,128,640]{2,1,0:T(8,128)(2,1)S(1)}, u32[]{:S(2)}, u32[]{:S(2)}) collective-permute-start(bf16[2,128,640]{2,1,0:T(8,128)(2,1)S(1)} %maximum_maximum_fusion), channel_id=1, source_target_pairs={{0,2},{1,3},{2,0},{3,1},{4,6},{5,7},{6,4},{7,5},{8,10},{9,11},{10,... | collective-permute-start | bytes 983048 | tf_op jit(solution)/shard_map/ppermute | solution.py:74
  13.3 8.7 %collective-permute-start = (bf16[288,128]{1,0:T(8,128)(2,1)S(1)}, bf16[288,128]{1,0:T(8,128)(2,1)S(1)}, u32[]{:S(2)}, u32[]{:S(2)}) collective-permute-start(bf16[288,128]{1,0:T(8,128)(2,1)S(1)} %copy-done.25), channel_id=1, source_target_pairs={{0,2},{1,3},{2,0},{3,1},{4,6},{5,7},{6,4},{7,5},{8,10},{9,11},{10,... | collective-permute-start | bytes 221192 | tf_op jit(solution)/shard_map/ppermute | solution.py:69
  22.1 20.4 %collective-permute-start.5 = (bf16[4,576,128]{2,1,0:T(8,128)(2,1)S(1)}, bf16[4,576,128]{2,1,0:T(8,128)(2,1)}, u32[]{:S(2)}, u32[]{:S(2)}) collective-permute-start(bf16[4,576,128]{2,1,0:T(8,128)(2,1)S(1)} %pad_maximum_fusion.4.refs_1_), channel_id=1, source_target_pairs={{0,4},{1,5},{2,6},{3,7},{4,0},{5,1},{6,2},{7,3},{8,12},{9,13},{10,... | collective-permute-start | bytes 1769480 | tf_op jit(solution)/shard_map/ppermute | solution.py:69
  23.7 18.8 %collective-permute-start.6 = (bf16[4,576,128]{2,1,0:T(8,128)(2,1)S(1)}, bf16[4,576,128]{2,1,0:T(8,128)(2,1)S(1)}, u32[]{:S(2)}, u32[]{:S(2)}) collective-permute-start(bf16[4,576,128]{2,1,0:T(8,128)(2,1)S(1)} %pad_maximum_fusion.4.refs_1_), channel_id=1, source_target_pairs={{0,2},{1,3},{2,0},{3,1},{4,6},{5,7},{6,4},{7,5},{8,10},{9,11},{10,... | collective-permute-start | bytes 1769480 | tf_op jit(solution)/shard_map/ppermute | solution.py:69
  25.3 17.2 %collective-permute-start.7 = (bf16[2,2,128,640]{3,2,1,0:T(8,128)(2,1)S(1)}, bf16[2,2,128,640]{3,2,1,0:T(8,128)(2,1)S(1)}, u32[]{:S(2)}, u32[]{:S(2)}) collective-permute-start(bf16[2,2,128,640]{3,2,1,0:T(8,128)(2,1)S(1)} %pad_maximum_fusion.1), channel_id=1, source_target_pairs={{0,1},{1,0},{2,3},{3,2},{4,5},{5,4},{6,7},{7,6},{8,9},{9,8},{10,11... | collective-permute-start | bytes 1966088 | tf_op jit(solution)/shard_map/ppermute | solution.py:74
  26.0 6.9 %collective-permute-start.10 = (bf16[2,288,128]{2,1,0:T(8,128)(2,1)}, bf16[2,288,128]{2,1,0:T(8,128)(2,1)S(1)}, u32[]{:S(2)}, u32[]{:S(2)}) collective-permute-start(bf16[2,288,128]{2,1,0:T(8,128)(2,1)} %pad_maximum_fusion.11), channel_id=1, source_target_pairs={{0,24},{1,25},{2,26},{3,27},{4,28},{5,29},{6,30},{7,31},{8,0},{9,1... | collective-permute-start | bytes 442376 | tf_op jit(solution)/shard_map/ppermute | solution.py:69
  26.8 9.5 %collective-permute-start.8 = (bf16[2,288,128]{2,1,0:T(8,128)(2,1)}, bf16[2,288,128]{2,1,0:T(8,128)(2,1)}, u32[]{:S(2)}, u32[]{:S(2)}) collective-permute-start(bf16[2,288,128]{2,1,0:T(8,128)(2,1)} %pad_maximum_fusion.11), channel_id=1, source_target_pairs={{0,8},{1,9},{2,10},{3,11},{4,12},{5,13},{6,14},{7,15},{8,16},{9,17... | collective-permute-start | bytes 442376 | tf_op jit(solution)/shard_map/ppermute | solution.py:69
  32.9 9.6 %collective-permute-start.9 = (bf16[2,288,128]{2,1,0:T(8,128)(2,1)}, bf16[2,288,128]{2,1,0:T(8,128)(2,1)}, u32[]{:S(2)}, u32[]{:S(2)}) collective-permute-start(bf16[2,288,128]{2,1,0:T(8,128)(2,1)} %pad_maximum_fusion.11), channel_id=1, source_target_pairs={{0,16},{1,17},{2,18},{3,19},{4,20},{5,21},{6,22},{7,23},{8,24},{9,... | collective-permute-start | bytes 442376 | tf_op jit(solution)/shard_map/ppermute | solution.py:69
  45.5 13.3 %collective-permute-start.12 = (bf16[8,288,128]{2,1,0:T(8,128)(2,1)S(1)}, bf16[8,288,128]{2,1,0:T(8,128)(2,1)}, u32[]{:S(2)}, u32[]{:S(2)}) collective-permute-start(bf16[8,288,128]{2,1,0:T(8,128)(2,1)S(1)} %constant_dynamic-update-slice_fusion.refs_9_), channel_id=1, source_target_pairs={{0,4},{1,5},{2,6},{3,7},{4,0},{5,1},{6,2},{7,3},{8,12},{9,13},{10,... | collective-permute-start | bytes 1769480 | tf_op jit(solution)/shard_map/ppermute | solution.py:69
  46.1 15.2 %collective-permute-start.16 = (bf16[8,288,128]{2,1,0:T(8,128)(2,1)S(1)}, bf16[8,288,128]{2,1,0:T(8,128)(2,1)S(1)}, u32[]{:S(2)}, u32[]{:S(2)}) collective-permute-start(bf16[8,288,128]{2,1,0:T(8,128)(2,1)S(1)} %constant_dynamic-update-slice_fusion.refs_9_), channel_id=1, source_target_pairs={{0,1},{1,0},{2,3},{3,2},{4,5},{5,4},{6,7},{7,6},{8,9},{9,8},{10,11... | collective-permute-start | bytes 1769480 | tf_op jit(solution)/shard_map/ppermute | solution.py:69
  46.1 16.1 %collective-permute-start.11 = (bf16[4,576,128]{2,1,0:T(8,128)(2,1)}, bf16[4,576,128]{2,1,0:T(8,128)(2,1)}, u32[]{:S(2)}, u32[]{:S(2)}) collective-permute-start(bf16[4,576,128]{2,1,0:T(8,128)(2,1)} %collective-permute-done.5.refs_2_), channel_id=1, source_target_pairs={{0,2},{1,3},{2,0},{3,1},{4,6},{5,7},{6,4},{7,5},{8,10},{9,11},{10,... | collective-permute-start | bytes 1769480 | tf_op jit(solution)/shard_map/ppermute | solution.py:69
  46.6 15.5 %collective-permute-start.14 = (bf16[4,576,128]{2,1,0:T(8,128)(2,1)}, bf16[4,576,128]{2,1,0:T(8,128)(2,1)S(1)}, u32[]{:S(2)}, u32[]{:S(2)}) collective-permute-start(bf16[4,576,128]{2,1,0:T(8,128)(2,1)} %collective-permute-done.5.refs_2_), channel_id=1, source_target_pairs={{0,1},{1,0},{2,3},{3,2},{4,5},{5,4},{6,7},{7,6},{8,9},{9,8},{10,11... | collective-permute-start | bytes 1769480 | tf_op jit(solution)/shard_map/ppermute | solution.py:69
  46.8 15.3 %collective-permute-start.13 = (bf16[4,576,128]{2,1,0:T(8,128)(2,1)S(1)}, bf16[4,576,128]{2,1,0:T(8,128)(2,1)S(1)}, u32[]{:S(2)}, u32[]{:S(2)}) collective-permute-start(bf16[4,576,128]{2,1,0:T(8,128)(2,1)S(1)} %pad_maximum_fusion.4.refs_1_), channel_id=1, source_target_pairs={{0,1},{1,0},{2,3},{3,2},{4,5},{5,4},{6,7},{7,6},{8,9},{9,8},{10,11... | collective-permute-start | bytes 1769480 | tf_op jit(solution)/shard_map/ppermute | solution.py:69
  58.8 3.3 %collective-permute-start.15 = (bf16[4,576,128]{2,1,0:T(8,128)(2,1)S(1)}, bf16[4,576,128]{2,1,0:T(8,128)(2,1)S(1)}, u32[]{:S(2)}, u32[]{:S(2)}) collective-permute-start(bf16[4,576,128]{2,1,0:T(8,128)(2,1)S(1)} %copy-done.8), channel_id=1, source_target_pairs={{0,1},{1,0},{2,3},{3,2},{4,5},{5,4},{6,7},{7,6},{8,9},{9,8},{10,11... | collective-permute-start | bytes 1769480 | tf_op jit(solution)/shard_map/ppermute | solution.py:69
  100.1 4.1 %collective-permute-start.24 = (bf16[8,288,128]{2,1,0:T(8,128)(2,1)S(1)}, bf16[8,288,128]{2,1,0:T(8,128)(2,1)S(1)}, u32[]{:S(2)}, u32[]{:S(2)}) collective-permute-start(bf16[8,288,128]{2,1,0:T(8,128)(2,1)S(1)} %get-tuple-element.129), channel_id=1, source_target_pairs={{0,1},{1,0},{2,3},{3,2},{4,5},{5,4},{6,7},{7,6},{8,9},{9,8},{10,11... | collective-permute-start | bytes 1769480 | tf_op jit(solution)/shard_map/ppermute | solution.py:69
  100.2 6.7 %collective-permute-start.25 = (bf16[2,2,128,384]{3,2,1,0:T(8,128)(2,1)S(1)}, bf16[2,2,128,384]{3,2,1,0:T(8,128)(2,1)S(1)}, u32[]{:S(2)}, u32[]{:S(2)}) collective-permute-start(bf16[2,2,128,384]{3,2,1,0:T(8,128)(2,1)S(1)} %get-tuple-element.131), channel_id=1, source_target_pairs={{0,1},{1,0},{2,3},{3,2},{4,5},{5,4},{6,7},{7,6},{8,9},{9,8},{10,11... | collective-permute-start | bytes 1179656 | tf_op jit(solution)/shard_map/ppermute | solution.py:74
  100.6 6.4 %collective-permute-start.23 = (bf16[12,576,128]{2,1,0:T(8,128)(2,1)}, bf16[12,576,128]{2,1,0:T(8,128)(2,1)S(1)}, u32[]{:S(2)}, u32[]{:S(2)}) collective-permute-start(bf16[12,576,128]{2,1,0:T(8,128)(2,1)} %get-tuple-element.128), channel_id=1, source_target_pairs={{0,1},{1,0},{2,3},{3,2},{4,5},{5,4},{6,7},{7,6},{8,9},{9,8},{10,11... | collective-permute-start | bytes 5308424 | tf_op jit(solution)/shard_map/ppermute | solution.py:69
  104.4 15.4 %collective-permute-start.22 = (bf16[8,288,128]{2,1,0:T(8,128)(2,1)S(1)}, bf16[8,288,128]{2,1,0:T(8,128)(2,1)S(1)}, u32[]{:S(2)}, u32[]{:S(2)}) collective-permute-start(bf16[8,288,128]{2,1,0:T(8,128)(2,1)S(1)} %get-tuple-element.192), channel_id=1, source_target_pairs={{0,4},{1,5},{2,6},{3,7},{4,0},{5,1},{6,2},{7,3},{8,12},{9,13},{10,... | collective-permute-start | bytes 1769480 | tf_op jit(solution)/shard_map/ppermute | solution.py:69
  106.3 15.7 %collective-permute-start.21 = (bf16[2400,128]{1,0:T(8,128)(2,1)S(1)}, bf16[2400,128]{1,0:T(8,128)(2,1)S(1)}, u32[]{:S(2)}, u32[]{:S(2)}) collective-permute-start(bf16[2400,128]{1,0:T(8,128)(2,1)S(1)} %pad_maximum_fusion.2), channel_id=1, source_target_pairs={{0,2},{1,3},{2,0},{3,1},{4,6},{5,7},{6,4},{7,5},{8,10},{9,11},{10,... | collective-permute-start | bytes 1843208 | tf_op jit(solution)/shard_map/ppermute | solution.py:69
  122.2 14.9 %collective-permute-start.26 = (bf16[2400,128]{1,0:T(8,128)(2,1)S(1)}, bf16[2400,128]{1,0:T(8,128)(2,1)S(1)}, u32[]{:S(2)}, u32[]{:S(2)}) collective-permute-start(bf16[2400,128]{1,0:T(8,128)(2,1)S(1)} %pad_maximum_fusion.3), channel_id=1, source_target_pairs={{0,4},{1,5},{2,6},{3,7},{4,0},{5,1},{6,2},{7,3},{8,12},{9,13},{10,... | collective-permute-start | bytes 1843208 | tf_op jit(solution)/shard_map/ppermute | solution.py:69
  122.8 14.4 %collective-permute-start.27 = (bf16[4,576,128]{2,1,0:T(8,128)(2,1)}, bf16[4,576,128]{2,1,0:T(8,128)(2,1)}, u32[]{:S(2)}, u32[]{:S(2)}) collective-permute-start(bf16[4,576,128]{2,1,0:T(8,128)(2,1)} %get-tuple-element.136), channel_id=1, source_target_pairs={{0,2},{1,3},{2,0},{3,1},{4,6},{5,7},{6,4},{7,5},{8,10},{9,11},{10,... | collective-permute-start | bytes 1769480 | tf_op jit(solution)/shard_map/ppermute | solution.py:69
  123.5 8.8 %collective-permute-start.28 = (bf16[2,288,128]{2,1,0:T(8,128)(2,1)S(1)}, bf16[2,288,128]{2,1,0:T(8,128)(2,1)}, u32[]{:S(2)}, u32[]{:S(2)}) collective-permute-start(bf16[2,288,128]{2,1,0:T(8,128)(2,1)S(1)} %get-tuple-element.189), channel_id=1, source_target_pairs={{0,8},{1,9},{2,10},{3,11},{4,12},{5,13},{6,14},{7,15},{8,16},{9,17... | collective-permute-start | bytes 442376 | tf_op jit(solution)/shard_map/ppermute | solution.py:69
  124.0 12.2 %collective-permute-start.29 = (bf16[2,288,128]{2,1,0:T(8,128)(2,1)S(1)}, bf16[2,288,128]{2,1,0:T(8,128)(2,1)}, u32[]{:S(2)}, u32[]{:S(2)}) collective-permute-start(bf16[2,288,128]{2,1,0:T(8,128)(2,1)S(1)} %get-tuple-element.188), channel_id=1, source_target_pairs={{0,16},{1,17},{2,18},{3,19},{4,20},{5,21},{6,22},{7,23},{8,24},{9,... | collective-permute-start | bytes 442376 | tf_op jit(solution)/shard_map/ppermute | solution.py:69
  127.0 9.1 %collective-permute-start.30 = (bf16[2,288,128]{2,1,0:T(8,128)(2,1)S(1)}, bf16[2,288,128]{2,1,0:T(8,128)(2,1)}, u32[]{:S(2)}, u32[]{:S(2)}) collective-permute-start(bf16[2,288,128]{2,1,0:T(8,128)(2,1)S(1)} %get-tuple-element.187), channel_id=1, source_target_pairs={{0,24},{1,25},{2,26},{3,27},{4,28},{5,29},{6,30},{7,31},{8,0},{9,1... | collective-permute-start | bytes 442376 | tf_op jit(solution)/shard_map/ppermute | solution.py:69
  139.3 8.5 %collective-permute-start.34 = (bf16[672,128]{1,0:T(8,128)(2,1)S(1)}, bf16[672,128]{1,0:T(8,128)(2,1)S(1)}, u32[]{:S(2)}, u32[]{:S(2)}) collective-permute-start(bf16[672,128]{1,0:T(8,128)(2,1)S(1)} %get-tuple-element.211), channel_id=1, source_target_pairs={{0,24},{1,25},{2,26},{3,27},{4,28},{5,29},{6,30},{7,31},{8,0},{9,1... | collective-permute-start | bytes 516104 | tf_op jit(solution)/shard_map/ppermute | solution.py:69
  142.4 16.0 %collective-permute-start.33 = (bf16[672,128]{1,0:T(8,128)(2,1)S(1)}, bf16[672,128]{1,0:T(8,128)(2,1)S(1)}, u32[]{:S(2)}, u32[]{:S(2)}) collective-permute-start(bf16[672,128]{1,0:T(8,128)(2,1)S(1)} %get-tuple-element.212), channel_id=1, source_target_pairs={{0,16},{1,17},{2,18},{3,19},{4,20},{5,21},{6,22},{7,23},{8,24},{9,... | collective-permute-start | bytes 516104 | tf_op jit(solution)/shard_map/ppermute | solution.py:69
  143.2 15.2 %collective-permute-start.32 = (bf16[672,128]{1,0:T(8,128)(2,1)S(1)}, bf16[672,128]{1,0:T(8,128)(2,1)S(1)}, u32[]{:S(2)}, u32[]{:S(2)}) collective-permute-start(bf16[672,128]{1,0:T(8,128)(2,1)S(1)} %get-tuple-element.213), channel_id=1, source_target_pairs={{0,8},{1,9},{2,10},{3,11},{4,12},{5,13},{6,14},{7,15},{8,16},{9,17... | collective-permute-start | bytes 516104 | tf_op jit(solution)/shard_map/ppermute | solution.py:69
  145.0 18.3 %collective-permute-start.35 = (bf16[288,128]{1,0:T(8,128)(2,1)S(1)}, bf16[288,128]{1,0:T(8,128)(2,1)S(1)}, u32[]{:S(2)}, u32[]{:S(2)}) collective-permute-start(bf16[288,128]{1,0:T(8,128)(2,1)S(1)} %get-tuple-element.193), channel_id=1, source_target_pairs={{0,2},{1,3},{2,0},{3,1},{4,6},{5,7},{6,4},{7,5},{8,10},{9,11},{10,... | collective-permute-start | bytes 221192 | tf_op jit(solution)/shard_map/ppermute | solution.py:69
  147.2 12.1 %collective-permute-start.31 = (bf16[2,128,384]{2,1,0:T(8,128)(2,1)S(1)}, bf16[2,128,384]{2,1,0:T(8,128)(2,1)S(1)}, u32[]{:S(2)}, u32[]{:S(2)}) collective-permute-start(bf16[2,128,384]{2,1,0:T(8,128)(2,1)S(1)} %get-tuple-element.205), channel_id=1, source_target_pairs={{0,2},{1,3},{2,0},{3,1},{4,6},{5,7},{6,4},{7,5},{8,10},{9,11},{10,... | collective-permute-start | bytes 589832 | tf_op jit(solution)/shard_map/ppermute | solution.py:74
  (35 other events, 244.7 us)

commit v4 on v3

--- a/solution.py
+++ b/solution.py
@@ -26,9 +26,12 @@
 WIDE = 640
 BLOCKS = 32
 BLOCK_ROWS = 864
-VECTOR_ROWS = 48
 HEAD_ROWS = 576
 TAIL_ROWS = BLOCK_ROWS - HEAD_ROWS
+VECTOR_ROWS = 48
+PART = 4 * HEAD_ROWS
+FIRST_AT = 4 * PART
+FIRST_ROWS = 2 * PART + 2 * VECTOR_ROWS
 SIZES = {"z": 4, "y": 2, "x": 2, "c": 2}
 ROWS = 128
 F32 = jnp.float32
@@ -83,40 +86,40 @@
     tx = moved(tail, "x", 1)
     two = across(packed, 2)
     head, tail, tx, two, *hz = together(head, tail, tx, two, *hz)
-    near = jnp.stack([packed, two])
     own = jnp.stack([head] + hz)
     pair = jnp.stack([tail, tx])
-    far = across(near, 1)
     ay = moved(own, "y", 1)
     ax = moved(own, "x", 1)
     tz = [moved(pair, "z", s) for s in (1, 2, 3)]
-    own, pair, ay, ax, near, far, others, *tz = together(own, pair, ay, ax, near, far, others, *tz)
-    tokens = jnp.stack([near[0], far[0], near[1], far[1]])
-    tables = place_tables(tokens)
+    near = jnp.stack([packed, two])
+    tables = place_tables(near)
+    own, pair, ay, ax, near, tables, others, *tz = together(own, pair, ay, ax, near, tables, others, *tz)
     eight = jnp.concatenate([pair] + tz)
+    far = across(near, 1)
     axy = moved(ay, "x", 1)
     ty = moved(eight, "y", 1)
     ac = moved(own, "c", 1)
     acy = moved(ay, "c", 1)
     acx = moved(ax, "c", 1)
     tc = moved(eight, "c", 1)
-    axy, ty, ac, acy, acx, tc, tokens, *tables = together(axy, ty, ac, acy, acx, tc, tokens, *tables)
+    axy, ty, ac, acy, acx, tc, far = together(axy, ty, ac, acy, acx, tc, far)
     acxy = moved(axy, "c", 1)
     tcy = moved(ty, "c", 1)
     heads = [own, ay, ax, axy, ac, acy, acx, acxy]
-    return heads, [eight, ty, tc, tcy], tokens, tables, others
+    return heads, [eight, ty, tc, tcy], (near, far), tables, others
+
+
+def places_of(tokens):
+    found = tokens[..., MODEL_WIDTH : MODEL_WIDTH + 2].astype(F32)
+    return found[..., 0] * 16.0 + found[..., 1]
 
 
 def place_tables(tokens):
-    found = tokens[..., MODEL_WIDTH : MODEL_WIDTH + 2].astype(F32)
-    place_all = found[..., 0] * 16.0 + found[..., 1]
     half_dim = HEAD_SIZE // 2
     frequency = THETA ** (-2.0 * jnp.arange(half_dim, dtype=F32) / HEAD_SIZE)
-    angles = place_all[..., None] * jnp.tile(frequency, 4)
+    angles = places_of(tokens)[..., None] * jnp.tile(frequency, 4)
     sign = jnp.where(jnp.arange(LANES) % HEAD_SIZE < half_dim, -1.0, 1.0).astype(F32)
-    place_q = place_all[0][..., None]
-    place_k = jnp.transpose(place_all, (1, 0, 2)).reshape(2, 1, 4 * ROWS)
-    return jnp.cos(angles), jnp.sin(angles) * sign, place_q, place_k
+    return jnp.cos(angles), jnp.sin(angles) * sign
 
 
 def fold(order, relative):
@@ -133,10 +136,14 @@
         for number in range(BLOCKS):
             found = coordinates(number)
             entries.append(fold(order, {n: (mine[n] - found[n]) % SIZES[n] for n in SIZES}))
-    for order in (("x", "y", "z"), ("y", "z", "x")):
-        for number in range(0, BLOCKS, 2):
-            found = coordinates(number)
-            entries.append(fold(order, {n: (found[n] - mine[n]) % SIZES[n] for n in SIZES}))
+    for number in range(0, BLOCKS, 2):
+        found = coordinates(number)
+        slot = fold(("x", "y", "z"), {n: (found[n] - mine[n]) % SIZES[n] for n in SIZES})
+        entries.append(slot * HEAD_ROWS + jnp.where(slot < 12, 0, FIRST_AT - 12 * HEAD_ROWS))
+    for number in range(0, BLOCKS, 2):
+        found = coordinates(number)
+        slot = fold(("y", "z", "x"), {n: (found[n] - mine[n]) % SIZES[n] for n in SIZES})
+        entries.append(slot * TAIL_ROWS + jnp.where(slot < 8, 12 * HEAD_ROWS, FIRST_AT + 4 * HEAD_ROWS - 8 * TAIL_ROWS))
     entries.append(mine["c"])
     return jnp.stack([jnp.asarray(entry, jnp.int32) for entry in entries])
 
@@ -144,64 +151,110 @@
 AT_HEAD, AT_TAIL, TO_HEAD, TO_TAIL, MY_CORE = 0, BLOCKS, 2 * BLOCKS, 2 * BLOCKS + 16, 2 * BLOCKS + 32
 
 
-def summed(kept, received):
-    return kept.astype(F32) + received.astype(F32)
-
-
-def packed_vector(vector):
-    high = lax.reduce_precision(vector, 8, 7)
-    return jnp.concatenate([high.astype(BF16), (vector - high).astype(BF16)])
-
-
-def unpacked_vector(rows):
-    return rows[:VECTOR_ROWS].astype(F32) + rows[VECTOR_ROWS:].astype(F32)
-
-
-def scatter_blocks(head_sends, head_keep, tail_sends, tail_keep, vector, dkv_send, dkv_keep):
-    head_first, head_rest = head_sends
-    tail_first, tail_rest = tail_sends
-    h1 = moved(head_first, "c", 1)
-    t1 = moved(tail_first, "c", 1)
-    hr = moved(head_rest, "c", 1)
-    tr = moved(tail_rest, "c", 1)
-    dr = across(dkv_send, 1)
-    h1, t1 = together(h1, t1)
-    cut = 4 * HEAD_ROWS
-    hx = summed(head_keep[12:].reshape(cut, LANES), h1[:cut]).astype(BF16)
-    vector = unpacked_vector(vector) + unpacked_vector(h1[cut:])
-    vector = packed_vector(vector)
-    ty = summed(tail_keep[8:], t1).astype(BF16)
-    hx1 = moved(jnp.concatenate([hx, vector]), "x", 1)
-    tr1 = moved(ty, "y", 1)
-    hx = summed(head_keep[8:12], hr[8:]).astype(BF16)
-    hy = summed(head_keep[4:8], hr[4:8]).reshape(cut, LANES)
-    hz = summed(head_keep[:4], hr[:4])
-    tail = summed(tail_keep[:8], tr)
-    dkv = summed(dkv_keep, dr).astype(BF16)
-    hx1, tr1, hx, hy, hz, tail, dkv, vector = together(hx1, tr1, hx, hy, hz, tail, dkv, vector)
-    hy = summed(hy, hx1[:cut]).astype(BF16)
-    vector = packed_vector(unpacked_vector(vector) + unpacked_vector(hx1[cut:]))
-    tz = [summed(tail[2 * s : 2 * s + 2], tr1[2 * s : 2 * s + 2]).astype(BF16) for s in (1, 2, 3)]
-    hy1 = moved(jnp.concatenate([hy, vector]), "y", 1)
-    hx1 = moved(hx, "x", 1)
-    tzr = [moved(tz[s - 1], "z", s) for s in (1, 2, 3)]
-    tail = summed(tail[:2], tr1[:2])
-    hy1, hx1, tail, dkv, vector, *tzr = together(hy1, hx1, tail, dkv, vector, *tzr)
-    vector = packed_vector(unpacked_vector(vector) + unpacked_vector(hy1[cut:]))
-    hy1 = hy1[:cut].reshape(4, HEAD_ROWS, LANES)
-    head = [summed(summed(hz[s], hx1[s]), hy1[s]) for s in range(4)]
-    tx = summed(summed(tail[1], tzr[0][1]), summed(tzr[1][1], tzr[2][1])).astype(BF16)
-    tail = summed(summed(tail[0], tzr[0][0]), summed(tzr[1][0], tzr[2][0]))
-    hzr = [moved(jnp.concatenate([head[s].astype(BF16), vector]), "z", s) for s in (1, 2, 3)]
-    dr = across(dkv[1], 2)
-    txr = moved(tx, "x", 1)
+def rows_of(*counts):
+    return [jax.ShapeDtypeStruct((count, LANES), BF16) for count in counts]
+
+
+def on_chip(kernel, name, shapes, *arrays):
+    vmem = pl.BlockSpec(memory_space=pltpu.VMEM)
+    return pl.pallas_call(
+        kernel,
+        out_shape=tuple(shapes),
+        in_specs=[vmem] * len(arrays),
+        out_specs=(vmem,) * len(shapes),
+        name=name,
+    )(*arrays)
+
+
+def summed(*parts):
+    total = parts[0].astype(F32)
+    for part in parts[1:]:
+        total = total + part.astype(F32)
+    return total
+
+
+def summed_vector(mine, other):
+    total = summed(mine[0:VECTOR_ROWS], other[0:VECTOR_ROWS]) + summed(mine[VECTOR_ROWS:], other[VECTOR_ROWS:])
+    high = total.astype(BF16)
+    return jnp.concatenate([high, (total - high.astype(F32)).astype(BF16)], axis=0)
+
+
+def first_kernel(keep, got, hx, ty, vector):
+    hx[0:PART, :] = summed(keep[0:PART, :], got[0:PART, :]).astype(BF16)
+    ty[...] = summed(keep[PART : 2 * PART, :], got[PART : 2 * PART, :]).astype(BF16)
+    total = summed_vector(keep[2 * PART :, :], got[2 * PART :, :])
+    hx[PART:, :] = total
+    vector[...] = total
+
+
+def rest_kernel(keep, got, hx, mid, low, tail):
+    for at, ref in enumerate((low, mid, hx, tail)):
+        rows = slice(PART * at, PART * at + PART)
+        ref[...] = summed(keep[rows, :], got[rows, :]).astype(BF16)
+
+
+def middle_kernel(mid, hx, mine, tail, ty, hy, one, two, three, own, vector):
+    hy[0:PART, :] = summed(mid[...], hx[0:PART, :]).astype(BF16)
+    total = summed_vector(mine[...], hx[PART:, :])
+    hy[PART:, :] = total
+    vector[...] = total
+    for at, ref in enumerate((own, one, two, three)):
+        rows = slice(HEAD_ROWS * at, HEAD_ROWS * at + HEAD_ROWS)
+        ref[...] = summed(tail[rows, :], ty[rows, :]).astype(BF16)
+
+
+def last_kernel(low, hx, hy, mine, tail, got_one, got_two, got_three, one, two, three, tx, vector, own, own_tail):
+    total = summed_vector(mine[...], hy[PART:, :])
+    vector[...] = total
+    for at, ref in enumerate((own, one, two, three)):
+        rows = slice(HEAD_ROWS * at, HEAD_ROWS * at + HEAD_ROWS)
+        found = summed(low[rows, :], hx[rows, :], hy[rows, :])
+        if at == 0:
+            own[...] = found
+        else:
+            ref[0:HEAD_ROWS, :] = found.astype(BF16)
+            ref[HEAD_ROWS:, :] = total
+    found = summed(tail[...], got_one[...], got_two[...], got_three[...])
+    own_tail[...] = found[0:TAIL_ROWS]
+    tx[...] = found[TAIL_ROWS:].astype(BF16)
+
+
+def scatter_blocks(send_first, send_rest, keep_first, keep_rest, pairs, make_input):
+    float_rows = lambda count: jax.ShapeDtypeStruct((count, LANES), F32)
+    got_first = moved(send_first, "c", 1)
+    got_rest = moved(send_rest, "c", 1)
+    parts = [pairs[0]] + [across(pairs[d], d) for d in (1, 2, 3)]
+    hx, ty, vector = on_chip(first_kernel, "sum_first", rows_of(PART + 2 * VECTOR_ROWS, PART, 2 * VECTOR_ROWS), keep_first, got_first)
+    got_hx = moved(hx, "x", 1)
+    got_ty = moved(ty, "y", 1)
+    hx, mid, low, tail = on_chip(rest_kernel, "sum_rest", rows_of(PART, PART, PART, PART), keep_rest, got_rest)
+    input_grad = make_input(parts)
+    got_hx, got_ty, hx, mid, low, tail, vector, input_grad = together(got_hx, got_ty, hx, mid, low, tail, vector, input_grad)
+    hy, one, two, three, tail, vector = on_chip(
+        middle_kernel,
+        "sum_middle",
+        rows_of(PART + 2 * VECTOR_ROWS, HEAD_ROWS, HEAD_ROWS, HEAD_ROWS, HEAD_ROWS, 2 * VECTOR_ROWS),
+        mid, got_hx, vector, tail, got_ty,
+    )
+    got_hy = moved(hy, "y", 1)
+    got_hx = moved(hx, "x", 1)
+    got_tz = [moved(part, "z", s + 1) for s, part in enumerate((one, two, three))]
+    got_hy, got_hx, low, tail, vector, *got_tz = together(got_hy, got_hx, low, tail, vector, *got_tz)
+    one, two, three, tx, vector, own, own_tail = on_chip(
+        last_kernel,
+        "sum_last",
+        rows_of(*(HEAD_ROWS + 2 * VECTOR_ROWS,) * 3, TAIL_ROWS, 2 * VECTOR_ROWS) + [float_rows(HEAD_ROWS), float_rows(TAIL_ROWS)],
+        low, got_hx, got_hy, vector, tail, *got_tz,
+    )
+    got_hz = [moved(part, "z", s + 1) for s, part in enumerate((one, two, three))]
+    got_tx = moved(tx, "x", 1)
     place = coordinates(device_number() // inner_count())["z"]
-    parts = jnp.stack([vector] + [part[HEAD_ROWS:] for part in hzr])
-    vector = sum(
-        unpacked_vector(lax.dynamic_index_in_dim(parts, (place - z) % 4, 0, keepdims=False))
-        for z in range(4)
-    )
-    return head[0], hzr, tail, txr, vector, (dkv[0], dr)
+    stacked = jnp.stack([vector] + [part[HEAD_ROWS:] for part in got_hz])
+    total = sum(
+        summed(found[:VECTOR_ROWS], found[VECTOR_ROWS:])
+        for found in (lax.dynamic_index_in_dim(stacked, (place - z) % 4, 0, keepdims=False) for z in range(4))
+    )
+    return (own, *got_hz, own_tail, got_tx), total, input_grad
 
 
 def lower_lanes(shape):
@@ -398,9 +451,12 @@
     slots = refs[0]
     head_parts = refs[1:9]
     tail_parts = refs[9:13]
-    (tokens_ref, cos_ref, sin_ref, place_q_ref, place_k_ref, gains_ref, bias_q_ref, bias_kv_ref, grad_ref) = refs[13:22]
-    (block_out_ref, head_first, head_rest, head_keep_out, tail_first, tail_rest, tail_keep_out, vector_out, dkv_send, dkv_keep, dq_wq_ref, d_mid_ref, w_kv) = refs[22:35]
-    (raw_head, raw_tail, w_q, w_out, w_gate, w_up, w_down, normed_all, hidden_all, keys, values, queries, probs, attended, act_all, block_acc, d_hidden, d_attended, dkv_all, d_query, head_send, head_keep, tail_send, tail_keep, vector_ref, sems) = refs[35:]
+    tokens_pair, cos_pair, sin_pair = refs[13:15], refs[15:17], refs[17:19]
+    (place_q_ref, place_k_ref, gains_ref, bias_q_ref, bias_kv_ref, grad_ref) = refs[19:25]
+    (block_out_ref, send_first, send_rest, keep_first, keep_rest) = refs[25:30]
+    dkv_refs = refs[30:34]
+    (dq_wq_ref, d_mid_ref, w_kv) = refs[34:37]
+    (raw_head, raw_tail, w_q, w_out, w_gate, w_up, w_down, normed_all, hidden_all, keys, values, queries, probs, attended, act_all, block_acc, d_hidden, d_attended, dkv_all, d_query, send_all, keep_all, vector_ref, sems) = refs[37:]
 
     copies = []
     for k, part in enumerate(head_parts):
@@ -413,6 +469,9 @@
         copy.wait()
 
     core = slots[MY_CORE]
+
+    def at_slot(pair, slot):
+        return pair[slot % 2].at[slot // 2]
 
     def head_tile(block):
         return raw_head.at[slots[AT_HEAD + block]]
@@ -454,30 +513,31 @@
     gain_two = gains_ref[1:2, :]
     low_rows = lower_lanes((ROWS, LANES))
 
-    @pl.loop(0, 8)
-    def _(step):
-        slot, mb = step // 2, step % 2
-        first = pl.multiple_of(mb * 512 + slot * ROWS, ROWS)
+    @pl.loop(0, 2)
+    def _(mb):
         lane = lax.broadcasted_iota(jnp.int32, (ROWS, WIDE), 1)
-        x = jnp.where(lane < MODEL_WIDTH, tokens_ref[slot, mb].astype(F32), 0.0)
-        normed, _ = normed_rows(x)
-        hidden = (normed * gain_one).astype(BF16)
-        normed_all[pl.ds(first, ROWS), :] = normed
-        hidden_all[pl.ds(first, ROWS), :] = hidden
-        pair = product(hidden, w_kv[...]) + bias_kv_ref[...]
-        cosines, sines = cos_ref[slot, mb], sin_ref[slot, mb]
+        for slot in range(4):
+            rows = pl.ds(pl.multiple_of(mb * 512 + slot * ROWS, ROWS), ROWS)
+            x = jnp.where(lane < MODEL_WIDTH, at_slot(tokens_pair, slot)[mb].astype(F32), 0.0)
+            normed, _ = normed_rows(x)
+            normed_all[rows, :] = normed
+            hidden_all[rows, :] = (normed * gain_one).astype(BF16)
+        rows = pl.ds(pl.multiple_of(mb * 512, 512), 512)
+        pair = product(hidden_all[rows, :], w_kv[...]) + bias_kv_ref[...]
+        cosines = jnp.concatenate([at_slot(cos_pair, slot)[mb] for slot in range(4)], axis=0)
+        sines = jnp.concatenate([at_slot(sin_pair, slot)[mb] for slot in range(4)], axis=0)
         key_a = rope(pair[:, 0:128], cosines, sines)
         key_b = rope(pair[:, 256:384], cosines, sines)
         value_a, value_b = pair[:, 128:256], pair[:, 256:384]
+        low_keys = lower_lanes((512, LANES))
         turned = half_turn(key_a)
-        rows = pl.ds(first, ROWS)
-        keys[rows, 0:128] = jnp.where(low_rows, key_a, turned).astype(BF16)
-        keys[rows, 128:256] = jnp.where(low_rows, turned, key_a).astype(BF16)
-        keys[rows, 256:384] = jnp.where(low_rows, key_b, half_turn(key_b)).astype(BF16)
+        keys[rows, 0:128] = jnp.where(low_keys, key_a, turned).astype(BF16)
+        keys[rows, 128:256] = jnp.where(low_keys, turned, key_a).astype(BF16)
+        keys[rows, 256:384] = jnp.where(low_keys, key_b, half_turn(key_b)).astype(BF16)
         turned = half_turn(value_a)
-        values[rows, 0:128] = jnp.where(low_rows, value_a, turned).astype(BF16)
-        values[rows, 128:256] = jnp.where(low_rows, turned, value_a).astype(BF16)
-        values[rows, 256:384] = jnp.where(low_rows, half_turn(value_b), value_b).astype(BF16)
+        values[rows, 0:128] = jnp.where(low_keys, value_a, turned).astype(BF16)
+        values[rows, 128:256] = jnp.where(low_keys, turned, value_a).astype(BF16)
+        values[rows, 256:384] = jnp.where(low_keys, half_turn(value_b), value_b).astype(BF16)
 
     def heads_of(ref, rows, group):
         stacked = []
@@ -496,7 +556,7 @@
     def _(mb):
         rows = pl.ds(pl.multiple_of(mb * ROWS, ROWS), ROWS)
         key_rows = pl.ds(pl.multiple_of(mb * 512, 512), 512)
-        cosines, sines = cos_ref[0, mb], sin_ref[0, mb]
+        cosines, sines = cos_pair[0][0, mb], sin_pair[0][0, mb]
         made = product(hidden_all[pl.ds(pl.multiple_of(mb * 512, 512), ROWS), :], w_q[...]) + bias_q_ref[...]
         for k in range(5):
             queries[rows, LANES * k : LANES * k + LANES] = rope(
@@ -519,21 +579,22 @@
             attended[rows, LANES * k : LANES * k + LANES] = tile.astype(BF16)
 
     lane = lax.broadcasted_iota(jnp.int32, (2 * ROWS, WIDE), 1)
-    x_own = tokens_ref[0].astype(F32).reshape(2 * ROWS, WIDE)
+    x_own = tokens_pair[0][0].astype(F32).reshape(2 * ROWS, WIDE)
     x_own = jnp.where(lane < MODEL_WIDTH, x_own, 0.0)
     resid_mid = x_own + product(attended[...], w_out[...])
     normed_two, scale_two = normed_rows(resid_mid)
     hidden_two = (normed_two * gain_two).astype(BF16)
+    hidden_turned = hidden_two.T
     grad_low = grad_ref[...]
     block_acc[...] = resid_mid
     d_hidden[...] = jnp.zeros_like(d_hidden)
 
-    def store_pair(at, even, odd, send, keep, table, rows):
-        slot = slots[table + at]
-        send[slot, rows, :] = jnp.where(core == 0, odd, even).astype(BF16)
-        keep[slot, rows, :] = jnp.where(core == 0, even, odd).astype(BF16)
-
-    def feed_forward(chunk, first, send, keep, table):
+    def store_pair(at, even, odd, table, first):
+        rows = pl.ds(pl.multiple_of(slots[table + at] + first, 16), even.shape[0])
+        send_all[rows, :] = jnp.where(core == 0, odd, even).astype(BF16)
+        keep_all[rows, :] = jnp.where(core == 0, even, odd).astype(BF16)
+
+    def feed_forward(chunk, first, table):
         cols = pl.ds(pl.multiple_of(chunk * 512, 512), 512)
         gate = product(hidden_two, w_gate[:, cols])
         up = product(hidden_two, w_up[:, cols])
@@ -546,26 +607,25 @@
         d_up = (d_act * gate * sigma).astype(BF16)
         d_gate = (d_act * up * sigma * (1.0 + gate * (1.0 - sigma))).astype(BF16)
         d_hidden[...] += times_transposed(d_gate, w_gate[:, cols]) + times_transposed(d_up, w_up[:, cols])
-        rows = pl.ds(pl.multiple_of((chunk - first) * 288, 288), 288)
         for base, cotangent in ((4, d_gate), (8, d_up)):
-            made = rows_product(hidden_two, cotangent)
+            made = product(hidden_turned, cotangent)
             for k in range(4):
                 part = made[144 * k : 144 * k + 144, :]
                 even = jnp.concatenate([part[0:72, LANES * j : LANES * j + LANES] for j in range(4)], axis=0)
                 odd = jnp.concatenate([part[72:144, LANES * j : LANES * j + LANES] for j in range(4)], axis=0)
-                store_pair(base + k, even, odd, send, keep, table, rows)
+                store_pair(base + k, even, odd, table, (chunk - first) * 288)
 
     @pl.loop(0, 2)
     def _(chunk):
-        feed_forward(chunk, 0, head_send, head_keep, TO_HEAD)
-
-    feed_forward(2, 2, tail_send, tail_keep, TO_TAIL)
+        feed_forward(chunk, 0, TO_HEAD)
+
+    feed_forward(2, 2, TO_TAIL)
 
     def store_rows(at, even, odd):
         even_head, even_tail = even
         odd_head, odd_tail = odd
-        store_pair(at, even_head, odd_head, head_send, head_keep, TO_HEAD, slice(0, HEAD_ROWS))
-        store_pair(at, even_tail, odd_tail, tail_send, tail_keep, TO_TAIL, slice(0, TAIL_ROWS))
+        store_pair(at, even_head, odd_head, TO_HEAD, 0)
+        store_pair(at, even_tail, odd_tail, TO_TAIL, 0)
 
     @pl.loop(0, 4)
     def _(k):
@@ -606,20 +666,19 @@
             d_value = rows_product(found.astype(BF16), cotangent)
             d_keys.append(d_key + half_turn(d_key))
             d_values.append(d_value + half_turn(d_value))
-        cosines, sines = cos_ref[0, mb], sin_ref[0, mb]
+        cosines, sines = cos_pair[0][0, mb], sin_pair[0][0, mb]
         for k, tile in enumerate(tiles_of_heads(parts)):
             d_query[rows, LANES * k : LANES * k + LANES] = rope_back(tile, cosines, sines).astype(BF16)
         low_keys = lower_lanes((512, LANES))
-        cosines = cos_ref[:, mb].reshape(512, LANES)
-        sines = sin_ref[:, mb].reshape(512, LANES)
+        cosines = jnp.concatenate([at_slot(cos_pair, slot)[mb] for slot in range(4)], axis=0)
+        sines = jnp.concatenate([at_slot(sin_pair, slot)[mb] for slot in range(4)], axis=0)
         key_a = rope_back(jnp.where(low_keys, d_keys[0], d_keys[1]), cosines, sines)
         key_b = rope_back(d_keys[2], cosines, sines)
         dkv_all[key_rows, 0:128] = key_a.astype(BF16)
         dkv_all[key_rows, 128:256] = jnp.where(low_keys, d_values[0], d_values[1]).astype(BF16)
         dkv_all[key_rows, 256:384] = jnp.where(low_keys, key_b, d_values[2]).astype(BF16)
         for slot in range(4):
-            target = dkv_send if slot % 2 else dkv_keep
-            target[slot // 2, mb] = dkv_all[pl.ds(pl.multiple_of(mb * 512 + slot * ROWS, ROWS), ROWS), :]
+            dkv_refs[slot][mb] = dkv_all[pl.ds(pl.multiple_of(mb * 512 + slot * ROWS, ROWS), ROWS), :]
 
     dkv = dkv_all[...]
     d_q = d_query[...]
@@ -652,19 +711,16 @@
         [vector_ref[:, LANES * k : LANES * k + LANES] for k in range(5)] + [jnp.zeros((8, LANES), F32)], axis=0
     )
     high = vector.astype(BF16)
-    vector_out[0:VECTOR_ROWS, :] = high
-    vector_out[VECTOR_ROWS:, :] = (vector - high.astype(F32)).astype(BF16)
+    rest = (vector - high.astype(F32)).astype(BF16)
+    at = FIRST_AT + 2 * PART
+    for ref in (send_all, keep_all):
+        ref[at : at + VECTOR_ROWS, :] = high
+        ref[at + VECTOR_ROWS : at + 2 * VECTOR_ROWS, :] = rest
     copies = [
-        pltpu.make_async_copy(head_send.at[12 + k], head_first.at[pl.ds(HEAD_ROWS * k, HEAD_ROWS)], sems.at[6 + k])
-        for k in range(4)
-    ]
-    copies += [
-        pltpu.make_async_copy(vector_out, head_first.at[pl.ds(4 * HEAD_ROWS, 2 * VECTOR_ROWS)], sems.at[0]),
-        pltpu.make_async_copy(tail_send.at[pl.ds(8, 8)], tail_first, sems.at[1]),
-        pltpu.make_async_copy(head_send.at[pl.ds(0, 12)], head_rest, sems.at[2]),
-        pltpu.make_async_copy(tail_send.at[pl.ds(0, 8)], tail_rest, sems.at[3]),
-        pltpu.make_async_copy(head_keep, head_keep_out, sems.at[4]),
-        pltpu.make_async_copy(tail_keep, tail_keep_out, sems.at[5]),
+        pltpu.make_async_copy(send_all.at[pl.ds(FIRST_AT, FIRST_ROWS)], send_first, sems.at[0]),
+        pltpu.make_async_copy(send_all.at[pl.ds(0, FIRST_AT)], send_rest, sems.at[1]),
+        pltpu.make_async_copy(keep_all.at[pl.ds(FIRST_AT, FIRST_ROWS)], keep_first, sems.at[2]),
+        pltpu.make_async_copy(keep_all.at[pl.ds(0, FIRST_AT)], keep_rest, sems.at[3]),
     ]
     for copy in copies:
         copy.start()
@@ -672,7 +728,7 @@
         copy.wait()
 
 
-def run_layer(slots, heads, tails, tokens, cosines, sines, place_q, place_k, gains, bias_q, bias_kv, grad):
+def run_layer(slots, heads, tails, *others):
     shape = jax.ShapeDtypeStruct
     vmem = pl.BlockSpec(memory_space=pltpu.VMEM)
     anywhere = pl.BlockSpec(memory_space=pl.ANY)
@@ -697,43 +753,40 @@
         ((256, WIDE), BF16),
         ((1024, 384), BF16),
         ((256, WIDE), BF16),
-        ((16, HEAD_ROWS, LANES), BF16),
-        ((16, HEAD_ROWS, LANES), BF16),
-        ((16, TAIL_ROWS, LANES), BF16),
-        ((16, TAIL_ROWS, LANES), BF16),
+        ((FIRST_AT + FIRST_ROWS, LANES), BF16),
+        ((FIRST_AT + FIRST_ROWS, LANES), BF16),
         ((8, WIDE), F32),
     ]
     return pl.pallas_call(
         layer_kernel,
         out_shape=(
             shape((2, MODEL_WIDTH, ROWS), BF16),
-            shape((4 * HEAD_ROWS + 2 * VECTOR_ROWS, LANES), BF16),
-            shape((12, HEAD_ROWS, LANES), BF16),
-            shape((16, HEAD_ROWS, LANES), BF16),
-            shape((8, TAIL_ROWS, LANES), BF16),
-            shape((8, TAIL_ROWS, LANES), BF16),
-            shape((16, TAIL_ROWS, LANES), BF16),
-            shape((2 * VECTOR_ROWS, LANES), BF16),
-            shape((2, 2, ROWS, 384), BF16),
-            shape((2, 2, ROWS, 384), BF16),
+            shape((FIRST_ROWS, LANES), BF16),
+            shape((FIRST_AT, LANES), BF16),
+            shape((FIRST_ROWS, LANES), BF16),
+            shape((FIRST_AT, LANES), BF16),
+            shape((2, ROWS, 384), BF16),
+            shape((2, ROWS, 384), BF16),
+            shape((2, ROWS, 384), BF16),
+            shape((2, ROWS, 384), BF16),
             shape((256, WIDE), F32),
             shape((256, WIDE), F32),
             shape((WIDE, 384), BF16),
         ),
-        in_specs=[pl.BlockSpec(memory_space=pltpu.SMEM)] + [anywhere] * 12 + [vmem] * 9,
-        out_specs=(vmem,) + (anywhere,) * 6 + (vmem,) * 6,
+        in_specs=[pl.BlockSpec(memory_space=pltpu.SMEM)] + [anywhere] * 12 + [vmem] * 12,
+        out_specs=(vmem,) + (anywhere,) * 4 + (vmem,) * 7,
         scratch_shapes=[pltpu.VMEM(dims, kind) for dims, kind in scratch]
         + [pltpu.SemaphoreType.DMA((12,))],
         compiler_params=pltpu.CompilerParams(vmem_limit_bytes=50 * 1024 * 1024),
         name="layer",
-    )(slots, *heads, *tails, tokens, cosines, sines, place_q, place_k, gains, bias_q, bias_kv, grad)
-
-
-def input_kernel(tokens_ref, gains_ref, w_kv_ref, dq_wq_ref, d_mid_ref, own_ref, other_ref, out_ref):
+    )(slots, *heads, *tails, *others)
+
+
+def input_kernel(tokens_ref, gains_ref, w_kv_ref, dq_wq_ref, d_mid_ref, own_ref, one_ref, two_ref, three_ref, out_ref):
     lane = lax.broadcasted_iota(jnp.int32, (2 * ROWS, WIDE), 1)
     x = jnp.where(lane < MODEL_WIDTH, tokens_ref[0].astype(F32).reshape(2 * ROWS, WIDE), 0.0)
     normed, scale = normed_rows(x)
-    total = own_ref[...].astype(F32) + other_ref[...].astype(F32)
+    total = summed(own_ref[...], one_ref[...], two_ref[...], three_ref[...])
     total = total.reshape(2 * ROWS, 384).astype(BF16)
     d_norm = (dq_wq_ref[...] + times_transposed(total, w_kv_ref[...])) * gains_ref[0:1, :]
     d_input = d_mid_ref[...] + scale * (d_norm - normed * row_mean(d_norm * normed))
@@ -745,7 +798,7 @@
     return pl.pallas_call(
         input_kernel,
         out_shape=jax.ShapeDtypeStruct((2, MODEL_WIDTH, ROWS), BF16),
-        in_specs=[pl.BlockSpec(memory_space=pltpu.VMEM)] * 7,
+        in_specs=[pl.BlockSpec(memory_space=pltpu.VMEM)] * 9,
         out_specs=pl.BlockSpec(memory_space=pltpu.VMEM),
         name="input_grad",
     )(tokens, gains, w_kv, dq_wq, d_mid, *parts)
@@ -805,19 +858,19 @@
     bias_kv = bias_tiles(vectors[1728:1920], vectors[1920:2112]).reshape(1, 384)
     grad = jnp.pad(out_grad.reshape(2 * ROWS, MODEL_WIDTH), padding)
     others = (slot_table(), gains, bias_q, bias_kv, grad)
-    heads, tails, tokens, tables, others = gather_all(head, tail, packed, others)
+    heads, tails, (near, far), (cosines, sines), others = gather_all(head, tail, packed, others)
     slots, gains, bias_q, bias_kv, grad = others
-
-    (block_out, head_first, head_rest, head_keep, tail_first, tail_rest, tail_keep, vector, dkv_send, dkv_keep, dq_wq, d_mid, w_kv) = run_layer(
-        slots, heads, tails, tokens, *tables, gains, bias_q, bias_kv, grad
-    )
-    head, hzr, tail, txr, vector, pairs = scatter_blocks(
-        (head_first, head_rest), head_keep, (tail_first, tail_rest), tail_keep, vector, dkv_send, dkv_keep
-    )
-    input_grad = run_input(tokens, gains, w_kv, dq_wq, d_mid, pairs)
-    head, input_grad = together(head, input_grad)
+    cosines_far, sines_far = place_tables(far)
+    place_all = jnp.stack([places_of(near), places_of(far)], axis=1)
+    place_q = place_all[0, 0][..., None]
+    place_k = jnp.transpose(place_all.reshape(4, 2, ROWS), (1, 0, 2)).reshape(2, 1, 4 * ROWS)
+
+    (block_out, send_first, send_rest, keep_first, keep_rest, *pairs, dq_wq, d_mid, w_kv) = run_layer(
+        slots, heads, tails, near, far, cosines, cosines_far, sines, sines_far, place_q, place_k, gains, bias_q, bias_kv, grad
+    )
+    make_input = lambda parts: run_input(near, gains, w_kv, dq_wq, d_mid, parts)
+    parts, vector, input_grad = scatter_blocks(send_first, send_rest, keep_first, keep_rest, pairs, make_input)
     state = (weights, first_moment, second_moment)
-    parts = (head, *hzr, tail, txr)
     if inner_count() == 1:
         updated = finish(kind, parts, [array.reshape(BLOCK_ROWS, LANES) for array in state])
         new_weights, new_first, new_second = [array.reshape(-1) for array in updated]

time: 168 us -> 184 us (1.095)
  Pallas kernels: 41.6 us -> 52.9 us
  waiting for transfers between devices: 67.8 us -> 75.8 us
  other arithmetic: 11.4 us -> 5.13 us
  starting transfers between devices: 32.8 us -> 37.3 us
  local copies, waits for them, and re-layouts: 12.4 us -> 10.4 us
    ppermute x4 -> x5, waiting for transfers between devices: 0.01 us -> 20.6 us  [across(): lax.ppermute(buffer, 'ctx', [(i, i ^ distance) for i in range(count)])]
    ppermute x32 -> x30, waiting for transfers between devices: 67.8 us -> 55.3 us  [moved(): return lax.ppermute(buffer, ('dp', 'ctx'), pairs)]
    pallas_call x0 -> x4, Pallas kernels: none -> 12.3 us  [on_chip(): pl.pallas_call(kernel, out_shape=tuple(shapes), in_specs=[vmem] * len(arr...]
    convert_element_type x10 -> x3, other arithmetic: 4.64 us -> 0.31 us  [places_of(): found = tokens[..., MODEL_WIDTH:MODEL_WIDTH + 2].astype(F32)]
    ppermute x32 -> x30, starting transfers between devices: 30.3 us -> 33.2 us  [moved(): return lax.ppermute(buffer, ('dp', 'ctx'), pairs)]
    ppermute x4 -> x5, starting transfers between devices: 2.54 us -> 4.08 us  [across(): lax.ppermute(buffer, 'ctx', [(i, i ^ distance) for i in range(count)])]
    unnamed x64 -> x74, local copies, waits for them, and re-layouts: 7.36 us -> 6.07 us
  transfers between devices with their start and end apart: 36 -> 35, of which waited for: 15 -> 19; matrix products, arithmetic and copies ran while one was open for 8% -> 5% of each run, Pallas kernels for 2% -> 5%
where the time goes in v4:
time: 184 us
  waiting for transfers between devices  75.8 us (41%)
  Pallas kernels  52.9 us (29%)
  starting transfers between devices  37.3 us (20%)
  local copies, waits for them, and re-layouts  10.4 us (6%)
  other arithmetic  5.13 us (3%)
  between operations  2.14 us (1%)
    ppermute x30, waiting for transfers between devices, moved(): return lax.ppermute(buffer, ('dp', 'ctx'), pairs)  55.3 us
    ppermute x30, starting transfers between devices, moved(): return lax.ppermute(buffer, ('dp', 'ctx'), pairs)  33.2 us
    pallas_call x1, Pallas kernels, run_layer(): pl.pallas_call(layer_kernel, out_shape=(shape((2, MODEL_WIDTH, ROWS), BF1...  32.1 us
    ppermute x5, waiting for transfers between devices, across(): lax.ppermute(buffer, 'ctx', [(i, i ^ distance) for i in range(count)])  20.6 us
    pallas_call x4, Pallas kernels, on_chip(): pl.pallas_call(kernel, out_shape=tuple(shapes), in_specs=[vmem] * len(arr...  12.3 us
    unnamed x74, local copies, waits for them, and re-layouts  6.07 us
    ppermute x5, starting transfers between devices, across(): lax.ppermute(buffer, 'ctx', [(i, i ^ distance) for i in range(count)])  4.08 us
  transfers between devices with their start and end apart: 35, of which 19 were waited for; matrix products, arithmetic and copies ran while one was open for 5% of the time, Pallas kernels for 5%

profile of v4, /device:TPU:0, one launch (start us, length us, event | category | flops | bytes accessed | tf_op | source)
XLA Modules:
  0.0 183.7 jit_solution(8070249253251440958)
XLA Ops:
  0.7 1.9 %to_tiles.1 = (bf16[576,128]{1,0:T(8,128)(2,1)}, bf16[288,128]{1,0:T(8,128)(2,1)}) custom-call(s32[1]{0:T(128)} %bitcast.kind_ref, f32[864,128]{1,0:T(8,128)} %bitcast.156), custom_call_target="tpu_custom_call" | custom-call | tf_op jit(solution)/shard_map/to_tiles/pallas_call | solution.py:311
  2.6 2.9 %collective-permute-start.2 = (bf16[576,128]{1,0:T(8,128)(2,1)}, bf16[576,128]{1,0:T(8,128)(2,1)S(1)}, u32[]{:S(2)}, u32[]{:S(2)}) collective-permute-start(bf16[576,128]{1,0:T(8,128)(2,1)} %get-tuple-element.100), channel_id=1, source_target_pairs={{0,8},{1,9},{2,10},{3,11},{4,12},{5,13},{6,14},{7,15},{8,16},{9,17... | collective-permute-start | bytes 442376 | tf_op jit(solution)/shard_map/ppermute | solution.py:72
  5.5 2.7 %collective-permute-start.3 = (bf16[576,128]{1,0:T(8,128)(2,1)}, bf16[576,128]{1,0:T(8,128)(2,1)S(1)}, u32[]{:S(2)}, u32[]{:S(2)}) collective-permute-start(bf16[576,128]{1,0:T(8,128)(2,1)} %get-tuple-element.100), channel_id=1, source_target_pairs={{0,16},{1,17},{2,18},{3,19},{4,20},{5,21},{6,22},{7,23},{8,24},{9,... | collective-permute-start | bytes 442376 | tf_op jit(solution)/shard_map/ppermute | solution.py:72
  11.8 1.6 collective-permute-start.1
  17.4 4.7 %collective-permute-done = bf16[288,128]{1,0:T(8,128)(2,1)S(1)} collective-permute-done((bf16[288,128]{1,0:T(8,128)(2,1)}, bf16[288,128]{1,0:T(8,128)(2,1)S(1)}, u32[]{:S(2)}, u32[]{:S(2)}) %collective-permute-start) | collective-permute-done | bytes 73760 | tf_op jit(solution)/shard_map/ppermute | solution.py:72
  22.2 1.6 collective-permute-start.5
  23.8 1.5 collective-permute-start.6
  26.5 2.7 %collective-permute-start.9 = (bf16[2,288,128]{2,1,0:T(8,128)(2,1)S(1)}, bf16[2,288,128]{2,1,0:T(8,128)(2,1)S(1)}, u32[]{:S(2)}, u32[]{:S(2)}) collective-permute-start(bf16[2,288,128]{2,1,0:T(8,128)(2,1)S(1)} %pad_maximum_fusion.2), channel_id=1, source_target_pairs={{0,24},{1,25},{2,26},{3,27},{4,28},{5,29},{6,30},{7,31},{8,0},{9,1... | collective-permute-start | bytes 442376 | tf_op jit(solution)/shard_map/ppermute | solution.py:72
  30.6 3.0 %collective-permute-done.7 = bf16[2,288,128]{2,1,0:T(8,128)(2,1)S(1)} collective-permute-done((bf16[2,288,128]{2,1,0:T(8,128)(2,1)S(1)}, bf16[2,288,128]{2,1,0:T(8,128)(2,1)S(1)}, u32[]{:S(2)}, u32[]{:S(2)}) %collective-permute-start.7) | collective-permute-done | bytes 147488 | tf_op jit(solution)/shard_map/ppermute | solution.py:72
  33.7 3.3 %collective-permute-done.8 = bf16[2,288,128]{2,1,0:T(8,128)(2,1)S(1)} collective-permute-done((bf16[2,288,128]{2,1,0:T(8,128)(2,1)S(1)}, bf16[2,288,128]{2,1,0:T(8,128)(2,1)S(1)}, u32[]{:S(2)}, u32[]{:S(2)}) %collective-permute-start.8) | collective-permute-done | bytes 147488 | tf_op jit(solution)/shard_map/ppermute | solution.py:72
  37.7 1.3 collective-permute-start.10
  39.5 12.6 %collective-permute-done.11.refs_10_ = bf16[8,288,128]{2,1,0:T(8,128)(2,1)S(1)} collective-permute-done((bf16[8,288,128]{2,1,0:T(8,128)(2,1)S(1)}, bf16[8,288,128]{2,1,0:T(8,128)(2,1)S(1)}, u32[]{:S(2)}, u32[]{:S(2)}) %collective-permute-start.11) | collective-permute-done | bytes 589856 | tf_op jit(solution)/shard_map/ppermute | solution.py:72
  58.7 32.1 %layer.1 = (bf16[2,576,128]{2,1,0:T(8,128)(2,1)}, bf16[4704,128]{1,0:T(8,128)(2,1)}, bf16[9216,128]{1,0:T(8,128)(2,1)}, bf16[4704,128]{1,0:T(8,128)(2,1)}, bf16[...) custom-call(s32[97]{0:T(128)S(1)} %stack.459.refs_0_, ...), custom_call_target="tpu_custom_call" | custom-call | tf_op jit(solution)/shard_map/layer/pallas_call | solution.py:760
  92.8 5.9 %collective-permute-done.19.got = bf16[4704,128]{1,0:T(8,128)(2,1)} collective-permute-done((bf16[4704,128]{1,0:T(8,128)(2,1)}, bf16[4704,128]{1,0:T(8,128)(2,1)}, u32[]{:S(2)}, u32[]{:S(2)}) %collective-permute-start.19) | collective-permute-done | bytes 1204256 | tf_op jit(solution)/shard_map/ppermute | solution.py:72
  98.7 2.9 %sum_first.1 = (bf16[2400,128]{1,0:T(8,128)(2,1)}, bf16[2304,128]{1,0:T(8,128)(2,1)}, bf16[96,128]{1,0:T(8,128)(2,1)}) custom-call(bf16[4704,128]{1,0:T(8,128)(2,1)} %get-tuple-element.130.keep, bf16[4704,128]{1,0:T(8,128)(2,1)} %collective-permute-done.19.got), custom_call_target="tpu_custom_call" | custom-call | tf_op jit(solution)/shard_map/sum_first/pallas_call | solution.py:160
  102.9 1.2 collective-permute-start.24
  105.3 17.4 %collective-permute-done.24.two_ref = bf16[2,128,384]{2,1,0:T(8,128)(2,1)S(1)} collective-permute-done((bf16[2,128,384]{2,1,0:T(8,128)(2,1)S(1)}, bf16[2,128,384]{2,1,0:T(8,128)(2,1)S(1)}, u32[]{:S(2)}, u32[]{:S(2)}) %collective-permute-start.24) | collective-permute-done | bytes 196640 | tf_op jit(solution)/shard_map/ppermute | solution.py:77
  122.7 3.0 %collective-permute-done.25.three_ref = bf16[2,128,384]{2,1,0:T(8,128)(2,1)S(1)} collective-permute-done((bf16[2,128,384]{2,1,0:T(8,128)(2,1)S(1)}, bf16[2,128,384]{2,1,0:T(8,128)(2,1)S(1)}, u32[]{:S(2)}, u32[]{:S(2)}) %collective-permute-start.25) | collective-permute-done | bytes 196640 | tf_op jit(solution)/shard_map/ppermute | solution.py:77
  126.4 3.2 %input_grad.1 = bf16[2,576,128]{2,1,0:T(8,128)(2,1)} custom-call(bf16[2,2,128,640]{3,2,1,0:T(8,128)(2,1)} %copy-done.3, f32[2,640]{1,0:T(2,128)} %copy-done.2, bf16[640,384]{1,0:T(8,128)(2,1)} %copy-done, f32[256,640]{1,0:T(8,128)} %get-tuple-element.142.dq_wq_ref, f32[256,640]{1,0:T(8,128)} %get-tuple-element.143.d_mid_ref, bf16[2,128,384]{2,1,0:T(8,128)(2,1)} %copy-done.1, ...), custom_call_target="tpu_custom_call" | custom-call | tf_op jit(solution)/shard_map/input_grad/pallas_call | solution.py:798
  129.7 1.4 copy-done.4
  131.0 3.9 %sum_rest.1 = (bf16[2304,128]{1,0:T(8,128)(2,1)}, bf16[2304,128]{1,0:T(8,128)(2,1)}, bf16[2304,128]{1,0:T(8,128)(2,1)}, bf16[2304,128]{1,0:T(8,128)(2,1)}) custom-call(bf16[9216,128]{1,0:T(8,128)(2,1)} %get-tuple-element.134.keep, bf16[9216,128]{1,0:T(8,128)(2,1)} %copy-done.4), custom_call_target="tpu_custom_call" | custom-call | tf_op jit(solution)/shard_map/sum_rest/pallas_call | solution.py:160
  135.0 2.8 %sum_middle.1 = (bf16[2400,128]{1,0:T(8,128)(2,1)}, bf16[576,128]{1,0:T(8,128)(2,1)}, bf16[576,128]{1,0:T(8,128)(2,1)}, bf16[576,128]{1,0:T(8,128)(2,1)}, bf16[5...) custom-call(bf16[2304,128]{1,0:T(8,128)(2,1)} %get-tuple-element.149.mid, bf16[2400,128]{1,0:T(8,128)(2,1)} %collective-permute-done.20.hx, ...), custom_call_target="tpu_custom_call" | custom-call | tf_op jit(solution)/shard_map/sum_middle/pallas_call | solution.py:160
  139.2 3.4 %collective-permute-start.28 = (bf16[576,128]{1,0:T(8,128)(2,1)}, bf16[576,128]{1,0:T(8,128)(2,1)S(1)}, u32[]{:S(2)}, u32[]{:S(2)}) collective-permute-start(bf16[576,128]{1,0:T(8,128)(2,1)} %get-tuple-element.159), channel_id=1, source_target_pairs={{0,8},{1,9},{2,10},{3,11},{4,12},{5,13},{6,14},{7,15},{8,16},{9,17... | collective-permute-start | bytes 442376 | tf_op jit(solution)/shard_map/ppermute | solution.py:72
  143.0 2.0 %collective-permute-start.30 = (bf16[576,128]{1,0:T(8,128)(2,1)}, bf16[576,128]{1,0:T(8,128)(2,1)S(1)}, u32[]{:S(2)}, u32[]{:S(2)}) collective-permute-start(bf16[576,128]{1,0:T(8,128)(2,1)} %get-tuple-element.161), channel_id=1, source_target_pairs={{0,24},{1,25},{2,26},{3,27},{4,28},{5,29},{6,30},{7,31},{8,0},{9,1... | collective-permute-start | bytes 442376 | tf_op jit(solution)/shard_map/ppermute | solution.py:72
  145.0 3.1 %collective-permute-done.28.got_one = bf16[576,128]{1,0:T(8,128)(2,1)S(1)} collective-permute-done((bf16[576,128]{1,0:T(8,128)(2,1)}, bf16[576,128]{1,0:T(8,128)(2,1)S(1)}, u32[]{:S(2)}, u32[]{:S(2)}) %collective-permute-start.28) | collective-permute-done | bytes 147488 | tf_op jit(solution)/shard_map/ppermute | solution.py:72
  148.0 5.1 %collective-permute-done.29.got_two = bf16[576,128]{1,0:T(8,128)(2,1)S(1)} collective-permute-done((bf16[576,128]{1,0:T(8,128)(2,1)}, bf16[576,128]{1,0:T(8,128)(2,1)S(1)}, u32[]{:S(2)}, u32[]{:S(2)}) %collective-permute-start.29) | collective-permute-done | bytes 147488 | tf_op jit(solution)/shard_map/ppermute | solution.py:72
  155.0 2.7 %sum_last.1 = (bf16[672,128]{1,0:T(8,128)(2,1)}, bf16[672,128]{1,0:T(8,128)(2,1)}, bf16[672,128]{1,0:T(8,128)(2,1)}, bf16[288,128]{1,0:T(8,128)(2,1)}, bf16[96,1...) custom-call(bf16[2304,128]{1,0:T(8,128)(2,1)} %get-tuple-element.162.low, bf16[2304,128]{1,0:T(8,128)(2,1)} %copy-done.17, ...), custom_call_target="tpu_custom_call" | custom-call | tf_op jit(solution)/shard_map/sum_last/pallas_call | solution.py:160
  157.7 4.6 %collective-permute-start.33 = (bf16[672,128]{1,0:T(8,128)(2,1)}, bf16[672,128]{1,0:T(8,128)(2,1)S(1)}, u32[]{:S(2)}, u32[]{:S(2)}) collective-permute-start(bf16[672,128]{1,0:T(8,128)(2,1)} %get-tuple-element.173), channel_id=1, source_target_pairs={{0,24},{1,25},{2,26},{3,27},{4,28},{5,29},{6,30},{7,31},{8,0},{9,1... | collective-permute-start | bytes 516104 | tf_op jit(solution)/shard_map/ppermute | solution.py:72
  162.9 1.5 collective-permute-start.34
  164.4 3.0 %collective-permute-done.33.three_ref = bf16[672,128]{1,0:T(8,128)(2,1)S(1)} collective-permute-done((bf16[672,128]{1,0:T(8,128)(2,1)}, bf16[672,128]{1,0:T(8,128)(2,1)S(1)}, u32[]{:S(2)}, u32[]{:S(2)}) %collective-permute-start.33) | collective-permute-done | bytes 172064 | tf_op jit(solution)/shard_map/ppermute | solution.py:72
  167.4 10.5 %collective-permute-done.32.two_ref = bf16[672,128]{1,0:T(8,128)(2,1)S(1)} collective-permute-done((bf16[672,128]{1,0:T(8,128)(2,1)}, bf16[672,128]{1,0:T(8,128)(2,1)S(1)}, u32[]{:S(2)}, u32[]{:S(2)}) %collective-permute-start.32) | collective-permute-done | bytes 172064 | tf_op jit(solution)/shard_map/ppermute | solution.py:72
  180.3 3.4 %finish.1 = (f32[864,128]{1,0:T(8,128)}, f32[864,128]{1,0:T(8,128)}, f32[864,128]{1,0:T(8,128)}) custom-call(s32[1]{0:T(128)} %bitcast.kind_ref, f32[576,128]{1,0:T(8,128)} %get-tuple-element.170.head_ref, bf16[672,128]{1,0:T(8,128)(2,1)} %copy-done.21, bf16[672,128]{1,0:T(8,128)(2,1)} %copy-done.20, bf16[672,128]{1,0:T(8,128)(2,1)} %copy-done.19, ...), custom_call_target="tpu_custom_call" | custom-call | tf_op jit(solution)/shard_map/finish/pallas_call | solution.py:386
  (172 shorter events, 28.6 us)
Async XLA Ops:
  2.6 19.5 %collective-permute-start.2 = (bf16[576,128]{1,0:T(8,128)(2,1)}, bf16[576,128]{1,0:T(8,128)(2,1)S(1)}, u32[]{:S(2)}, u32[]{:S(2)}) collective-permute-start(bf16[576,128]{1,0:T(8,128)(2,1)} %get-tuple-element.100), channel_id=1, source_target_pairs={{0,8},{1,9},{2,10},{3,11},{4,12},{5,13},{6,14},{7,15},{8,16},{9,17... | collective-permute-start | bytes 442376 | tf_op jit(solution)/shard_map/ppermute | solution.py:72
  5.5 16.6 %collective-permute-start.3 = (bf16[576,128]{1,0:T(8,128)(2,1)}, bf16[576,128]{1,0:T(8,128)(2,1)S(1)}, u32[]{:S(2)}, u32[]{:S(2)}) collective-permute-start(bf16[576,128]{1,0:T(8,128)(2,1)} %get-tuple-element.100), channel_id=1, source_target_pairs={{0,16},{1,17},{2,18},{3,19},{4,20},{5,21},{6,22},{7,23},{8,24},{9,... | collective-permute-start | bytes 442376 | tf_op jit(solution)/shard_map/ppermute | solution.py:72
  8.2 13.9 %collective-permute-start.4 = (bf16[576,128]{1,0:T(8,128)(2,1)}, bf16[576,128]{1,0:T(8,128)(2,1)S(1)}, u32[]{:S(2)}, u32[]{:S(2)}) collective-permute-start(bf16[576,128]{1,0:T(8,128)(2,1)} %get-tuple-element.100), channel_id=1, source_target_pairs={{0,24},{1,25},{2,26},{3,27},{4,28},{5,29},{6,30},{7,31},{8,0},{9,1... | collective-permute-start | bytes 442376 | tf_op jit(solution)/shard_map/ppermute | solution.py:72
  11.8 10.3 %collective-permute-start.1 = (bf16[2,128,640]{2,1,0:T(8,128)(2,1)S(1)}, bf16[2,128,640]{2,1,0:T(8,128)(2,1)S(1)}, u32[]{:S(2)}, u32[]{:S(2)}) collective-permute-start(bf16[2,128,640]{2,1,0:T(8,128)(2,1)S(1)} %maximum_maximum_fusion), channel_id=1, source_target_pairs={{0,2},{1,3},{2,0},{3,1},{4,6},{5,7},{6,4},{7,5},{8,10},{9,11},{10,... | collective-permute-start | bytes 983048 | tf_op jit(solution)/shard_map/ppermute | solution.py:77
  13.4 8.7 %collective-permute-start = (bf16[288,128]{1,0:T(8,128)(2,1)}, bf16[288,128]{1,0:T(8,128)(2,1)S(1)}, u32[]{:S(2)}, u32[]{:S(2)}) collective-permute-start(bf16[288,128]{1,0:T(8,128)(2,1)} %get-tuple-element.104), channel_id=1, source_target_pairs={{0,2},{1,3},{2,0},{3,1},{4,6},{5,7},{6,4},{7,5},{8,10},{9,11},{10,... | collective-permute-start | bytes 221192 | tf_op jit(solution)/shard_map/ppermute | solution.py:72
  22.2 14.8 %collective-permute-start.5 = (bf16[4,576,128]{2,1,0:T(8,128)(2,1)S(1)}, bf16[4,576,128]{2,1,0:T(8,128)(2,1)S(1)}, u32[]{:S(2)}, u32[]{:S(2)}) collective-permute-start(bf16[4,576,128]{2,1,0:T(8,128)(2,1)S(1)} %pad_maximum_fusion.1.refs_1_), channel_id=1, source_target_pairs={{0,4},{1,5},{2,6},{3,7},{4,0},{5,1},{6,2},{7,3},{8,12},{9,13},{10,... | collective-permute-start | bytes 1769480 | tf_op jit(solution)/shard_map/ppermute | solution.py:72
  23.8 13.2 %collective-permute-start.6 = (bf16[4,576,128]{2,1,0:T(8,128)(2,1)S(1)}, bf16[4,576,128]{2,1,0:T(8,128)(2,1)S(1)}, u32[]{:S(2)}, u32[]{:S(2)}) collective-permute-start(bf16[4,576,128]{2,1,0:T(8,128)(2,1)S(1)} %pad_maximum_fusion.1.refs_1_), channel_id=1, source_target_pairs={{0,2},{1,3},{2,0},{3,1},{4,6},{5,7},{6,4},{7,5},{8,10},{9,11},{10,... | collective-permute-start | bytes 1769480 | tf_op jit(solution)/shard_map/ppermute | solution.py:72
  25.3 8.4 %collective-permute-start.7 = (bf16[2,288,128]{2,1,0:T(8,128)(2,1)S(1)}, bf16[2,288,128]{2,1,0:T(8,128)(2,1)S(1)}, u32[]{:S(2)}, u32[]{:S(2)}) collective-permute-start(bf16[2,288,128]{2,1,0:T(8,128)(2,1)S(1)} %pad_maximum_fusion.2), channel_id=1, source_target_pairs={{0,8},{1,9},{2,10},{3,11},{4,12},{5,13},{6,14},{7,15},{8,16},{9,17... | collective-permute-start | bytes 442376 | tf_op jit(solution)/shard_map/ppermute | solution.py:72
  26.1 10.8 %collective-permute-start.8 = (bf16[2,288,128]{2,1,0:T(8,128)(2,1)S(1)}, bf16[2,288,128]{2,1,0:T(8,128)(2,1)S(1)}, u32[]{:S(2)}, u32[]{:S(2)}) collective-permute-start(bf16[2,288,128]{2,1,0:T(8,128)(2,1)S(1)} %pad_maximum_fusion.2), channel_id=1, source_target_pairs={{0,16},{1,17},{2,18},{3,19},{4,20},{5,21},{6,22},{7,23},{8,24},{9,... | collective-permute-start | bytes 442376 | tf_op jit(solution)/shard_map/ppermute | solution.py:72
  26.5 10.5 %collective-permute-start.9 = (bf16[2,288,128]{2,1,0:T(8,128)(2,1)S(1)}, bf16[2,288,128]{2,1,0:T(8,128)(2,1)S(1)}, u32[]{:S(2)}, u32[]{:S(2)}) collective-permute-start(bf16[2,288,128]{2,1,0:T(8,128)(2,1)S(1)} %pad_maximum_fusion.2), channel_id=1, source_target_pairs={{0,24},{1,25},{2,26},{3,27},{4,28},{5,29},{6,30},{7,31},{8,0},{9,1... | collective-permute-start | bytes 442376 | tf_op jit(solution)/shard_map/ppermute | solution.py:72
  37.1 15.0 %collective-permute-start.11 = (bf16[8,288,128]{2,1,0:T(8,128)(2,1)S(1)}, bf16[8,288,128]{2,1,0:T(8,128)(2,1)S(1)}, u32[]{:S(2)}, u32[]{:S(2)}) collective-permute-start(bf16[8,288,128]{2,1,0:T(8,128)(2,1)S(1)} %constant_dynamic-update-slice_fusion.refs_9_), channel_id=1, source_target_pairs={{0,4},{1,5},{2,6},{3,7},{4,0},{5,1},{6,2},{7,3},{8,12},{9,13},{10,... | collective-permute-start | bytes 1769480 | tf_op jit(solution)/shard_map/ppermute | solution.py:72
  37.7 14.4 %collective-permute-start.15 = (bf16[8,288,128]{2,1,0:T(8,128)(2,1)S(1)}, bf16[8,288,128]{2,1,0:T(8,128)(2,1)S(1)}, u32[]{:S(2)}, u32[]{:S(2)}) collective-permute-start(bf16[8,288,128]{2,1,0:T(8,128)(2,1)S(1)} %constant_dynamic-update-slice_fusion.refs_9_), channel_id=1, source_target_pairs={{0,1},{1,0},{2,3},{3,2},{4,5},{5,4},{6,7},{7,6},{8,9},{9,8},{10,11... | collective-permute-start | bytes 1769480 | tf_op jit(solution)/shard_map/ppermute | solution.py:72
  37.7 15.7 %collective-permute-start.10 = (bf16[4,576,128]{2,1,0:T(8,128)(2,1)S(1)}, bf16[4,576,128]{2,1,0:T(8,128)(2,1)S(1)}, u32[]{:S(2)}, u32[]{:S(2)}) collective-permute-start(bf16[4,576,128]{2,1,0:T(8,128)(2,1)S(1)} %collective-permute-done.5.refs_2_), channel_id=1, source_target_pairs={{0,2},{1,3},{2,0},{3,1},{4,6},{5,7},{6,4},{7,5},{8,10},{9,11},{10,... | collective-permute-start | bytes 1769480 | tf_op jit(solution)/shard_map/ppermute | solution.py:72
  39.0 15.1 %collective-permute-start.13 = (bf16[4,576,128]{2,1,0:T(8,128)(2,1)S(1)}, bf16[4,576,128]{2,1,0:T(8,128)(2,1)S(1)}, u32[]{:S(2)}, u32[]{:S(2)}) collective-permute-start(bf16[4,576,128]{2,1,0:T(8,128)(2,1)S(1)} %collective-permute-done.5.refs_2_), channel_id=1, source_target_pairs={{0,1},{1,0},{2,3},{3,2},{4,5},{5,4},{6,7},{7,6},{8,9},{9,8},{10,11... | collective-permute-start | bytes 1769480 | tf_op jit(solution)/shard_map/ppermute | solution.py:72
  39.2 15.8 %collective-permute-start.16 = (bf16[2,2,128,640]{3,2,1,0:T(8,128)(2,1)S(1)}, bf16[2,2,128,640]{3,2,1,0:T(8,128)(2,1)S(1)}, u32[]{:S(2)}, u32[]{:S(2)}) collective-permute-start(bf16[2,2,128,640]{3,2,1,0:T(8,128)(2,1)S(1)} %pad_maximum_fusion.refs_13_.tokens_ref), channel_id=1, source_target_pairs={{0,1},{1,0},{2,3},{3,2},{4,5},{5,4},{6,7},{7,6},{8,9},{9,8},{10,11... | collective-permute-start | bytes 1966088 | tf_op jit(solution)/shard_map/ppermute | solution.py:77
  52.1 2.8 %collective-permute-start.14 = (bf16[4,576,128]{2,1,0:T(8,128)(2,1)S(1)}, bf16[4,576,128]{2,1,0:T(8,128)(2,1)S(1)}, u32[]{:S(2)}, u32[]{:S(2)}) collective-permute-start(bf16[4,576,128]{2,1,0:T(8,128)(2,1)S(1)} %collective-permute-done.6.refs_3_), channel_id=1, source_target_pairs={{0,1},{1,0},{2,3},{3,2},{4,5},{5,4},{6,7},{7,6},{8,9},{9,8},{10,11... | collective-permute-start | bytes 1769480 | tf_op jit(solution)/shard_map/ppermute | solution.py:72
  55.1 2.8 %collective-permute-start.18 = (bf16[8,288,128]{2,1,0:T(8,128)(2,1)S(1)}, bf16[8,288,128]{2,1,0:T(8,128)(2,1)S(1)}, u32[]{:S(2)}, u32[]{:S(2)}) collective-permute-start(bf16[8,288,128]{2,1,0:T(8,128)(2,1)S(1)} %collective-permute-done.11.refs_10_), channel_id=1, source_target_pairs={{0,1},{1,0},{2,3},{3,2},{4,5},{5,4},{6,7},{7,6},{8,9},{9,8},{10,11... | collective-permute-start | bytes 1769480 | tf_op jit(solution)/shard_map/ppermute | solution.py:72
  92.3 37.3 %collective-permute-start.22 = (bf16[9216,128]{1,0:T(8,128)(2,1)}, bf16[9216,128]{1,0:T(8,128)(2,1)S(1)}, u32[]{:S(2)}, u32[]{:S(2)}) collective-permute-start(bf16[9216,128]{1,0:T(8,128)(2,1)} %get-tuple-element.135), channel_id=1, source_target_pairs={{0,1},{1,0},{2,3},{3,2},{4,5},{5,4},{6,7},{7,6},{8,9},{9,8},{10,11... | collective-permute-start | bytes 7077896 | tf_op jit(solution)/shard_map/ppermute | solution.py:72
  92.5 6.3 %collective-permute-start.19 = (bf16[4704,128]{1,0:T(8,128)(2,1)}, bf16[4704,128]{1,0:T(8,128)(2,1)}, u32[]{:S(2)}, u32[]{:S(2)}) collective-permute-start(bf16[4704,128]{1,0:T(8,128)(2,1)} %get-tuple-element.131), channel_id=1, source_target_pairs={{0,1},{1,0},{2,3},{3,2},{4,5},{5,4},{6,7},{7,6},{8,9},{9,8},{10,11... | collective-permute-start | bytes 3612680 | tf_op jit(solution)/shard_map/ppermute | solution.py:72
  101.6 33.3 %collective-permute-start.20 = (bf16[2400,128]{1,0:T(8,128)(2,1)}, bf16[2400,128]{1,0:T(8,128)(2,1)}, u32[]{:S(2)}, u32[]{:S(2)}) collective-permute-start(bf16[2400,128]{1,0:T(8,128)(2,1)} %get-tuple-element.132), channel_id=1, source_target_pairs={{0,2},{1,3},{2,0},{3,1},{4,6},{5,7},{6,4},{7,5},{8,10},{9,11},{10,... | collective-permute-start | bytes 1843208 | tf_op jit(solution)/shard_map/ppermute | solution.py:72
  102.2 32.8 %collective-permute-start.21 = (bf16[2304,128]{1,0:T(8,128)(2,1)}, bf16[2304,128]{1,0:T(8,128)(2,1)}, u32[]{:S(2)}, u32[]{:S(2)}) collective-permute-start(bf16[2304,128]{1,0:T(8,128)(2,1)} %get-tuple-element.133), channel_id=1, source_target_pairs={{0,4},{1,5},{2,6},{3,7},{4,0},{5,1},{6,2},{7,3},{8,12},{9,13},{10,... | collective-permute-start | bytes 1769480 | tf_op jit(solution)/shard_map/ppermute | solution.py:72
  102.9 19.8 %collective-permute-start.24 = (bf16[2,128,384]{2,1,0:T(8,128)(2,1)S(1)}, bf16[2,128,384]{2,1,0:T(8,128)(2,1)S(1)}, u32[]{:S(2)}, u32[]{:S(2)}) collective-permute-start(bf16[2,128,384]{2,1,0:T(8,128)(2,1)S(1)} %get-tuple-element.146), channel_id=1, source_target_pairs={{0,2},{1,3},{2,0},{3,1},{4,6},{5,7},{6,4},{7,5},{8,10},{9,11},{10,... | collective-permute-start | bytes 589832 | tf_op jit(solution)/shard_map/ppermute | solution.py:77
  104.4 21.4 %collective-permute-start.25 = (bf16[2,128,384]{2,1,0:T(8,128)(2,1)S(1)}, bf16[2,128,384]{2,1,0:T(8,128)(2,1)S(1)}, u32[]{:S(2)}, u32[]{:S(2)}) collective-permute-start(bf16[2,128,384]{2,1,0:T(8,128)(2,1)S(1)} %get-tuple-element.147), channel_id=1, source_target_pairs={{0,3},{1,2},{2,1},{3,0},{4,7},{5,6},{6,5},{7,4},{8,11},{9,10},{10,... | collective-permute-start | bytes 589832 | tf_op jit(solution)/shard_map/ppermute | solution.py:77
  137.8 16.4 %collective-permute-start.26 = (bf16[2400,128]{1,0:T(8,128)(2,1)}, bf16[2400,128]{1,0:T(8,128)(2,1)S(1)}, u32[]{:S(2)}, u32[]{:S(2)}) collective-permute-start(bf16[2400,128]{1,0:T(8,128)(2,1)} %get-tuple-element.154), channel_id=1, source_target_pairs={{0,4},{1,5},{2,6},{3,7},{4,0},{5,1},{6,2},{7,3},{8,12},{9,13},{10,... | collective-permute-start | bytes 1843208 | tf_op jit(solution)/shard_map/ppermute | solution.py:72
  138.3 15.4 %collective-permute-start.27 = (bf16[2304,128]{1,0:T(8,128)(2,1)S(1)}, bf16[2304,128]{1,0:T(8,128)(2,1)S(1)}, u32[]{:S(2)}, u32[]{:S(2)}) collective-permute-start(bf16[2304,128]{1,0:T(8,128)(2,1)S(1)} %copy-done.34), channel_id=1, source_target_pairs={{0,2},{1,3},{2,0},{3,1},{4,6},{5,7},{6,4},{7,5},{8,10},{9,11},{10,... | collective-permute-start | bytes 1769480 | tf_op jit(solution)/shard_map/ppermute | solution.py:72
  139.2 8.8 %collective-permute-start.28 = (bf16[576,128]{1,0:T(8,128)(2,1)}, bf16[576,128]{1,0:T(8,128)(2,1)S(1)}, u32[]{:S(2)}, u32[]{:S(2)}) collective-permute-start(bf16[576,128]{1,0:T(8,128)(2,1)} %get-tuple-element.159), channel_id=1, source_target_pairs={{0,8},{1,9},{2,10},{3,11},{4,12},{5,13},{6,14},{7,15},{8,16},{9,17... | collective-permute-start | bytes 442376 | tf_op jit(solution)/shard_map/ppermute | solution.py:72
  142.6 10.6 %collective-permute-start.29 = (bf16[576,128]{1,0:T(8,128)(2,1)}, bf16[576,128]{1,0:T(8,128)(2,1)S(1)}, u32[]{:S(2)}, u32[]{:S(2)}) collective-permute-start(bf16[576,128]{1,0:T(8,128)(2,1)} %get-tuple-element.160), channel_id=1, source_target_pairs={{0,16},{1,17},{2,18},{3,19},{4,20},{5,21},{6,22},{7,23},{8,24},{9,... | collective-permute-start | bytes 442376 | tf_op jit(solution)/shard_map/ppermute | solution.py:72
  143.0 10.2 %collective-permute-start.30 = (bf16[576,128]{1,0:T(8,128)(2,1)}, bf16[576,128]{1,0:T(8,128)(2,1)S(1)}, u32[]{:S(2)}, u32[]{:S(2)}) collective-permute-start(bf16[576,128]{1,0:T(8,128)(2,1)} %get-tuple-element.161), channel_id=1, source_target_pairs={{0,24},{1,25},{2,26},{3,27},{4,28},{5,29},{6,30},{7,31},{8,0},{9,1... | collective-permute-start | bytes 442376 | tf_op jit(solution)/shard_map/ppermute | solution.py:72
  157.7 9.7 %collective-permute-start.33 = (bf16[672,128]{1,0:T(8,128)(2,1)}, bf16[672,128]{1,0:T(8,128)(2,1)S(1)}, u32[]{:S(2)}, u32[]{:S(2)}) collective-permute-start(bf16[672,128]{1,0:T(8,128)(2,1)} %get-tuple-element.173), channel_id=1, source_target_pairs={{0,24},{1,25},{2,26},{3,27},{4,28},{5,29},{6,30},{7,31},{8,0},{9,1... | collective-permute-start | bytes 516104 | tf_op jit(solution)/shard_map/ppermute | solution.py:72
  162.3 15.7 %collective-permute-start.32 = (bf16[672,128]{1,0:T(8,128)(2,1)}, bf16[672,128]{1,0:T(8,128)(2,1)S(1)}, u32[]{:S(2)}, u32[]{:S(2)}) collective-permute-start(bf16[672,128]{1,0:T(8,128)(2,1)} %get-tuple-element.172), channel_id=1, source_target_pairs={{0,16},{1,17},{2,18},{3,19},{4,20},{5,21},{6,22},{7,23},{8,24},{9,... | collective-permute-start | bytes 516104 | tf_op jit(solution)/shard_map/ppermute | solution.py:72
  162.9 15.1 %collective-permute-start.31 = (bf16[672,128]{1,0:T(8,128)(2,1)}, bf16[672,128]{1,0:T(8,128)(2,1)S(1)}, u32[]{:S(2)}, u32[]{:S(2)}) collective-permute-start(bf16[672,128]{1,0:T(8,128)(2,1)} %get-tuple-element.171), channel_id=1, source_target_pairs={{0,8},{1,9},{2,10},{3,11},{4,12},{5,13},{6,14},{7,15},{8,16},{9,17... | collective-permute-start | bytes 516104 | tf_op jit(solution)/shard_map/ppermute | solution.py:72
  162.9 16.8 %collective-permute-start.34 = (bf16[288,128]{1,0:T(8,128)(2,1)}, bf16[288,128]{1,0:T(8,128)(2,1)S(1)}, u32[]{:S(2)}, u32[]{:S(2)}) collective-permute-start(bf16[288,128]{1,0:T(8,128)(2,1)} %get-tuple-element.175), channel_id=1, source_target_pairs={{0,2},{1,3},{2,0},{3,1},{4,6},{5,7},{6,4},{7,5},{8,10},{9,11},{10,... | collective-permute-start | bytes 221192 | tf_op jit(solution)/shard_map/ppermute | solution.py:72
  (39 other events, 352.2 us)

commit v5 on v4

--- a/solution.py
+++ b/solution.py
@@ -31,7 +31,10 @@
 VECTOR_ROWS = 48
 PART = 4 * HEAD_ROWS
 FIRST_AT = 4 * PART
-FIRST_ROWS = 2 * PART + 2 * VECTOR_ROWS
+TAIL_AT = FIRST_AT + PART + 2 * VECTOR_ROWS
+ALL_ROWS = TAIL_AT + PART
+SEND_PARTS = [(FIRST_AT, PART + 2 * VECTOR_ROWS), (TAIL_AT, PART), (0, 3 * PART), (3 * PART, PART)]
+KEEP_PARTS = SEND_PARTS[:2] + [(PART * k, PART) for k in range(4)]
 SIZES = {"z": 4, "y": 2, "x": 2, "c": 2}
 ROWS = 128
 F32 = jnp.float32
@@ -143,27 +146,12 @@
     for number in range(0, BLOCKS, 2):
         found = coordinates(number)
         slot = fold(("y", "z", "x"), {n: (found[n] - mine[n]) % SIZES[n] for n in SIZES})
-        entries.append(slot * TAIL_ROWS + jnp.where(slot < 8, 12 * HEAD_ROWS, FIRST_AT + 4 * HEAD_ROWS - 8 * TAIL_ROWS))
+        entries.append(slot * TAIL_ROWS + jnp.where(slot < 8, 3 * PART, TAIL_AT - 8 * TAIL_ROWS))
     entries.append(mine["c"])
     return jnp.stack([jnp.asarray(entry, jnp.int32) for entry in entries])
 
 
 AT_HEAD, AT_TAIL, TO_HEAD, TO_TAIL, MY_CORE = 0, BLOCKS, 2 * BLOCKS, 2 * BLOCKS + 16, 2 * BLOCKS + 32
-
-
-def rows_of(*counts):
-    return [jax.ShapeDtypeStruct((count, LANES), BF16) for count in counts]
-
-
-def on_chip(kernel, name, shapes, *arrays):
-    vmem = pl.BlockSpec(memory_space=pltpu.VMEM)
-    return pl.pallas_call(
-        kernel,
-        out_shape=tuple(shapes),
-        in_specs=[vmem] * len(arrays),
-        out_specs=(vmem,) * len(shapes),
-        name=name,
-    )(*arrays)
 
 
 def summed(*parts):
@@ -174,87 +162,53 @@
 
 
 def summed_vector(mine, other):
-    total = summed(mine[0:VECTOR_ROWS], other[0:VECTOR_ROWS]) + summed(mine[VECTOR_ROWS:], other[VECTOR_ROWS:])
-    high = total.astype(BF16)
-    return jnp.concatenate([high, (total - high.astype(F32)).astype(BF16)], axis=0)
-
-
-def first_kernel(keep, got, hx, ty, vector):
-    hx[0:PART, :] = summed(keep[0:PART, :], got[0:PART, :]).astype(BF16)
-    ty[...] = summed(keep[PART : 2 * PART, :], got[PART : 2 * PART, :]).astype(BF16)
-    total = summed_vector(keep[2 * PART :, :], got[2 * PART :, :])
-    hx[PART:, :] = total
-    vector[...] = total
-
-
-def rest_kernel(keep, got, hx, mid, low, tail):
-    for at, ref in enumerate((low, mid, hx, tail)):
-        rows = slice(PART * at, PART * at + PART)
-        ref[...] = summed(keep[rows, :], got[rows, :]).astype(BF16)
-
-
-def middle_kernel(mid, hx, mine, tail, ty, hy, one, two, three, own, vector):
-    hy[0:PART, :] = summed(mid[...], hx[0:PART, :]).astype(BF16)
-    total = summed_vector(mine[...], hx[PART:, :])
-    hy[PART:, :] = total
-    vector[...] = total
-    for at, ref in enumerate((own, one, two, three)):
-        rows = slice(HEAD_ROWS * at, HEAD_ROWS * at + HEAD_ROWS)
-        ref[...] = summed(tail[rows, :], ty[rows, :]).astype(BF16)
-
-
-def last_kernel(low, hx, hy, mine, tail, got_one, got_two, got_three, one, two, three, tx, vector, own, own_tail):
-    total = summed_vector(mine[...], hy[PART:, :])
-    vector[...] = total
-    for at, ref in enumerate((own, one, two, three)):
-        rows = slice(HEAD_ROWS * at, HEAD_ROWS * at + HEAD_ROWS)
-        found = summed(low[rows, :], hx[rows, :], hy[rows, :])
-        if at == 0:
-            own[...] = found
-        else:
-            ref[0:HEAD_ROWS, :] = found.astype(BF16)
-            ref[HEAD_ROWS:, :] = total
-    found = summed(tail[...], got_one[...], got_two[...], got_three[...])
-    own_tail[...] = found[0:TAIL_ROWS]
-    tx[...] = found[TAIL_ROWS:].astype(BF16)
-
-
-def scatter_blocks(send_first, send_rest, keep_first, keep_rest, pairs, make_input):
-    float_rows = lambda count: jax.ShapeDtypeStruct((count, LANES), F32)
-    got_first = moved(send_first, "c", 1)
-    got_rest = moved(send_rest, "c", 1)
-    parts = [pairs[0]] + [across(pairs[d], d) for d in (1, 2, 3)]
-    hx, ty, vector = on_chip(first_kernel, "sum_first", rows_of(PART + 2 * VECTOR_ROWS, PART, 2 * VECTOR_ROWS), keep_first, got_first)
+    total = summed(mine[:VECTOR_ROWS], other[:VECTOR_ROWS]) + summed(mine[VECTOR_ROWS:], other[VECTOR_ROWS:])
+    high = lax.reduce_precision(total, 8, 7)
+    return jnp.concatenate([high.astype(BF16), (total - high).astype(BF16)])
+
+
+def scatter_blocks(sends, keeps, dkv_send, dkv_keep, make_input):
+    keep_head, keep_tail, keep_low, keep_mid, keep_far, keep_rest = keeps
+    got_head, got_tail = moved(sends[0], "c", 1), moved(sends[1], "c", 1)
+    got_head, got_tail, rest_head, rest_tail, dkv_send = together(got_head, got_tail, *sends[2:], dkv_send)
+    got_rest_head, got_rest_tail = moved(rest_head, "c", 1), moved(rest_tail, "c", 1)
+    got_dkv = across(dkv_send, 1)
+    vector = summed_vector(keep_head[PART:], got_head[PART:])
+    hx = jnp.concatenate([summed(keep_head[:PART], got_head[:PART]).astype(BF16), vector])
+    ty = summed(keep_tail, got_tail).astype(BF16)
     got_hx = moved(hx, "x", 1)
     got_ty = moved(ty, "y", 1)
-    hx, mid, low, tail = on_chip(rest_kernel, "sum_rest", rows_of(PART, PART, PART, PART), keep_rest, got_rest)
-    input_grad = make_input(parts)
-    got_hx, got_ty, hx, mid, low, tail, vector, input_grad = together(got_hx, got_ty, hx, mid, low, tail, vector, input_grad)
-    hy, one, two, three, tail, vector = on_chip(
-        middle_kernel,
-        "sum_middle",
-        rows_of(PART + 2 * VECTOR_ROWS, HEAD_ROWS, HEAD_ROWS, HEAD_ROWS, HEAD_ROWS, 2 * VECTOR_ROWS),
-        mid, got_hx, vector, tail, got_ty,
-    )
+    low, mid, far = [
+        summed(keep, got_rest_head[PART * k : PART * k + PART]).astype(BF16)
+        for k, keep in enumerate((keep_low, keep_mid, keep_far))
+    ]
+    tail = summed(keep_rest, got_rest_tail).astype(BF16)
+    dkv = summed(dkv_keep, got_dkv).astype(BF16)
+    got_hx, got_ty, low, mid, far, tail, dkv, vector = together(got_hx, got_ty, low, mid, far, tail, dkv, vector)
+    vector = summed_vector(vector, got_hx[PART:])
+    hy = jnp.concatenate([summed(mid, got_hx[:PART]).astype(BF16), vector])
+    cuts = [slice(HEAD_ROWS * k, HEAD_ROWS * k + HEAD_ROWS) for k in range(4)]
+    tz = [summed(tail[cut], got_ty[cut]).astype(BF16) for cut in cuts]
     got_hy = moved(hy, "y", 1)
-    got_hx = moved(hx, "x", 1)
-    got_tz = [moved(part, "z", s + 1) for s, part in enumerate((one, two, three))]
-    got_hy, got_hx, low, tail, vector, *got_tz = together(got_hy, got_hx, low, tail, vector, *got_tz)
-    one, two, three, tx, vector, own, own_tail = on_chip(
-        last_kernel,
-        "sum_last",
-        rows_of(*(HEAD_ROWS + 2 * VECTOR_ROWS,) * 3, TAIL_ROWS, 2 * VECTOR_ROWS) + [float_rows(HEAD_ROWS), float_rows(TAIL_ROWS)],
-        low, got_hx, got_hy, vector, tail, *got_tz,
-    )
-    got_hz = [moved(part, "z", s + 1) for s, part in enumerate((one, two, three))]
-    got_tx = moved(tx, "x", 1)
+    got_far = moved(far, "x", 1)
+    got_tz = [moved(tz[s], "z", s) for s in (1, 2, 3)]
+    got_hy, got_far, low, own_tail, vector, dkv, *got_tz = together(got_hy, got_far, low, tz[0], vector, dkv, *got_tz)
+    vector = summed_vector(vector, got_hy[PART:])
+    head = [summed(low[cut], got_far[cut], got_hy[cut]) for cut in cuts]
+    got_hz = [moved(jnp.concatenate([head[s].astype(BF16), vector]), "z", s) for s in (1, 2, 3)]
+    got_dkv = across(dkv[1], 2)
+    tx = summed(own_tail[TAIL_ROWS:], *[part[TAIL_ROWS:] for part in got_tz]).astype(BF16)
+    own_tail = summed(own_tail[:TAIL_ROWS], *[part[:TAIL_ROWS] for part in got_tz])
+    input_grad = make_input((dkv[0], got_dkv))
+    tx, input_grad = together(tx, input_grad)
+    got_tx, vector = together(moved(tx, "x", 1), vector)
     place = coordinates(device_number() // inner_count())["z"]
     stacked = jnp.stack([vector] + [part[HEAD_ROWS:] for part in got_hz])
     total = sum(
         summed(found[:VECTOR_ROWS], found[VECTOR_ROWS:])
         for found in (lax.dynamic_index_in_dim(stacked, (place - z) % 4, 0, keepdims=False) for z in range(4))
     )
-    return (own, *got_hz, own_tail, got_tx), total, input_grad
+    return (head[0], *got_hz, own_tail, got_tx), total, input_grad
 
 
 def lower_lanes(shape):
@@ -453,10 +407,9 @@
     tail_parts = refs[9:13]
     tokens_pair, cos_pair, sin_pair = refs[13:15], refs[15:17], refs[17:19]
     (place_q_ref, place_k_ref, gains_ref, bias_q_ref, bias_kv_ref, grad_ref) = refs[19:25]
-    (block_out_ref, send_first, send_rest, keep_first, keep_rest) = refs[25:30]
-    dkv_refs = refs[30:34]
-    (dq_wq_ref, d_mid_ref, w_kv) = refs[34:37]
-    (raw_head, raw_tail, w_q, w_out, w_gate, w_up, w_down, normed_all, hidden_all, keys, values, queries, probs, attended, act_all, block_acc, d_hidden, d_attended, dkv_all, d_query, send_all, keep_all, vector_ref, sems) = refs[37:]
+    block_out_ref, parts_out = refs[25], refs[26:36]
+    (dkv_send, dkv_keep, dq_wq_ref, d_mid_ref, w_kv) = refs[36:41]
+    (raw_head, raw_tail, w_q, w_out, w_gate, w_up, w_down, normed_all, hidden_all, keys, values, queries, probs, attended, act_all, block_acc, d_hidden, d_attended, dkv_all, d_query, send_all, keep_all, vector_ref, sems) = refs[41:]
 
     copies = []
     for k, part in enumerate(head_parts):
@@ -678,7 +631,8 @@
         dkv_all[key_rows, 128:256] = jnp.where(low_keys, d_values[0], d_values[1]).astype(BF16)
         dkv_all[key_rows, 256:384] = jnp.where(low_keys, key_b, d_values[2]).astype(BF16)
         for slot in range(4):
-            dkv_refs[slot][mb] = dkv_all[pl.ds(pl.multiple_of(mb * 512 + slot * ROWS, ROWS), ROWS), :]
+            target = dkv_send if slot % 2 else dkv_keep
+            target[slot // 2, mb] = dkv_all[pl.ds(pl.multiple_of(mb * 512 + slot * ROWS, ROWS), ROWS), :]
 
     dkv = dkv_all[...]
     d_q = d_query[...]
@@ -712,15 +666,15 @@
     )
     high = vector.astype(BF16)
     rest = (vector - high.astype(F32)).astype(BF16)
-    at = FIRST_AT + 2 * PART
+    at = FIRST_AT + PART
     for ref in (send_all, keep_all):
         ref[at : at + VECTOR_ROWS, :] = high
         ref[at + VECTOR_ROWS : at + 2 * VECTOR_ROWS, :] = rest
     copies = [
-        pltpu.make_async_copy(send_all.at[pl.ds(FIRST_AT, FIRST_ROWS)], send_first, sems.at[0]),
-        pltpu.make_async_copy(send_all.at[pl.ds(0, FIRST_AT)], send_rest, sems.at[1]),
-        pltpu.make_async_copy(keep_all.at[pl.ds(FIRST_AT, FIRST_ROWS)], keep_first, sems.at[2]),
-        pltpu.make_async_copy(keep_all.at[pl.ds(0, FIRST_AT)], keep_rest, sems.at[3]),
+        pltpu.make_async_copy(ref.at[pl.ds(first, count)], out, sems.at[k])
+        for k, (ref, out, (first, count)) in enumerate(
+            zip([send_all] * 4 + [keep_all] * 6, parts_out, SEND_PARTS + KEEP_PARTS)
+        )
     ]
     for copy in copies:
         copy.start()
@@ -753,28 +707,23 @@
         ((256, WIDE), BF16),
         ((1024, 384), BF16),
         ((256, WIDE), BF16),
-        ((FIRST_AT + FIRST_ROWS, LANES), BF16),
-        ((FIRST_AT + FIRST_ROWS, LANES), BF16),
+        ((ALL_ROWS, LANES), BF16),
+        ((ALL_ROWS, LANES), BF16),
         ((8, WIDE), F32),
     ]
     return pl.pallas_call(
         layer_kernel,
         out_shape=(
             shape((2, MODEL_WIDTH, ROWS), BF16),
-            shape((FIRST_ROWS, LANES), BF16),
-            shape((FIRST_AT, LANES), BF16),
-            shape((FIRST_ROWS, LANES), BF16),
-            shape((FIRST_AT, LANES), BF16),
-            shape((2, ROWS, 384), BF16),
-            shape((2, ROWS, 384), BF16),
-            shape((2, ROWS, 384), BF16),
-            shape((2, ROWS, 384), BF16),
+            *[shape((count, LANES), BF16) for _, count in SEND_PARTS + KEEP_PARTS],
+            shape((2, 2, ROWS, 384), BF16),
+            shape((2, 2, ROWS, 384), BF16),
             shape((256, WIDE), F32),
             shape((256, WIDE), F32),
             shape((WIDE, 384), BF16),
         ),
         in_specs=[pl.BlockSpec(memory_space=pltpu.SMEM)] + [anywhere] * 12 + [vmem] * 12,
-        out_specs=(vmem,) + (anywhere,) * 4 + (vmem,) * 7,
+        out_specs=(vmem,) + (anywhere,) * 10 + (vmem,) * 5,
         scratch_shapes=[pltpu.VMEM(dims, kind) for dims, kind in scratch]
         + [pltpu.SemaphoreType.DMA((12,))],
         compiler_params=pltpu.CompilerParams(vmem_limit_bytes=50 * 1024 * 1024),
@@ -782,11 +731,11 @@
     )(slots, *heads, *tails, *others)
 
 
-def input_kernel(tokens_ref, gains_ref, w_kv_ref, dq_wq_ref, d_mid_ref, own_ref, one_ref, two_ref, three_ref, out_ref):
+def input_kernel(tokens_ref, gains_ref, w_kv_ref, dq_wq_ref, d_mid_ref, own_ref, other_ref, out_ref):
     lane = lax.broadcasted_iota(jnp.int32, (2 * ROWS, WIDE), 1)
     x = jnp.where(lane < MODEL_WIDTH, tokens_ref[0].astype(F32).reshape(2 * ROWS, WIDE), 0.0)
     normed, scale = normed_rows(x)
-    total = summed(own_ref[...], one_ref[...], two_ref[...], three_ref[...])
+    total = summed(own_ref[...], other_ref[...])
     total = total.reshape(2 * ROWS, 384).astype(BF16)
     d_norm = (dq_wq_ref[...] + times_transposed(total, w_kv_ref[...])) * gains_ref[0:1, :]
     d_input = d_mid_ref[...] + scale * (d_norm - normed * row_mean(d_norm * normed))
@@ -798,8 +747,9 @@
     return pl.pallas_call(
         input_kernel,
         out_shape=jax.ShapeDtypeStruct((2, MODEL_WIDTH, ROWS), BF16),
-        in_specs=[pl.BlockSpec(memory_space=pltpu.VMEM)] * 9,
+        in_specs=[pl.BlockSpec(memory_space=pltpu.VMEM)] * 7,
         out_specs=pl.BlockSpec(memory_space=pltpu.VMEM),
+        cost_estimate=pl.CostEstimate(flops=3_500_000_000, bytes_accessed=6_000_000, transcendentals=0),
         name="input_grad",
     )(tokens, gains, w_kv, dq_wq, d_mid, *parts)
 
@@ -865,11 +815,13 @@
     place_q = place_all[0, 0][..., None]
     place_k = jnp.transpose(place_all.reshape(4, 2, ROWS), (1, 0, 2)).reshape(2, 1, 4 * ROWS)
 
-    (block_out, send_first, send_rest, keep_first, keep_rest, *pairs, dq_wq, d_mid, w_kv) = run_layer(
+    block_out, *found = run_layer(
         slots, heads, tails, near, far, cosines, cosines_far, sines, sines_far, place_q, place_k, gains, bias_q, bias_kv, grad
     )
+    sends, keeps = found[:4], found[4:10]
+    dkv_send, dkv_keep, dq_wq, d_mid, w_kv = found[10:]
     make_input = lambda parts: run_input(near, gains, w_kv, dq_wq, d_mid, parts)
-    parts, vector, input_grad = scatter_blocks(send_first, send_rest, keep_first, keep_rest, pairs, make_input)
+    parts, vector, input_grad = scatter_blocks(sends, keeps, dkv_send, dkv_keep, make_input)
     state = (weights, first_moment, second_moment)
     if inner_count() == 1:
         updated = finish(kind, parts, [array.reshape(BLOCK_ROWS, LANES) for array in state])

time: 184 us -> 166 us (0.902)
  Pallas kernels: 52.9 us -> 40 us
  waiting for transfers between devices: 75.8 us -> 68 us
  other arithmetic: 5.13 us -> 11.1 us
  local copies, waits for them, and re-layouts: 10.4 us -> 5.87 us
    ppermute x5 -> x4, waiting for transfers between devices: 20.6 us -> 0.01 us  [across(): lax.ppermute(buffer, 'ctx', [(i, i ^ distance) for i in range(count)])]
    ppermute x30 -> x32, waiting for transfers between devices: 55.3 us -> 68 us  [moved(): return lax.ppermute(buffer, ('dp', 'ctx'), pairs)]
    pallas_call x4 -> x0, Pallas kernels: 12.3 us -> none  [on_chip(): pl.pallas_call(kernel, out_shape=tuple(shapes), in_specs=[vmem] * len(arr...]
    convert_element_type x0 -> x11, other arithmetic: none -> 4.11 us  [the longest x1 1.22 us: scatter_blocks(): ty = summed(keep_tail, got_tail).astype(BF16)]
    unnamed x74 -> x72, local copies, waits for them, and re-layouts: 6.07 us -> 2.29 us
    ppermute x30 -> x32, starting transfers between devices: 33.2 us -> 34.4 us  [moved(): return lax.ppermute(buffer, ('dp', 'ctx'), pairs)]
    ppermute x5 -> x4, starting transfers between devices: 4.08 us -> 3.49 us  [across(): lax.ppermute(buffer, 'ctx', [(i, i ^ distance) for i in range(count)])]
  transfers between devices with their start and end apart: 35 -> 36, of which waited for: 19 -> 18; matrix products, arithmetic and copies ran while one was open for 5% -> 8% of each run, Pallas kernels for 5% -> 2%
where the time goes in v5:
time: 166 us; the launch traced here: 165 us
  waiting for transfers between devices  68 us (41%)
  Pallas kernels  40 us (24%)
  starting transfers between devices  37.9 us (23%)
  other arithmetic  11.1 us (7%)
  local copies, waits for them, and re-layouts  5.87 us (4%)
  between operations  2.26 us (1%)
    ppermute x32, waiting for transfers between devices, moved(): return lax.ppermute(buffer, ('dp', 'ctx'), pairs)  68 us
    ppermute x32, starting transfers between devices, moved(): return lax.ppermute(buffer, ('dp', 'ctx'), pairs)  34.4 us
    pallas_call x1, Pallas kernels, run_layer(): pl.pallas_call(layer_kernel, out_shape=(shape((2, MODEL_WIDTH, ROWS), BF1...  31.6 us
    ppermute x4, starting transfers between devices, across(): lax.ppermute(buffer, 'ctx', [(i, i ^ distance) for i in range(count)])  3.49 us
    pallas_call x1, Pallas kernels, finish(): pl.pallas_call(flat_kernel, out_shape=(flat,) * count, in_specs=[pl.Block...  3.36 us
  transfers between devices with their start and end apart: 36, of which 18 were waited for; matrix products, arithmetic and copies ran while one was open for 8% of the time, Pallas kernels for 2%

profile of v5, /device:TPU:0, one launch (start us, length us, event | category | flops | bytes accessed | tf_op | source)
XLA Modules:
  0.0 165.1 jit_solution(11937985059317621106)
XLA Ops:
  0.7 1.9 %to_tiles.1 = (bf16[576,128]{1,0:T(8,128)(2,1)}, bf16[288,128]{1,0:T(8,128)(2,1)}) custom-call(s32[1]{0:T(128)} %bitcast.kind_ref, f32[864,128]{1,0:T(8,128)} %bitcast.160), custom_call_target="tpu_custom_call" | custom-call | tf_op jit(solution)/shard_map/to_tiles/pallas_call | solution.py:265
  2.5 2.9 %collective-permute-start.2 = (bf16[576,128]{1,0:T(8,128)(2,1)}, bf16[576,128]{1,0:T(8,128)(2,1)S(1)}, u32[]{:S(2)}, u32[]{:S(2)}) collective-permute-start(bf16[576,128]{1,0:T(8,128)(2,1)} %get-tuple-element.94), channel_id=1, source_target_pairs={{0,8},{1,9},{2,10},{3,11},{4,12},{5,13},{6,14},{7,15},{8,16},{9,17... | collective-permute-start | bytes 442376 | tf_op jit(solution)/shard_map/ppermute | solution.py:75
  5.4 2.7 %collective-permute-start.3 = (bf16[576,128]{1,0:T(8,128)(2,1)}, bf16[576,128]{1,0:T(8,128)(2,1)S(1)}, u32[]{:S(2)}, u32[]{:S(2)}) collective-permute-start(bf16[576,128]{1,0:T(8,128)(2,1)} %get-tuple-element.94), channel_id=1, source_target_pairs={{0,16},{1,17},{2,18},{3,19},{4,20},{5,21},{6,22},{7,23},{8,24},{9,... | collective-permute-start | bytes 442376 | tf_op jit(solution)/shard_map/ppermute | solution.py:75
  8.2 1.2 collective-permute-start.4
  10.3 1.2 copy.40
  11.7 1.6 collective-permute-start.1
  15.8 6.2 %collective-permute-done = bf16[288,128]{1,0:T(8,128)(2,1)S(1)} collective-permute-done((bf16[288,128]{1,0:T(8,128)(2,1)S(1)}, bf16[288,128]{1,0:T(8,128)(2,1)S(1)}, u32[]{:S(2)}, u32[]{:S(2)}) %collective-permute-start) | collective-permute-done | bytes 73760 | tf_op jit(solution)/shard_map/ppermute | solution.py:75
  22.1 1.6 collective-permute-start.5
  23.7 1.5 collective-permute-start.6
  26.5 2.6 %collective-permute-start.9 = (bf16[2,288,128]{2,1,0:T(8,128)(2,1)S(1)}, bf16[2,288,128]{2,1,0:T(8,128)(2,1)S(1)}, u32[]{:S(2)}, u32[]{:S(2)}) collective-permute-start(bf16[2,288,128]{2,1,0:T(8,128)(2,1)S(1)} %pad_maximum_fusion.10), channel_id=1, source_target_pairs={{0,24},{1,25},{2,26},{3,27},{4,28},{5,29},{6,30},{7,31},{8,0},{9,1... | collective-permute-start | bytes 442376 | tf_op jit(solution)/shard_map/ppermute | solution.py:75
  30.5 3.0 %collective-permute-done.7 = bf16[2,288,128]{2,1,0:T(8,128)(2,1)S(1)} collective-permute-done((bf16[2,288,128]{2,1,0:T(8,128)(2,1)S(1)}, bf16[2,288,128]{2,1,0:T(8,128)(2,1)S(1)}, u32[]{:S(2)}, u32[]{:S(2)}) %collective-permute-start.7) | collective-permute-done | bytes 147488 | tf_op jit(solution)/shard_map/ppermute | solution.py:75
  33.6 3.3 %collective-permute-done.8 = bf16[2,288,128]{2,1,0:T(8,128)(2,1)S(1)} collective-permute-done((bf16[2,288,128]{2,1,0:T(8,128)(2,1)S(1)}, bf16[2,288,128]{2,1,0:T(8,128)(2,1)S(1)}, u32[]{:S(2)}, u32[]{:S(2)}) %collective-permute-start.8) | collective-permute-done | bytes 147488 | tf_op jit(solution)/shard_map/ppermute | solution.py:75
  37.6 1.3 collective-permute-start.10
  39.4 12.6 %collective-permute-done.11.refs_10_ = bf16[8,288,128]{2,1,0:T(8,128)(2,1)S(1)} collective-permute-done((bf16[8,288,128]{2,1,0:T(8,128)(2,1)S(1)}, bf16[8,288,128]{2,1,0:T(8,128)(2,1)S(1)}, u32[]{:S(2)}, u32[]{:S(2)}) %collective-permute-start.11) | collective-permute-done | bytes 589856 | tf_op jit(solution)/shard_map/ppermute | solution.py:75
  58.6 31.6 %layer.1 = (bf16[2,576,128]{2,1,0:T(8,128)(2,1)}, bf16[2400,128]{1,0:T(8,128)(2,1)}, bf16[2304,128]{1,0:T(8,128)(2,1)S(1)}, bf16[6912,128]{1,0:T(8,128)(2,1)}, b...) custom-call(s32[97]{0:T(128)S(1)} %stack.459.refs_0_, ...), custom_call_target="tpu_custom_call" | custom-call | tf_op jit(solution)/shard_map/layer/pallas_call | solution.py:714
  90.8 2.4 %collective-permute-done.20 = bf16[2304,128]{1,0:T(8,128)(2,1)S(1)} collective-permute-done((bf16[2304,128]{1,0:T(8,128)(2,1)S(1)}, bf16[2304,128]{1,0:T(8,128)(2,1)S(1)}, u32[]{:S(2)}, u32[]{:S(2)}) %collective-permute-start.20) | collective-permute-done | bytes 589856 | tf_op jit(solution)/shard_map/ppermute | solution.py:75
  93.8 1.2 add_convert_fusion.5
  97.1 1.4 collective-permute-done.23
  99.0 11.8 %collective-permute-done.22 = bf16[2304,128]{1,0:T(8,128)(2,1)S(1)} collective-permute-done((bf16[2304,128]{1,0:T(8,128)(2,1)S(1)}, bf16[2304,128]{1,0:T(8,128)(2,1)S(1)}, u32[]{:S(2)}, u32[]{:S(2)}) %collective-permute-start.22) | collective-permute-done | bytes 589856 | tf_op jit(solution)/shard_map/ppermute | solution.py:75
  112.5 1.6 collective-permute-start.26
  115.5 3.7 %collective-permute-start.28 = (bf16[576,128]{1,0:T(8,128)(2,1)}, bf16[576,128]{1,0:T(8,128)(2,1)}, u32[]{:S(2)}, u32[]{:S(2)}) collective-permute-start(bf16[576,128]{1,0:T(8,128)(2,1)} %get-tuple-element.211), channel_id=1, source_target_pairs={{0,8},{1,9},{2,10},{3,11},{4,12},{5,13},{6,14},{7,15},{8,16},{9,17... | collective-permute-start | bytes 442376 | tf_op jit(solution)/shard_map/ppermute | solution.py:75
  119.2 2.4 %collective-permute-start.30 = (bf16[576,128]{1,0:T(8,128)(2,1)}, bf16[576,128]{1,0:T(8,128)(2,1)}, u32[]{:S(2)}, u32[]{:S(2)}) collective-permute-start(bf16[576,128]{1,0:T(8,128)(2,1)} %get-tuple-element.209), channel_id=1, source_target_pairs={{0,24},{1,25},{2,26},{3,27},{4,28},{5,29},{6,30},{7,31},{8,0},{9,1... | collective-permute-start | bytes 442376 | tf_op jit(solution)/shard_map/ppermute | solution.py:75
  122.2 2.1 %collective-permute-done.28 = bf16[576,128]{1,0:T(8,128)(2,1)} collective-permute-done((bf16[576,128]{1,0:T(8,128)(2,1)}, bf16[576,128]{1,0:T(8,128)(2,1)}, u32[]{:S(2)}, u32[]{:S(2)}) %collective-permute-start.28) | collective-permute-done | bytes 147488 | tf_op jit(solution)/shard_map/ppermute | solution.py:75
  124.4 4.7 %collective-permute-done.29 = bf16[576,128]{1,0:T(8,128)(2,1)} collective-permute-done((bf16[576,128]{1,0:T(8,128)(2,1)}, bf16[576,128]{1,0:T(8,128)(2,1)}, u32[]{:S(2)}, u32[]{:S(2)}) %collective-permute-start.29) | collective-permute-done | bytes 147488 | tf_op jit(solution)/shard_map/ppermute | solution.py:75
  129.8 1.5 collective-permute-start.31
  132.3 5.0 %collective-permute-start.34 = (bf16[672,128]{1,0:T(8,128)(2,1)S(1)}, bf16[672,128]{1,0:T(8,128)(2,1)S(1)}, u32[]{:S(2)}, u32[]{:S(2)}) collective-permute-start(bf16[672,128]{1,0:T(8,128)(2,1)S(1)} %get-tuple-element.225), channel_id=1, source_target_pairs={{0,24},{1,25},{2,26},{3,27},{4,28},{5,29},{6,30},{7,31},{8,0},{9,1... | collective-permute-start | bytes 516104 | tf_op jit(solution)/shard_map/ppermute | solution.py:75
  138.0 1.8 %convert_add_fusion.1 = (f32[288,128]{1,0:T(8,128)}, bf16[288,128]{1,0:T(8,128)(2,1)S(1)}) fusion(bf16[576,128]{1,0:T(8,128)(2,1)} %collective-permute-done.30, bf16[576,128]{1,0:T(8,128)(2,1)} %collective-permute-done.29, bf16[576,128]{1,0:T(8,128)(2,1)} %collective-permute-done.28, bf16[576,128]{1,0:T(8,128)(2,1)S(1)} %get-tuple-element.149), kind=kLoop, calls=%fused_computation.51 | loop fusion | flops 552960 | bytes 811008 | tf_op jit(solution)/shard_map/add | solution.py:160
  139.8 2.4 %collective-permute-done.34.three_ref = bf16[672,128]{1,0:T(8,128)(2,1)S(1)} collective-permute-done((bf16[672,128]{1,0:T(8,128)(2,1)S(1)}, bf16[672,128]{1,0:T(8,128)(2,1)S(1)}, u32[]{:S(2)}, u32[]{:S(2)}) %collective-permute-start.34) | collective-permute-done | bytes 172064 | tf_op jit(solution)/shard_map/ppermute | solution.py:75
  142.1 10.4 %collective-permute-done.33.two_ref = bf16[672,128]{1,0:T(8,128)(2,1)S(1)} collective-permute-done((bf16[672,128]{1,0:T(8,128)(2,1)S(1)}, bf16[672,128]{1,0:T(8,128)(2,1)S(1)}, u32[]{:S(2)}, u32[]{:S(2)}) %collective-permute-start.33) | collective-permute-done | bytes 172064 | tf_op jit(solution)/shard_map/ppermute | solution.py:75
  153.3 3.2 %input_grad.1 = bf16[2,576,128]{2,1,0:T(8,128)(2,1)} custom-call(bf16[2,2,128,640]{3,2,1,0:T(8,128)(2,1)} %copy-done.2, f32[2,640]{1,0:T(2,128)} %copy-done, bf16[640,384]{1,0:T(8,128)(2,1)} %copy-done.1, f32[256,640]{1,0:T(8,128)} %get-tuple-element.154.dq_wq_ref, f32[256,640]{1,0:T(8,128)} %get-tuple-element.155.d_mid_ref, ...), custom_call_target="tpu_custom_call" | custom-call | flops 3500000000 | bytes 6000000 | tf_op jit(solution)/shard_map/input_grad/pallas_call | solution.py:747
  156.9 3.8 %collective-permute-done.35.other_ref = bf16[288,128]{1,0:T(8,128)(2,1)S(1)} collective-permute-done((bf16[288,128]{1,0:T(8,128)(2,1)S(1)}, bf16[288,128]{1,0:T(8,128)(2,1)S(1)}, u32[]{:S(2)}, u32[]{:S(2)}) %collective-permute-start.35) | collective-permute-done | bytes 73760 | tf_op jit(solution)/shard_map/ppermute | solution.py:75
  161.7 3.4 %finish.1 = (f32[864,128]{1,0:T(8,128)}, f32[864,128]{1,0:T(8,128)}, f32[864,128]{1,0:T(8,128)}) custom-call(s32[1]{0:T(128)} %bitcast.kind_ref, f32[576,128]{1,0:T(8,128)} %get-tuple-element.203.head_ref, bf16[672,128]{1,0:T(8,128)(2,1)} %copy-done.24, bf16[672,128]{1,0:T(8,128)(2,1)} %copy-done.23, bf16[672,128]{1,0:T(8,128)(2,1)} %copy-done.22, ...), custom_call_target="tpu_custom_call" | custom-call | tf_op jit(solution)/shard_map/finish/pallas_call | solution.py:340
  (187 shorter events, 25.1 us)
Async XLA Ops:
  2.5 19.4 %collective-permute-start.2 = (bf16[576,128]{1,0:T(8,128)(2,1)}, bf16[576,128]{1,0:T(8,128)(2,1)S(1)}, u32[]{:S(2)}, u32[]{:S(2)}) collective-permute-start(bf16[576,128]{1,0:T(8,128)(2,1)} %get-tuple-element.94), channel_id=1, source_target_pairs={{0,8},{1,9},{2,10},{3,11},{4,12},{5,13},{6,14},{7,15},{8,16},{9,17... | collective-permute-start | bytes 442376 | tf_op jit(solution)/shard_map/ppermute | solution.py:75
  5.4 16.5 %collective-permute-start.3 = (bf16[576,128]{1,0:T(8,128)(2,1)}, bf16[576,128]{1,0:T(8,128)(2,1)S(1)}, u32[]{:S(2)}, u32[]{:S(2)}) collective-permute-start(bf16[576,128]{1,0:T(8,128)(2,1)} %get-tuple-element.94), channel_id=1, source_target_pairs={{0,16},{1,17},{2,18},{3,19},{4,20},{5,21},{6,22},{7,23},{8,24},{9,... | collective-permute-start | bytes 442376 | tf_op jit(solution)/shard_map/ppermute | solution.py:75
  8.2 13.8 %collective-permute-start.4 = (bf16[576,128]{1,0:T(8,128)(2,1)}, bf16[576,128]{1,0:T(8,128)(2,1)S(1)}, u32[]{:S(2)}, u32[]{:S(2)}) collective-permute-start(bf16[576,128]{1,0:T(8,128)(2,1)} %get-tuple-element.94), channel_id=1, source_target_pairs={{0,24},{1,25},{2,26},{3,27},{4,28},{5,29},{6,30},{7,31},{8,0},{9,1... | collective-permute-start | bytes 442376 | tf_op jit(solution)/shard_map/ppermute | solution.py:75
  11.7 10.3 %collective-permute-start.1 = (bf16[2,128,640]{2,1,0:T(8,128)(2,1)S(1)}, bf16[2,128,640]{2,1,0:T(8,128)(2,1)S(1)}, u32[]{:S(2)}, u32[]{:S(2)}) collective-permute-start(bf16[2,128,640]{2,1,0:T(8,128)(2,1)S(1)} %maximum_maximum_fusion), channel_id=1, source_target_pairs={{0,2},{1,3},{2,0},{3,1},{4,6},{5,7},{6,4},{7,5},{8,10},{9,11},{10,... | collective-permute-start | bytes 983048 | tf_op jit(solution)/shard_map/ppermute | solution.py:80
  13.3 8.7 %collective-permute-start = (bf16[288,128]{1,0:T(8,128)(2,1)S(1)}, bf16[288,128]{1,0:T(8,128)(2,1)S(1)}, u32[]{:S(2)}, u32[]{:S(2)}) collective-permute-start(bf16[288,128]{1,0:T(8,128)(2,1)S(1)} %copy-done.28), channel_id=1, source_target_pairs={{0,2},{1,3},{2,0},{3,1},{4,6},{5,7},{6,4},{7,5},{8,10},{9,11},{10,... | collective-permute-start | bytes 221192 | tf_op jit(solution)/shard_map/ppermute | solution.py:75
  22.1 14.8 %collective-permute-start.5 = (bf16[4,576,128]{2,1,0:T(8,128)(2,1)S(1)}, bf16[4,576,128]{2,1,0:T(8,128)(2,1)S(1)}, u32[]{:S(2)}, u32[]{:S(2)}) collective-permute-start(bf16[4,576,128]{2,1,0:T(8,128)(2,1)S(1)} %pad_maximum_fusion.3.refs_1_), channel_id=1, source_target_pairs={{0,4},{1,5},{2,6},{3,7},{4,0},{5,1},{6,2},{7,3},{8,12},{9,13},{10,... | collective-permute-start | bytes 1769480 | tf_op jit(solution)/shard_map/ppermute | solution.py:75
  23.7 13.2 %collective-permute-start.6 = (bf16[4,576,128]{2,1,0:T(8,128)(2,1)S(1)}, bf16[4,576,128]{2,1,0:T(8,128)(2,1)S(1)}, u32[]{:S(2)}, u32[]{:S(2)}) collective-permute-start(bf16[4,576,128]{2,1,0:T(8,128)(2,1)S(1)} %pad_maximum_fusion.3.refs_1_), channel_id=1, source_target_pairs={{0,2},{1,3},{2,0},{3,1},{4,6},{5,7},{6,4},{7,5},{8,10},{9,11},{10,... | collective-permute-start | bytes 1769480 | tf_op jit(solution)/shard_map/ppermute | solution.py:75
  25.2 8.4 %collective-permute-start.7 = (bf16[2,288,128]{2,1,0:T(8,128)(2,1)S(1)}, bf16[2,288,128]{2,1,0:T(8,128)(2,1)S(1)}, u32[]{:S(2)}, u32[]{:S(2)}) collective-permute-start(bf16[2,288,128]{2,1,0:T(8,128)(2,1)S(1)} %pad_maximum_fusion.10), channel_id=1, source_target_pairs={{0,8},{1,9},{2,10},{3,11},{4,12},{5,13},{6,14},{7,15},{8,16},{9,17... | collective-permute-start | bytes 442376 | tf_op jit(solution)/shard_map/ppermute | solution.py:75
  26.0 10.8 %collective-permute-start.8 = (bf16[2,288,128]{2,1,0:T(8,128)(2,1)S(1)}, bf16[2,288,128]{2,1,0:T(8,128)(2,1)S(1)}, u32[]{:S(2)}, u32[]{:S(2)}) collective-permute-start(bf16[2,288,128]{2,1,0:T(8,128)(2,1)S(1)} %pad_maximum_fusion.10), channel_id=1, source_target_pairs={{0,16},{1,17},{2,18},{3,19},{4,20},{5,21},{6,22},{7,23},{8,24},{9,... | collective-permute-start | bytes 442376 | tf_op jit(solution)/shard_map/ppermute | solution.py:75
  26.5 10.4 %collective-permute-start.9 = (bf16[2,288,128]{2,1,0:T(8,128)(2,1)S(1)}, bf16[2,288,128]{2,1,0:T(8,128)(2,1)S(1)}, u32[]{:S(2)}, u32[]{:S(2)}) collective-permute-start(bf16[2,288,128]{2,1,0:T(8,128)(2,1)S(1)} %pad_maximum_fusion.10), channel_id=1, source_target_pairs={{0,24},{1,25},{2,26},{3,27},{4,28},{5,29},{6,30},{7,31},{8,0},{9,1... | collective-permute-start | bytes 442376 | tf_op jit(solution)/shard_map/ppermute | solution.py:75
  37.0 15.0 %collective-permute-start.11 = (bf16[8,288,128]{2,1,0:T(8,128)(2,1)S(1)}, bf16[8,288,128]{2,1,0:T(8,128)(2,1)S(1)}, u32[]{:S(2)}, u32[]{:S(2)}) collective-permute-start(bf16[8,288,128]{2,1,0:T(8,128)(2,1)S(1)} %constant_dynamic-update-slice_fusion.refs_9_), channel_id=1, source_target_pairs={{0,4},{1,5},{2,6},{3,7},{4,0},{5,1},{6,2},{7,3},{8,12},{9,13},{10,... | collective-permute-start | bytes 1769480 | tf_op jit(solution)/shard_map/ppermute | solution.py:75
  37.6 14.5 %collective-permute-start.15 = (bf16[8,288,128]{2,1,0:T(8,128)(2,1)S(1)}, bf16[8,288,128]{2,1,0:T(8,128)(2,1)S(1)}, u32[]{:S(2)}, u32[]{:S(2)}) collective-permute-start(bf16[8,288,128]{2,1,0:T(8,128)(2,1)S(1)} %constant_dynamic-update-slice_fusion.refs_9_), channel_id=1, source_target_pairs={{0,1},{1,0},{2,3},{3,2},{4,5},{5,4},{6,7},{7,6},{8,9},{9,8},{10,11... | collective-permute-start | bytes 1769480 | tf_op jit(solution)/shard_map/ppermute | solution.py:75
  37.6 15.7 %collective-permute-start.10 = (bf16[4,576,128]{2,1,0:T(8,128)(2,1)S(1)}, bf16[4,576,128]{2,1,0:T(8,128)(2,1)S(1)}, u32[]{:S(2)}, u32[]{:S(2)}) collective-permute-start(bf16[4,576,128]{2,1,0:T(8,128)(2,1)S(1)} %collective-permute-done.5.refs_2_), channel_id=1, source_target_pairs={{0,2},{1,3},{2,0},{3,1},{4,6},{5,7},{6,4},{7,5},{8,10},{9,11},{10,... | collective-permute-start | bytes 1769480 | tf_op jit(solution)/shard_map/ppermute | solution.py:75
  38.9 15.2 %collective-permute-start.13 = (bf16[4,576,128]{2,1,0:T(8,128)(2,1)S(1)}, bf16[4,576,128]{2,1,0:T(8,128)(2,1)S(1)}, u32[]{:S(2)}, u32[]{:S(2)}) collective-permute-start(bf16[4,576,128]{2,1,0:T(8,128)(2,1)S(1)} %collective-permute-done.5.refs_2_), channel_id=1, source_target_pairs={{0,1},{1,0},{2,3},{3,2},{4,5},{5,4},{6,7},{7,6},{8,9},{9,8},{10,11... | collective-permute-start | bytes 1769480 | tf_op jit(solution)/shard_map/ppermute | solution.py:75
  39.1 15.8 %collective-permute-start.16 = (bf16[2,2,128,640]{3,2,1,0:T(8,128)(2,1)S(1)}, bf16[2,2,128,640]{3,2,1,0:T(8,128)(2,1)S(1)}, u32[]{:S(2)}, u32[]{:S(2)}) collective-permute-start(bf16[2,2,128,640]{3,2,1,0:T(8,128)(2,1)S(1)} %pad_maximum_fusion.refs_13_.tokens_ref), channel_id=1, source_target_pairs={{0,1},{1,0},{2,3},{3,2},{4,5},{5,4},{6,7},{7,6},{8,9},{9,8},{10,11... | collective-permute-start | bytes 1966088 | tf_op jit(solution)/shard_map/ppermute | solution.py:80
  52.0 2.8 %collective-permute-start.14 = (bf16[4,576,128]{2,1,0:T(8,128)(2,1)S(1)}, bf16[4,576,128]{2,1,0:T(8,128)(2,1)S(1)}, u32[]{:S(2)}, u32[]{:S(2)}) collective-permute-start(bf16[4,576,128]{2,1,0:T(8,128)(2,1)S(1)} %collective-permute-done.6.refs_3_), channel_id=1, source_target_pairs={{0,1},{1,0},{2,3},{3,2},{4,5},{5,4},{6,7},{7,6},{8,9},{9,8},{10,11... | collective-permute-start | bytes 1769480 | tf_op jit(solution)/shard_map/ppermute | solution.py:75
  90.2 3.0 %collective-permute-start.19 = (bf16[2400,128]{1,0:T(8,128)(2,1)}, bf16[2400,128]{1,0:T(8,128)(2,1)S(1)}, u32[]{:S(2)}, u32[]{:S(2)}) collective-permute-start(bf16[2400,128]{1,0:T(8,128)(2,1)} %get-tuple-element.125), channel_id=1, source_target_pairs={{0,1},{1,0},{2,3},{3,2},{4,5},{5,4},{6,7},{7,6},{8,9},{9,8},{10,11... | collective-permute-start | bytes 1843208 | tf_op jit(solution)/shard_map/ppermute | solution.py:75
  93.2 3.6 %collective-permute-start.25 = (bf16[2,2,128,384]{3,2,1,0:T(8,128)(2,1)S(1)}, bf16[2,2,128,384]{3,2,1,0:T(8,128)(2,1)S(1)}, u32[]{:S(2)}, u32[]{:S(2)}) collective-permute-start(bf16[2,2,128,384]{3,2,1,0:T(8,128)(2,1)S(1)} %get-tuple-element.140), channel_id=1, source_target_pairs={{0,1},{1,0},{2,3},{3,2},{4,5},{5,4},{6,7},{7,6},{8,9},{9,8},{10,11... | collective-permute-start | bytes 1179656 | tf_op jit(solution)/shard_map/ppermute | solution.py:80
  93.3 3.6 %collective-permute-start.24 = (bf16[2304,128]{1,0:T(8,128)(2,1)S(1)}, bf16[2304,128]{1,0:T(8,128)(2,1)S(1)}, u32[]{:S(2)}, u32[]{:S(2)}) collective-permute-start(bf16[2304,128]{1,0:T(8,128)(2,1)S(1)} %get-tuple-element.138), channel_id=1, source_target_pairs={{0,1},{1,0},{2,3},{3,2},{4,5},{5,4},{6,7},{7,6},{8,9},{9,8},{10,11... | collective-permute-start | bytes 1769480 | tf_op jit(solution)/shard_map/ppermute | solution.py:75
  93.7 4.8 %collective-permute-start.23 = (bf16[6912,128]{1,0:T(8,128)(2,1)}, bf16[6912,128]{1,0:T(8,128)(2,1)S(1)}, u32[]{:S(2)}, u32[]{:S(2)}) collective-permute-start(bf16[6912,128]{1,0:T(8,128)(2,1)} %get-tuple-element.134), channel_id=1, source_target_pairs={{0,1},{1,0},{2,3},{3,2},{4,5},{5,4},{6,7},{7,6},{8,9},{9,8},{10,11... | collective-permute-start | bytes 5308424 | tf_op jit(solution)/shard_map/ppermute | solution.py:75
  95.1 15.7 %collective-permute-start.22 = (bf16[2304,128]{1,0:T(8,128)(2,1)S(1)}, bf16[2304,128]{1,0:T(8,128)(2,1)S(1)}, u32[]{:S(2)}, u32[]{:S(2)}) collective-permute-start(bf16[2304,128]{1,0:T(8,128)(2,1)S(1)} %add_convert_fusion.5), channel_id=1, source_target_pairs={{0,4},{1,5},{2,6},{3,7},{4,0},{5,1},{6,2},{7,3},{8,12},{9,13},{10,... | collective-permute-start | bytes 1769480 | tf_op jit(solution)/shard_map/ppermute | solution.py:75
  95.9 15.9 %collective-permute-start.21 = (bf16[2400,128]{1,0:T(8,128)(2,1)S(1)}, bf16[2400,128]{1,0:T(8,128)(2,1)S(1)}, u32[]{:S(2)}, u32[]{:S(2)}) collective-permute-start(bf16[2400,128]{1,0:T(8,128)(2,1)S(1)} %pad_maximum_fusion.1), channel_id=1, source_target_pairs={{0,2},{1,3},{2,0},{3,1},{4,6},{5,7},{6,4},{7,5},{8,10},{9,11},{10,... | collective-permute-start | bytes 1843208 | tf_op jit(solution)/shard_map/ppermute | solution.py:75
  112.5 16.6 %collective-permute-start.26 = (bf16[2400,128]{1,0:T(8,128)(2,1)S(1)}, bf16[2400,128]{1,0:T(8,128)(2,1)S(1)}, u32[]{:S(2)}, u32[]{:S(2)}) collective-permute-start(bf16[2400,128]{1,0:T(8,128)(2,1)S(1)} %pad_maximum_fusion.2), channel_id=1, source_target_pairs={{0,4},{1,5},{2,6},{3,7},{4,0},{5,1},{6,2},{7,3},{8,12},{9,13},{10,... | collective-permute-start | bytes 1843208 | tf_op jit(solution)/shard_map/ppermute | solution.py:75
  114.1 15.0 %collective-permute-start.27 = (bf16[2304,128]{1,0:T(8,128)(2,1)S(1)}, bf16[2304,128]{1,0:T(8,128)(2,1)S(1)}, u32[]{:S(2)}, u32[]{:S(2)}) collective-permute-start(bf16[2304,128]{1,0:T(8,128)(2,1)S(1)} %get-tuple-element.144), channel_id=1, source_target_pairs={{0,2},{1,3},{2,0},{3,1},{4,6},{5,7},{6,4},{7,5},{8,10},{9,11},{10,... | collective-permute-start | bytes 1769480 | tf_op jit(solution)/shard_map/ppermute | solution.py:75
  115.5 8.9 %collective-permute-start.28 = (bf16[576,128]{1,0:T(8,128)(2,1)}, bf16[576,128]{1,0:T(8,128)(2,1)}, u32[]{:S(2)}, u32[]{:S(2)}) collective-permute-start(bf16[576,128]{1,0:T(8,128)(2,1)} %get-tuple-element.211), channel_id=1, source_target_pairs={{0,8},{1,9},{2,10},{3,11},{4,12},{5,13},{6,14},{7,15},{8,16},{9,17... | collective-permute-start | bytes 442376 | tf_op jit(solution)/shard_map/ppermute | solution.py:75
  119.2 9.9 %collective-permute-start.29 = (bf16[576,128]{1,0:T(8,128)(2,1)}, bf16[576,128]{1,0:T(8,128)(2,1)}, u32[]{:S(2)}, u32[]{:S(2)}) collective-permute-start(bf16[576,128]{1,0:T(8,128)(2,1)} %get-tuple-element.210), channel_id=1, source_target_pairs={{0,16},{1,17},{2,18},{3,19},{4,20},{5,21},{6,22},{7,23},{8,24},{9,... | collective-permute-start | bytes 442376 | tf_op jit(solution)/shard_map/ppermute | solution.py:75
  119.2 9.9 %collective-permute-start.30 = (bf16[576,128]{1,0:T(8,128)(2,1)}, bf16[576,128]{1,0:T(8,128)(2,1)}, u32[]{:S(2)}, u32[]{:S(2)}) collective-permute-start(bf16[576,128]{1,0:T(8,128)(2,1)} %get-tuple-element.209), channel_id=1, source_target_pairs={{0,24},{1,25},{2,26},{3,27},{4,28},{5,29},{6,30},{7,31},{8,0},{9,1... | collective-permute-start | bytes 442376 | tf_op jit(solution)/shard_map/ppermute | solution.py:75
  129.8 22.7 %collective-permute-start.31 = (bf16[2,128,384]{2,1,0:T(8,128)(2,1)S(1)}, bf16[2,128,384]{2,1,0:T(8,128)(2,1)S(1)}, u32[]{:S(2)}, u32[]{:S(2)}) collective-permute-start(bf16[2,128,384]{2,1,0:T(8,128)(2,1)S(1)} %get-tuple-element.219), channel_id=1, source_target_pairs={{0,2},{1,3},{2,0},{3,1},{4,6},{5,7},{6,4},{7,5},{8,10},{9,11},{10,... | collective-permute-start | bytes 589832 | tf_op jit(solution)/shard_map/ppermute | solution.py:80
  132.3 9.8 %collective-permute-start.34 = (bf16[672,128]{1,0:T(8,128)(2,1)S(1)}, bf16[672,128]{1,0:T(8,128)(2,1)S(1)}, u32[]{:S(2)}, u32[]{:S(2)}) collective-permute-start(bf16[672,128]{1,0:T(8,128)(2,1)S(1)} %get-tuple-element.225), channel_id=1, source_target_pairs={{0,24},{1,25},{2,26},{3,27},{4,28},{5,29},{6,30},{7,31},{8,0},{9,1... | collective-permute-start | bytes 516104 | tf_op jit(solution)/shard_map/ppermute | solution.py:75
  137.3 15.2 %collective-permute-start.33 = (bf16[672,128]{1,0:T(8,128)(2,1)S(1)}, bf16[672,128]{1,0:T(8,128)(2,1)S(1)}, u32[]{:S(2)}, u32[]{:S(2)}) collective-permute-start(bf16[672,128]{1,0:T(8,128)(2,1)S(1)} %get-tuple-element.226), channel_id=1, source_target_pairs={{0,16},{1,17},{2,18},{3,19},{4,20},{5,21},{6,22},{7,23},{8,24},{9,... | collective-permute-start | bytes 516104 | tf_op jit(solution)/shard_map/ppermute | solution.py:75
  137.5 19.5 %collective-permute-start.32 = (bf16[672,128]{1,0:T(8,128)(2,1)S(1)}, bf16[672,128]{1,0:T(8,128)(2,1)S(1)}, u32[]{:S(2)}, u32[]{:S(2)}) collective-permute-start(bf16[672,128]{1,0:T(8,128)(2,1)S(1)} %get-tuple-element.227), channel_id=1, source_target_pairs={{0,8},{1,9},{2,10},{3,11},{4,12},{5,13},{6,14},{7,15},{8,16},{9,17... | collective-permute-start | bytes 516104 | tf_op jit(solution)/shard_map/ppermute | solution.py:75
  156.4 4.4 %collective-permute-start.35 = (bf16[288,128]{1,0:T(8,128)(2,1)S(1)}, bf16[288,128]{1,0:T(8,128)(2,1)S(1)}, u32[]{:S(2)}, u32[]{:S(2)}) collective-permute-start(bf16[288,128]{1,0:T(8,128)(2,1)S(1)} %get-tuple-element.162), channel_id=1, source_target_pairs={{0,2},{1,3},{2,0},{3,1},{4,6},{5,7},{6,4},{7,5},{8,10},{9,11},{10,... | collective-permute-start | bytes 221192 | tf_op jit(solution)/shard_map/ppermute | solution.py:75
  (39 other events, 286.1 us)

commit v6 on v5

--- a/solution.py
+++ b/solution.py
@@ -28,7 +28,7 @@
 BLOCK_ROWS = 864
 HEAD_ROWS = 576
 TAIL_ROWS = BLOCK_ROWS - HEAD_ROWS
-VECTOR_ROWS = 48
+VECTOR_ROWS = 24
 PART = 4 * HEAD_ROWS
 FIRST_AT = 4 * PART
 TAIL_AT = FIRST_AT + PART + 2 * VECTOR_ROWS
@@ -132,6 +132,14 @@
     return slot
 
 
+def head_row(slot, z, _):
+    return slot * PART + jnp.where(slot < 3, 0, FIRST_AT - 3 * PART) + z * HEAD_ROWS
+
+
+def tail_row(slot, z, inside):
+    return jnp.where(slot < 1, 3 * PART, TAIL_AT) + (2 * z + inside) * TAIL_ROWS
+
+
 def slot_table():
     mine = coordinates(device_number() // inner_count())
     entries = []
@@ -139,19 +147,19 @@
         for number in range(BLOCKS):
             found = coordinates(number)
             entries.append(fold(order, {n: (mine[n] - found[n]) % SIZES[n] for n in SIZES}))
-    for number in range(0, BLOCKS, 2):
-        found = coordinates(number)
-        slot = fold(("x", "y", "z"), {n: (found[n] - mine[n]) % SIZES[n] for n in SIZES})
-        entries.append(slot * HEAD_ROWS + jnp.where(slot < 12, 0, FIRST_AT - 12 * HEAD_ROWS))
-    for number in range(0, BLOCKS, 2):
-        found = coordinates(number)
-        slot = fold(("y", "z", "x"), {n: (found[n] - mine[n]) % SIZES[n] for n in SIZES})
-        entries.append(slot * TAIL_ROWS + jnp.where(slot < 8, 3 * PART, TAIL_AT - 8 * TAIL_ROWS))
+    for order, start in ((("x", "y"), head_row), (("y",), tail_row)):
+        for number in range(0, BLOCKS, 2):
+            found = coordinates(number)
+            slot = fold(order, {n: (found[n] - mine[n]) % SIZES[n] for n in SIZES})
+            inside = (found["x"] - mine["x"]) % SIZES["x"]
+            entries.append(start(slot, found["z"], inside))
     entries.append(mine["c"])
+    entries.append(mine["z"])
     return jnp.stack([jnp.asarray(entry, jnp.int32) for entry in entries])
 
 
-AT_HEAD, AT_TAIL, TO_HEAD, TO_TAIL, MY_CORE = 0, BLOCKS, 2 * BLOCKS, 2 * BLOCKS + 16, 2 * BLOCKS + 32
+AT_HEAD, AT_TAIL, TO_HEAD, TO_TAIL = 0, BLOCKS, 2 * BLOCKS, 2 * BLOCKS + 16
+MY_CORE, MY_Z = 2 * BLOCKS + 32, 2 * BLOCKS + 33
 
 
 def summed(*parts):
@@ -167,7 +175,7 @@
     return jnp.concatenate([high.astype(BF16), (total - high).astype(BF16)])
 
 
-def scatter_blocks(sends, keeps, dkv_send, dkv_keep, make_input):
+def scatter_blocks(sends, keeps, dkv_send, dkv_keep):
     keep_head, keep_tail, keep_low, keep_mid, keep_far, keep_rest = keeps
     got_head, got_tail = moved(sends[0], "c", 1), moved(sends[1], "c", 1)
     got_head, got_tail, rest_head, rest_tail, dkv_send = together(got_head, got_tail, *sends[2:], dkv_send)
@@ -185,30 +193,26 @@
     tail = summed(keep_rest, got_rest_tail).astype(BF16)
     dkv = summed(dkv_keep, got_dkv).astype(BF16)
     got_hx, got_ty, low, mid, far, tail, dkv, vector = together(got_hx, got_ty, low, mid, far, tail, dkv, vector)
+    place = coordinates(device_number() // inner_count())["z"]
+
+    def part_for(array, shift):
+        return lax.dynamic_slice_in_dim(array, HEAD_ROWS * ((place + shift) % SIZES["z"]), HEAD_ROWS, 0)
+
     vector = summed_vector(vector, got_hx[PART:])
     hy = jnp.concatenate([summed(mid, got_hx[:PART]).astype(BF16), vector])
-    cuts = [slice(HEAD_ROWS * k, HEAD_ROWS * k + HEAD_ROWS) for k in range(4)]
-    tz = [summed(tail[cut], got_ty[cut]).astype(BF16) for cut in cuts]
+    tz = [summed(part_for(tail, s), part_for(got_ty, s)).astype(BF16) for s in range(4)]
     got_hy = moved(hy, "y", 1)
     got_far = moved(far, "x", 1)
     got_tz = [moved(tz[s], "z", s) for s in (1, 2, 3)]
     got_hy, got_far, low, own_tail, vector, dkv, *got_tz = together(got_hy, got_far, low, tz[0], vector, dkv, *got_tz)
     vector = summed_vector(vector, got_hy[PART:])
-    head = [summed(low[cut], got_far[cut], got_hy[cut]) for cut in cuts]
+    head = [summed(part_for(low, s), part_for(got_far, s), part_for(got_hy, s)) for s in range(4)]
     got_hz = [moved(jnp.concatenate([head[s].astype(BF16), vector]), "z", s) for s in (1, 2, 3)]
-    got_dkv = across(dkv[1], 2)
     tx = summed(own_tail[TAIL_ROWS:], *[part[TAIL_ROWS:] for part in got_tz]).astype(BF16)
     own_tail = summed(own_tail[:TAIL_ROWS], *[part[:TAIL_ROWS] for part in got_tz])
-    input_grad = make_input((dkv[0], got_dkv))
-    tx, input_grad = together(tx, input_grad)
-    got_tx, vector = together(moved(tx, "x", 1), vector)
-    place = coordinates(device_number() // inner_count())["z"]
-    stacked = jnp.stack([vector] + [part[HEAD_ROWS:] for part in got_hz])
-    total = sum(
-        summed(found[:VECTOR_ROWS], found[VECTOR_ROWS:])
-        for found in (lax.dynamic_index_in_dim(stacked, (place - z) % 4, 0, keepdims=False) for z in range(4))
-    )
-    return (head[0], *got_hz, own_tail, got_tx), total, input_grad
+    got_tx = moved(tx, "x", 1)
+    got_dkv = across(dkv[1], 2)
+    return (head[0], *got_hz, own_tail, got_tx, vector), (dkv[0], got_dkv)
 
 
 def lower_lanes(shape):
@@ -281,13 +285,33 @@
     )(kind, flat)
 
 
-def flat_kernel(kind_ref, head_ref, one_ref, two_ref, three_ref, tail_ref, other_ref, *refs):
-    kind = kind_ref[0]
-    tiles, narrow, flat_ref = refs[-3:]
+def finish_kernel(table_ref, head_ref, one_ref, two_ref, three_ref, tail_ref, other_ref, mine_ref, *refs):
+    kind, place = table_ref[0], table_ref[1]
+    tiles, narrow, flat_ref, vector_parts = refs[-4:]
+    tokens_ref, gains_ref, w_kv_ref, dq_wq_ref, d_mid_ref, own_dkv, other_dkv = refs[:7]
+    states = refs[7:-4]
     tiles[0:HEAD_ROWS, :] = (head_ref[...] + one_ref[0:HEAD_ROWS, :].astype(F32)) + (
         two_ref[0:HEAD_ROWS, :].astype(F32) + three_ref[0:HEAD_ROWS, :].astype(F32)
     )
     tiles[HEAD_ROWS:BLOCK_ROWS, :] = tail_ref[...] + other_ref[...].astype(F32)
+
+    for at, ref in enumerate((mine_ref, one_ref, two_ref, three_ref)):
+        rows = ref.shape[0]
+        part = ref[rows - 2 * VECTOR_ROWS : rows, :].astype(F32)
+        vector_parts[at] = part[:VECTOR_ROWS] + part[VECTOR_ROWS:]
+    vector = vector_parts[lax.rem(place, 4)]
+    for z in (1, 2, 3):
+        vector = vector + vector_parts[lax.rem(place + 4 - z, 4)]
+
+    lane = lax.broadcasted_iota(jnp.int32, (2 * ROWS, WIDE), 1)
+    x = jnp.where(lane < MODEL_WIDTH, tokens_ref[0].astype(F32).reshape(2 * ROWS, WIDE), 0.0)
+    normed, scale = normed_rows(x)
+    total = summed(own_dkv[...], other_dkv[...]).reshape(2 * ROWS, 384).astype(BF16)
+    d_norm = (dq_wq_ref[...] + times_transposed(total, w_kv_ref[...])) * gains_ref[0:1, :]
+    d_input = d_mid_ref[...] + scale * (d_norm - normed * row_mean(d_norm * normed))
+    out_ref = states[-1]
+    for mb in range(2):
+        out_ref[mb] = d_input[ROWS * mb : ROWS * mb + ROWS].T[0:MODEL_WIDTH].astype(BF16)
 
     @pl.when(kind == 0)
     def _():
@@ -320,35 +344,43 @@
         flat_ref[pl.ds(2, 288, stride=3), :] = jnp.where(low, odd, last)
 
 
-    if len(refs) == 4:
-        refs[0][...] = flat_ref[...]
+    if len(states) == 3:
+        states[0][...], states[1][...] = flat_ref[...], vector
         return
-    weight_ref, first_ref, second_ref, new_weight, new_first, new_second = refs[:6]
+    old_vectors, old_block, new_vectors, new_block = states[0:3], states[3:6], states[6:9], states[9:12]
+    found = adamw(old_vectors[0][...], vector, old_vectors[1][...], old_vectors[2][...], RATE_VECTOR, 0.0)
+    for ref, value in zip(new_vectors, found):
+        ref[...] = value
 
     @pl.loop(0, 6)
     def _(k):
         rows = pl.ds(pl.multiple_of(k * 144, 8), 144)
-        new_weight[rows, :], new_first[rows, :], new_second[rows, :] = adamw(
-            weight_ref[rows, :], flat_ref[rows, :], first_ref[rows, :], second_ref[rows, :], RATE_MATRIX, DECAY
+        found = adamw(
+            old_block[0][rows, :], flat_ref[rows, :], old_block[1][rows, :], old_block[2][rows, :], RATE_MATRIX, DECAY
         )
-
-
-def finish(kind, parts, state):
+        for ref, value in zip(new_block, found):
+            ref[rows, :] = value
+
+
+def finish(table, parts, inputs, state):
     vmem = pl.BlockSpec(memory_space=pltpu.VMEM)
     flat = jax.ShapeDtypeStruct((BLOCK_ROWS, LANES), F32)
-    count = max(1, len(state))
+    vector = jax.ShapeDtypeStruct((VECTOR_ROWS, LANES), F32)
+    shapes = (vector,) * 3 + (flat,) * 3 if state else (flat, vector)
+    shapes += (jax.ShapeDtypeStruct((2, MODEL_WIDTH, ROWS), BF16),)
     return pl.pallas_call(
-        flat_kernel,
-        out_shape=(flat,) * count,
-        in_specs=[pl.BlockSpec(memory_space=pltpu.SMEM)] + [vmem] * (6 + len(state)),
-        out_specs=(vmem,) * count,
+        finish_kernel,
+        out_shape=shapes,
+        in_specs=[pl.BlockSpec(memory_space=pltpu.SMEM)] + [vmem] * (len(parts) + len(inputs) + len(state)),
+        out_specs=(vmem,) * len(shapes),
         scratch_shapes=[
             pltpu.VMEM((BLOCK_ROWS, LANES), F32),
             pltpu.VMEM((HEAD_ROWS, LANES), F32),
             pltpu.VMEM((BLOCK_ROWS, LANES), F32),
+            pltpu.VMEM((4, VECTOR_ROWS, LANES), F32),
         ],
         name="finish",
-    )(kind, *parts, *state)
+    )(table, *parts, *inputs, *state)
 
 
 def product(left, right):
@@ -409,17 +441,24 @@
     (place_q_ref, place_k_ref, gains_ref, bias_q_ref, bias_kv_ref, grad_ref) = refs[19:25]
     block_out_ref, parts_out = refs[25], refs[26:36]
     (dkv_send, dkv_keep, dq_wq_ref, d_mid_ref, w_kv) = refs[36:41]
-    (raw_head, raw_tail, w_q, w_out, w_gate, w_up, w_down, normed_all, hidden_all, keys, values, queries, probs, attended, act_all, block_acc, d_hidden, d_attended, dkv_all, d_query, send_all, keep_all, vector_ref, sems) = refs[41:]
-
-    copies = []
-    for k, part in enumerate(head_parts):
-        copies.append(pltpu.make_async_copy(part, raw_head.at[pl.ds(4 * k, 4)], sems.at[k]))
-    for k, part in enumerate(tail_parts):
-        copies.append(pltpu.make_async_copy(part, raw_tail.at[pl.ds(8 * k, 8)], sems.at[8 + k]))
-    for copy in copies:
+    (raw_head, raw_tail, w_q, w_out, w_gate, w_up, w_down, normed_all, hidden_all, keys, values, queries, probs, attended, act_all, block_acc, d_hidden, d_attended, dkv_all, d_query, send_all, keep_all, vector_ref, outs, sems, out_sems) = refs[41:]
+
+    place = slots[MY_Z]
+
+    def fetches(shift, sem):
+        at = lax.rem(place + shift, 4)
+        copies = []
+        for k, part in enumerate(head_parts):
+            copies.append(pltpu.make_async_copy(part.at[at], raw_head.at[4 * k + at], sems.at[sem + k]))
+        for k, part in enumerate(tail_parts):
+            rows = pl.ds(2 * at, 2)
+            copies.append(pltpu.make_async_copy(part.at[rows], raw_tail.at[pl.ds(8 * k + 2 * at, 2)], sems.at[sem + 8 + k]))
+        return copies
+
+    attention_blocks = fetches(0, 0)
+    other_blocks = fetches(1, 12) + fetches(2, 24) + fetches(3, 36)
+    for copy in attention_blocks + other_blocks:
         copy.start()
-    for copy in copies:
-        copy.wait()
 
     core = slots[MY_CORE]
 
@@ -431,36 +470,6 @@
 
     def tail_tile(block):
         return raw_tail.at[slots[AT_TAIL + block]]
-
-    for ref in (w_q, w_out, w_gate, w_up, w_kv):
-        ref[576:640, :] = jnp.zeros((64, ref.shape[1]), BF16)
-    for k in range(3):
-        place_rows(w_q, head_tile(k), tail_tile(k), 192 * k)
-        place_rows(w_out, head_tile(5 + k), tail_tile(5 + k), 192 * k)
-    for k in range(8):
-        place_rows(w_down, head_tile(24 + k), tail_tile(24 + k), 192 * k)
-    w_kv[0:576, 0:128] = head_tile(3)[...]
-    w_kv[0:576, 128:256] = head_tile(4)[...]
-    rest_key = tail_tile(3)[...].astype(F32)
-    rest_value = tail_tile(4)[...].astype(F32)
-    low = lower_lanes(rest_key.shape)
-    w_kv[0:288, 256:384] = jnp.where(low, rest_key, half_turn(rest_value)).astype(BF16)
-    w_kv[288:576, 256:384] = jnp.where(low, half_turn(rest_key), rest_value).astype(BF16)
-    for ref, base in ((w_gate, 8), (w_up, 16)):
-        for k in range(4):
-            for i in range(6):
-                if i < 4:
-                    even = head_tile(base + 2 * k)[144 * i : 144 * i + 144, :].astype(F32)
-                    odd = head_tile(base + 2 * k + 1)[144 * i : 144 * i + 144, :].astype(F32)
-                else:
-                    even = tail_tile(base + 2 * k)[144 * (i - 4) : 144 * (i - 4) + 144, :].astype(F32)
-                    odd = tail_tile(base + 2 * k + 1)[144 * (i - 4) : 144 * (i - 4) + 144, :].astype(F32)
-                ref[144 * k : 144 * k + 144, 256 * i : 256 * i + 128] = jnp.concatenate(
-                    [even[0:72], odd[0:72]], axis=0
-                ).astype(BF16)
-                ref[144 * k : 144 * k + 144, 256 * i + 128 : 256 * i + 256] = jnp.concatenate(
-                    [even[72:144], odd[72:144]], axis=0
-                ).astype(BF16)
 
     gain_one = gains_ref[0:1, :]
     gain_two = gains_ref[1:2, :]
@@ -475,6 +484,24 @@
             normed, _ = normed_rows(x)
             normed_all[rows, :] = normed
             hidden_all[rows, :] = (normed * gain_one).astype(BF16)
+
+    for copy in attention_blocks:
+        copy.wait()
+    for ref in (w_q, w_out, w_gate, w_up, w_kv):
+        ref[576:640, :] = jnp.zeros((64, ref.shape[1]), BF16)
+    for k in range(3):
+        place_rows(w_q, head_tile(k), tail_tile(k), 192 * k)
+        place_rows(w_out, head_tile(5 + k), tail_tile(5 + k), 192 * k)
+    w_kv[0:576, 0:128] = head_tile(3)[...]
+    w_kv[0:576, 128:256] = head_tile(4)[...]
+    rest_key = tail_tile(3)[...].astype(F32)
+    rest_value = tail_tile(4)[...].astype(F32)
+    low = lower_lanes(rest_key.shape)
+    w_kv[0:288, 256:384] = jnp.where(low, rest_key, half_turn(rest_value)).astype(BF16)
+    w_kv[288:576, 256:384] = jnp.where(low, half_turn(rest_key), rest_value).astype(BF16)
+
+    @pl.loop(0, 2)
+    def _(mb):
         rows = pl.ds(pl.multiple_of(mb * 512, 512), 512)
         pair = product(hidden_all[rows, :], w_kv[...]) + bias_kv_ref[...]
         cosines = jnp.concatenate([at_slot(cos_pair, slot)[mb] for slot in range(4)], axis=0)
@@ -512,24 +539,44 @@
         cosines, sines = cos_pair[0][0, mb], sin_pair[0][0, mb]
         made = product(hidden_all[pl.ds(pl.multiple_of(mb * 512, 512), ROWS), :], w_q[...]) + bias_q_ref[...]
         for k in range(5):
-            queries[rows, LANES * k : LANES * k + LANES] = rope(
-                made[:, LANES * k : LANES * k + LANES], cosines, sines
-            ).astype(BF16)
-        allowed = place_q_ref[mb] >= place_k_ref[mb]
-        allowed = jnp.concatenate([allowed.astype(F32)] * 3, axis=0) > 0.5
+            turned = rope(made[:, LANES * k : LANES * k + LANES], cosines, sines)
+            queries[rows, LANES * k : LANES * k + LANES] = (turned * HEAD_SIZE ** (-0.5)).astype(BF16)
+        masked = jnp.where(place_q_ref[mb] >= place_k_ref[mb], 0.0, MASKED)
+        masked = jnp.concatenate([masked] * 3, axis=0)
         parts = []
         for group in range(KEY_VALUE_HEADS):
             lanes = slice(LANES * group, LANES * group + LANES)
             scores = times_transposed(heads_of(queries, rows, group), keys[key_rows, lanes])
-            scores = jnp.where(allowed, scores * HEAD_SIZE ** (-0.5), MASKED)
+            scores = scores + masked
             top = jnp.max(scores, axis=-1, keepdims=True)
             powers = jnp.exp(scores - top)
             found = powers * (1.0 / jnp.sum(powers, axis=-1, keepdims=True))
             probs[mb, group] = found
             out = product(found.astype(BF16), values[key_rows, lanes])
+            outs[mb, group] = out
             parts += [out[ROWS * k : ROWS * k + ROWS] for k in range(3)]
         for k, tile in enumerate(tiles_of_heads(parts)):
             attended[rows, LANES * k : LANES * k + LANES] = tile.astype(BF16)
+
+    for copy in other_blocks:
+        copy.wait()
+    for k in range(8):
+        place_rows(w_down, head_tile(24 + k), tail_tile(24 + k), 192 * k)
+    for ref, base in ((w_gate, 8), (w_up, 16)):
+        for k in range(4):
+            for i in range(6):
+                if i < 4:
+                    even = head_tile(base + 2 * k)[144 * i : 144 * i + 144, :].astype(F32)
+                    odd = head_tile(base + 2 * k + 1)[144 * i : 144 * i + 144, :].astype(F32)
+                else:
+                    even = tail_tile(base + 2 * k)[144 * (i - 4) : 144 * (i - 4) + 144, :].astype(F32)
+                    odd = tail_tile(base + 2 * k + 1)[144 * (i - 4) : 144 * (i - 4) + 144, :].astype(F32)
+                ref[144 * k : 144 * k + 144, 256 * i : 256 * i + 128] = jnp.concatenate(
+                    [even[0:72], odd[0:72]], axis=0
+                ).astype(BF16)
+                ref[144 * k : 144 * k + 144, 256 * i + 128 : 256 * i + 256] = jnp.concatenate(
+                    [even[72:144], odd[72:144]], axis=0
+                ).astype(BF16)
 
     lane = lax.broadcasted_iota(jnp.int32, (2 * ROWS, WIDE), 1)
     x_own = tokens_pair[0][0].astype(F32).reshape(2 * ROWS, WIDE)
@@ -585,12 +632,33 @@
         made = rows_product(act_all[:, pl.ds(pl.multiple_of(k * 384, 128), 384)], grad_low)
         store_rows(12 + k, tiles_of_rows(made[0:192]), tiles_of_rows(made[192:384]))
 
+    def deliveries(first, count, sem):
+        copies = []
+        for base, outs_of in ((send_all, parts_out[0:4]), (keep_all, parts_out[4:10])):
+            rest = [(outs_of[2], PART * k) for k in range(3)] if len(outs_of) == 4 else [(out, 0) for out in outs_of[2:5]]
+            targets = [(outs_of[0], 0, FIRST_AT), (outs_of[1], 0, TAIL_AT)]
+            targets += [(out, into, PART * k) for k, (out, into) in enumerate(rest)]
+            targets.append((outs_of[-1], 0, 3 * PART))
+            for out, into, start in targets:
+                rows = HEAD_ROWS * count
+                copies.append(
+                    pltpu.make_async_copy(
+                        base.at[pl.ds(start + HEAD_ROWS * first, rows)],
+                        out.at[pl.ds(into + HEAD_ROWS * first, rows)],
+                        out_sems.at[sem + len(copies)],
+                    )
+                )
+        return copies
+
+    early = deliveries(1, 3, 12)
+    for copy in early:
+        copy.start()
+
     for mb in range(2):
         block_out_ref[mb] = block_acc[ROWS * mb : ROWS * mb + ROWS, :].T[0:MODEL_WIDTH].astype(BF16)
 
     d_two = d_hidden[...]
-    vector_ref[...] = jnp.zeros_like(vector_ref)
-    vector_ref[1:2, :] = jnp.sum(d_two * normed_two, axis=0, keepdims=True)
+    gain_two_sum = jnp.sum(d_two * normed_two, axis=0, keepdims=True)
     d_norm = d_two * gain_two
     d_mid = grad_low.astype(F32) + scale_two * (d_norm - normed_two * row_mean(d_norm * normed_two))
     d_mid_ref[...] = d_mid
@@ -611,11 +679,11 @@
             cotangent = heads_of(d_attended, rows, group)
             found = probs[mb, group]
             d_probs = times_transposed(cotangent, values[key_rows, lanes])
-            delta = jnp.sum(found * d_probs, axis=-1, keepdims=True)
+            delta = jnp.sum(outs[mb, group] * cotangent.astype(F32), axis=-1, keepdims=True)
             d_scores = (found * (d_probs - delta)).astype(BF16)
             out = product(d_scores, keys[key_rows, lanes]) * HEAD_SIZE ** (-0.5)
             parts += [out[ROWS * k : ROWS * k + ROWS] for k in range(3)]
-            d_key = rows_product(d_scores, query_rows) * HEAD_SIZE ** (-0.5)
+            d_key = rows_product(d_scores, query_rows)
             d_value = rows_product(found.astype(BF16), cotangent)
             d_keys.append(d_key + half_turn(d_key))
             d_values.append(d_value + half_turn(d_value))
@@ -638,15 +706,14 @@
     d_q = d_query[...]
     dq_wq = times_transposed(d_q, w_q[...])
     dq_wq_ref[...] = dq_wq
-    vector_ref[2:3, :] = jnp.sum(d_q.astype(F32), axis=0, keepdims=True)
-    vector_ref[3:4, 0:384] = jnp.sum(dkv.astype(F32), axis=0, keepdims=True)
+    bias_q_sum = jnp.sum(d_q.astype(F32), axis=0, keepdims=True)
+    bias_kv_sum = jnp.sum(dkv.astype(F32), axis=0, keepdims=True)
     gain_sum = jnp.zeros((1, WIDE), F32)
     for mb in range(2):
         gain_sum += jnp.sum(dq_wq[ROWS * mb : ROWS * mb + ROWS] * normed_all[512 * mb : 512 * mb + ROWS, :], axis=0, keepdims=True)
     for k in range(4):
         part = slice(256 * k, 256 * k + 256)
         gain_sum += jnp.sum(times_transposed(dkv_all[part, :], w_kv[...]) * normed_all[part, :], axis=0, keepdims=True)
-    vector_ref[0:1, :] = gain_sum
 
     hidden_own = jnp.concatenate([hidden_all[0:ROWS, :], hidden_all[512 : 512 + ROWS, :]], axis=0)
     grad_q = rows_product(hidden_own, d_q)
@@ -661,24 +728,35 @@
     store_rows(1, query_tiles[2], key_tiles)
     store_rows(2, value_tiles, out_tiles[0])
     store_rows(3, out_tiles[1], out_tiles[2])
-    vector = jnp.concatenate(
-        [vector_ref[:, LANES * k : LANES * k + LANES] for k in range(5)] + [jnp.zeros((8, LANES), F32)], axis=0
-    )
-    high = vector.astype(BF16)
-    rest = (vector - high.astype(F32)).astype(BF16)
+    def flat_rows(first, second, third, pair):
+        tile = lambda row, k: row[:, LANES * k : LANES * k + LANES]
+        low = lower_lanes((1, LANES))
+        across_two = lambda one, two: jnp.where(low, half_turn(one), half_turn(two))
+        lines = [tile(first, k) for k in range(4)]
+        lines.append(side_by_side(tile(first, 4), tile(second, 0)))
+        lines += [across_two(tile(second, k), tile(second, k + 1)) for k in range(4)]
+        lines += [tile(third, k) for k in range(4)]
+        lines.append(side_by_side(tile(third, 4), tile(pair, 0)))
+        lines.append(across_two(tile(pair, 0), tile(pair, 2)))
+        lines.append(tile(pair, 1))
+        lines.append(jnp.where(low, half_turn(tile(pair, 2)), 0.0))
+        return lines
+
     at = FIRST_AT + PART
+    for row, line in enumerate(flat_rows(gain_sum, gain_two_sum, bias_q_sum, bias_kv_sum)):
+        vector_ref[row : row + 1, :] = line
+    vector_ref[17:24, :] = jnp.zeros((7, LANES), F32)
+    vector = vector_ref[...]
+    high = vector.astype(BF16).astype(F32)
+    both = jnp.concatenate([high, vector - high], axis=0).astype(BF16)
     for ref in (send_all, keep_all):
-        ref[at : at + VECTOR_ROWS, :] = high
-        ref[at + VECTOR_ROWS : at + 2 * VECTOR_ROWS, :] = rest
-    copies = [
-        pltpu.make_async_copy(ref.at[pl.ds(first, count)], out, sems.at[k])
-        for k, (ref, out, (first, count)) in enumerate(
-            zip([send_all] * 4 + [keep_all] * 6, parts_out, SEND_PARTS + KEEP_PARTS)
-        )
-    ]
-    for copy in copies:
+        ref[at : at + 2 * VECTOR_ROWS, :] = both
+    last = deliveries(0, 1, 0)
+    last.append(pltpu.make_async_copy(send_all.at[pl.ds(at, 2 * VECTOR_ROWS)], parts_out[0].at[pl.ds(PART, 2 * VECTOR_ROWS)], out_sems.at[24]))
+    last.append(pltpu.make_async_copy(keep_all.at[pl.ds(at, 2 * VECTOR_ROWS)], parts_out[4].at[pl.ds(PART, 2 * VECTOR_ROWS)], out_sems.at[25]))
+    for copy in last:
         copy.start()
-    for copy in copies:
+    for copy in early + last:
         copy.wait()
 
 
@@ -709,7 +787,8 @@
         ((256, WIDE), BF16),
         ((ALL_ROWS, LANES), BF16),
         ((ALL_ROWS, LANES), BF16),
-        ((8, WIDE), F32),
+        ((VECTOR_ROWS, LANES), F32),
+        ((2, 3, 384, LANES), F32),
     ]
     return pl.pallas_call(
         layer_kernel,
@@ -725,33 +804,10 @@
         in_specs=[pl.BlockSpec(memory_space=pltpu.SMEM)] + [anywhere] * 12 + [vmem] * 12,
         out_specs=(vmem,) + (anywhere,) * 10 + (vmem,) * 5,
         scratch_shapes=[pltpu.VMEM(dims, kind) for dims, kind in scratch]
-        + [pltpu.SemaphoreType.DMA((12,))],
+        + [pltpu.SemaphoreType.DMA((48,)), pltpu.SemaphoreType.DMA((26,))],
         compiler_params=pltpu.CompilerParams(vmem_limit_bytes=50 * 1024 * 1024),
         name="layer",
     )(slots, *heads, *tails, *others)
-
-
-def input_kernel(tokens_ref, gains_ref, w_kv_ref, dq_wq_ref, d_mid_ref, own_ref, other_ref, out_ref):
-    lane = lax.broadcasted_iota(jnp.int32, (2 * ROWS, WIDE), 1)
-    x = jnp.where(lane < MODEL_WIDTH, tokens_ref[0].astype(F32).reshape(2 * ROWS, WIDE), 0.0)
-    normed, scale = normed_rows(x)
-    total = summed(own_ref[...], other_ref[...])
-    total = total.reshape(2 * ROWS, 384).astype(BF16)
-    d_norm = (dq_wq_ref[...] + times_transposed(total, w_kv_ref[...])) * gains_ref[0:1, :]
-    d_input = d_mid_ref[...] + scale * (d_norm - normed * row_mean(d_norm * normed))
-    for mb in range(2):
-        out_ref[mb] = d_input[ROWS * mb : ROWS * mb + ROWS].T[0:MODEL_WIDTH].astype(BF16)
-
-
-def run_input(tokens, gains, w_kv, dq_wq, d_mid, parts):
-    return pl.pallas_call(
-        input_kernel,
-        out_shape=jax.ShapeDtypeStruct((2, MODEL_WIDTH, ROWS), BF16),
-        in_specs=[pl.BlockSpec(memory_space=pltpu.VMEM)] * 7,
-        out_specs=pl.BlockSpec(memory_space=pltpu.VMEM),
-        cost_estimate=pl.CostEstimate(flops=3_500_000_000, bytes_accessed=6_000_000, transcendentals=0),
-        name="input_grad",
-    )(tokens, gains, w_kv, dq_wq, d_mid, *parts)
 
 
 def adamw(param, grad, mom_one, mom_two, rate, decay):
@@ -807,9 +863,15 @@
     bias_q = jnp.pad(vectors[2 * MODEL_WIDTH : 3 * MODEL_WIDTH].reshape(1, MODEL_WIDTH), padding)
     bias_kv = bias_tiles(vectors[1728:1920], vectors[1920:2112]).reshape(1, 384)
     grad = jnp.pad(out_grad.reshape(2 * ROWS, MODEL_WIDTH), padding)
-    others = (slot_table(), gains, bias_q, bias_kv, grad)
+    spare = VECTOR_ROWS * LANES - vectors.shape[0]
+    vector_state = [
+        jnp.pad(array, (0, spare), constant_values=1.0).reshape(VECTOR_ROWS, LANES)
+        for array in (vectors, vector_first, vector_second)
+    ]
+    table = jnp.concatenate([kind, (coordinates(device_number() // inner_count())["z"]).astype(jnp.int32).reshape(1)])
+    others = (slot_table(), gains, bias_q, bias_kv, grad, vector_state, table)
     heads, tails, (near, far), (cosines, sines), others = gather_all(head, tail, packed, others)
-    slots, gains, bias_q, bias_kv, grad = others
+    slots, gains, bias_q, bias_kv, grad, vector_state, table = others
     cosines_far, sines_far = place_tables(far)
     place_all = jnp.stack([places_of(near), places_of(far)], axis=1)
     place_q = place_all[0, 0][..., None]
@@ -820,46 +882,28 @@
     )
     sends, keeps = found[:4], found[4:10]
     dkv_send, dkv_keep, dq_wq, d_mid, w_kv = found[10:]
-    make_input = lambda parts: run_input(near, gains, w_kv, dq_wq, d_mid, parts)
-    parts, vector, input_grad = scatter_blocks(sends, keeps, dkv_send, dkv_keep, make_input)
+    parts, pairs = scatter_blocks(sends, keeps, dkv_send, dkv_keep)
+    inputs = (near, gains, w_kv, dq_wq, d_mid, *pairs)
     state = (weights, first_moment, second_moment)
     if inner_count() == 1:
-        updated = finish(kind, parts, [array.reshape(BLOCK_ROWS, LANES) for array in state])
-        new_weights, new_first, new_second = [array.reshape(-1) for array in updated]
+        blocks = [array.reshape(BLOCK_ROWS, LANES) for array in state]
+        *updated, input_grad = finish(table, parts, inputs, [*vector_state, *blocks])
+        new_vector_state = [array.reshape(-1)[: vectors.shape[0]] for array in updated[:3]]
+        new_state = [array.reshape(-1) for array in updated[3:]]
     else:
+        block_grad, vector, input_grad = finish(table, parts, inputs, [])
         vector = lax.psum(vector, "ctx")
         vector = lax.psum(vector, "dp", axis_index_groups=inner_groups())
-        (block_grad,) = finish(kind, parts, [])
         grad_own = own_slice(block_grad.reshape(-1))
-        new_weights, new_first, new_second = adamw(
-            weights, grad_own, first_moment, second_moment, RATE_MATRIX, DECAY
-        )
-    vector = jnp.transpose(vector.reshape(6, 8, LANES), (1, 0, 2)).reshape(8, 6 * LANES)
-    pair = vector[3]
-    vector_grad = jnp.concatenate(
-        [
-            vector[0, :MODEL_WIDTH],
-            vector[1, :MODEL_WIDTH],
-            vector[2, :MODEL_WIDTH],
-            pair[0:128],
-            pair[256:320],
-            pair[128:256],
-            pair[320:384],
-        ]
-    )
-    new_vectors, new_vector_first, new_vector_second = adamw(
-        vectors, vector_grad, vector_first, vector_second, RATE_VECTOR, 0.0
-    )
+        vector_grad = vector.reshape(-1)[: vectors.shape[0]]
+        new_state = adamw(weights, grad_own, first_moment, second_moment, RATE_MATRIX, DECAY)
+        new_vector_state = adamw(vectors, vector_grad, vector_first, vector_second, RATE_VECTOR, 0.0)
     shape = tokens_in.shape
     return (
         jnp.transpose(block_out, (0, 2, 1)).reshape(shape),
         jnp.transpose(input_grad, (0, 2, 1)).reshape(shape),
-        new_weights,
-        new_first,
-        new_second,
-        new_vectors,
-        new_vector_first,
-        new_vector_second,
+        *new_state,
+        *new_vector_state,
     )
 
 

time: 166 us -> 151 us (0.910)
  waiting for transfers between devices: 68 us -> 54.5 us
  Pallas kernels: 40 us -> 35.5 us
  local copies, waits for them, and re-layouts: 5.87 us -> 8.44 us
    ppermute x32, waiting for transfers between devices: 68 us -> 46.2 us  [moved(): return lax.ppermute(buffer, ('dp', 'ctx'), pairs)]
    ppermute x4, waiting for transfers between devices: 0.01 us -> 8.36 us  [across(): lax.ppermute(buffer, 'ctx', [(i, i ^ distance) for i in range(count)])]
    pallas_call x1, Pallas kernels: 31.6 us -> 28.6 us  [run_layer(): pl.pallas_call(layer_kernel, out_shape=(shape((2, MODEL_WIDTH, ROWS), BF1...]
    convert_element_type x1 -> x2, other arithmetic: 0.86 us -> 2.71 us  [the longest x1 1.99 us: scatter_blocks(): summed(part_for(tail, s), part_for(got_ty, s)).astype(BF16)]
    add x1 -> x0, other arithmetic: 1.8 us -> none  [summed(): total = total + part.astype(F32)]
    ppermute x4, starting transfers between devices: 3.49 us -> 1.75 us  [across(): lax.ppermute(buffer, 'ctx', [(i, i ^ distance) for i in range(count)])]
    unnamed x72 -> x80, local copies, waits for them, and re-layouts: 2.29 us -> 3.86 us
    pallas_call x2 -> x1, Pallas kernels: 6.52 us -> 5.05 us  [finish(): pl.pallas_call(finish_kernel, out_shape=shapes, in_specs=[pl.BlockSpec(me...]
  transfers between devices with their start and end apart: 36 -> 36, of which waited for: 18 -> 18; matrix products, arithmetic and copies ran while one was open for 8% -> 9% of each run, Pallas kernels for 2% -> 0%
where the time goes in v6:
time: 151 us; the launch traced here: 150 us
  waiting for transfers between devices  54.5 us (36%)
  starting transfers between devices  36.7 us (24%)
  Pallas kernels  35.5 us (24%)
  other arithmetic  12.7 us (8%)
  local copies, waits for them, and re-layouts  8.44 us (6%)
  between operations  1.88 us (1%)
    ppermute x32, waiting for transfers between devices, moved(): return lax.ppermute(buffer, ('dp', 'ctx'), pairs)  46.2 us
    ppermute x32, starting transfers between devices, moved(): return lax.ppermute(buffer, ('dp', 'ctx'), pairs)  34.9 us
    pallas_call x1, Pallas kernels, run_layer(): pl.pallas_call(layer_kernel, out_shape=(shape((2, MODEL_WIDTH, ROWS), BF1...  28.6 us
    ppermute x4, waiting for transfers between devices, across(): lax.ppermute(buffer, 'ctx', [(i, i ^ distance) for i in range(count)])  8.36 us
    pallas_call x1, Pallas kernels, finish(): pl.pallas_call(finish_kernel, out_shape=shapes, in_specs=[pl.BlockSpec(me...  5.05 us
    unnamed x80, local copies, waits for them, and re-layouts  3.86 us
  transfers between devices with their start and end apart: 36, of which 18 were waited for; matrix products, arithmetic and copies ran while one was open for 9% of the time, Pallas kernels for 0%

profile of v6, /device:TPU:0, one launch (start us, length us, event | category | flops | bytes accessed | tf_op | source)
XLA Modules:
  0.0 149.7 jit_solution(16998111096973639347)
XLA Ops:
  0.7 1.9 %to_tiles.1 = (bf16[576,128]{1,0:T(8,128)(2,1)}, bf16[288,128]{1,0:T(8,128)(2,1)}) custom-call(s32[1]{0:T(128)} %bitcast.kind_ref, f32[864,128]{1,0:T(8,128)} %bitcast.154), custom_call_target="tpu_custom_call" | custom-call | tf_op jit(solution)/shard_map/to_tiles/pallas_call | solution.py:269
  2.5 2.9 %collective-permute-start.2 = (bf16[576,128]{1,0:T(8,128)(2,1)}, bf16[576,128]{1,0:T(8,128)(2,1)S(1)}, u32[]{:S(2)}, u32[]{:S(2)}) collective-permute-start(bf16[576,128]{1,0:T(8,128)(2,1)} %get-tuple-element.98), channel_id=1, source_target_pairs={{0,8},{1,9},{2,10},{3,11},{4,12},{5,13},{6,14},{7,15},{8,16},{9,17... | collective-permute-start | bytes 442376 | tf_op jit(solution)/shard_map/ppermute | solution.py:75
  5.4 2.7 %collective-permute-start.3 = (bf16[576,128]{1,0:T(8,128)(2,1)}, bf16[576,128]{1,0:T(8,128)(2,1)S(1)}, u32[]{:S(2)}, u32[]{:S(2)}) collective-permute-start(bf16[576,128]{1,0:T(8,128)(2,1)} %get-tuple-element.98), channel_id=1, source_target_pairs={{0,16},{1,17},{2,18},{3,19},{4,20},{5,21},{6,22},{7,23},{8,24},{9,... | collective-permute-start | bytes 442376 | tf_op jit(solution)/shard_map/ppermute | solution.py:75
  8.1 1.2 collective-permute-start.4
  9.4 1.5 collective-permute-start
  11.8 1.2 copy.39
  18.0 3.6 %collective-permute-done.1 = bf16[2,128,640]{2,1,0:T(8,128)(2,1)S(1)} collective-permute-done((bf16[2,128,640]{2,1,0:T(8,128)(2,1)S(1)}, bf16[2,128,640]{2,1,0:T(8,128)(2,1)S(1)}, u32[]{:S(2)}, u32[]{:S(2)}) %collective-permute-start.1) | collective-permute-done | bytes 327712 | tf_op jit(solution)/shard_map/ppermute | solution.py:80
  21.7 1.6 %collective-permute-start.5 = (bf16[4,576,128]{2,1,0:T(8,128)(2,1)S(1)}, bf16[4,576,128]{2,1,0:T(8,128)(2,1)S(1)}, u32[]{:S(2)}, u32[]{:S(2)}) collective-permute-start(bf16[4,576,128]{2,1,0:T(8,128)(2,1)S(1)} %pad_maximum_fusion.3.refs_1_), channel_id=1, source_target_pairs={{0,4},{1,5},{2,6},{3,7},{4,0},{5,1},{6,2},{7,3},{8,12},{9,13},{10,... | collective-permute-start | bytes 1769480 | tf_op jit(solution)/shard_map/ppermute | solution.py:75
  25.0 1.4 collective-permute-start.8
  26.4 1.6 %collective-permute-start.9 = (bf16[2,288,128]{2,1,0:T(8,128)(2,1)S(1)}, bf16[2,288,128]{2,1,0:T(8,128)(2,1)S(1)}, u32[]{:S(2)}, u32[]{:S(2)}) collective-permute-start(bf16[2,288,128]{2,1,0:T(8,128)(2,1)S(1)} %pad_maximum_fusion.10), channel_id=1, source_target_pairs={{0,24},{1,25},{2,26},{3,27},{4,28},{5,29},{6,30},{7,31},{8,0},{9,1... | collective-permute-start | bytes 442376 | tf_op jit(solution)/shard_map/ppermute | solution.py:75
  29.5 3.0 %collective-permute-done.7 = bf16[2,288,128]{2,1,0:T(8,128)(2,1)S(1)} collective-permute-done((bf16[2,288,128]{2,1,0:T(8,128)(2,1)S(1)}, bf16[2,288,128]{2,1,0:T(8,128)(2,1)S(1)}, u32[]{:S(2)}, u32[]{:S(2)}) %collective-permute-start.7) | collective-permute-done | bytes 147488 | tf_op jit(solution)/shard_map/ppermute | solution.py:75
  32.5 3.3 %collective-permute-done.8 = bf16[2,288,128]{2,1,0:T(8,128)(2,1)S(1)} collective-permute-done((bf16[2,288,128]{2,1,0:T(8,128)(2,1)S(1)}, bf16[2,288,128]{2,1,0:T(8,128)(2,1)S(1)}, u32[]{:S(2)}, u32[]{:S(2)}) %collective-permute-start.8) | collective-permute-done | bytes 147488 | tf_op jit(solution)/shard_map/ppermute | solution.py:75
  36.0 1.1 collective-permute-start.10
  38.4 12.5 %collective-permute-done.10.refs_4_ = bf16[4,576,128]{2,1,0:T(8,128)(2,1)S(1)} collective-permute-done((bf16[4,576,128]{2,1,0:T(8,128)(2,1)S(1)}, bf16[4,576,128]{2,1,0:T(8,128)(2,1)S(1)}, u32[]{:S(2)}, u32[]{:S(2)}) %collective-permute-start.10) | collective-permute-done | bytes 589856 | tf_op jit(solution)/shard_map/ppermute | solution.py:75
  57.5 28.6 %layer.1 = (bf16[2,576,128]{2,1,0:T(8,128)(2,1)}, bf16[2352,128]{1,0:T(8,128)(2,1)}, bf16[2304,128]{1,0:T(8,128)(2,1)S(1)}, bf16[6912,128]{1,0:T(8,128)(2,1)}, b...) custom-call(s32[98]{0:T(128)S(1)} %stack.448.refs_0_, ...), custom_call_target="tpu_custom_call" | custom-call | tf_op jit(solution)/shard_map/layer/pallas_call | solution.py:793
  86.7 2.4 %collective-permute-done.20 = bf16[2304,128]{1,0:T(8,128)(2,1)S(1)} collective-permute-done((bf16[2304,128]{1,0:T(8,128)(2,1)S(1)}, bf16[2304,128]{1,0:T(8,128)(2,1)S(1)}, u32[]{:S(2)}, u32[]{:S(2)}) %collective-permute-start.20) | collective-permute-done | bytes 589856 | tf_op jit(solution)/shard_map/ppermute | solution.py:75
  89.8 1.4 add_convert_fusion.6
  91.3 1.2 collective-permute-start.21
  93.7 3.9 %collective-permute-done.25 = bf16[2,2,128,384]{3,2,1,0:T(8,128)(2,1)S(1)} collective-permute-done((bf16[2,2,128,384]{3,2,1,0:T(8,128)(2,1)S(1)}, bf16[2,2,128,384]{3,2,1,0:T(8,128)(2,1)S(1)}, u32[]{:S(2)}, u32[]{:S(2)}) %collective-permute-start.25) | collective-permute-done | bytes 393248 | tf_op jit(solution)/shard_map/ppermute | solution.py:80
  99.1 1.3 add_convert_fusion.2
  100.3 8.6 %collective-permute-done.22 = bf16[2304,128]{1,0:T(8,128)(2,1)S(1)} collective-permute-done((bf16[2304,128]{1,0:T(8,128)(2,1)S(1)}, bf16[2304,128]{1,0:T(8,128)(2,1)S(1)}, u32[]{:S(2)}, u32[]{:S(2)}) %collective-permute-start.22) | collective-permute-done | bytes 589856 | tf_op jit(solution)/shard_map/ppermute | solution.py:75
  110.6 2.0 %add_convert_fusion.11 = (bf16[576,128]{1,0:T(8,128)(2,1)}, bf16[576,128]{1,0:T(8,128)(2,1)}, bf16[576,128]{1,0:T(8,128)(2,1)}, bf16[576,128]{1,0:T(8,128)(2,1)S(1)}) fusion(bf16[2304,128]{1,0:T(8,128)(2,1)} %copy-done.18, s32[]{:T(128)S(6)} %select_n.938, bf16[2304,128]{1,0:T(8,128)(2,1)S(1)} %add_convert_fusion.1, s32[]{:T(128)S(6)} %select_n.936, ...), kind=kLoop, calls=%fused_computation.23 | loop fusion | flops 1179648 | bytes 1769488 | tf_op jit(solution)/shard_map/convert_element_type | solution.py:203
  112.6 3.7 %collective-permute-start.28 = (bf16[576,128]{1,0:T(8,128)(2,1)}, bf16[576,128]{1,0:T(8,128)(2,1)S(1)}, u32[]{:S(2)}, u32[]{:S(2)}) collective-permute-start(bf16[576,128]{1,0:T(8,128)(2,1)} %get-tuple-element.213), channel_id=1, source_target_pairs={{0,8},{1,9},{2,10},{3,11},{4,12},{5,13},{6,14},{7,15},{8,16},{9,17... | collective-permute-start | bytes 442376 | tf_op jit(solution)/shard_map/ppermute | solution.py:75
  116.4 2.4 %collective-permute-start.30 = (bf16[576,128]{1,0:T(8,128)(2,1)}, bf16[576,128]{1,0:T(8,128)(2,1)S(1)}, u32[]{:S(2)}, u32[]{:S(2)}) collective-permute-start(bf16[576,128]{1,0:T(8,128)(2,1)} %get-tuple-element.211), channel_id=1, source_target_pairs={{0,24},{1,25},{2,26},{3,27},{4,28},{5,29},{6,30},{7,31},{8,0},{9,1... | collective-permute-start | bytes 442376 | tf_op jit(solution)/shard_map/ppermute | solution.py:75
  118.7 2.3 %collective-permute-done.28 = bf16[576,128]{1,0:T(8,128)(2,1)S(1)} collective-permute-done((bf16[576,128]{1,0:T(8,128)(2,1)}, bf16[576,128]{1,0:T(8,128)(2,1)S(1)}, u32[]{:S(2)}, u32[]{:S(2)}) %collective-permute-start.28) | collective-permute-done | bytes 147488 | tf_op jit(solution)/shard_map/ppermute | solution.py:75
  121.0 5.3 %collective-permute-done.29 = bf16[576,128]{1,0:T(8,128)(2,1)S(1)} collective-permute-done((bf16[576,128]{1,0:T(8,128)(2,1)}, bf16[576,128]{1,0:T(8,128)(2,1)S(1)}, u32[]{:S(2)}, u32[]{:S(2)}) %collective-permute-start.29) | collective-permute-done | bytes 147488 | tf_op jit(solution)/shard_map/ppermute | solution.py:75
  128.0 3.6 %collective-permute-start.31 = (bf16[624,128]{1,0:T(8,128)(2,1)S(1)}, bf16[624,128]{1,0:T(8,128)(2,1)S(1)}, u32[]{:S(2)}, u32[]{:S(2)}) collective-permute-start(bf16[624,128]{1,0:T(8,128)(2,1)S(1)} %get-tuple-element.227), channel_id=1, source_target_pairs={{0,8},{1,9},{2,10},{3,11},{4,12},{5,13},{6,14},{7,15},{8,16},{9,17... | collective-permute-start | bytes 479240 | tf_op jit(solution)/shard_map/ppermute | solution.py:75
  131.6 2.6 %collective-permute-start.32 = (bf16[624,128]{1,0:T(8,128)(2,1)S(1)}, bf16[624,128]{1,0:T(8,128)(2,1)S(1)}, u32[]{:S(2)}, u32[]{:S(2)}) collective-permute-start(bf16[624,128]{1,0:T(8,128)(2,1)S(1)} %get-tuple-element.226), channel_id=1, source_target_pairs={{0,16},{1,17},{2,18},{3,19},{4,20},{5,21},{6,22},{7,23},{8,24},{9,... | collective-permute-start | bytes 479240 | tf_op jit(solution)/shard_map/ppermute | solution.py:75
  134.9 1.1 collective-permute-start.35
  138.3 4.3 %collective-permute-done.34.other_ref = bf16[288,128]{1,0:T(8,128)(2,1)S(1)} collective-permute-done((bf16[288,128]{1,0:T(8,128)(2,1)S(1)}, bf16[288,128]{1,0:T(8,128)(2,1)S(1)}, u32[]{:S(2)}, u32[]{:S(2)}) %collective-permute-start.34) | collective-permute-done | bytes 73760 | tf_op jit(solution)/shard_map/ppermute | solution.py:75
  142.6 1.1 collective-permute-done.32.two_ref
  144.5 5.1 %finish.1 = (f32[24,128]{1,0:T(8,128)}, f32[24,128]{1,0:T(8,128)}, f32[24,128]{1,0:T(8,128)}, f32[864,128]{1,0:T(8,128)}, f32[864,128]{1,0:T(8,128)}, /*index=5*/f32[864,128]{1,0:T(8,128)}, bf16[2,576,128]{2,1,0:T(8,128)(2,1)}) custom-call(s32[2]{0:T(128)} %pad_add_fusion.table_ref, f32[576,128]{1,0:T(8,128)} %get-tuple-element.205.head_ref, ...), custom_call_target="tpu_custom_call" | custom-call | tf_op jit(solution)/shard_map/finish/pallas_call | solution.py:371
  (185 shorter events, 27.8 us)
Async XLA Ops:
  2.5 14.7 %collective-permute-start.2 = (bf16[576,128]{1,0:T(8,128)(2,1)}, bf16[576,128]{1,0:T(8,128)(2,1)S(1)}, u32[]{:S(2)}, u32[]{:S(2)}) collective-permute-start(bf16[576,128]{1,0:T(8,128)(2,1)} %get-tuple-element.98), channel_id=1, source_target_pairs={{0,8},{1,9},{2,10},{3,11},{4,12},{5,13},{6,14},{7,15},{8,16},{9,17... | collective-permute-start | bytes 442376 | tf_op jit(solution)/shard_map/ppermute | solution.py:75
  5.4 12.6 %collective-permute-start.3 = (bf16[576,128]{1,0:T(8,128)(2,1)}, bf16[576,128]{1,0:T(8,128)(2,1)S(1)}, u32[]{:S(2)}, u32[]{:S(2)}) collective-permute-start(bf16[576,128]{1,0:T(8,128)(2,1)} %get-tuple-element.98), channel_id=1, source_target_pairs={{0,16},{1,17},{2,18},{3,19},{4,20},{5,21},{6,22},{7,23},{8,24},{9,... | collective-permute-start | bytes 442376 | tf_op jit(solution)/shard_map/ppermute | solution.py:75
  8.1 9.9 %collective-permute-start.4 = (bf16[576,128]{1,0:T(8,128)(2,1)}, bf16[576,128]{1,0:T(8,128)(2,1)S(1)}, u32[]{:S(2)}, u32[]{:S(2)}) collective-permute-start(bf16[576,128]{1,0:T(8,128)(2,1)} %get-tuple-element.98), channel_id=1, source_target_pairs={{0,24},{1,25},{2,26},{3,27},{4,28},{5,29},{6,30},{7,31},{8,0},{9,1... | collective-permute-start | bytes 442376 | tf_op jit(solution)/shard_map/ppermute | solution.py:75
  9.4 7.9 %collective-permute-start = (bf16[288,128]{1,0:T(8,128)(2,1)}, bf16[288,128]{1,0:T(8,128)(2,1)S(1)}, u32[]{:S(2)}, u32[]{:S(2)}) collective-permute-start(bf16[288,128]{1,0:T(8,128)(2,1)} %get-tuple-element.102), channel_id=1, source_target_pairs={{0,2},{1,3},{2,0},{3,1},{4,6},{5,7},{6,4},{7,5},{8,10},{9,11},{10,... | collective-permute-start | bytes 221192 | tf_op jit(solution)/shard_map/ppermute | solution.py:75
  13.2 8.4 %collective-permute-start.1 = (bf16[2,128,640]{2,1,0:T(8,128)(2,1)S(1)}, bf16[2,128,640]{2,1,0:T(8,128)(2,1)S(1)}, u32[]{:S(2)}, u32[]{:S(2)}) collective-permute-start(bf16[2,128,640]{2,1,0:T(8,128)(2,1)S(1)} %maximum_maximum_fusion), channel_id=1, source_target_pairs={{0,2},{1,3},{2,0},{3,1},{4,6},{5,7},{6,4},{7,5},{8,10},{9,11},{10,... | collective-permute-start | bytes 983048 | tf_op jit(solution)/shard_map/ppermute | solution.py:80
  21.7 14.1 %collective-permute-start.5 = (bf16[4,576,128]{2,1,0:T(8,128)(2,1)S(1)}, bf16[4,576,128]{2,1,0:T(8,128)(2,1)S(1)}, u32[]{:S(2)}, u32[]{:S(2)}) collective-permute-start(bf16[4,576,128]{2,1,0:T(8,128)(2,1)S(1)} %pad_maximum_fusion.3.refs_1_), channel_id=1, source_target_pairs={{0,4},{1,5},{2,6},{3,7},{4,0},{5,1},{6,2},{7,3},{8,12},{9,13},{10,... | collective-permute-start | bytes 1769480 | tf_op jit(solution)/shard_map/ppermute | solution.py:75
  23.3 12.7 %collective-permute-start.6 = (bf16[4,576,128]{2,1,0:T(8,128)(2,1)S(1)}, bf16[4,576,128]{2,1,0:T(8,128)(2,1)S(1)}, u32[]{:S(2)}, u32[]{:S(2)}) collective-permute-start(bf16[4,576,128]{2,1,0:T(8,128)(2,1)S(1)} %pad_maximum_fusion.3.refs_1_), channel_id=1, source_target_pairs={{0,2},{1,3},{2,0},{3,1},{4,6},{5,7},{6,4},{7,5},{8,10},{9,11},{10,... | collective-permute-start | bytes 1769480 | tf_op jit(solution)/shard_map/ppermute | solution.py:75
  24.1 8.4 %collective-permute-start.7 = (bf16[2,288,128]{2,1,0:T(8,128)(2,1)S(1)}, bf16[2,288,128]{2,1,0:T(8,128)(2,1)S(1)}, u32[]{:S(2)}, u32[]{:S(2)}) collective-permute-start(bf16[2,288,128]{2,1,0:T(8,128)(2,1)S(1)} %pad_maximum_fusion.10), channel_id=1, source_target_pairs={{0,8},{1,9},{2,10},{3,11},{4,12},{5,13},{6,14},{7,15},{8,16},{9,17... | collective-permute-start | bytes 442376 | tf_op jit(solution)/shard_map/ppermute | solution.py:75
  25.0 10.8 %collective-permute-start.8 = (bf16[2,288,128]{2,1,0:T(8,128)(2,1)S(1)}, bf16[2,288,128]{2,1,0:T(8,128)(2,1)S(1)}, u32[]{:S(2)}, u32[]{:S(2)}) collective-permute-start(bf16[2,288,128]{2,1,0:T(8,128)(2,1)S(1)} %pad_maximum_fusion.10), channel_id=1, source_target_pairs={{0,16},{1,17},{2,18},{3,19},{4,20},{5,21},{6,22},{7,23},{8,24},{9,... | collective-permute-start | bytes 442376 | tf_op jit(solution)/shard_map/ppermute | solution.py:75
  26.4 9.4 %collective-permute-start.9 = (bf16[2,288,128]{2,1,0:T(8,128)(2,1)S(1)}, bf16[2,288,128]{2,1,0:T(8,128)(2,1)S(1)}, u32[]{:S(2)}, u32[]{:S(2)}) collective-permute-start(bf16[2,288,128]{2,1,0:T(8,128)(2,1)S(1)} %pad_maximum_fusion.10), channel_id=1, source_target_pairs={{0,24},{1,25},{2,26},{3,27},{4,28},{5,29},{6,30},{7,31},{8,0},{9,1... | collective-permute-start | bytes 442376 | tf_op jit(solution)/shard_map/ppermute | solution.py:75
  36.0 14.8 %collective-permute-start.10 = (bf16[4,576,128]{2,1,0:T(8,128)(2,1)S(1)}, bf16[4,576,128]{2,1,0:T(8,128)(2,1)S(1)}, u32[]{:S(2)}, u32[]{:S(2)}) collective-permute-start(bf16[4,576,128]{2,1,0:T(8,128)(2,1)S(1)} %collective-permute-done.5.refs_2_), channel_id=1, source_target_pairs={{0,2},{1,3},{2,0},{3,1},{4,6},{5,7},{6,4},{7,5},{8,10},{9,11},{10,... | collective-permute-start | bytes 1769480 | tf_op jit(solution)/shard_map/ppermute | solution.py:75
  37.3 14.0 %collective-permute-start.11 = (bf16[8,288,128]{2,1,0:T(8,128)(2,1)S(1)}, bf16[8,288,128]{2,1,0:T(8,128)(2,1)S(1)}, u32[]{:S(2)}, u32[]{:S(2)}) collective-permute-start(bf16[8,288,128]{2,1,0:T(8,128)(2,1)S(1)} %constant_dynamic-update-slice_fusion.refs_9_), channel_id=1, source_target_pairs={{0,4},{1,5},{2,6},{3,7},{4,0},{5,1},{6,2},{7,3},{8,12},{9,13},{10,... | collective-permute-start | bytes 1769480 | tf_op jit(solution)/shard_map/ppermute | solution.py:75
  37.9 14.0 %collective-permute-start.13 = (bf16[4,576,128]{2,1,0:T(8,128)(2,1)S(1)}, bf16[4,576,128]{2,1,0:T(8,128)(2,1)S(1)}, u32[]{:S(2)}, u32[]{:S(2)}) collective-permute-start(bf16[4,576,128]{2,1,0:T(8,128)(2,1)S(1)} %collective-permute-done.5.refs_2_), channel_id=1, source_target_pairs={{0,1},{1,0},{2,3},{3,2},{4,5},{5,4},{6,7},{7,6},{8,9},{9,8},{10,11... | collective-permute-start | bytes 1769480 | tf_op jit(solution)/shard_map/ppermute | solution.py:75
  37.9 15.0 %collective-permute-start.15 = (bf16[8,288,128]{2,1,0:T(8,128)(2,1)S(1)}, bf16[8,288,128]{2,1,0:T(8,128)(2,1)S(1)}, u32[]{:S(2)}, u32[]{:S(2)}) collective-permute-start(bf16[8,288,128]{2,1,0:T(8,128)(2,1)S(1)} %constant_dynamic-update-slice_fusion.refs_9_), channel_id=1, source_target_pairs={{0,1},{1,0},{2,3},{3,2},{4,5},{5,4},{6,7},{7,6},{8,9},{9,8},{10,11... | collective-permute-start | bytes 1769480 | tf_op jit(solution)/shard_map/ppermute | solution.py:75
  38.4 13.4 %collective-permute-start.12 = (bf16[4,576,128]{2,1,0:T(8,128)(2,1)S(1)}, bf16[4,576,128]{2,1,0:T(8,128)(2,1)S(1)}, u32[]{:S(2)}, u32[]{:S(2)}) collective-permute-start(bf16[4,576,128]{2,1,0:T(8,128)(2,1)S(1)} %pad_maximum_fusion.3.refs_1_), channel_id=1, source_target_pairs={{0,1},{1,0},{2,3},{3,2},{4,5},{5,4},{6,7},{7,6},{8,9},{9,8},{10,11... | collective-permute-start | bytes 1769480 | tf_op jit(solution)/shard_map/ppermute | solution.py:75
  86.1 2.9 %collective-permute-start.19 = (bf16[2352,128]{1,0:T(8,128)(2,1)}, bf16[2352,128]{1,0:T(8,128)(2,1)S(1)}, u32[]{:S(2)}, u32[]{:S(2)}) collective-permute-start(bf16[2352,128]{1,0:T(8,128)(2,1)} %get-tuple-element.130), channel_id=1, source_target_pairs={{0,1},{1,0},{2,3},{3,2},{4,5},{5,4},{6,7},{7,6},{8,9},{9,8},{10,11... | collective-permute-start | bytes 1806344 | tf_op jit(solution)/shard_map/ppermute | solution.py:75
  86.3 2.7 %collective-permute-start.20 = (bf16[2304,128]{1,0:T(8,128)(2,1)S(1)}, bf16[2304,128]{1,0:T(8,128)(2,1)S(1)}, u32[]{:S(2)}, u32[]{:S(2)}) collective-permute-start(bf16[2304,128]{1,0:T(8,128)(2,1)S(1)} %get-tuple-element.131), channel_id=1, source_target_pairs={{0,1},{1,0},{2,3},{3,2},{4,5},{5,4},{6,7},{7,6},{8,9},{9,8},{10,11... | collective-permute-start | bytes 1769480 | tf_op jit(solution)/shard_map/ppermute | solution.py:75
  91.3 17.7 %collective-permute-start.21 = (bf16[2352,128]{1,0:T(8,128)(2,1)S(1)}, bf16[2352,128]{1,0:T(8,128)(2,1)S(1)}, u32[]{:S(2)}, u32[]{:S(2)}) collective-permute-start(bf16[2352,128]{1,0:T(8,128)(2,1)S(1)} %pad_maximum_fusion.1), channel_id=1, source_target_pairs={{0,2},{1,3},{2,0},{3,1},{4,6},{5,7},{6,4},{7,5},{8,10},{9,11},{10,... | collective-permute-start | bytes 1806344 | tf_op jit(solution)/shard_map/ppermute | solution.py:75
  92.4 5.4 %collective-permute-start.23 = (bf16[6912,128]{1,0:T(8,128)(2,1)S(1)}, bf16[6912,128]{1,0:T(8,128)(2,1)S(1)}, u32[]{:S(2)}, u32[]{:S(2)}) collective-permute-start(bf16[6912,128]{1,0:T(8,128)(2,1)S(1)} %copy-done.37), channel_id=1, source_target_pairs={{0,1},{1,0},{2,3},{3,2},{4,5},{5,4},{6,7},{7,6},{8,9},{9,8},{10,11... | collective-permute-start | bytes 5308424 | tf_op jit(solution)/shard_map/ppermute | solution.py:75
  92.4 5.2 %collective-permute-start.24 = (bf16[2304,128]{1,0:T(8,128)(2,1)S(1)}, bf16[2304,128]{1,0:T(8,128)(2,1)S(1)}, u32[]{:S(2)}, u32[]{:S(2)}) collective-permute-start(bf16[2304,128]{1,0:T(8,128)(2,1)S(1)} %get-tuple-element.143), channel_id=1, source_target_pairs={{0,1},{1,0},{2,3},{3,2},{4,5},{5,4},{6,7},{7,6},{8,9},{9,8},{10,11... | collective-permute-start | bytes 1769480 | tf_op jit(solution)/shard_map/ppermute | solution.py:75
  92.9 4.6 %collective-permute-start.25 = (bf16[2,2,128,384]{3,2,1,0:T(8,128)(2,1)S(1)}, bf16[2,2,128,384]{3,2,1,0:T(8,128)(2,1)S(1)}, u32[]{:S(2)}, u32[]{:S(2)}) collective-permute-start(bf16[2,2,128,384]{3,2,1,0:T(8,128)(2,1)S(1)} %get-tuple-element.145), channel_id=1, source_target_pairs={{0,1},{1,0},{2,3},{3,2},{4,5},{5,4},{6,7},{7,6},{8,9},{9,8},{10,11... | collective-permute-start | bytes 1179656 | tf_op jit(solution)/shard_map/ppermute | solution.py:80
  93.1 15.8 %collective-permute-start.22 = (bf16[2304,128]{1,0:T(8,128)(2,1)S(1)}, bf16[2304,128]{1,0:T(8,128)(2,1)S(1)}, u32[]{:S(2)}, u32[]{:S(2)}) collective-permute-start(bf16[2304,128]{1,0:T(8,128)(2,1)S(1)} %add_convert_fusion.5), channel_id=1, source_target_pairs={{0,4},{1,5},{2,6},{3,7},{4,0},{5,1},{6,2},{7,3},{8,12},{9,13},{10,... | collective-permute-start | bytes 1769480 | tf_op jit(solution)/shard_map/ppermute | solution.py:75
  109.1 17.1 %collective-permute-start.26 = (bf16[2352,128]{1,0:T(8,128)(2,1)S(1)}, bf16[2352,128]{1,0:T(8,128)(2,1)S(1)}, u32[]{:S(2)}, u32[]{:S(2)}) collective-permute-start(bf16[2352,128]{1,0:T(8,128)(2,1)S(1)} %pad_maximum_fusion.2), channel_id=1, source_target_pairs={{0,4},{1,5},{2,6},{3,7},{4,0},{5,1},{6,2},{7,3},{8,12},{9,13},{10,... | collective-permute-start | bytes 1806344 | tf_op jit(solution)/shard_map/ppermute | solution.py:75
  109.7 16.5 %collective-permute-start.27 = (bf16[2304,128]{1,0:T(8,128)(2,1)}, bf16[2304,128]{1,0:T(8,128)(2,1)S(1)}, u32[]{:S(2)}, u32[]{:S(2)}) collective-permute-start(bf16[2304,128]{1,0:T(8,128)(2,1)} %get-tuple-element.149), channel_id=1, source_target_pairs={{0,2},{1,3},{2,0},{3,1},{4,6},{5,7},{6,4},{7,5},{8,10},{9,11},{10,... | collective-permute-start | bytes 1769480 | tf_op jit(solution)/shard_map/ppermute | solution.py:75
  112.6 8.3 %collective-permute-start.28 = (bf16[576,128]{1,0:T(8,128)(2,1)}, bf16[576,128]{1,0:T(8,128)(2,1)S(1)}, u32[]{:S(2)}, u32[]{:S(2)}) collective-permute-start(bf16[576,128]{1,0:T(8,128)(2,1)} %get-tuple-element.213), channel_id=1, source_target_pairs={{0,8},{1,9},{2,10},{3,11},{4,12},{5,13},{6,14},{7,15},{8,16},{9,17... | collective-permute-start | bytes 442376 | tf_op jit(solution)/shard_map/ppermute | solution.py:75
  116.4 9.9 %collective-permute-start.29 = (bf16[576,128]{1,0:T(8,128)(2,1)}, bf16[576,128]{1,0:T(8,128)(2,1)S(1)}, u32[]{:S(2)}, u32[]{:S(2)}) collective-permute-start(bf16[576,128]{1,0:T(8,128)(2,1)} %get-tuple-element.212), channel_id=1, source_target_pairs={{0,16},{1,17},{2,18},{3,19},{4,20},{5,21},{6,22},{7,23},{8,24},{9,... | collective-permute-start | bytes 442376 | tf_op jit(solution)/shard_map/ppermute | solution.py:75
  116.4 9.9 %collective-permute-start.30 = (bf16[576,128]{1,0:T(8,128)(2,1)}, bf16[576,128]{1,0:T(8,128)(2,1)S(1)}, u32[]{:S(2)}, u32[]{:S(2)}) collective-permute-start(bf16[576,128]{1,0:T(8,128)(2,1)} %get-tuple-element.211), channel_id=1, source_target_pairs={{0,24},{1,25},{2,26},{3,27},{4,28},{5,29},{6,30},{7,31},{8,0},{9,1... | collective-permute-start | bytes 442376 | tf_op jit(solution)/shard_map/ppermute | solution.py:75
  128.0 14.7 %collective-permute-start.31 = (bf16[624,128]{1,0:T(8,128)(2,1)S(1)}, bf16[624,128]{1,0:T(8,128)(2,1)S(1)}, u32[]{:S(2)}, u32[]{:S(2)}) collective-permute-start(bf16[624,128]{1,0:T(8,128)(2,1)S(1)} %get-tuple-element.227), channel_id=1, source_target_pairs={{0,8},{1,9},{2,10},{3,11},{4,12},{5,13},{6,14},{7,15},{8,16},{9,17... | collective-permute-start | bytes 479240 | tf_op jit(solution)/shard_map/ppermute | solution.py:75
  131.6 12.1 %collective-permute-start.32 = (bf16[624,128]{1,0:T(8,128)(2,1)S(1)}, bf16[624,128]{1,0:T(8,128)(2,1)S(1)}, u32[]{:S(2)}, u32[]{:S(2)}) collective-permute-start(bf16[624,128]{1,0:T(8,128)(2,1)S(1)} %get-tuple-element.226), channel_id=1, source_target_pairs={{0,16},{1,17},{2,18},{3,19},{4,20},{5,21},{6,22},{7,23},{8,24},{9,... | collective-permute-start | bytes 479240 | tf_op jit(solution)/shard_map/ppermute | solution.py:75
  134.2 9.5 %collective-permute-start.33 = (bf16[624,128]{1,0:T(8,128)(2,1)S(1)}, bf16[624,128]{1,0:T(8,128)(2,1)S(1)}, u32[]{:S(2)}, u32[]{:S(2)}) collective-permute-start(bf16[624,128]{1,0:T(8,128)(2,1)S(1)} %get-tuple-element.225), channel_id=1, source_target_pairs={{0,24},{1,25},{2,26},{3,27},{4,28},{5,29},{6,30},{7,31},{8,0},{9,1... | collective-permute-start | bytes 479240 | tf_op jit(solution)/shard_map/ppermute | solution.py:75
  134.9 8.8 %collective-permute-start.35 = (bf16[2,128,384]{2,1,0:T(8,128)(2,1)S(1)}, bf16[2,128,384]{2,1,0:T(8,128)(2,1)S(1)}, u32[]{:S(2)}, u32[]{:S(2)}) collective-permute-start(bf16[2,128,384]{2,1,0:T(8,128)(2,1)S(1)} %get-tuple-element.221), channel_id=1, source_target_pairs={{0,2},{1,3},{2,0},{3,1},{4,6},{5,7},{6,4},{7,5},{8,10},{9,11},{10,... | collective-permute-start | bytes 589832 | tf_op jit(solution)/shard_map/ppermute | solution.py:80
  136.7 5.9 %collective-permute-start.34 = (bf16[288,128]{1,0:T(8,128)(2,1)S(1)}, bf16[288,128]{1,0:T(8,128)(2,1)S(1)}, u32[]{:S(2)}, u32[]{:S(2)}) collective-permute-start(bf16[288,128]{1,0:T(8,128)(2,1)S(1)} %get-tuple-element.219), channel_id=1, source_target_pairs={{0,2},{1,3},{2,0},{3,1},{4,6},{5,7},{6,4},{7,5},{8,10},{9,11},{10,... | collective-permute-start | bytes 221192 | tf_op jit(solution)/shard_map/ppermute | solution.py:75
  (43 other events, 238.9 us)

commit v7 on v6

--- a/solution.py
+++ b/solution.py
@@ -37,6 +37,7 @@
 KEEP_PARTS = SEND_PARTS[:2] + [(PART * k, PART) for k in range(4)]
 SIZES = {"z": 4, "y": 2, "x": 2, "c": 2}
 ROWS = 128
+HALF = 64
 F32 = jnp.float32
 BF16 = jnp.bfloat16
 
@@ -69,7 +70,7 @@
     pairs = []
     for number in range(BLOCKS):
         found = coordinates(number)
-        found[name] = (found[name] + shift) % SIZES[name]
+        found[name] = found[name] ^ shift
         target = number_of(found)
         pairs += [(number * inner + k, target * inner + k) for k in range(inner)]
     return lax.ppermute(buffer, ("dp", "ctx"), pairs)
@@ -146,12 +147,12 @@
     for order in (("c", "x", "y", "z"), ("c", "y", "z", "x")):
         for number in range(BLOCKS):
             found = coordinates(number)
-            entries.append(fold(order, {n: (mine[n] - found[n]) % SIZES[n] for n in SIZES}))
+            entries.append(fold(order, {n: mine[n] ^ found[n] for n in SIZES}))
     for order, start in ((("x", "y"), head_row), (("y",), tail_row)):
         for number in range(0, BLOCKS, 2):
             found = coordinates(number)
-            slot = fold(order, {n: (found[n] - mine[n]) % SIZES[n] for n in SIZES})
-            inside = (found["x"] - mine["x"]) % SIZES["x"]
+            slot = fold(order, {n: mine[n] ^ found[n] for n in SIZES})
+            inside = mine["x"] ^ found["x"]
             entries.append(start(slot, found["z"], inside))
     entries.append(mine["c"])
     entries.append(mine["z"])
@@ -196,7 +197,7 @@
     place = coordinates(device_number() // inner_count())["z"]
 
     def part_for(array, shift):
-        return lax.dynamic_slice_in_dim(array, HEAD_ROWS * ((place + shift) % SIZES["z"]), HEAD_ROWS, 0)
+        return lax.dynamic_slice_in_dim(array, HEAD_ROWS * (place ^ shift), HEAD_ROWS, 0)
 
     vector = summed_vector(vector, got_hx[PART:])
     hy = jnp.concatenate([summed(mid, got_hx[:PART]).astype(BF16), vector])
@@ -299,9 +300,9 @@
         rows = ref.shape[0]
         part = ref[rows - 2 * VECTOR_ROWS : rows, :].astype(F32)
         vector_parts[at] = part[:VECTOR_ROWS] + part[VECTOR_ROWS:]
-    vector = vector_parts[lax.rem(place, 4)]
+    vector = vector_parts[place]
     for z in (1, 2, 3):
-        vector = vector + vector_parts[lax.rem(place + 4 - z, 4)]
+        vector = vector + vector_parts[jnp.bitwise_xor(place, z)]
 
     lane = lax.broadcasted_iota(jnp.int32, (2 * ROWS, WIDE), 1)
     x = jnp.where(lane < MODEL_WIDTH, tokens_ref[0].astype(F32).reshape(2 * ROWS, WIDE), 0.0)
@@ -441,12 +442,12 @@
     (place_q_ref, place_k_ref, gains_ref, bias_q_ref, bias_kv_ref, grad_ref) = refs[19:25]
     block_out_ref, parts_out = refs[25], refs[26:36]
     (dkv_send, dkv_keep, dq_wq_ref, d_mid_ref, w_kv) = refs[36:41]
-    (raw_head, raw_tail, w_q, w_out, w_gate, w_up, w_down, normed_all, hidden_all, keys, values, queries, probs, attended, act_all, block_acc, d_hidden, d_attended, dkv_all, d_query, send_all, keep_all, vector_ref, outs, sems, out_sems) = refs[41:]
+    (raw_head, raw_tail, w_q, w_out, w_gate, w_up, w_down, normed_all, hidden_all, keys, values, queries, probs_low, probs_high, attended, act_all, block_acc, d_hidden, d_attended, dkv_all, d_query, send_all, keep_all, vector_ref, outs, sems, out_sems) = refs[41:]
 
     place = slots[MY_Z]
 
     def fetches(shift, sem):
-        at = lax.rem(place + shift, 4)
+        at = jnp.bitwise_xor(place, shift)
         copies = []
         for k, part in enumerate(head_parts):
             copies.append(pltpu.make_async_copy(part.at[at], raw_head.at[4 * k + at], sems.at[sem + k]))
@@ -462,6 +463,15 @@
 
     core = slots[MY_CORE]
 
+    def key_rows_of(mb, slot, half):
+        return pl.ds(pl.multiple_of(mb * 512 + half * 256 + slot * HALF, HALF), HALF)
+
+    def in_key_order(pair, mb):
+        return jnp.concatenate(
+            [at_slot(pair, slot)[mb, HALF * half : HALF * half + HALF, :] for half in range(2) for slot in range(4)],
+            axis=0,
+        )
+
     def at_slot(pair, slot):
         return pair[slot % 2].at[slot // 2]
 
@@ -473,17 +483,19 @@
 
     gain_one = gains_ref[0:1, :]
     gain_two = gains_ref[1:2, :]
-    low_rows = lower_lanes((ROWS, LANES))
+    low_rows = lower_lanes((HALF, LANES))
 
     @pl.loop(0, 2)
     def _(mb):
         lane = lax.broadcasted_iota(jnp.int32, (ROWS, WIDE), 1)
         for slot in range(4):
-            rows = pl.ds(pl.multiple_of(mb * 512 + slot * ROWS, ROWS), ROWS)
             x = jnp.where(lane < MODEL_WIDTH, at_slot(tokens_pair, slot)[mb].astype(F32), 0.0)
             normed, _ = normed_rows(x)
-            normed_all[rows, :] = normed
-            hidden_all[rows, :] = (normed * gain_one).astype(BF16)
+            hidden = (normed * gain_one).astype(BF16)
+            for half in range(2):
+                rows = key_rows_of(mb, slot, half)
+                normed_all[rows, :] = normed[HALF * half : HALF * half + HALF]
+                hidden_all[rows, :] = hidden[HALF * half : HALF * half + HALF]
 
     for copy in attention_blocks:
         copy.wait()
@@ -504,8 +516,7 @@
     def _(mb):
         rows = pl.ds(pl.multiple_of(mb * 512, 512), 512)
         pair = product(hidden_all[rows, :], w_kv[...]) + bias_kv_ref[...]
-        cosines = jnp.concatenate([at_slot(cos_pair, slot)[mb] for slot in range(4)], axis=0)
-        sines = jnp.concatenate([at_slot(sin_pair, slot)[mb] for slot in range(4)], axis=0)
+        cosines, sines = in_key_order(cos_pair, mb), in_key_order(sin_pair, mb)
         key_a = rope(pair[:, 0:128], cosines, sines)
         key_b = rope(pair[:, 256:384], cosines, sines)
         value_a, value_b = pair[:, 128:256], pair[:, 256:384]
@@ -537,26 +548,31 @@
         rows = pl.ds(pl.multiple_of(mb * ROWS, ROWS), ROWS)
         key_rows = pl.ds(pl.multiple_of(mb * 512, 512), 512)
         cosines, sines = cos_pair[0][0, mb], sin_pair[0][0, mb]
-        made = product(hidden_all[pl.ds(pl.multiple_of(mb * 512, 512), ROWS), :], w_q[...]) + bias_q_ref[...]
+        hidden = jnp.concatenate([hidden_all[key_rows_of(mb, 0, half), :] for half in range(2)], axis=0)
+        made = product(hidden, w_q[...]) + bias_q_ref[...]
         for k in range(5):
             turned = rope(made[:, LANES * k : LANES * k + LANES], cosines, sines)
             queries[rows, LANES * k : LANES * k + LANES] = (turned * HEAD_SIZE ** (-0.5)).astype(BF16)
-        masked = jnp.where(place_q_ref[mb] >= place_k_ref[mb], 0.0, MASKED)
-        masked = jnp.concatenate([masked] * 3, axis=0)
-        parts = []
-        for group in range(KEY_VALUE_HEADS):
-            lanes = slice(LANES * group, LANES * group + LANES)
-            scores = times_transposed(heads_of(queries, rows, group), keys[key_rows, lanes])
-            scores = scores + masked
-            top = jnp.max(scores, axis=-1, keepdims=True)
-            powers = jnp.exp(scores - top)
-            found = powers * (1.0 / jnp.sum(powers, axis=-1, keepdims=True))
-            probs[mb, group] = found
-            out = product(found.astype(BF16), values[key_rows, lanes])
-            outs[mb, group] = out
-            parts += [out[ROWS * k : ROWS * k + ROWS] for k in range(3)]
-        for k, tile in enumerate(tiles_of_heads(parts)):
-            attended[rows, LANES * k : LANES * k + LANES] = tile.astype(BF16)
+        place_q, place_k = place_q_ref[mb], place_k_ref[mb]
+        for half, probs in enumerate((probs_low, probs_high)):
+            count = 256 * (half + 1)
+            own = pl.ds(pl.multiple_of(mb * ROWS + HALF * half, HALF), HALF)
+            masked = jnp.where(place_q[HALF * half : HALF * half + HALF] >= place_k[:, 0:count], 0.0, MASKED)
+            masked = jnp.concatenate([masked] * 3, axis=0)
+            seen = pl.ds(pl.multiple_of(mb * 512, 512), count)
+            parts = []
+            for group in range(KEY_VALUE_HEADS):
+                lanes = slice(LANES * group, LANES * group + LANES)
+                scores = times_transposed(heads_of(queries, own, group), keys[seen, lanes]) + masked
+                top = jnp.max(scores, axis=-1, keepdims=True)
+                powers = jnp.exp(scores - top)
+                found = powers * (1.0 / jnp.sum(powers, axis=-1, keepdims=True))
+                probs[mb, group] = found
+                out = product(found.astype(BF16), values[seen, lanes])
+                outs[mb, 2 * group + half] = out
+                parts += [out[HALF * k : HALF * k + HALF] for k in range(3)]
+            for k, tile in enumerate(tiles_of_heads(parts)):
+                attended[own, LANES * k : LANES * k + LANES] = tile.astype(BF16)
 
     for copy in other_blocks:
         copy.wait()
@@ -670,29 +686,37 @@
     def _(mb):
         rows = pl.ds(pl.multiple_of(mb * ROWS, ROWS), ROWS)
         key_rows = pl.ds(pl.multiple_of(mb * 512, 512), 512)
-        parts = []
         d_keys = []
         d_values = []
+        parts = ([], [])
         for group in range(KEY_VALUE_HEADS):
             lanes = slice(LANES * group, LANES * group + LANES)
-            query_rows = heads_of(queries, rows, group)
-            cotangent = heads_of(d_attended, rows, group)
-            found = probs[mb, group]
-            d_probs = times_transposed(cotangent, values[key_rows, lanes])
-            delta = jnp.sum(outs[mb, group] * cotangent.astype(F32), axis=-1, keepdims=True)
-            d_scores = (found * (d_probs - delta)).astype(BF16)
-            out = product(d_scores, keys[key_rows, lanes]) * HEAD_SIZE ** (-0.5)
-            parts += [out[ROWS * k : ROWS * k + ROWS] for k in range(3)]
-            d_key = rows_product(d_scores, query_rows)
-            d_value = rows_product(found.astype(BF16), cotangent)
+            d_key, d_value = [], []
+            for half, probs in enumerate((probs_low, probs_high)):
+                own = pl.ds(pl.multiple_of(mb * ROWS + HALF * half, HALF), HALF)
+                seen = pl.ds(pl.multiple_of(mb * 512, 512), 256 * (half + 1))
+                query_rows = heads_of(queries, own, group)
+                cotangent = heads_of(d_attended, own, group)
+                found = probs[mb, group]
+                d_probs = times_transposed(cotangent, values[seen, lanes])
+                delta = jnp.sum(outs[mb, 2 * group + half] * cotangent.astype(F32), axis=-1, keepdims=True)
+                d_scores = (found * (d_probs - delta)).astype(BF16)
+                out = product(d_scores, keys[seen, lanes]) * HEAD_SIZE ** (-0.5)
+                parts[half].extend(out[HALF * k : HALF * k + HALF] for k in range(3))
+                d_key.append(rows_product(d_scores, query_rows))
+                d_value.append(rows_product(found.astype(BF16), cotangent))
+            d_key = jnp.concatenate([d_key[0] + d_key[1][0:256], d_key[1][256:512]], axis=0)
+            d_value = jnp.concatenate([d_value[0] + d_value[1][0:256], d_value[1][256:512]], axis=0)
             d_keys.append(d_key + half_turn(d_key))
             d_values.append(d_value + half_turn(d_value))
-        cosines, sines = cos_pair[0][0, mb], sin_pair[0][0, mb]
-        for k, tile in enumerate(tiles_of_heads(parts)):
-            d_query[rows, LANES * k : LANES * k + LANES] = rope_back(tile, cosines, sines).astype(BF16)
+        for half in range(2):
+            own = pl.ds(pl.multiple_of(mb * ROWS + HALF * half, HALF), HALF)
+            cosines = cos_pair[0][0, mb, HALF * half : HALF * half + HALF, :]
+            sines = sin_pair[0][0, mb, HALF * half : HALF * half + HALF, :]
+            for k, tile in enumerate(tiles_of_heads(parts[half])):
+                d_query[own, LANES * k : LANES * k + LANES] = rope_back(tile, cosines, sines).astype(BF16)
         low_keys = lower_lanes((512, LANES))
-        cosines = jnp.concatenate([at_slot(cos_pair, slot)[mb] for slot in range(4)], axis=0)
-        sines = jnp.concatenate([at_slot(sin_pair, slot)[mb] for slot in range(4)], axis=0)
+        cosines, sines = in_key_order(cos_pair, mb), in_key_order(sin_pair, mb)
         key_a = rope_back(jnp.where(low_keys, d_keys[0], d_keys[1]), cosines, sines)
         key_b = rope_back(d_keys[2], cosines, sines)
         dkv_all[key_rows, 0:128] = key_a.astype(BF16)
@@ -700,7 +724,8 @@
         dkv_all[key_rows, 256:384] = jnp.where(low_keys, key_b, d_values[2]).astype(BF16)
         for slot in range(4):
             target = dkv_send if slot % 2 else dkv_keep
-            target[slot // 2, mb] = dkv_all[pl.ds(pl.multiple_of(mb * 512 + slot * ROWS, ROWS), ROWS), :]
+            for half in range(2):
+                target[slot // 2, mb, HALF * half : HALF * half + HALF, :] = dkv_all[key_rows_of(mb, slot, half), :]
 
     dkv = dkv_all[...]
     d_q = d_query[...]
@@ -709,13 +734,15 @@
     bias_q_sum = jnp.sum(d_q.astype(F32), axis=0, keepdims=True)
     bias_kv_sum = jnp.sum(dkv.astype(F32), axis=0, keepdims=True)
     gain_sum = jnp.zeros((1, WIDE), F32)
-    for mb in range(2):
-        gain_sum += jnp.sum(dq_wq[ROWS * mb : ROWS * mb + ROWS] * normed_all[512 * mb : 512 * mb + ROWS, :], axis=0, keepdims=True)
+    for at in range(4):
+        gain_sum += jnp.sum(
+            dq_wq[HALF * at : HALF * at + HALF] * normed_all[256 * at : 256 * at + HALF, :], axis=0, keepdims=True
+        )
     for k in range(4):
         part = slice(256 * k, 256 * k + 256)
         gain_sum += jnp.sum(times_transposed(dkv_all[part, :], w_kv[...]) * normed_all[part, :], axis=0, keepdims=True)
 
-    hidden_own = jnp.concatenate([hidden_all[0:ROWS, :], hidden_all[512 : 512 + ROWS, :]], axis=0)
+    hidden_own = jnp.concatenate([hidden_all[256 * at : 256 * at + HALF, :] for at in range(4)], axis=0)
     grad_q = rows_product(hidden_own, d_q)
     grad_kv = rows_product(hidden_all[...], dkv)
     rest = grad_kv[0:576, 256:384]
@@ -777,7 +804,8 @@
         ((1024, 384), BF16),
         ((1024, 384), BF16),
         ((256, WIDE), BF16),
-        ((2, 3, 384, 512), F32),
+        ((2, 3, 192, 256), F32),
+        ((2, 3, 192, 512), F32),
         ((256, WIDE), BF16),
         ((256, FF), BF16),
         ((256, WIDE), F32),
@@ -788,7 +816,7 @@
         ((ALL_ROWS, LANES), BF16),
         ((ALL_ROWS, LANES), BF16),
         ((VECTOR_ROWS, LANES), F32),
-        ((2, 3, 384, LANES), F32),
+        ((2, 6, 192, LANES), F32),
     ]
     return pl.pallas_call(
         layer_kernel,
@@ -875,7 +903,7 @@
     cosines_far, sines_far = place_tables(far)
     place_all = jnp.stack([places_of(near), places_of(far)], axis=1)
     place_q = place_all[0, 0][..., None]
-    place_k = jnp.transpose(place_all.reshape(4, 2, ROWS), (1, 0, 2)).reshape(2, 1, 4 * ROWS)
+    place_k = jnp.transpose(place_all.reshape(4, 2, 2, HALF), (1, 2, 0, 3)).reshape(2, 1, 4 * ROWS)
 
     block_out, *found = run_layer(
         slots, heads, tails, near, far, cosines, cosines_far, sines, sines_far, place_q, place_k, gains, bias_q, bias_kv, grad

time: 151 us -> 155 us (1.026)
  waiting for transfers between devices: 54.5 us -> 60.4 us
  starting transfers between devices: 36.7 us -> 33.9 us
  Pallas kernels: 35.5 us -> 38.1 us
    ppermute x32, waiting for transfers between devices: 46.2 us -> 60.4 us  [moved(): return lax.ppermute(buffer, ('dp', 'ctx'), pairs)]
    ppermute x4, waiting for transfers between devices: 8.36 us -> 0.01 us  [across(): lax.ppermute(buffer, 'ctx', [(i, i ^ distance) for i in range(count)])]
    ppermute x32, starting transfers between devices: 34.9 us -> 30.5 us  [moved(): return lax.ppermute(buffer, ('dp', 'ctx'), pairs)]
    pallas_call x1, Pallas kernels: 28.6 us -> 31.1 us  [run_layer(): pl.pallas_call(layer_kernel, out_shape=(shape((2, MODEL_WIDTH, ROWS), BF1...]
    ppermute x4, starting transfers between devices: 1.75 us -> 3.48 us  [across(): lax.ppermute(buffer, 'ctx', [(i, i ^ distance) for i in range(count)])]
    unnamed x80 -> x74, local copies, waits for them, and re-layouts: 3.86 us -> 4.03 us
  transfers between devices with their start and end apart: 36 -> 36, of which waited for: 18 -> 13; matrix products, arithmetic and copies ran while one was open for 9% -> 10% of each run, Pallas kernels for 0% -> 0%
where the time goes in v7:
time: 155 us
  waiting for transfers between devices  60.4 us (39%)
  Pallas kernels  38.1 us (25%)
  starting transfers between devices  33.9 us (22%)
  other arithmetic  11.8 us (8%)
  local copies, waits for them, and re-layouts  8.81 us (6%)
    ppermute x32, waiting for transfers between devices, moved(): return lax.ppermute(buffer, ('dp', 'ctx'), pairs)  60.4 us
    pallas_call x1, Pallas kernels, run_layer(): pl.pallas_call(layer_kernel, out_shape=(shape((2, MODEL_WIDTH, ROWS), BF1...  31.1 us
    ppermute x32, starting transfers between devices, moved(): return lax.ppermute(buffer, ('dp', 'ctx'), pairs)  30.5 us
    pallas_call x1, Pallas kernels, finish(): pl.pallas_call(finish_kernel, out_shape=shapes, in_specs=[pl.BlockSpec(me...  5.05 us
    unnamed x74, local copies, waits for them, and re-layouts  4.03 us
    ppermute x4, starting transfers between devices, across(): lax.ppermute(buffer, 'ctx', [(i, i ^ distance) for i in range(count)])  3.48 us
  transfers between devices with their start and end apart: 36, of which 13 were waited for; matrix products, arithmetic and copies ran while one was open for 10% of the time, Pallas kernels for 0%

profile of v7, /device:TPU:0, one launch (start us, length us, event | category | flops | bytes accessed | tf_op | source)
XLA Modules:
  0.0 154.5 jit_solution(11642718560693316153)
XLA Ops:
  0.7 1.9 %to_tiles.1 = (bf16[576,128]{1,0:T(8,128)(2,1)}, bf16[288,128]{1,0:T(8,128)(2,1)}) custom-call(s32[1]{0:T(128)} %bitcast.kind_ref, f32[864,128]{1,0:T(8,128)} %bitcast.150), custom_call_target="tpu_custom_call" | custom-call | tf_op jit(solution)/shard_map/to_tiles/pallas_call | solution.py:270
  2.5 2.9 %collective-permute-start.2 = (bf16[576,128]{1,0:T(8,128)(2,1)}, bf16[576,128]{1,0:T(8,128)(2,1)S(1)}, u32[]{:S(2)}, u32[]{:S(2)}) collective-permute-start(bf16[576,128]{1,0:T(8,128)(2,1)} %get-tuple-element.98), channel_id=1, source_target_pairs={{0,8},{1,9},{2,10},{3,11},{4,12},{5,13},{6,14},{7,15},{8,0},{9,1},... | collective-permute-start | bytes 442376 | tf_op jit(solution)/shard_map/ppermute | solution.py:76
  5.4 2.7 %collective-permute-start.3 = (bf16[576,128]{1,0:T(8,128)(2,1)}, bf16[576,128]{1,0:T(8,128)(2,1)S(1)}, u32[]{:S(2)}, u32[]{:S(2)}) collective-permute-start(bf16[576,128]{1,0:T(8,128)(2,1)} %get-tuple-element.98), channel_id=1, source_target_pairs={{0,16},{1,17},{2,18},{3,19},{4,20},{5,21},{6,22},{7,23},{8,24},{9,... | collective-permute-start | bytes 442376 | tf_op jit(solution)/shard_map/ppermute | solution.py:76
  9.1 1.2 copy.39
  10.5 1.8 %collective-permute-start.1 = (bf16[2,128,640]{2,1,0:T(8,128)(2,1)S(1)}, bf16[2,128,640]{2,1,0:T(8,128)(2,1)S(1)}, u32[]{:S(2)}, u32[]{:S(2)}) collective-permute-start(bf16[2,128,640]{2,1,0:T(8,128)(2,1)S(1)} %maximum_maximum_fusion), channel_id=1, source_target_pairs={{0,2},{1,3},{2,0},{3,1},{4,6},{5,7},{6,4},{7,5},{8,10},{9,11},{10,... | collective-permute-start | bytes 983048 | tf_op jit(solution)/shard_map/ppermute | solution.py:81
  15.6 5.5 %collective-permute-done = bf16[288,128]{1,0:T(8,128)(2,1)S(1)} collective-permute-done((bf16[288,128]{1,0:T(8,128)(2,1)S(1)}, bf16[288,128]{1,0:T(8,128)(2,1)S(1)}, u32[]{:S(2)}, u32[]{:S(2)}) %collective-permute-start) | collective-permute-done | bytes 73760 | tf_op jit(solution)/shard_map/ppermute | solution.py:76
  21.2 1.6 %collective-permute-start.5 = (bf16[4,576,128]{2,1,0:T(8,128)(2,1)S(1)}, bf16[4,576,128]{2,1,0:T(8,128)(2,1)S(1)}, u32[]{:S(2)}, u32[]{:S(2)}) collective-permute-start(bf16[4,576,128]{2,1,0:T(8,128)(2,1)S(1)} %pad_maximum_fusion.3.refs_1_), channel_id=1, source_target_pairs={{0,4},{1,5},{2,6},{3,7},{4,0},{5,1},{6,2},{7,3},{8,12},{9,13},{10,... | collective-permute-start | bytes 1769480 | tf_op jit(solution)/shard_map/ppermute | solution.py:76
  22.8 1.5 collective-permute-start.6
  24.3 1.0 collective-permute-start.7
  25.3 3.2 %collective-permute-start.8 = (bf16[2,288,128]{2,1,0:T(8,128)(2,1)S(1)}, bf16[2,288,128]{2,1,0:T(8,128)(2,1)S(1)}, u32[]{:S(2)}, u32[]{:S(2)}) collective-permute-start(bf16[2,288,128]{2,1,0:T(8,128)(2,1)S(1)} %pad_maximum_fusion.10), channel_id=1, source_target_pairs={{0,16},{1,17},{2,18},{3,19},{4,20},{5,21},{6,22},{7,23},{8,24},{9,... | collective-permute-start | bytes 442376 | tf_op jit(solution)/shard_map/ppermute | solution.py:76
  29.1 1.0 fusion
  30.2 7.6 %collective-permute-done.8 = bf16[2,288,128]{2,1,0:T(8,128)(2,1)S(1)} collective-permute-done((bf16[2,288,128]{2,1,0:T(8,128)(2,1)S(1)}, bf16[2,288,128]{2,1,0:T(8,128)(2,1)S(1)}, u32[]{:S(2)}, u32[]{:S(2)}) %collective-permute-start.8) | collective-permute-done | bytes 147488 | tf_op jit(solution)/shard_map/ppermute | solution.py:76
  39.6 8.8 %collective-permute-done.11.refs_10_ = bf16[8,288,128]{2,1,0:T(8,128)(2,1)} collective-permute-done((bf16[8,288,128]{2,1,0:T(8,128)(2,1)S(1)}, bf16[8,288,128]{2,1,0:T(8,128)(2,1)}, u32[]{:S(2)}, u32[]{:S(2)}) %collective-permute-start.11) | collective-permute-done | bytes 589856 | tf_op jit(solution)/shard_map/ppermute | solution.py:76
  49.6 4.7 %collective-permute-done.10.refs_4_ = bf16[4,576,128]{2,1,0:T(8,128)(2,1)} collective-permute-done((bf16[4,576,128]{2,1,0:T(8,128)(2,1)S(1)}, bf16[4,576,128]{2,1,0:T(8,128)(2,1)}, u32[]{:S(2)}, u32[]{:S(2)}) %collective-permute-start.10) | collective-permute-done | bytes 589856 | tf_op jit(solution)/shard_map/ppermute | solution.py:76
  58.4 31.1 %layer.1 = (bf16[2,576,128]{2,1,0:T(8,128)(2,1)}, bf16[2352,128]{1,0:T(8,128)(2,1)}, bf16[2304,128]{1,0:T(8,128)(2,1)S(1)}, bf16[6912,128]{1,0:T(8,128)(2,1)}, b...) custom-call(s32[98]{0:T(128)S(1)} %stack.448.refs_0_, ...), custom_call_target="tpu_custom_call" | custom-call | tf_op jit(solution)/shard_map/layer/pallas_call | solution.py:821
  90.2 2.4 %collective-permute-done.20 = bf16[2304,128]{1,0:T(8,128)(2,1)S(1)} collective-permute-done((bf16[2304,128]{1,0:T(8,128)(2,1)S(1)}, bf16[2304,128]{1,0:T(8,128)(2,1)S(1)}, u32[]{:S(2)}, u32[]{:S(2)}) %collective-permute-start.20) | collective-permute-done | bytes 589856 | tf_op jit(solution)/shard_map/ppermute | solution.py:76
  93.2 1.2 add_convert_fusion.5
  94.4 1.6 %collective-permute-start.22 = (bf16[2304,128]{1,0:T(8,128)(2,1)S(1)}, bf16[2304,128]{1,0:T(8,128)(2,1)S(1)}, u32[]{:S(2)}, u32[]{:S(2)}) collective-permute-start(bf16[2304,128]{1,0:T(8,128)(2,1)S(1)} %add_convert_fusion.5), channel_id=1, source_target_pairs={{0,4},{1,5},{2,6},{3,7},{4,0},{5,1},{6,2},{7,3},{8,12},{9,13},{10,... | collective-permute-start | bytes 1769480 | tf_op jit(solution)/shard_map/ppermute | solution.py:76
  98.4 1.3 add_convert_fusion.2
  99.7 10.4 %collective-permute-done.22 = bf16[2304,128]{1,0:T(8,128)(2,1)S(1)} collective-permute-done((bf16[2304,128]{1,0:T(8,128)(2,1)S(1)}, bf16[2304,128]{1,0:T(8,128)(2,1)S(1)}, u32[]{:S(2)}, u32[]{:S(2)}) %collective-permute-start.22) | collective-permute-done | bytes 589856 | tf_op jit(solution)/shard_map/ppermute | solution.py:76
  110.1 1.8 %collective-permute-done.21 = bf16[2352,128]{1,0:T(8,128)(2,1)S(1)} collective-permute-done((bf16[2352,128]{1,0:T(8,128)(2,1)S(1)}, bf16[2352,128]{1,0:T(8,128)(2,1)S(1)}, u32[]{:S(2)}, u32[]{:S(2)}) %collective-permute-start.21) | collective-permute-done | bytes 602144 | tf_op jit(solution)/shard_map/ppermute | solution.py:76
  113.2 2.0 %add_convert_fusion.11 = (bf16[576,128]{1,0:T(8,128)(2,1)}, bf16[576,128]{1,0:T(8,128)(2,1)}, bf16[576,128]{1,0:T(8,128)(2,1)}, bf16[576,128]{1,0:T(8,128)(2,1)S(1)}) fusion(bf16[2304,128]{1,0:T(8,128)(2,1)} %copy-done.19, s32[]{:T(128)S(6)} %select_n.207, bf16[2304,128]{1,0:T(8,128)(2,1)S(1)} %add_convert_fusion.1, s32[]{:T(128)S(6)} %select_n.206, ...), kind=kLoop, calls=%fused_computation.23 | loop fusion | flops 1179648 | bytes 1769488 | tf_op jit(solution)/shard_map/convert_element_type | solution.py:204
  115.2 2.3 %collective-permute-start.28 = (bf16[576,128]{1,0:T(8,128)(2,1)}, bf16[576,128]{1,0:T(8,128)(2,1)S(1)}, u32[]{:S(2)}, u32[]{:S(2)}) collective-permute-start(bf16[576,128]{1,0:T(8,128)(2,1)} %get-tuple-element.213), channel_id=1, source_target_pairs={{0,8},{1,9},{2,10},{3,11},{4,12},{5,13},{6,14},{7,15},{8,0},{9,1},... | collective-permute-start | bytes 442376 | tf_op jit(solution)/shard_map/ppermute | solution.py:76
  118.3 1.6 %collective-permute-start.30 = (bf16[576,128]{1,0:T(8,128)(2,1)}, bf16[576,128]{1,0:T(8,128)(2,1)S(1)}, u32[]{:S(2)}, u32[]{:S(2)}) collective-permute-start(bf16[576,128]{1,0:T(8,128)(2,1)} %get-tuple-element.211), channel_id=1, source_target_pairs={{0,24},{1,25},{2,26},{3,27},{4,28},{5,29},{6,30},{7,31},{8,16},{9,... | collective-permute-start | bytes 442376 | tf_op jit(solution)/shard_map/ppermute | solution.py:76
  119.9 2.4 %collective-permute-done.28 = bf16[576,128]{1,0:T(8,128)(2,1)S(1)} collective-permute-done((bf16[576,128]{1,0:T(8,128)(2,1)}, bf16[576,128]{1,0:T(8,128)(2,1)S(1)}, u32[]{:S(2)}, u32[]{:S(2)}) %collective-permute-start.28) | collective-permute-done | bytes 147488 | tf_op jit(solution)/shard_map/ppermute | solution.py:76
  122.4 8.3 %collective-permute-done.29 = bf16[576,128]{1,0:T(8,128)(2,1)S(1)} collective-permute-done((bf16[576,128]{1,0:T(8,128)(2,1)}, bf16[576,128]{1,0:T(8,128)(2,1)S(1)}, u32[]{:S(2)}, u32[]{:S(2)}) %collective-permute-start.29) | collective-permute-done | bytes 147488 | tf_op jit(solution)/shard_map/ppermute | solution.py:76
  132.4 2.3 %collective-permute-start.31 = (bf16[624,128]{1,0:T(8,128)(2,1)S(1)}, bf16[624,128]{1,0:T(8,128)(2,1)S(1)}, u32[]{:S(2)}, u32[]{:S(2)}) collective-permute-start(bf16[624,128]{1,0:T(8,128)(2,1)S(1)} %get-tuple-element.227), channel_id=1, source_target_pairs={{0,8},{1,9},{2,10},{3,11},{4,12},{5,13},{6,14},{7,15},{8,0},{9,1},... | collective-permute-start | bytes 479240 | tf_op jit(solution)/shard_map/ppermute | solution.py:76
  135.4 1.7 %collective-permute-start.33 = (bf16[624,128]{1,0:T(8,128)(2,1)S(1)}, bf16[624,128]{1,0:T(8,128)(2,1)S(1)}, u32[]{:S(2)}, u32[]{:S(2)}) collective-permute-start(bf16[624,128]{1,0:T(8,128)(2,1)S(1)} %get-tuple-element.225), channel_id=1, source_target_pairs={{0,24},{1,25},{2,26},{3,27},{4,28},{5,29},{6,30},{7,31},{8,16},{9,... | collective-permute-start | bytes 479240 | tf_op jit(solution)/shard_map/ppermute | solution.py:76
  137.8 1.3 collective-permute-start.35
  141.2 3.1 %collective-permute-done.34.other_ref = bf16[288,128]{1,0:T(8,128)(2,1)S(1)} collective-permute-done((bf16[288,128]{1,0:T(8,128)(2,1)S(1)}, bf16[288,128]{1,0:T(8,128)(2,1)S(1)}, u32[]{:S(2)}, u32[]{:S(2)}) %collective-permute-start.34) | collective-permute-done | bytes 73760 | tf_op jit(solution)/shard_map/ppermute | solution.py:76
  144.3 4.2 %collective-permute-done.32.two_ref = bf16[624,128]{1,0:T(8,128)(2,1)S(1)} collective-permute-done((bf16[624,128]{1,0:T(8,128)(2,1)S(1)}, bf16[624,128]{1,0:T(8,128)(2,1)S(1)}, u32[]{:S(2)}, u32[]{:S(2)}) %collective-permute-start.32) | collective-permute-done | bytes 159776 | tf_op jit(solution)/shard_map/ppermute | solution.py:76
  149.3 5.1 %finish.1 = (f32[24,128]{1,0:T(8,128)}, f32[24,128]{1,0:T(8,128)}, f32[24,128]{1,0:T(8,128)}, f32[864,128]{1,0:T(8,128)}, f32[864,128]{1,0:T(8,128)}, /*index=5*/f32[864,128]{1,0:T(8,128)}, bf16[2,576,128]{2,1,0:T(8,128)(2,1)}) custom-call(s32[2]{0:T(128)} %pad_add_fusion.table_ref, f32[576,128]{1,0:T(8,128)} %get-tuple-element.205.head_ref, ...), custom_call_target="tpu_custom_call" | custom-call | tf_op jit(solution)/shard_map/finish/pallas_call | solution.py:372
  (181 shorter events, 23.6 us)
Async XLA Ops:
  2.5 18.5 %collective-permute-start.2 = (bf16[576,128]{1,0:T(8,128)(2,1)}, bf16[576,128]{1,0:T(8,128)(2,1)S(1)}, u32[]{:S(2)}, u32[]{:S(2)}) collective-permute-start(bf16[576,128]{1,0:T(8,128)(2,1)} %get-tuple-element.98), channel_id=1, source_target_pairs={{0,8},{1,9},{2,10},{3,11},{4,12},{5,13},{6,14},{7,15},{8,0},{9,1},... | collective-permute-start | bytes 442376 | tf_op jit(solution)/shard_map/ppermute | solution.py:76
  5.4 15.6 %collective-permute-start.3 = (bf16[576,128]{1,0:T(8,128)(2,1)}, bf16[576,128]{1,0:T(8,128)(2,1)S(1)}, u32[]{:S(2)}, u32[]{:S(2)}) collective-permute-start(bf16[576,128]{1,0:T(8,128)(2,1)} %get-tuple-element.98), channel_id=1, source_target_pairs={{0,16},{1,17},{2,18},{3,19},{4,20},{5,21},{6,22},{7,23},{8,24},{9,... | collective-permute-start | bytes 442376 | tf_op jit(solution)/shard_map/ppermute | solution.py:76
  8.1 12.9 %collective-permute-start.4 = (bf16[576,128]{1,0:T(8,128)(2,1)}, bf16[576,128]{1,0:T(8,128)(2,1)S(1)}, u32[]{:S(2)}, u32[]{:S(2)}) collective-permute-start(bf16[576,128]{1,0:T(8,128)(2,1)} %get-tuple-element.98), channel_id=1, source_target_pairs={{0,24},{1,25},{2,26},{3,27},{4,28},{5,29},{6,30},{7,31},{8,16},{9,... | collective-permute-start | bytes 442376 | tf_op jit(solution)/shard_map/ppermute | solution.py:76
  10.5 10.6 %collective-permute-start.1 = (bf16[2,128,640]{2,1,0:T(8,128)(2,1)S(1)}, bf16[2,128,640]{2,1,0:T(8,128)(2,1)S(1)}, u32[]{:S(2)}, u32[]{:S(2)}) collective-permute-start(bf16[2,128,640]{2,1,0:T(8,128)(2,1)S(1)} %maximum_maximum_fusion), channel_id=1, source_target_pairs={{0,2},{1,3},{2,0},{3,1},{4,6},{5,7},{6,4},{7,5},{8,10},{9,11},{10,... | collective-permute-start | bytes 983048 | tf_op jit(solution)/shard_map/ppermute | solution.py:81
  12.3 8.8 %collective-permute-start = (bf16[288,128]{1,0:T(8,128)(2,1)S(1)}, bf16[288,128]{1,0:T(8,128)(2,1)S(1)}, u32[]{:S(2)}, u32[]{:S(2)}) collective-permute-start(bf16[288,128]{1,0:T(8,128)(2,1)S(1)} %copy-done.30), channel_id=1, source_target_pairs={{0,2},{1,3},{2,0},{3,1},{4,6},{5,7},{6,4},{7,5},{8,10},{9,11},{10,... | collective-permute-start | bytes 221192 | tf_op jit(solution)/shard_map/ppermute | solution.py:76
  21.2 16.6 %collective-permute-start.5 = (bf16[4,576,128]{2,1,0:T(8,128)(2,1)S(1)}, bf16[4,576,128]{2,1,0:T(8,128)(2,1)S(1)}, u32[]{:S(2)}, u32[]{:S(2)}) collective-permute-start(bf16[4,576,128]{2,1,0:T(8,128)(2,1)S(1)} %pad_maximum_fusion.3.refs_1_), channel_id=1, source_target_pairs={{0,4},{1,5},{2,6},{3,7},{4,0},{5,1},{6,2},{7,3},{8,12},{9,13},{10,... | collective-permute-start | bytes 1769480 | tf_op jit(solution)/shard_map/ppermute | solution.py:76
  22.8 15.0 %collective-permute-start.6 = (bf16[4,576,128]{2,1,0:T(8,128)(2,1)S(1)}, bf16[4,576,128]{2,1,0:T(8,128)(2,1)S(1)}, u32[]{:S(2)}, u32[]{:S(2)}) collective-permute-start(bf16[4,576,128]{2,1,0:T(8,128)(2,1)S(1)} %pad_maximum_fusion.3.refs_1_), channel_id=1, source_target_pairs={{0,2},{1,3},{2,0},{3,1},{4,6},{5,7},{6,4},{7,5},{8,10},{9,11},{10,... | collective-permute-start | bytes 1769480 | tf_op jit(solution)/shard_map/ppermute | solution.py:76
  24.3 5.9 %collective-permute-start.7 = (bf16[2,288,128]{2,1,0:T(8,128)(2,1)S(1)}, bf16[2,288,128]{2,1,0:T(8,128)(2,1)S(1)}, u32[]{:S(2)}, u32[]{:S(2)}) collective-permute-start(bf16[2,288,128]{2,1,0:T(8,128)(2,1)S(1)} %pad_maximum_fusion.10), channel_id=1, source_target_pairs={{0,8},{1,9},{2,10},{3,11},{4,12},{5,13},{6,14},{7,15},{8,0},{9,1},... | collective-permute-start | bytes 442376 | tf_op jit(solution)/shard_map/ppermute | solution.py:76
  25.3 12.5 %collective-permute-start.8 = (bf16[2,288,128]{2,1,0:T(8,128)(2,1)S(1)}, bf16[2,288,128]{2,1,0:T(8,128)(2,1)S(1)}, u32[]{:S(2)}, u32[]{:S(2)}) collective-permute-start(bf16[2,288,128]{2,1,0:T(8,128)(2,1)S(1)} %pad_maximum_fusion.10), channel_id=1, source_target_pairs={{0,16},{1,17},{2,18},{3,19},{4,20},{5,21},{6,22},{7,23},{8,24},{9,... | collective-permute-start | bytes 442376 | tf_op jit(solution)/shard_map/ppermute | solution.py:76
  28.5 9.4 %collective-permute-start.9 = (bf16[2,288,128]{2,1,0:T(8,128)(2,1)S(1)}, bf16[2,288,128]{2,1,0:T(8,128)(2,1)S(1)}, u32[]{:S(2)}, u32[]{:S(2)}) collective-permute-start(bf16[2,288,128]{2,1,0:T(8,128)(2,1)S(1)} %pad_maximum_fusion.10), channel_id=1, source_target_pairs={{0,24},{1,25},{2,26},{3,27},{4,28},{5,29},{6,30},{7,31},{8,16},{9,... | collective-permute-start | bytes 442376 | tf_op jit(solution)/shard_map/ppermute | solution.py:76
  38.0 10.5 %collective-permute-start.11 = (bf16[8,288,128]{2,1,0:T(8,128)(2,1)S(1)}, bf16[8,288,128]{2,1,0:T(8,128)(2,1)}, u32[]{:S(2)}, u32[]{:S(2)}) collective-permute-start(bf16[8,288,128]{2,1,0:T(8,128)(2,1)S(1)} %constant_dynamic-update-slice_fusion.refs_9_), channel_id=1, source_target_pairs={{0,4},{1,5},{2,6},{3,7},{4,0},{5,1},{6,2},{7,3},{8,12},{9,13},{10,... | collective-permute-start | bytes 1769480 | tf_op jit(solution)/shard_map/ppermute | solution.py:76
  38.5 9.9 %collective-permute-start.15 = (bf16[8,288,128]{2,1,0:T(8,128)(2,1)S(1)}, bf16[8,288,128]{2,1,0:T(8,128)(2,1)S(1)}, u32[]{:S(2)}, u32[]{:S(2)}) collective-permute-start(bf16[8,288,128]{2,1,0:T(8,128)(2,1)S(1)} %constant_dynamic-update-slice_fusion.refs_9_), channel_id=1, source_target_pairs={{0,1},{1,0},{2,3},{3,2},{4,5},{5,4},{6,7},{7,6},{8,9},{9,8},{10,11... | collective-permute-start | bytes 1769480 | tf_op jit(solution)/shard_map/ppermute | solution.py:76
  38.5 15.8 %collective-permute-start.10 = (bf16[4,576,128]{2,1,0:T(8,128)(2,1)S(1)}, bf16[4,576,128]{2,1,0:T(8,128)(2,1)}, u32[]{:S(2)}, u32[]{:S(2)}) collective-permute-start(bf16[4,576,128]{2,1,0:T(8,128)(2,1)S(1)} %collective-permute-done.5.refs_2_), channel_id=1, source_target_pairs={{0,2},{1,3},{2,0},{3,1},{4,6},{5,7},{6,4},{7,5},{8,10},{9,11},{10,... | collective-permute-start | bytes 1769480 | tf_op jit(solution)/shard_map/ppermute | solution.py:76
  39.1 15.3 %collective-permute-start.13 = (bf16[4,576,128]{2,1,0:T(8,128)(2,1)S(1)}, bf16[4,576,128]{2,1,0:T(8,128)(2,1)S(1)}, u32[]{:S(2)}, u32[]{:S(2)}) collective-permute-start(bf16[4,576,128]{2,1,0:T(8,128)(2,1)S(1)} %collective-permute-done.5.refs_2_), channel_id=1, source_target_pairs={{0,1},{1,0},{2,3},{3,2},{4,5},{5,4},{6,7},{7,6},{8,9},{9,8},{10,11... | collective-permute-start | bytes 1769480 | tf_op jit(solution)/shard_map/ppermute | solution.py:76
  39.3 15.1 %collective-permute-start.16 = (bf16[2,2,128,640]{3,2,1,0:T(8,128)(2,1)S(1)}, bf16[2,2,128,640]{3,2,1,0:T(8,128)(2,1)S(1)}, u32[]{:S(2)}, u32[]{:S(2)}) collective-permute-start(bf16[2,2,128,640]{3,2,1,0:T(8,128)(2,1)S(1)} %pad_maximum_fusion.refs_13_.refs_0_), channel_id=1, source_target_pairs={{0,1},{1,0},{2,3},{3,2},{4,5},{5,4},{6,7},{7,6},{8,9},{9,8},{10,11... | collective-permute-start | bytes 1966088 | tf_op jit(solution)/shard_map/ppermute | solution.py:81
  48.4 6.0 %collective-permute-start.12 = (bf16[4,576,128]{2,1,0:T(8,128)(2,1)S(1)}, bf16[4,576,128]{2,1,0:T(8,128)(2,1)S(1)}, u32[]{:S(2)}, u32[]{:S(2)}) collective-permute-start(bf16[4,576,128]{2,1,0:T(8,128)(2,1)S(1)} %pad_maximum_fusion.3.refs_1_), channel_id=1, source_target_pairs={{0,1},{1,0},{2,3},{3,2},{4,5},{5,4},{6,7},{7,6},{8,9},{9,8},{10,11... | collective-permute-start | bytes 1769480 | tf_op jit(solution)/shard_map/ppermute | solution.py:76
  48.4 6.0 %collective-permute-start.14 = (bf16[4,576,128]{2,1,0:T(8,128)(2,1)S(1)}, bf16[4,576,128]{2,1,0:T(8,128)(2,1)S(1)}, u32[]{:S(2)}, u32[]{:S(2)}) collective-permute-start(bf16[4,576,128]{2,1,0:T(8,128)(2,1)S(1)} %collective-permute-done.6.refs_3_), channel_id=1, source_target_pairs={{0,1},{1,0},{2,3},{3,2},{4,5},{5,4},{6,7},{7,6},{8,9},{9,8},{10,11... | collective-permute-start | bytes 1769480 | tf_op jit(solution)/shard_map/ppermute | solution.py:76
  92.5 4.3 %collective-permute-start.25 = (bf16[2,2,128,384]{3,2,1,0:T(8,128)(2,1)S(1)}, bf16[2,2,128,384]{3,2,1,0:T(8,128)(2,1)S(1)}, u32[]{:S(2)}, u32[]{:S(2)}) collective-permute-start(bf16[2,2,128,384]{3,2,1,0:T(8,128)(2,1)S(1)} %get-tuple-element.145), channel_id=1, source_target_pairs={{0,1},{1,0},{2,3},{3,2},{4,5},{5,4},{6,7},{7,6},{8,9},{9,8},{10,11... | collective-permute-start | bytes 1179656 | tf_op jit(solution)/shard_map/ppermute | solution.py:81
  92.7 4.3 %collective-permute-start.24 = (bf16[2304,128]{1,0:T(8,128)(2,1)S(1)}, bf16[2304,128]{1,0:T(8,128)(2,1)S(1)}, u32[]{:S(2)}, u32[]{:S(2)}) collective-permute-start(bf16[2304,128]{1,0:T(8,128)(2,1)S(1)} %get-tuple-element.143), channel_id=1, source_target_pairs={{0,1},{1,0},{2,3},{3,2},{4,5},{5,4},{6,7},{7,6},{8,9},{9,8},{10,11... | collective-permute-start | bytes 1769480 | tf_op jit(solution)/shard_map/ppermute | solution.py:76
  93.0 4.8 %collective-permute-start.23 = (bf16[6912,128]{1,0:T(8,128)(2,1)}, bf16[6912,128]{1,0:T(8,128)(2,1)S(1)}, u32[]{:S(2)}, u32[]{:S(2)}) collective-permute-start(bf16[6912,128]{1,0:T(8,128)(2,1)} %get-tuple-element.139), channel_id=1, source_target_pairs={{0,1},{1,0},{2,3},{3,2},{4,5},{5,4},{6,7},{7,6},{8,9},{9,8},{10,11... | collective-permute-start | bytes 5308424 | tf_op jit(solution)/shard_map/ppermute | solution.py:76
  94.4 15.7 %collective-permute-start.22 = (bf16[2304,128]{1,0:T(8,128)(2,1)S(1)}, bf16[2304,128]{1,0:T(8,128)(2,1)S(1)}, u32[]{:S(2)}, u32[]{:S(2)}) collective-permute-start(bf16[2304,128]{1,0:T(8,128)(2,1)S(1)} %add_convert_fusion.5), channel_id=1, source_target_pairs={{0,4},{1,5},{2,6},{3,7},{4,0},{5,1},{6,2},{7,3},{8,12},{9,13},{10,... | collective-permute-start | bytes 1769480 | tf_op jit(solution)/shard_map/ppermute | solution.py:76
  96.2 15.6 %collective-permute-start.21 = (bf16[2352,128]{1,0:T(8,128)(2,1)S(1)}, bf16[2352,128]{1,0:T(8,128)(2,1)S(1)}, u32[]{:S(2)}, u32[]{:S(2)}) collective-permute-start(bf16[2352,128]{1,0:T(8,128)(2,1)S(1)} %pad_maximum_fusion.1), channel_id=1, source_target_pairs={{0,2},{1,3},{2,0},{3,1},{4,6},{5,7},{6,4},{7,5},{8,10},{9,11},{10,... | collective-permute-start | bytes 1806344 | tf_op jit(solution)/shard_map/ppermute | solution.py:76
  112.1 18.6 %collective-permute-start.26 = (bf16[2352,128]{1,0:T(8,128)(2,1)S(1)}, bf16[2352,128]{1,0:T(8,128)(2,1)S(1)}, u32[]{:S(2)}, u32[]{:S(2)}) collective-permute-start(bf16[2352,128]{1,0:T(8,128)(2,1)S(1)} %pad_maximum_fusion.2), channel_id=1, source_target_pairs={{0,4},{1,5},{2,6},{3,7},{4,0},{5,1},{6,2},{7,3},{8,12},{9,13},{10,... | collective-permute-start | bytes 1806344 | tf_op jit(solution)/shard_map/ppermute | solution.py:76
  112.7 18.0 %collective-permute-start.27 = (bf16[2304,128]{1,0:T(8,128)(2,1)}, bf16[2304,128]{1,0:T(8,128)(2,1)S(1)}, u32[]{:S(2)}, u32[]{:S(2)}) collective-permute-start(bf16[2304,128]{1,0:T(8,128)(2,1)} %get-tuple-element.149), channel_id=1, source_target_pairs={{0,2},{1,3},{2,0},{3,1},{4,6},{5,7},{6,4},{7,5},{8,10},{9,11},{10,... | collective-permute-start | bytes 1769480 | tf_op jit(solution)/shard_map/ppermute | solution.py:76
  115.2 7.2 %collective-permute-start.28 = (bf16[576,128]{1,0:T(8,128)(2,1)}, bf16[576,128]{1,0:T(8,128)(2,1)S(1)}, u32[]{:S(2)}, u32[]{:S(2)}) collective-permute-start(bf16[576,128]{1,0:T(8,128)(2,1)} %get-tuple-element.213), channel_id=1, source_target_pairs={{0,8},{1,9},{2,10},{3,11},{4,12},{5,13},{6,14},{7,15},{8,0},{9,1},... | collective-permute-start | bytes 442376 | tf_op jit(solution)/shard_map/ppermute | solution.py:76
  117.5 13.1 %collective-permute-start.29 = (bf16[576,128]{1,0:T(8,128)(2,1)}, bf16[576,128]{1,0:T(8,128)(2,1)S(1)}, u32[]{:S(2)}, u32[]{:S(2)}) collective-permute-start(bf16[576,128]{1,0:T(8,128)(2,1)} %get-tuple-element.212), channel_id=1, source_target_pairs={{0,16},{1,17},{2,18},{3,19},{4,20},{5,21},{6,22},{7,23},{8,24},{9,... | collective-permute-start | bytes 442376 | tf_op jit(solution)/shard_map/ppermute | solution.py:76
  118.3 12.4 %collective-permute-start.30 = (bf16[576,128]{1,0:T(8,128)(2,1)}, bf16[576,128]{1,0:T(8,128)(2,1)S(1)}, u32[]{:S(2)}, u32[]{:S(2)}) collective-permute-start(bf16[576,128]{1,0:T(8,128)(2,1)} %get-tuple-element.211), channel_id=1, source_target_pairs={{0,24},{1,25},{2,26},{3,27},{4,28},{5,29},{6,30},{7,31},{8,16},{9,... | collective-permute-start | bytes 442376 | tf_op jit(solution)/shard_map/ppermute | solution.py:76
  132.4 11.9 %collective-permute-start.31 = (bf16[624,128]{1,0:T(8,128)(2,1)S(1)}, bf16[624,128]{1,0:T(8,128)(2,1)S(1)}, u32[]{:S(2)}, u32[]{:S(2)}) collective-permute-start(bf16[624,128]{1,0:T(8,128)(2,1)S(1)} %get-tuple-element.227), channel_id=1, source_target_pairs={{0,8},{1,9},{2,10},{3,11},{4,12},{5,13},{6,14},{7,15},{8,0},{9,1},... | collective-permute-start | bytes 479240 | tf_op jit(solution)/shard_map/ppermute | solution.py:76
  134.6 13.9 %collective-permute-start.32 = (bf16[624,128]{1,0:T(8,128)(2,1)S(1)}, bf16[624,128]{1,0:T(8,128)(2,1)S(1)}, u32[]{:S(2)}, u32[]{:S(2)}) collective-permute-start(bf16[624,128]{1,0:T(8,128)(2,1)S(1)} %get-tuple-element.226), channel_id=1, source_target_pairs={{0,16},{1,17},{2,18},{3,19},{4,20},{5,21},{6,22},{7,23},{8,24},{9,... | collective-permute-start | bytes 479240 | tf_op jit(solution)/shard_map/ppermute | solution.py:76
  135.4 13.1 %collective-permute-start.33 = (bf16[624,128]{1,0:T(8,128)(2,1)S(1)}, bf16[624,128]{1,0:T(8,128)(2,1)S(1)}, u32[]{:S(2)}, u32[]{:S(2)}) collective-permute-start(bf16[624,128]{1,0:T(8,128)(2,1)S(1)} %get-tuple-element.225), channel_id=1, source_target_pairs={{0,24},{1,25},{2,26},{3,27},{4,28},{5,29},{6,30},{7,31},{8,16},{9,... | collective-permute-start | bytes 479240 | tf_op jit(solution)/shard_map/ppermute | solution.py:76
  137.8 10.7 %collective-permute-start.35 = (bf16[2,128,384]{2,1,0:T(8,128)(2,1)S(1)}, bf16[2,128,384]{2,1,0:T(8,128)(2,1)S(1)}, u32[]{:S(2)}, u32[]{:S(2)}) collective-permute-start(bf16[2,128,384]{2,1,0:T(8,128)(2,1)S(1)} %get-tuple-element.221), channel_id=1, source_target_pairs={{0,2},{1,3},{2,0},{3,1},{4,6},{5,7},{6,4},{7,5},{8,10},{9,11},{10,... | collective-permute-start | bytes 589832 | tf_op jit(solution)/shard_map/ppermute | solution.py:81
  139.8 4.4 %collective-permute-start.34 = (bf16[288,128]{1,0:T(8,128)(2,1)S(1)}, bf16[288,128]{1,0:T(8,128)(2,1)S(1)}, u32[]{:S(2)}, u32[]{:S(2)}) collective-permute-start(bf16[288,128]{1,0:T(8,128)(2,1)S(1)} %get-tuple-element.219), channel_id=1, source_target_pairs={{0,2},{1,3},{2,0},{3,1},{4,6},{5,7},{6,4},{7,5},{8,10},{9,11},{10,... | collective-permute-start | bytes 221192 | tf_op jit(solution)/shard_map/ppermute | solution.py:76
  (40 other events, 238.6 us)

commit v8 on v6

--- a/solution.py
+++ b/solution.py
@@ -29,6 +29,7 @@
 HEAD_ROWS = 576
 TAIL_ROWS = BLOCK_ROWS - HEAD_ROWS
 VECTOR_ROWS = 24
+STEP_ROWS = 432
 PART = 4 * HEAD_ROWS
 FIRST_AT = 4 * PART
 TAIL_AT = FIRST_AT + PART + 2 * VECTOR_ROWS
@@ -84,32 +85,34 @@
     return lax.optimization_barrier(arrays)
 
 
+def gather_at_once(rows):
+    if inner_count() == 1:
+        return lax.all_gather(rows, ("dp", "ctx"))
+    data_count, data_inner = lax.axis_size("dp"), inner_count() // lax.axis_size("ctx")
+    groups = [list(range(k, data_count, data_inner)) for k in range(data_inner)]
+    return lax.all_gather(rows, "dp", axis_index_groups=groups)
+
+
 def gather_all(head, tail, packed, others):
+    tails = gather_at_once(tail)
     hz = [moved(head, "z", s) for s in (1, 2, 3)]
-    tx = moved(tail, "x", 1)
     two = across(packed, 2)
-    head, tail, tx, two, *hz = together(head, tail, tx, two, *hz)
+    head, two, *hz = together(head, two, *hz)
     own = jnp.stack([head] + hz)
-    pair = jnp.stack([tail, tx])
     ay = moved(own, "y", 1)
     ax = moved(own, "x", 1)
-    tz = [moved(pair, "z", s) for s in (1, 2, 3)]
+    ac = moved(own, "c", 1)
     near = jnp.stack([packed, two])
     tables = place_tables(near)
-    own, pair, ay, ax, near, tables, others, *tz = together(own, pair, ay, ax, near, tables, others, *tz)
-    eight = jnp.concatenate([pair] + tz)
+    own, ay, ax, near, tables, others = together(own, ay, ax, near, tables, others)
     far = across(near, 1)
     axy = moved(ay, "x", 1)
-    ty = moved(eight, "y", 1)
-    ac = moved(own, "c", 1)
     acy = moved(ay, "c", 1)
     acx = moved(ax, "c", 1)
-    tc = moved(eight, "c", 1)
-    axy, ty, ac, acy, acx, tc, far = together(axy, ty, ac, acy, acx, tc, far)
+    axy, acy, acx, far = together(axy, acy, acx, far)
     acxy = moved(axy, "c", 1)
-    tcy = moved(ty, "c", 1)
     heads = [own, ay, ax, axy, ac, acy, acx, acxy]
-    return heads, [eight, ty, tc, tcy], (near, far), tables, others
+    return heads, tails, (near, far), tables, others
 
 
 def places_of(tokens):
@@ -143,10 +146,9 @@
 def slot_table():
     mine = coordinates(device_number() // inner_count())
     entries = []
-    for order in (("c", "x", "y", "z"), ("c", "y", "z", "x")):
-        for number in range(BLOCKS):
-            found = coordinates(number)
-            entries.append(fold(order, {n: (mine[n] - found[n]) % SIZES[n] for n in SIZES}))
+    for number in range(BLOCKS):
+        found = coordinates(number)
+        entries.append(fold(("c", "x", "y", "z"), {n: (mine[n] - found[n]) % SIZES[n] for n in SIZES}))
     for order, start in ((("x", "y"), head_row), (("y",), tail_row)):
         for number in range(0, BLOCKS, 2):
             found = coordinates(number)
@@ -158,8 +160,7 @@
     return jnp.stack([jnp.asarray(entry, jnp.int32) for entry in entries])
 
 
-AT_HEAD, AT_TAIL, TO_HEAD, TO_TAIL = 0, BLOCKS, 2 * BLOCKS, 2 * BLOCKS + 16
-MY_CORE, MY_Z = 2 * BLOCKS + 32, 2 * BLOCKS + 33
+AT_HEAD, TO_HEAD, TO_TAIL, MY_CORE, MY_Z = 0, BLOCKS, BLOCKS + 16, BLOCKS + 32, BLOCKS + 33
 
 
 def summed(*parts):
@@ -261,16 +262,16 @@
         narrow[pl.ds(1, 288, stride=2), :] = second
         tiles[576:864, :] = side_by_side(narrow[0:288, :], narrow[288:576, :])
 
-    head_ref[...] = tiles[0:HEAD_ROWS, :].astype(BF16)
-    tail_ref[...] = tiles[HEAD_ROWS:BLOCK_ROWS, :].astype(BF16)
+    head_ref[...] = tiles[0:STEP_ROWS, :].astype(BF16)
+    tail_ref[...] = tiles[STEP_ROWS:BLOCK_ROWS, :].astype(BF16)
 
 
 def to_tiles(kind, flat):
     return pl.pallas_call(
         tile_kernel,
         out_shape=(
-            jax.ShapeDtypeStruct((HEAD_ROWS, LANES), BF16),
-            jax.ShapeDtypeStruct((TAIL_ROWS, LANES), BF16),
+            jax.ShapeDtypeStruct((STEP_ROWS, LANES), BF16),
+            jax.ShapeDtypeStruct((BLOCK_ROWS - STEP_ROWS, LANES), BF16),
         ),
         in_specs=[
             pl.BlockSpec(memory_space=pltpu.SMEM),
@@ -417,11 +418,10 @@
     return value * scale, scale
 
 
-def place_rows(ref, head_tile, tail_tile, first):
-    for j in range(3):
-        ref[first : first + 192, LANES * j : LANES * j + LANES] = head_tile[192 * j : 192 * j + 192, :]
-    ref[first : first + 192, 384:512] = tail_tile[0:192, :]
-    rest = tail_tile[192:288, :].astype(F32)
+def place_rows(ref, read, first):
+    for j in range(4):
+        ref[first : first + 192, LANES * j : LANES * j + LANES] = read(192 * j, 192 * j + 192)
+    rest = read(768, 864).astype(F32)
     low = lower_lanes(rest.shape)
     ref[first : first + 96, 512:640] = jnp.where(low, rest, 0.0).astype(BF16)
     ref[first + 96 : first + 192, 512:640] = jnp.where(low, half_turn(rest), 0.0).astype(BF16)
@@ -436,27 +436,26 @@
 def layer_kernel(*refs):
     slots = refs[0]
     head_parts = refs[1:9]
-    tail_parts = refs[9:13]
-    tokens_pair, cos_pair, sin_pair = refs[13:15], refs[15:17], refs[17:19]
-    (place_q_ref, place_k_ref, gains_ref, bias_q_ref, bias_kv_ref, grad_ref) = refs[19:25]
-    block_out_ref, parts_out = refs[25], refs[26:36]
-    (dkv_send, dkv_keep, dq_wq_ref, d_mid_ref, w_kv) = refs[36:41]
-    (raw_head, raw_tail, w_q, w_out, w_gate, w_up, w_down, normed_all, hidden_all, keys, values, queries, probs, attended, act_all, block_acc, d_hidden, d_attended, dkv_all, d_query, send_all, keep_all, vector_ref, outs, sems, out_sems) = refs[41:]
+    tail_part = refs[9]
+    tokens_pair, cos_pair, sin_pair = refs[10:12], refs[12:14], refs[14:16]
+    (place_q_ref, place_k_ref, gains_ref, bias_q_ref, bias_kv_ref, grad_ref) = refs[16:22]
+    block_out_ref, parts_out = refs[22], refs[23:33]
+    (dkv_send, dkv_keep, dq_wq_ref, d_mid_ref, w_kv) = refs[33:38]
+    (raw_head, raw_tail, w_q, w_out, w_gate, w_up, w_down, normed_all, hidden_all, keys, values, queries, probs, attended, act_all, block_acc, d_hidden, d_attended, dkv_all, d_query, send_all, keep_all, vector_ref, outs, sems, out_sems) = refs[38:]
 
     place = slots[MY_Z]
 
     def fetches(shift, sem):
         at = lax.rem(place + shift, 4)
-        copies = []
-        for k, part in enumerate(head_parts):
-            copies.append(pltpu.make_async_copy(part.at[at], raw_head.at[4 * k + at], sems.at[sem + k]))
-        for k, part in enumerate(tail_parts):
-            rows = pl.ds(2 * at, 2)
-            copies.append(pltpu.make_async_copy(part.at[rows], raw_tail.at[pl.ds(8 * k + 2 * at, 2)], sems.at[sem + 8 + k]))
-        return copies
+        return [
+            pltpu.make_async_copy(part.at[at], raw_head.at[4 * k + at], sems.at[sem + k])
+            for k, part in enumerate(head_parts)
+        ]
 
     attention_blocks = fetches(0, 0)
-    other_blocks = fetches(1, 12) + fetches(2, 24) + fetches(3, 36)
+    attention_blocks.append(pltpu.make_async_copy(tail_part.at[pl.ds(0, 8)], raw_tail.at[pl.ds(0, 8)], sems.at[32]))
+    other_blocks = fetches(1, 8) + fetches(2, 16) + fetches(3, 24)
+    other_blocks.append(pltpu.make_async_copy(tail_part.at[pl.ds(8, 24)], raw_tail.at[pl.ds(8, 24)], sems.at[33]))
     for copy in attention_blocks + other_blocks:
         copy.start()
 
@@ -465,11 +464,16 @@
     def at_slot(pair, slot):
         return pair[slot % 2].at[slot // 2]
 
-    def head_tile(block):
-        return raw_head.at[slots[AT_HEAD + block]]
-
-    def tail_tile(block):
-        return raw_tail.at[slots[AT_TAIL + block]]
+    def reader(block):
+        def read(first, last):
+            parts = []
+            if first < STEP_ROWS:
+                parts.append(raw_head[slots[AT_HEAD + block], first : min(last, STEP_ROWS), :])
+            if last > STEP_ROWS:
+                parts.append(raw_tail[block, max(first, STEP_ROWS) - STEP_ROWS : last - STEP_ROWS, :])
+            return parts[0] if len(parts) == 1 else jnp.concatenate(parts, axis=0)
+
+        return read
 
     gain_one = gains_ref[0:1, :]
     gain_two = gains_ref[1:2, :]
@@ -490,12 +494,13 @@
     for ref in (w_q, w_out, w_gate, w_up, w_kv):
         ref[576:640, :] = jnp.zeros((64, ref.shape[1]), BF16)
     for k in range(3):
-        place_rows(w_q, head_tile(k), tail_tile(k), 192 * k)
-        place_rows(w_out, head_tile(5 + k), tail_tile(5 + k), 192 * k)
-    w_kv[0:576, 0:128] = head_tile(3)[...]
-    w_kv[0:576, 128:256] = head_tile(4)[...]
-    rest_key = tail_tile(3)[...].astype(F32)
-    rest_value = tail_tile(4)[...].astype(F32)
+        place_rows(w_q, reader(k), 192 * k)
+        place_rows(w_out, reader(5 + k), 192 * k)
+    for at in range(0, 576, 144):
+        w_kv[at : at + 144, 0:128] = reader(3)(at, at + 144)
+        w_kv[at : at + 144, 128:256] = reader(4)(at, at + 144)
+    rest_key = reader(3)(576, 864).astype(F32)
+    rest_value = reader(4)(576, 864).astype(F32)
     low = lower_lanes(rest_key.shape)
     w_kv[0:288, 256:384] = jnp.where(low, rest_key, half_turn(rest_value)).astype(BF16)
     w_kv[288:576, 256:384] = jnp.where(low, half_turn(rest_key), rest_value).astype(BF16)
@@ -561,16 +566,12 @@
     for copy in other_blocks:
         copy.wait()
     for k in range(8):
-        place_rows(w_down, head_tile(24 + k), tail_tile(24 + k), 192 * k)
+        place_rows(w_down, reader(24 + k), 192 * k)
     for ref, base in ((w_gate, 8), (w_up, 16)):
         for k in range(4):
             for i in range(6):
-                if i < 4:
-                    even = head_tile(base + 2 * k)[144 * i : 144 * i + 144, :].astype(F32)
-                    odd = head_tile(base + 2 * k + 1)[144 * i : 144 * i + 144, :].astype(F32)
-                else:
-                    even = tail_tile(base + 2 * k)[144 * (i - 4) : 144 * (i - 4) + 144, :].astype(F32)
-                    odd = tail_tile(base + 2 * k + 1)[144 * (i - 4) : 144 * (i - 4) + 144, :].astype(F32)
+                even = reader(base + 2 * k)(144 * i, 144 * i + 144).astype(F32)
+                odd = reader(base + 2 * k + 1)(144 * i, 144 * i + 144).astype(F32)
                 ref[144 * k : 144 * k + 144, 256 * i : 256 * i + 128] = jnp.concatenate(
                     [even[0:72], odd[0:72]], axis=0
                 ).astype(BF16)
@@ -765,8 +766,8 @@
     vmem = pl.BlockSpec(memory_space=pltpu.VMEM)
     anywhere = pl.BlockSpec(memory_space=pl.ANY)
     scratch = [
-        ((BLOCKS, HEAD_ROWS, LANES), BF16),
-        ((BLOCKS, TAIL_ROWS, LANES), BF16),
+        ((BLOCKS, STEP_ROWS, LANES), BF16),
+        ((BLOCKS, BLOCK_ROWS - STEP_ROWS, LANES), BF16),
         ((WIDE, WIDE), BF16),
         ((WIDE, WIDE), BF16),
         ((WIDE, FF), BF16),
@@ -801,13 +802,13 @@
             shape((256, WIDE), F32),
             shape((WIDE, 384), BF16),
         ),
-        in_specs=[pl.BlockSpec(memory_space=pltpu.SMEM)] + [anywhere] * 12 + [vmem] * 12,
+        in_specs=[pl.BlockSpec(memory_space=pltpu.SMEM)] + [anywhere] * 9 + [vmem] * 12,
         out_specs=(vmem,) + (anywhere,) * 10 + (vmem,) * 5,
         scratch_shapes=[pltpu.VMEM(dims, kind) for dims, kind in scratch]
         + [pltpu.SemaphoreType.DMA((48,)), pltpu.SemaphoreType.DMA((26,))],
         compiler_params=pltpu.CompilerParams(vmem_limit_bytes=50 * 1024 * 1024),
         name="layer",
-    )(slots, *heads, *tails, *others)
+    )(slots, *heads, tails, *others)
 
 
 def adamw(param, grad, mom_one, mom_two, rate, decay):

time: 151 us -> 176 us (1.17)
  waiting for transfers between devices: 54.5 us -> 71.7 us
  between operations: 1.88 us -> 14.5 us
  starting transfers between devices: 36.7 us -> 31.2 us
    all_gather x0 -> x1, waiting for transfers between devices: none -> 21.6 us  [gather_at_once(): return lax.all_gather(rows, ('dp', 'ctx'))]
    ppermute x32 -> x25, starting transfers between devices: 34.9 us -> 28.7 us  [moved(): return lax.ppermute(buffer, ('dp', 'ctx'), pairs)]
    ppermute x32 -> x25, waiting for transfers between devices: 46.2 us -> 41.3 us  [moved(): return lax.ppermute(buffer, ('dp', 'ctx'), pairs)]
    unnamed x80 -> x57, local copies, waits for them, and re-layouts: 3.86 us -> 3.77 us
  transfers between devices with their start and end apart: 36 -> 30, of which waited for: 18 -> 12; matrix products, arithmetic and copies ran while one was open for 9% -> 8% of each run, Pallas kernels for 0% -> 0%
where the time goes in v8:
time: 176 us; the launch traced here: 175 us
  waiting for transfers between devices  71.7 us (41%)
  Pallas kernels  36.3 us (21%)
  starting transfers between devices  31.2 us (18%)
  between operations  14.5 us (8%)
  other arithmetic  12.6 us (7%)
  local copies, waits for them, and re-layouts  8.33 us (5%)
    ppermute x25, waiting for transfers between devices, moved(): return lax.ppermute(buffer, ('dp', 'ctx'), pairs)  41.3 us
    pallas_call x1, Pallas kernels, run_layer(): pl.pallas_call(layer_kernel, out_shape=(shape((2, MODEL_WIDTH, ROWS), BF1...  29.4 us
    ppermute x25, starting transfers between devices, moved(): return lax.ppermute(buffer, ('dp', 'ctx'), pairs)  28.7 us
    all_gather x1, waiting for transfers between devices, gather_at_once(): return lax.all_gather(rows, ('dp', 'ctx'))  21.6 us
    ppermute x4, waiting for transfers between devices, across(): lax.ppermute(buffer, 'ctx', [(i, i ^ distance) for i in range(count)])  8.76 us
    pallas_call x1, Pallas kernels, finish(): pl.pallas_call(finish_kernel, out_shape=shapes, in_specs=[pl.BlockSpec(me...  5.05 us
    unnamed x57, local copies, waits for them, and re-layouts  3.77 us
  transfers between devices with their start and end apart: 30, of which 12 were waited for; matrix products, arithmetic and copies ran while one was open for 8% of the time, Pallas kernels for 0%

profile of v8, /device:TPU:0, one launch (start us, length us, event | category | flops | bytes accessed | tf_op | source)
XLA Modules:
  0.0 174.6 jit_solution(3382843487635704559)
XLA Ops:
  7.2 1.9 %to_tiles.1 = (bf16[432,128]{1,0:T(8,128)(2,1)}, bf16[432,128]{1,0:T(8,128)(2,1)}) custom-call(s32[1]{0:T(128)} %bitcast.kind_ref, f32[864,128]{1,0:T(8,128)} %bitcast.122), custom_call_target="tpu_custom_call" | custom-call | tf_op jit(solution)/shard_map/to_tiles/pallas_call | solution.py:270
  9.1 3.0 %collective-permute-start.1 = (bf16[432,128]{1,0:T(8,128)(2,1)}, bf16[432,128]{1,0:T(8,128)(2,1)S(1)}, u32[]{:S(2)}, u32[]{:S(2)}) collective-permute-start(bf16[432,128]{1,0:T(8,128)(2,1)} %get-tuple-element.88), channel_id=1, source_target_pairs={{0,8},{1,9},{2,10},{3,11},{4,12},{5,13},{6,14},{7,15},{8,16},{9,17... | collective-permute-start | bytes 331784 | tf_op jit(solution)/shard_map/ppermute | solution.py:76
  12.1 2.7 %collective-permute-start.2 = (bf16[432,128]{1,0:T(8,128)(2,1)}, bf16[432,128]{1,0:T(8,128)(2,1)S(1)}, u32[]{:S(2)}, u32[]{:S(2)}) collective-permute-start(bf16[432,128]{1,0:T(8,128)(2,1)} %get-tuple-element.88), channel_id=1, source_target_pairs={{0,16},{1,17},{2,18},{3,19},{4,20},{5,21},{6,22},{7,23},{8,24},{9,... | collective-permute-start | bytes 331784 | tf_op jit(solution)/shard_map/ppermute | solution.py:76
  14.8 1.2 collective-permute-start.3
  16.9 1.2 copy.39
  18.4 1.6 collective-permute-start
  22.8 5.1 %collective-permute-done = bf16[2,128,640]{2,1,0:T(8,128)(2,1)S(1)} collective-permute-done((bf16[2,128,640]{2,1,0:T(8,128)(2,1)S(1)}, bf16[2,128,640]{2,1,0:T(8,128)(2,1)S(1)}, u32[]{:S(2)}, u32[]{:S(2)}) %collective-permute-start) | collective-permute-done | bytes 327712 | tf_op jit(solution)/shard_map/ppermute | solution.py:81
  28.0 1.6 collective-permute-start.4
  29.6 1.5 collective-permute-start.5
  32.5 4.9 %collective-permute-done.4.refs_2_ = bf16[4,432,128]{2,1,0:T(8,128)(2,1)S(1)} collective-permute-done((bf16[4,432,128]{2,1,0:T(8,128)(2,1)S(1)}, bf16[4,432,128]{2,1,0:T(8,128)(2,1)S(1)}, u32[]{:S(2)}, u32[]{:S(2)}) %collective-permute-start.4) | collective-permute-done | bytes 442400 | tf_op jit(solution)/shard_map/ppermute | solution.py:76
  37.4 2.2 %collective-permute-done.5.refs_3_ = bf16[4,432,128]{2,1,0:T(8,128)(2,1)S(1)} collective-permute-done((bf16[4,432,128]{2,1,0:T(8,128)(2,1)S(1)}, bf16[4,432,128]{2,1,0:T(8,128)(2,1)S(1)}, u32[]{:S(2)}, u32[]{:S(2)}) %collective-permute-start.5) | collective-permute-done | bytes 442400 | tf_op jit(solution)/shard_map/ppermute | solution.py:76
  39.6 1.7 collective-permute-start.6
  42.3 9.4 %collective-permute-done.6.refs_4_ = bf16[4,432,128]{2,1,0:T(8,128)(2,1)S(1)} collective-permute-done((bf16[4,432,128]{2,1,0:T(8,128)(2,1)S(1)}, bf16[4,432,128]{2,1,0:T(8,128)(2,1)S(1)}, u32[]{:S(2)}, u32[]{:S(2)}) %collective-permute-start.6) | collective-permute-done | bytes 442400 | tf_op jit(solution)/shard_map/ppermute | solution.py:76
  54.1 21.6 %all-gather.3.cloned.1.call-done = bf16[13824,128]{1,0:T(8,128)(2,1)} async-done(((bf16[432,128]{1,0:T(8,128)(2,1)}), bf16[13824,128]{1,0:T(8,128)(2,1)}) %all-gather.3.cloned.1.call-update) | async-done | bytes 3538960 | tf_op jit(solution)/shard_map/all_gather | solution.py:90
  75.7 29.4 %layer.1 = (bf16[2,576,128]{2,1,0:T(8,128)(2,1)}, bf16[2352,128]{1,0:T(8,128)(2,1)}, bf16[2304,128]{1,0:T(8,128)(2,1)}, bf16[6912,128]{1,0:T(8,128)(2,1)}, bf16[...) custom-call(s32[66]{0:T(128)S(1)} %stack.308.refs_0_, ...), custom_call_target="tpu_custom_call" | custom-call | tf_op jit(solution)/shard_map/layer/pallas_call | solution.py:794
  105.6 2.6 %collective-permute-done.13 = bf16[2304,128]{1,0:T(8,128)(2,1)S(1)} collective-permute-done((bf16[2304,128]{1,0:T(8,128)(2,1)}, bf16[2304,128]{1,0:T(8,128)(2,1)S(1)}, u32[]{:S(2)}, u32[]{:S(2)}) %collective-permute-start.13) | collective-permute-done | bytes 589856 | tf_op jit(solution)/shard_map/ppermute | solution.py:76
  108.9 1.4 add_convert_fusion.6
  110.3 1.5 collective-permute-start.14
  113.3 3.7 %collective-permute-done.18 = bf16[2,2,128,384]{3,2,1,0:T(8,128)(2,1)S(1)} collective-permute-done((bf16[2,2,128,384]{3,2,1,0:T(8,128)(2,1)S(1)}, bf16[2,2,128,384]{3,2,1,0:T(8,128)(2,1)S(1)}, u32[]{:S(2)}, u32[]{:S(2)}) %collective-permute-start.18) | collective-permute-done | bytes 393248 | tf_op jit(solution)/shard_map/ppermute | solution.py:81
  118.5 1.3 add_convert_fusion.2
  119.8 8.6 %collective-permute-done.15 = bf16[2304,128]{1,0:T(8,128)(2,1)S(1)} collective-permute-done((bf16[2304,128]{1,0:T(8,128)(2,1)S(1)}, bf16[2304,128]{1,0:T(8,128)(2,1)S(1)}, u32[]{:S(2)}, u32[]{:S(2)}) %collective-permute-start.15) | collective-permute-done | bytes 589856 | tf_op jit(solution)/shard_map/ppermute | solution.py:76
  129.2 1.5 collective-permute-start.20
  130.7 2.0 %add_convert_fusion.11 = (bf16[576,128]{1,0:T(8,128)(2,1)}, bf16[576,128]{1,0:T(8,128)(2,1)}, bf16[576,128]{1,0:T(8,128)(2,1)}, bf16[576,128]{1,0:T(8,128)(2,1)S(1)}) fusion(bf16[2304,128]{1,0:T(8,128)(2,1)} %copy-done.5, s32[]{:T(128)S(6)} %select_n.682, bf16[2304,128]{1,0:T(8,128)(2,1)S(1)} %add_convert_fusion.1, s32[]{:T(128)S(6)} %select_n.680, ...), kind=kLoop, calls=%fused_computation.23 | loop fusion | flops 1179648 | bytes 1769488 | tf_op jit(solution)/shard_map/convert_element_type | solution.py:204
  133.6 1.7 collective-permute-start.22
  135.4 1.4 collective-permute-start.23
  136.7 4.8 %collective-permute-done.21 = bf16[576,128]{1,0:T(8,128)(2,1)S(1)} collective-permute-done((bf16[576,128]{1,0:T(8,128)(2,1)}, bf16[576,128]{1,0:T(8,128)(2,1)S(1)}, u32[]{:S(2)}, u32[]{:S(2)}) %collective-permute-start.21) | collective-permute-done | bytes 147488 | tf_op jit(solution)/shard_map/ppermute | solution.py:76
  141.6 4.5 %collective-permute-done.22 = bf16[576,128]{1,0:T(8,128)(2,1)S(1)} collective-permute-done((bf16[576,128]{1,0:T(8,128)(2,1)}, bf16[576,128]{1,0:T(8,128)(2,1)S(1)}, u32[]{:S(2)}, u32[]{:S(2)}) %collective-permute-start.22) | collective-permute-done | bytes 147488 | tf_op jit(solution)/shard_map/ppermute | solution.py:76
  147.8 3.3 %collective-permute-start.24 = (bf16[624,128]{1,0:T(8,128)(2,1)S(1)}, bf16[624,128]{1,0:T(8,128)(2,1)S(1)}, u32[]{:S(2)}, u32[]{:S(2)}) collective-permute-start(bf16[624,128]{1,0:T(8,128)(2,1)S(1)} %get-tuple-element.209), channel_id=1, source_target_pairs={{0,8},{1,9},{2,10},{3,11},{4,12},{5,13},{6,14},{7,15},{8,16},{9,17... | collective-permute-start | bytes 479240 | tf_op jit(solution)/shard_map/ppermute | solution.py:76
  151.9 1.6 collective-permute-start.26
  155.7 1.2 collective-permute-start.27
  157.6 4.2 %collective-permute-done.27.other_ref = bf16[288,128]{1,0:T(8,128)(2,1)S(1)} collective-permute-done((bf16[288,128]{1,0:T(8,128)(2,1)S(1)}, bf16[288,128]{1,0:T(8,128)(2,1)S(1)}, u32[]{:S(2)}, u32[]{:S(2)}) %collective-permute-start.27) | collective-permute-done | bytes 73760 | tf_op jit(solution)/shard_map/ppermute | solution.py:76
  162.7 5.0 %finish.1 = (f32[24,128]{1,0:T(8,128)}, f32[24,128]{1,0:T(8,128)}, f32[24,128]{1,0:T(8,128)}, f32[864,128]{1,0:T(8,128)}, f32[864,128]{1,0:T(8,128)}, /*index=5*/f32[864,128]{1,0:T(8,128)}, bf16[2,576,128]{2,1,0:T(8,128)(2,1)}) custom-call(s32[2]{0:T(128)} %pad_add_fusion.table_ref, f32[576,128]{1,0:T(8,128)} %get-tuple-element.187.head_ref, ...), custom_call_target="tpu_custom_call" | custom-call | tf_op jit(solution)/shard_map/finish/pallas_call | solution.py:372
  (149 shorter events, 20.8 us)
Async XLA Ops:
  7.2 68.5 %all-gather.3.cloned.1.call-start = ((), (), s32[]{:S(2)}) async-start(), calls=%async_computation | async-start | bytes 3649536 | tf_op jit(solution)/shard_map/all_gather | solution.py:90
  9.1 13.7 %collective-permute-start.1 = (bf16[432,128]{1,0:T(8,128)(2,1)}, bf16[432,128]{1,0:T(8,128)(2,1)S(1)}, u32[]{:S(2)}, u32[]{:S(2)}) collective-permute-start(bf16[432,128]{1,0:T(8,128)(2,1)} %get-tuple-element.88), channel_id=1, source_target_pairs={{0,8},{1,9},{2,10},{3,11},{4,12},{5,13},{6,14},{7,15},{8,16},{9,17... | collective-permute-start | bytes 331784 | tf_op jit(solution)/shard_map/ppermute | solution.py:76
  12.1 10.7 %collective-permute-start.2 = (bf16[432,128]{1,0:T(8,128)(2,1)}, bf16[432,128]{1,0:T(8,128)(2,1)S(1)}, u32[]{:S(2)}, u32[]{:S(2)}) collective-permute-start(bf16[432,128]{1,0:T(8,128)(2,1)} %get-tuple-element.88), channel_id=1, source_target_pairs={{0,16},{1,17},{2,18},{3,19},{4,20},{5,21},{6,22},{7,23},{8,24},{9,... | collective-permute-start | bytes 331784 | tf_op jit(solution)/shard_map/ppermute | solution.py:76
  14.8 8.0 %collective-permute-start.3 = (bf16[432,128]{1,0:T(8,128)(2,1)}, bf16[432,128]{1,0:T(8,128)(2,1)S(1)}, u32[]{:S(2)}, u32[]{:S(2)}) collective-permute-start(bf16[432,128]{1,0:T(8,128)(2,1)} %get-tuple-element.88), channel_id=1, source_target_pairs={{0,24},{1,25},{2,26},{3,27},{4,28},{5,29},{6,30},{7,31},{8,0},{9,1... | collective-permute-start | bytes 331784 | tf_op jit(solution)/shard_map/ppermute | solution.py:76
  18.4 9.5 %collective-permute-start = (bf16[2,128,640]{2,1,0:T(8,128)(2,1)S(1)}, bf16[2,128,640]{2,1,0:T(8,128)(2,1)S(1)}, u32[]{:S(2)}, u32[]{:S(2)}) collective-permute-start(bf16[2,128,640]{2,1,0:T(8,128)(2,1)S(1)} %maximum_maximum_fusion), channel_id=1, source_target_pairs={{0,2},{1,3},{2,0},{3,1},{4,6},{5,7},{6,4},{7,5},{8,10},{9,11},{10,... | collective-permute-start | bytes 983048 | tf_op jit(solution)/shard_map/ppermute | solution.py:81
  20.2 55.4 %copy-start = (f32[2,640]{1,0:T(2,128)}, f32[2,640]{1,0:T(2,128)S(1)}, u32[]{:S(2)}) copy-start(f32[2,640]{1,0:T(2,128)S(1)} %pad.22.refs_18_.refs_1_) | copy-start | bytes 15364
  28.0 9.4 %collective-permute-start.4 = (bf16[4,432,128]{2,1,0:T(8,128)(2,1)S(1)}, bf16[4,432,128]{2,1,0:T(8,128)(2,1)S(1)}, u32[]{:S(2)}, u32[]{:S(2)}) collective-permute-start(bf16[4,432,128]{2,1,0:T(8,128)(2,1)S(1)} %pad_maximum_fusion.3.refs_1_), channel_id=1, source_target_pairs={{0,4},{1,5},{2,6},{3,7},{4,0},{5,1},{6,2},{7,3},{8,12},{9,13},{10,... | collective-permute-start | bytes 1327112 | tf_op jit(solution)/shard_map/ppermute | solution.py:76
  29.6 10.1 %collective-permute-start.5 = (bf16[4,432,128]{2,1,0:T(8,128)(2,1)S(1)}, bf16[4,432,128]{2,1,0:T(8,128)(2,1)S(1)}, u32[]{:S(2)}, u32[]{:S(2)}) collective-permute-start(bf16[4,432,128]{2,1,0:T(8,128)(2,1)S(1)} %pad_maximum_fusion.3.refs_1_), channel_id=1, source_target_pairs={{0,2},{1,3},{2,0},{3,1},{4,6},{5,7},{6,4},{7,5},{8,10},{9,11},{10,... | collective-permute-start | bytes 1327112 | tf_op jit(solution)/shard_map/ppermute | solution.py:76
  31.1 22.2 %collective-permute-start.10 = (bf16[4,432,128]{2,1,0:T(8,128)(2,1)S(1)}, bf16[4,432,128]{2,1,0:T(8,128)(2,1)S(1)}, u32[]{:S(2)}, u32[]{:S(2)}) collective-permute-start(bf16[4,432,128]{2,1,0:T(8,128)(2,1)S(1)} %pad_maximum_fusion.3.refs_1_), channel_id=1, source_target_pairs={{0,1},{1,0},{2,3},{3,2},{4,5},{5,4},{6,7},{7,6},{8,9},{9,8},{10,11... | collective-permute-start | bytes 1327112 | tf_op jit(solution)/shard_map/ppermute | solution.py:76
  31.5 20.5 %copy-start.1 = (bf16[2,2,128,640]{3,2,1,0:T(8,128)(2,1)}, bf16[2,2,128,640]{3,2,1,0:T(8,128)(2,1)S(1)}, u32[]{:S(2)}) copy-start(bf16[2,2,128,640]{3,2,1,0:T(8,128)(2,1)S(1)} %pad_maximum_fusion.refs_10_.refs_0_) | copy-start | bytes 1966084
  39.6 12.1 %collective-permute-start.6 = (bf16[4,432,128]{2,1,0:T(8,128)(2,1)S(1)}, bf16[4,432,128]{2,1,0:T(8,128)(2,1)S(1)}, u32[]{:S(2)}, u32[]{:S(2)}) collective-permute-start(bf16[4,432,128]{2,1,0:T(8,128)(2,1)S(1)} %collective-permute-done.4.refs_2_), channel_id=1, source_target_pairs={{0,2},{1,3},{2,0},{3,1},{4,6},{5,7},{6,4},{7,5},{8,10},{9,11},{10,... | collective-permute-start | bytes 1327112 | tf_op jit(solution)/shard_map/ppermute | solution.py:76
  41.4 10.3 %collective-permute-start.7 = (bf16[4,432,128]{2,1,0:T(8,128)(2,1)S(1)}, bf16[4,432,128]{2,1,0:T(8,128)(2,1)S(1)}, u32[]{:S(2)}, u32[]{:S(2)}) collective-permute-start(bf16[4,432,128]{2,1,0:T(8,128)(2,1)S(1)} %collective-permute-done.4.refs_2_), channel_id=1, source_target_pairs={{0,1},{1,0},{2,3},{3,2},{4,5},{5,4},{6,7},{7,6},{8,9},{9,8},{10,11... | collective-permute-start | bytes 1327112 | tf_op jit(solution)/shard_map/ppermute | solution.py:76
  41.4 10.3 %collective-permute-start.8 = (bf16[4,432,128]{2,1,0:T(8,128)(2,1)S(1)}, bf16[4,432,128]{2,1,0:T(8,128)(2,1)S(1)}, u32[]{:S(2)}, u32[]{:S(2)}) collective-permute-start(bf16[4,432,128]{2,1,0:T(8,128)(2,1)S(1)} %collective-permute-done.5.refs_3_), channel_id=1, source_target_pairs={{0,1},{1,0},{2,3},{3,2},{4,5},{5,4},{6,7},{7,6},{8,9},{9,8},{10,11... | collective-permute-start | bytes 1327112 | tf_op jit(solution)/shard_map/ppermute | solution.py:76
  41.9 9.9 %collective-permute-start.9 = (bf16[2,2,128,640]{3,2,1,0:T(8,128)(2,1)S(1)}, bf16[2,2,128,640]{3,2,1,0:T(8,128)(2,1)S(1)}, u32[]{:S(2)}, u32[]{:S(2)}) collective-permute-start(bf16[2,2,128,640]{3,2,1,0:T(8,128)(2,1)S(1)} %pad_maximum_fusion.refs_10_.refs_0_), channel_id=1, source_target_pairs={{0,1},{1,0},{2,3},{3,2},{4,5},{5,4},{6,7},{7,6},{8,9},{9,8},{10,11... | collective-permute-start | bytes 1966088 | tf_op jit(solution)/shard_map/ppermute | solution.py:81
  51.8 2.3 %collective-permute-start.11 = (bf16[4,432,128]{2,1,0:T(8,128)(2,1)S(1)}, bf16[4,432,128]{2,1,0:T(8,128)(2,1)}, u32[]{:S(2)}, u32[]{:S(2)}) collective-permute-start(bf16[4,432,128]{2,1,0:T(8,128)(2,1)S(1)} %collective-permute-done.6.refs_4_), channel_id=1, source_target_pairs={{0,1},{1,0},{2,3},{3,2},{4,5},{5,4},{6,7},{7,6},{8,9},{9,8},{10,11... | collective-permute-start | bytes 1327112 | tf_op jit(solution)/shard_map/ppermute | solution.py:76
  105.0 3.1 %collective-permute-start.12 = (bf16[2352,128]{1,0:T(8,128)(2,1)}, bf16[2352,128]{1,0:T(8,128)(2,1)S(1)}, u32[]{:S(2)}, u32[]{:S(2)}) collective-permute-start(bf16[2352,128]{1,0:T(8,128)(2,1)} %get-tuple-element.112), channel_id=1, source_target_pairs={{0,1},{1,0},{2,3},{3,2},{4,5},{5,4},{6,7},{7,6},{8,9},{9,8},{10,11... | collective-permute-start | bytes 1806344 | tf_op jit(solution)/shard_map/ppermute | solution.py:76
  105.4 2.8 %collective-permute-start.13 = (bf16[2304,128]{1,0:T(8,128)(2,1)}, bf16[2304,128]{1,0:T(8,128)(2,1)S(1)}, u32[]{:S(2)}, u32[]{:S(2)}) collective-permute-start(bf16[2304,128]{1,0:T(8,128)(2,1)} %get-tuple-element.113), channel_id=1, source_target_pairs={{0,1},{1,0},{2,3},{3,2},{4,5},{5,4},{6,7},{7,6},{8,9},{9,8},{10,11... | collective-permute-start | bytes 1769480 | tf_op jit(solution)/shard_map/ppermute | solution.py:76
  110.3 18.0 %collective-permute-start.14 = (bf16[2352,128]{1,0:T(8,128)(2,1)S(1)}, bf16[2352,128]{1,0:T(8,128)(2,1)S(1)}, u32[]{:S(2)}, u32[]{:S(2)}) collective-permute-start(bf16[2352,128]{1,0:T(8,128)(2,1)S(1)} %pad_maximum_fusion.1), channel_id=1, source_target_pairs={{0,2},{1,3},{2,0},{3,1},{4,6},{5,7},{6,4},{7,5},{8,10},{9,11},{10,... | collective-permute-start | bytes 1806344 | tf_op jit(solution)/shard_map/ppermute | solution.py:76
  111.8 5.4 %collective-permute-start.16 = (bf16[6912,128]{1,0:T(8,128)(2,1)S(1)}, bf16[6912,128]{1,0:T(8,128)(2,1)S(1)}, u32[]{:S(2)}, u32[]{:S(2)}) collective-permute-start(bf16[6912,128]{1,0:T(8,128)(2,1)S(1)} %copy-done.26), channel_id=1, source_target_pairs={{0,1},{1,0},{2,3},{3,2},{4,5},{5,4},{6,7},{7,6},{8,9},{9,8},{10,11... | collective-permute-start | bytes 5308424 | tf_op jit(solution)/shard_map/ppermute | solution.py:76
  111.8 5.2 %collective-permute-start.17 = (bf16[2304,128]{1,0:T(8,128)(2,1)S(1)}, bf16[2304,128]{1,0:T(8,128)(2,1)S(1)}, u32[]{:S(2)}, u32[]{:S(2)}) collective-permute-start(bf16[2304,128]{1,0:T(8,128)(2,1)S(1)} %copy-done.27), channel_id=1, source_target_pairs={{0,1},{1,0},{2,3},{3,2},{4,5},{5,4},{6,7},{7,6},{8,9},{9,8},{10,11... | collective-permute-start | bytes 1769480 | tf_op jit(solution)/shard_map/ppermute | solution.py:76
  112.4 4.6 %collective-permute-start.18 = (bf16[2,2,128,384]{3,2,1,0:T(8,128)(2,1)S(1)}, bf16[2,2,128,384]{3,2,1,0:T(8,128)(2,1)S(1)}, u32[]{:S(2)}, u32[]{:S(2)}) collective-permute-start(bf16[2,2,128,384]{3,2,1,0:T(8,128)(2,1)S(1)} %get-tuple-element.127), channel_id=1, source_target_pairs={{0,1},{1,0},{2,3},{3,2},{4,5},{5,4},{6,7},{7,6},{8,9},{9,8},{10,11... | collective-permute-start | bytes 1179656 | tf_op jit(solution)/shard_map/ppermute | solution.py:81
  112.6 15.7 %collective-permute-start.15 = (bf16[2304,128]{1,0:T(8,128)(2,1)S(1)}, bf16[2304,128]{1,0:T(8,128)(2,1)S(1)}, u32[]{:S(2)}, u32[]{:S(2)}) collective-permute-start(bf16[2304,128]{1,0:T(8,128)(2,1)S(1)} %add_convert_fusion.5), channel_id=1, source_target_pairs={{0,4},{1,5},{2,6},{3,7},{4,0},{5,1},{6,2},{7,3},{8,12},{9,13},{10,... | collective-permute-start | bytes 1769480 | tf_op jit(solution)/shard_map/ppermute | solution.py:76
  128.6 17.5 %collective-permute-start.19 = (bf16[2352,128]{1,0:T(8,128)(2,1)S(1)}, bf16[2352,128]{1,0:T(8,128)(2,1)S(1)}, u32[]{:S(2)}, u32[]{:S(2)}) collective-permute-start(bf16[2352,128]{1,0:T(8,128)(2,1)S(1)} %pad_maximum_fusion.2), channel_id=1, source_target_pairs={{0,4},{1,5},{2,6},{3,7},{4,0},{5,1},{6,2},{7,3},{8,12},{9,13},{10,... | collective-permute-start | bytes 1806344 | tf_op jit(solution)/shard_map/ppermute | solution.py:76
  129.2 16.8 %collective-permute-start.20 = (bf16[2304,128]{1,0:T(8,128)(2,1)}, bf16[2304,128]{1,0:T(8,128)(2,1)S(1)}, u32[]{:S(2)}, u32[]{:S(2)}) collective-permute-start(bf16[2304,128]{1,0:T(8,128)(2,1)} %get-tuple-element.131), channel_id=1, source_target_pairs={{0,2},{1,3},{2,0},{3,1},{4,6},{5,7},{6,4},{7,5},{8,10},{9,11},{10,... | collective-permute-start | bytes 1769480 | tf_op jit(solution)/shard_map/ppermute | solution.py:76
  132.7 8.9 %collective-permute-start.21 = (bf16[576,128]{1,0:T(8,128)(2,1)}, bf16[576,128]{1,0:T(8,128)(2,1)S(1)}, u32[]{:S(2)}, u32[]{:S(2)}) collective-permute-start(bf16[576,128]{1,0:T(8,128)(2,1)} %get-tuple-element.195), channel_id=1, source_target_pairs={{0,8},{1,9},{2,10},{3,11},{4,12},{5,13},{6,14},{7,15},{8,16},{9,17... | collective-permute-start | bytes 442376 | tf_op jit(solution)/shard_map/ppermute | solution.py:76
  133.6 12.4 %collective-permute-start.22 = (bf16[576,128]{1,0:T(8,128)(2,1)}, bf16[576,128]{1,0:T(8,128)(2,1)S(1)}, u32[]{:S(2)}, u32[]{:S(2)}) collective-permute-start(bf16[576,128]{1,0:T(8,128)(2,1)} %get-tuple-element.194), channel_id=1, source_target_pairs={{0,16},{1,17},{2,18},{3,19},{4,20},{5,21},{6,22},{7,23},{8,24},{9,... | collective-permute-start | bytes 442376 | tf_op jit(solution)/shard_map/ppermute | solution.py:76
  135.4 10.7 %collective-permute-start.23 = (bf16[576,128]{1,0:T(8,128)(2,1)}, bf16[576,128]{1,0:T(8,128)(2,1)S(1)}, u32[]{:S(2)}, u32[]{:S(2)}) collective-permute-start(bf16[576,128]{1,0:T(8,128)(2,1)} %get-tuple-element.193), channel_id=1, source_target_pairs={{0,24},{1,25},{2,26},{3,27},{4,28},{5,29},{6,30},{7,31},{8,0},{9,1... | collective-permute-start | bytes 442376 | tf_op jit(solution)/shard_map/ppermute | solution.py:76
  147.8 14.0 %collective-permute-start.24 = (bf16[624,128]{1,0:T(8,128)(2,1)S(1)}, bf16[624,128]{1,0:T(8,128)(2,1)S(1)}, u32[]{:S(2)}, u32[]{:S(2)}) collective-permute-start(bf16[624,128]{1,0:T(8,128)(2,1)S(1)} %get-tuple-element.209), channel_id=1, source_target_pairs={{0,8},{1,9},{2,10},{3,11},{4,12},{5,13},{6,14},{7,15},{8,16},{9,17... | collective-permute-start | bytes 479240 | tf_op jit(solution)/shard_map/ppermute | solution.py:76
  151.1 10.8 %collective-permute-start.25 = (bf16[624,128]{1,0:T(8,128)(2,1)S(1)}, bf16[624,128]{1,0:T(8,128)(2,1)S(1)}, u32[]{:S(2)}, u32[]{:S(2)}) collective-permute-start(bf16[624,128]{1,0:T(8,128)(2,1)S(1)} %get-tuple-element.208), channel_id=1, source_target_pairs={{0,16},{1,17},{2,18},{3,19},{4,20},{5,21},{6,22},{7,23},{8,24},{9,... | collective-permute-start | bytes 479240 | tf_op jit(solution)/shard_map/ppermute | solution.py:76
  151.9 10.0 %collective-permute-start.26 = (bf16[624,128]{1,0:T(8,128)(2,1)S(1)}, bf16[624,128]{1,0:T(8,128)(2,1)S(1)}, u32[]{:S(2)}, u32[]{:S(2)}) collective-permute-start(bf16[624,128]{1,0:T(8,128)(2,1)S(1)} %get-tuple-element.207), channel_id=1, source_target_pairs={{0,24},{1,25},{2,26},{3,27},{4,28},{5,29},{6,30},{7,31},{8,0},{9,1... | collective-permute-start | bytes 479240 | tf_op jit(solution)/shard_map/ppermute | solution.py:76
  154.2 7.6 %collective-permute-start.28 = (bf16[2,128,384]{2,1,0:T(8,128)(2,1)S(1)}, bf16[2,128,384]{2,1,0:T(8,128)(2,1)S(1)}, u32[]{:S(2)}, u32[]{:S(2)}) collective-permute-start(bf16[2,128,384]{2,1,0:T(8,128)(2,1)S(1)} %get-tuple-element.203), channel_id=1, source_target_pairs={{0,2},{1,3},{2,0},{3,1},{4,6},{5,7},{6,4},{7,5},{8,10},{9,11},{10,... | collective-permute-start | bytes 589832 | tf_op jit(solution)/shard_map/ppermute | solution.py:81
  155.7 6.0 %collective-permute-start.27 = (bf16[288,128]{1,0:T(8,128)(2,1)S(1)}, bf16[288,128]{1,0:T(8,128)(2,1)S(1)}, u32[]{:S(2)}, u32[]{:S(2)}) collective-permute-start(bf16[288,128]{1,0:T(8,128)(2,1)S(1)} %get-tuple-element.201), channel_id=1, source_target_pairs={{0,2},{1,3},{2,0},{3,1},{4,6},{5,7},{6,4},{7,5},{8,10},{9,11},{10,... | collective-permute-start | bytes 221192 | tf_op jit(solution)/shard_map/ppermute | solution.py:76
  (27 other events, 67.5 us)
Sparse Core Ops, SparseCore 0:
  11.5 64.1 all-gather.2

commit v9 on v6

--- a/solution.py
+++ b/solution.py
@@ -288,8 +288,8 @@
 def finish_kernel(table_ref, head_ref, one_ref, two_ref, three_ref, tail_ref, other_ref, mine_ref, *refs):
     kind, place = table_ref[0], table_ref[1]
     tiles, narrow, flat_ref, vector_parts = refs[-4:]
-    tokens_ref, gains_ref, w_kv_ref, dq_wq_ref, d_mid_ref, own_dkv, other_dkv = refs[:7]
-    states = refs[7:-4]
+    tokens_ref, gains_ref, w_kv_ref, base_ref, own_dkv, other_dkv = refs[:6]
+    states = refs[6:-4]
     tiles[0:HEAD_ROWS, :] = (head_ref[...] + one_ref[0:HEAD_ROWS, :].astype(F32)) + (
         two_ref[0:HEAD_ROWS, :].astype(F32) + three_ref[0:HEAD_ROWS, :].astype(F32)
     )
@@ -304,11 +304,11 @@
         vector = vector + vector_parts[lax.rem(place + 4 - z, 4)]
 
     lane = lax.broadcasted_iota(jnp.int32, (2 * ROWS, WIDE), 1)
-    x = jnp.where(lane < MODEL_WIDTH, tokens_ref[0].astype(F32).reshape(2 * ROWS, WIDE), 0.0)
+    x = jnp.where(lane < MODEL_WIDTH, tokens_ref[...].astype(F32).reshape(2 * ROWS, WIDE), 0.0)
     normed, scale = normed_rows(x)
     total = summed(own_dkv[...], other_dkv[...]).reshape(2 * ROWS, 384).astype(BF16)
-    d_norm = (dq_wq_ref[...] + times_transposed(total, w_kv_ref[...])) * gains_ref[0:1, :]
-    d_input = d_mid_ref[...] + scale * (d_norm - normed * row_mean(d_norm * normed))
+    d_norm = times_transposed(total, w_kv_ref[...]) * gains_ref[0:1, :]
+    d_input = base_ref[...] + scale * (d_norm - normed * row_mean(d_norm * normed))
     out_ref = states[-1]
     for mb in range(2):
         out_ref[mb] = d_input[ROWS * mb : ROWS * mb + ROWS].T[0:MODEL_WIDTH].astype(BF16)
@@ -440,8 +440,8 @@
     tokens_pair, cos_pair, sin_pair = refs[13:15], refs[15:17], refs[17:19]
     (place_q_ref, place_k_ref, gains_ref, bias_q_ref, bias_kv_ref, grad_ref) = refs[19:25]
     block_out_ref, parts_out = refs[25], refs[26:36]
-    (dkv_send, dkv_keep, dq_wq_ref, d_mid_ref, w_kv) = refs[36:41]
-    (raw_head, raw_tail, w_q, w_out, w_gate, w_up, w_down, normed_all, hidden_all, keys, values, queries, probs, attended, act_all, block_acc, d_hidden, d_attended, dkv_all, d_query, send_all, keep_all, vector_ref, outs, sems, out_sems) = refs[41:]
+    (dkv_send, dkv_keep, base_ref, w_kv) = refs[36:40]
+    (raw_head, raw_tail, w_q, w_out, w_gate, w_up, w_down, normed_all, hidden_all, keys, values, queries, probs, attended, act_all, block_acc, d_hidden, d_attended, dkv_all, d_query, both_all, vector_ref, outs, sems, out_sems) = refs[40:]
 
     place = slots[MY_Z]
 
@@ -591,11 +591,11 @@
 
     def store_pair(at, even, odd, table, first):
         rows = pl.ds(pl.multiple_of(slots[table + at] + first, 16), even.shape[0])
-        send_all[rows, :] = jnp.where(core == 0, odd, even).astype(BF16)
-        keep_all[rows, :] = jnp.where(core == 0, even, odd).astype(BF16)
+        both_all[1 - core, rows, :] = even.astype(BF16)
+        both_all[core, rows, :] = odd.astype(BF16)
 
     def feed_forward(chunk, first, table):
-        cols = pl.ds(pl.multiple_of(chunk * 512, 512), 512)
+        cols = slice(chunk * 512, chunk * 512 + 512)
         gate = product(hidden_two, w_gate[:, cols])
         up = product(hidden_two, w_up[:, cols])
         sigma = 1.0 / (1.0 + jnp.exp(-gate))
@@ -615,10 +615,8 @@
                 odd = jnp.concatenate([part[72:144, LANES * j : LANES * j + LANES] for j in range(4)], axis=0)
                 store_pair(base + k, even, odd, table, (chunk - first) * 288)
 
-    @pl.loop(0, 2)
-    def _(chunk):
-        feed_forward(chunk, 0, TO_HEAD)
-
+    feed_forward(0, 0, TO_HEAD)
+    feed_forward(1, 0, TO_HEAD)
     feed_forward(2, 2, TO_TAIL)
 
     def store_rows(at, even, odd):
@@ -634,7 +632,7 @@
 
     def deliveries(first, count, sem):
         copies = []
-        for base, outs_of in ((send_all, parts_out[0:4]), (keep_all, parts_out[4:10])):
+        for base, outs_of in ((both_all.at[0], parts_out[0:4]), (both_all.at[1], parts_out[4:10])):
             rest = [(outs_of[2], PART * k) for k in range(3)] if len(outs_of) == 4 else [(out, 0) for out in outs_of[2:5]]
             targets = [(outs_of[0], 0, FIRST_AT), (outs_of[1], 0, TAIL_AT)]
             targets += [(out, into, PART * k) for k, (out, into) in enumerate(rest)]
@@ -661,7 +659,6 @@
     gain_two_sum = jnp.sum(d_two * normed_two, axis=0, keepdims=True)
     d_norm = d_two * gain_two
     d_mid = grad_low.astype(F32) + scale_two * (d_norm - normed_two * row_mean(d_norm * normed_two))
-    d_mid_ref[...] = d_mid
     d_branch = d_mid.astype(BF16)
     d_attended[...] = times_transposed(d_branch, w_out[...]).astype(BF16)
     grad_out = rows_product(attended[...], d_branch)
@@ -705,7 +702,10 @@
     dkv = dkv_all[...]
     d_q = d_query[...]
     dq_wq = times_transposed(d_q, w_q[...])
-    dq_wq_ref[...] = dq_wq
+    normed = jnp.concatenate([normed_all[512 * mb : 512 * mb + ROWS, :] for mb in range(2)], axis=0)
+    scale = lax.rsqrt(row_mean(x_own * x_own) + EPS_NORM)
+    d_norm = dq_wq * gain_one
+    base_ref[...] = d_mid + scale * (d_norm - normed * row_mean(d_norm * normed))
     bias_q_sum = jnp.sum(d_q.astype(F32), axis=0, keepdims=True)
     bias_kv_sum = jnp.sum(dkv.astype(F32), axis=0, keepdims=True)
     gain_sum = jnp.zeros((1, WIDE), F32)
@@ -749,11 +749,11 @@
     vector = vector_ref[...]
     high = vector.astype(BF16).astype(F32)
     both = jnp.concatenate([high, vector - high], axis=0).astype(BF16)
-    for ref in (send_all, keep_all):
-        ref[at : at + 2 * VECTOR_ROWS, :] = both
+    for k in range(2):
+        both_all[k, at : at + 2 * VECTOR_ROWS, :] = both
     last = deliveries(0, 1, 0)
-    last.append(pltpu.make_async_copy(send_all.at[pl.ds(at, 2 * VECTOR_ROWS)], parts_out[0].at[pl.ds(PART, 2 * VECTOR_ROWS)], out_sems.at[24]))
-    last.append(pltpu.make_async_copy(keep_all.at[pl.ds(at, 2 * VECTOR_ROWS)], parts_out[4].at[pl.ds(PART, 2 * VECTOR_ROWS)], out_sems.at[25]))
+    last.append(pltpu.make_async_copy(both_all.at[0, pl.ds(at, 2 * VECTOR_ROWS)], parts_out[0].at[pl.ds(PART, 2 * VECTOR_ROWS)], out_sems.at[24]))
+    last.append(pltpu.make_async_copy(both_all.at[1, pl.ds(at, 2 * VECTOR_ROWS)], parts_out[4].at[pl.ds(PART, 2 * VECTOR_ROWS)], out_sems.at[25]))
     for copy in last:
         copy.start()
     for copy in early + last:
@@ -785,8 +785,7 @@
         ((256, WIDE), BF16),
         ((1024, 384), BF16),
         ((256, WIDE), BF16),
-        ((ALL_ROWS, LANES), BF16),
-        ((ALL_ROWS, LANES), BF16),
+        ((2, ALL_ROWS, LANES), BF16),
         ((VECTOR_ROWS, LANES), F32),
         ((2, 3, 384, LANES), F32),
     ]
@@ -798,11 +797,10 @@
             shape((2, 2, ROWS, 384), BF16),
             shape((2, 2, ROWS, 384), BF16),
             shape((256, WIDE), F32),
-            shape((256, WIDE), F32),
             shape((WIDE, 384), BF16),
         ),
         in_specs=[pl.BlockSpec(memory_space=pltpu.SMEM)] + [anywhere] * 12 + [vmem] * 12,
-        out_specs=(vmem,) + (anywhere,) * 10 + (vmem,) * 5,
+        out_specs=(vmem,) + (anywhere,) * 10 + (vmem,) * 4,
         scratch_shapes=[pltpu.VMEM(dims, kind) for dims, kind in scratch]
         + [pltpu.SemaphoreType.DMA((48,)), pltpu.SemaphoreType.DMA((26,))],
         compiler_params=pltpu.CompilerParams(vmem_limit_bytes=50 * 1024 * 1024),
@@ -881,9 +879,9 @@
         slots, heads, tails, near, far, cosines, cosines_far, sines, sines_far, place_q, place_k, gains, bias_q, bias_kv, grad
     )
     sends, keeps = found[:4], found[4:10]
-    dkv_send, dkv_keep, dq_wq, d_mid, w_kv = found[10:]
+    dkv_send, dkv_keep, base, w_kv = found[10:]
     parts, pairs = scatter_blocks(sends, keeps, dkv_send, dkv_keep)
-    inputs = (near, gains, w_kv, dq_wq, d_mid, *pairs)
+    inputs = (packed, gains, w_kv, base, *pairs)
     state = (weights, first_moment, second_moment)
     if inner_count() == 1:
         blocks = [array.reshape(BLOCK_ROWS, LANES) for array in state]

time: 151 us -> 148 us (0.980)
  Pallas kernels: 35.5 us -> 33.7 us
    unnamed x80 -> x82, local copies, waits for them, and re-layouts: 3.86 us -> 3.72 us
  transfers between devices with their start and end apart: 36 -> 36, of which waited for: 18 -> 18; matrix products, arithmetic and copies ran while one was open for 9% -> 10% of each run, Pallas kernels for 0% -> 0%
where the time goes in v9:
time: 148 us; the launch traced here: 147 us
  waiting for transfers between devices  54.3 us (37%)
  starting transfers between devices  36.4 us (25%)
  Pallas kernels  33.7 us (23%)
  other arithmetic  12.6 us (9%)
  local copies, waits for them, and re-layouts  8.31 us (6%)
  between operations  1.88 us (1%)
    ppermute x32, waiting for transfers between devices, moved(): return lax.ppermute(buffer, ('dp', 'ctx'), pairs)  45.9 us
    ppermute x32, starting transfers between devices, moved(): return lax.ppermute(buffer, ('dp', 'ctx'), pairs)  34.7 us
    pallas_call x1, Pallas kernels, run_layer(): pl.pallas_call(layer_kernel, out_shape=(shape((2, MODEL_WIDTH, ROWS), BF1...  27.1 us
    ppermute x4, waiting for transfers between devices, across(): lax.ppermute(buffer, 'ctx', [(i, i ^ distance) for i in range(count)])  8.36 us
    pallas_call x1, Pallas kernels, finish(): pl.pallas_call(finish_kernel, out_shape=shapes, in_specs=[pl.BlockSpec(me...  4.76 us
    unnamed x82, local copies, waits for them, and re-layouts  3.72 us
  transfers between devices with their start and end apart: 36, of which 18 were waited for; matrix products, arithmetic and copies ran while one was open for 10% of the time, Pallas kernels for 0%

profile of v9, /device:TPU:0, one launch (start us, length us, event | category | flops | bytes accessed | tf_op | source)
XLA Modules:
  0.0 147.3 jit_solution(12413150537396112584)
XLA Ops:
  0.7 1.9 %to_tiles.1 = (bf16[576,128]{1,0:T(8,128)(2,1)}, bf16[288,128]{1,0:T(8,128)(2,1)}) custom-call(s32[1]{0:T(128)} %bitcast.kind_ref, f32[864,128]{1,0:T(8,128)} %bitcast.154), custom_call_target="tpu_custom_call" | custom-call | tf_op jit(solution)/shard_map/to_tiles/pallas_call | solution.py:269
  2.5 2.9 %collective-permute-start.2 = (bf16[576,128]{1,0:T(8,128)(2,1)}, bf16[576,128]{1,0:T(8,128)(2,1)S(1)}, u32[]{:S(2)}, u32[]{:S(2)}) collective-permute-start(bf16[576,128]{1,0:T(8,128)(2,1)} %get-tuple-element.97), channel_id=1, source_target_pairs={{0,8},{1,9},{2,10},{3,11},{4,12},{5,13},{6,14},{7,15},{8,16},{9,17... | collective-permute-start | bytes 442376 | tf_op jit(solution)/shard_map/ppermute | solution.py:75
  5.4 2.7 %collective-permute-start.3 = (bf16[576,128]{1,0:T(8,128)(2,1)}, bf16[576,128]{1,0:T(8,128)(2,1)S(1)}, u32[]{:S(2)}, u32[]{:S(2)}) collective-permute-start(bf16[576,128]{1,0:T(8,128)(2,1)} %get-tuple-element.97), channel_id=1, source_target_pairs={{0,16},{1,17},{2,18},{3,19},{4,20},{5,21},{6,22},{7,23},{8,24},{9,... | collective-permute-start | bytes 442376 | tf_op jit(solution)/shard_map/ppermute | solution.py:75
  8.1 1.2 collective-permute-start.4
  9.4 1.5 %collective-permute-start = (bf16[288,128]{1,0:T(8,128)(2,1)}, bf16[288,128]{1,0:T(8,128)(2,1)S(1)}, u32[]{:S(2)}, u32[]{:S(2)}) collective-permute-start(bf16[288,128]{1,0:T(8,128)(2,1)} %get-tuple-element.101), channel_id=1, source_target_pairs={{0,2},{1,3},{2,0},{3,1},{4,6},{5,7},{6,4},{7,5},{8,10},{9,11},{10,... | collective-permute-start | bytes 221192 | tf_op jit(solution)/shard_map/ppermute | solution.py:75
  11.8 1.2 copy.39
  18.0 3.6 %collective-permute-done.1 = bf16[2,128,640]{2,1,0:T(8,128)(2,1)S(1)} collective-permute-done((bf16[2,128,640]{2,1,0:T(8,128)(2,1)S(1)}, bf16[2,128,640]{2,1,0:T(8,128)(2,1)S(1)}, u32[]{:S(2)}, u32[]{:S(2)}) %collective-permute-start.1) | collective-permute-done | bytes 327712 | tf_op jit(solution)/shard_map/ppermute | solution.py:80
  21.7 1.6 %collective-permute-start.5 = (bf16[4,576,128]{2,1,0:T(8,128)(2,1)S(1)}, bf16[4,576,128]{2,1,0:T(8,128)(2,1)S(1)}, u32[]{:S(2)}, u32[]{:S(2)}) collective-permute-start(bf16[4,576,128]{2,1,0:T(8,128)(2,1)S(1)} %pad_maximum_fusion.3.refs_1_), channel_id=1, source_target_pairs={{0,4},{1,5},{2,6},{3,7},{4,0},{5,1},{6,2},{7,3},{8,12},{9,13},{10,... | collective-permute-start | bytes 1769480 | tf_op jit(solution)/shard_map/ppermute | solution.py:75
  25.0 1.4 collective-permute-start.8
  26.4 1.6 %collective-permute-start.9 = (bf16[2,288,128]{2,1,0:T(8,128)(2,1)S(1)}, bf16[2,288,128]{2,1,0:T(8,128)(2,1)S(1)}, u32[]{:S(2)}, u32[]{:S(2)}) collective-permute-start(bf16[2,288,128]{2,1,0:T(8,128)(2,1)S(1)} %pad_maximum_fusion.10), channel_id=1, source_target_pairs={{0,24},{1,25},{2,26},{3,27},{4,28},{5,29},{6,30},{7,31},{8,0},{9,1... | collective-permute-start | bytes 442376 | tf_op jit(solution)/shard_map/ppermute | solution.py:75
  29.5 3.0 %collective-permute-done.7 = bf16[2,288,128]{2,1,0:T(8,128)(2,1)S(1)} collective-permute-done((bf16[2,288,128]{2,1,0:T(8,128)(2,1)S(1)}, bf16[2,288,128]{2,1,0:T(8,128)(2,1)S(1)}, u32[]{:S(2)}, u32[]{:S(2)}) %collective-permute-start.7) | collective-permute-done | bytes 147488 | tf_op jit(solution)/shard_map/ppermute | solution.py:75
  32.5 3.3 %collective-permute-done.8 = bf16[2,288,128]{2,1,0:T(8,128)(2,1)S(1)} collective-permute-done((bf16[2,288,128]{2,1,0:T(8,128)(2,1)S(1)}, bf16[2,288,128]{2,1,0:T(8,128)(2,1)S(1)}, u32[]{:S(2)}, u32[]{:S(2)}) %collective-permute-start.8) | collective-permute-done | bytes 147488 | tf_op jit(solution)/shard_map/ppermute | solution.py:75
  36.1 1.1 collective-permute-start.10
  38.4 12.5 %collective-permute-done.10.refs_4_ = bf16[4,576,128]{2,1,0:T(8,128)(2,1)S(1)} collective-permute-done((bf16[4,576,128]{2,1,0:T(8,128)(2,1)S(1)}, bf16[4,576,128]{2,1,0:T(8,128)(2,1)S(1)}, u32[]{:S(2)}, u32[]{:S(2)}) %collective-permute-start.10) | collective-permute-done | bytes 589856 | tf_op jit(solution)/shard_map/ppermute | solution.py:75
  51.8 1.0 collective-permute-done.14.refs_7_
  57.5 27.1 %layer.1 = (bf16[2,576,128]{2,1,0:T(8,128)(2,1)}, bf16[2352,128]{1,0:T(8,128)(2,1)}, bf16[2304,128]{1,0:T(8,128)(2,1)S(1)}, bf16[6912,128]{1,0:T(8,128)(2,1)}, b...) custom-call(s32[98]{0:T(128)S(1)} %stack.448.refs_0_, ...), custom_call_target="tpu_custom_call" | custom-call | tf_op jit(solution)/shard_map/layer/pallas_call | solution.py:792
  85.2 2.4 %collective-permute-done.20 = bf16[2304,128]{1,0:T(8,128)(2,1)S(1)} collective-permute-done((bf16[2304,128]{1,0:T(8,128)(2,1)S(1)}, bf16[2304,128]{1,0:T(8,128)(2,1)S(1)}, u32[]{:S(2)}, u32[]{:S(2)}) %collective-permute-start.20) | collective-permute-done | bytes 589856 | tf_op jit(solution)/shard_map/ppermute | solution.py:75
  88.3 1.4 add_convert_fusion.6
  89.7 1.2 collective-permute-start.21
  92.2 3.8 %collective-permute-done.25 = bf16[2,2,128,384]{3,2,1,0:T(8,128)(2,1)S(1)} collective-permute-done((bf16[2,2,128,384]{3,2,1,0:T(8,128)(2,1)S(1)}, bf16[2,2,128,384]{3,2,1,0:T(8,128)(2,1)S(1)}, u32[]{:S(2)}, u32[]{:S(2)}) %collective-permute-start.25) | collective-permute-done | bytes 393248 | tf_op jit(solution)/shard_map/ppermute | solution.py:80
  97.5 1.3 add_convert_fusion.2
  98.8 8.6 %collective-permute-done.22 = bf16[2304,128]{1,0:T(8,128)(2,1)S(1)} collective-permute-done((bf16[2304,128]{1,0:T(8,128)(2,1)S(1)}, bf16[2304,128]{1,0:T(8,128)(2,1)S(1)}, u32[]{:S(2)}, u32[]{:S(2)}) %collective-permute-start.22) | collective-permute-done | bytes 589856 | tf_op jit(solution)/shard_map/ppermute | solution.py:75
  109.6 2.0 %add_convert_fusion.11 = (bf16[576,128]{1,0:T(8,128)(2,1)}, bf16[576,128]{1,0:T(8,128)(2,1)}, bf16[576,128]{1,0:T(8,128)(2,1)}, bf16[576,128]{1,0:T(8,128)(2,1)S(1)}) fusion(bf16[2304,128]{1,0:T(8,128)(2,1)} %copy-done.19, s32[]{:T(128)S(6)} %select_n.938, bf16[2304,128]{1,0:T(8,128)(2,1)S(1)} %add_convert_fusion.1, s32[]{:T(128)S(6)} %select_n.936, ...), kind=kLoop, calls=%fused_computation.23 | loop fusion | flops 1179648 | bytes 1769488 | tf_op jit(solution)/shard_map/convert_element_type | solution.py:203
  111.6 3.7 %collective-permute-start.28 = (bf16[576,128]{1,0:T(8,128)(2,1)}, bf16[576,128]{1,0:T(8,128)(2,1)S(1)}, u32[]{:S(2)}, u32[]{:S(2)}) collective-permute-start(bf16[576,128]{1,0:T(8,128)(2,1)} %get-tuple-element.211), channel_id=1, source_target_pairs={{0,8},{1,9},{2,10},{3,11},{4,12},{5,13},{6,14},{7,15},{8,16},{9,17... | collective-permute-start | bytes 442376 | tf_op jit(solution)/shard_map/ppermute | solution.py:75
  115.3 2.4 %collective-permute-start.30 = (bf16[576,128]{1,0:T(8,128)(2,1)}, bf16[576,128]{1,0:T(8,128)(2,1)S(1)}, u32[]{:S(2)}, u32[]{:S(2)}) collective-permute-start(bf16[576,128]{1,0:T(8,128)(2,1)} %get-tuple-element.209), channel_id=1, source_target_pairs={{0,24},{1,25},{2,26},{3,27},{4,28},{5,29},{6,30},{7,31},{8,0},{9,1... | collective-permute-start | bytes 442376 | tf_op jit(solution)/shard_map/ppermute | solution.py:75
  117.7 2.4 %collective-permute-done.28 = bf16[576,128]{1,0:T(8,128)(2,1)S(1)} collective-permute-done((bf16[576,128]{1,0:T(8,128)(2,1)}, bf16[576,128]{1,0:T(8,128)(2,1)S(1)}, u32[]{:S(2)}, u32[]{:S(2)}) %collective-permute-start.28) | collective-permute-done | bytes 147488 | tf_op jit(solution)/shard_map/ppermute | solution.py:75
  120.1 5.1 %collective-permute-done.29 = bf16[576,128]{1,0:T(8,128)(2,1)S(1)} collective-permute-done((bf16[576,128]{1,0:T(8,128)(2,1)}, bf16[576,128]{1,0:T(8,128)(2,1)S(1)}, u32[]{:S(2)}, u32[]{:S(2)}) %collective-permute-start.29) | collective-permute-done | bytes 147488 | tf_op jit(solution)/shard_map/ppermute | solution.py:75
  126.2 3.7 %collective-permute-start.31 = (bf16[624,128]{1,0:T(8,128)(2,1)S(1)}, bf16[624,128]{1,0:T(8,128)(2,1)S(1)}, u32[]{:S(2)}, u32[]{:S(2)}) collective-permute-start(bf16[624,128]{1,0:T(8,128)(2,1)S(1)} %get-tuple-element.225), channel_id=1, source_target_pairs={{0,8},{1,9},{2,10},{3,11},{4,12},{5,13},{6,14},{7,15},{8,16},{9,17... | collective-permute-start | bytes 479240 | tf_op jit(solution)/shard_map/ppermute | solution.py:75
  129.9 2.3 %collective-permute-start.32 = (bf16[624,128]{1,0:T(8,128)(2,1)S(1)}, bf16[624,128]{1,0:T(8,128)(2,1)S(1)}, u32[]{:S(2)}, u32[]{:S(2)}) collective-permute-start(bf16[624,128]{1,0:T(8,128)(2,1)S(1)} %get-tuple-element.224), channel_id=1, source_target_pairs={{0,16},{1,17},{2,18},{3,19},{4,20},{5,21},{6,22},{7,23},{8,24},{9,... | collective-permute-start | bytes 479240 | tf_op jit(solution)/shard_map/ppermute | solution.py:75
  133.1 1.1 collective-permute-start.35
  136.4 4.5 %collective-permute-done.34.other_ref = bf16[288,128]{1,0:T(8,128)(2,1)S(1)} collective-permute-done((bf16[288,128]{1,0:T(8,128)(2,1)S(1)}, bf16[288,128]{1,0:T(8,128)(2,1)S(1)}, u32[]{:S(2)}, u32[]{:S(2)}) %collective-permute-start.34) | collective-permute-done | bytes 73760 | tf_op jit(solution)/shard_map/ppermute | solution.py:75
  142.4 4.8 %finish.1 = (f32[24,128]{1,0:T(8,128)}, f32[24,128]{1,0:T(8,128)}, f32[24,128]{1,0:T(8,128)}, f32[864,128]{1,0:T(8,128)}, f32[864,128]{1,0:T(8,128)}, /*index=5*/f32[864,128]{1,0:T(8,128)}, bf16[2,576,128]{2,1,0:T(8,128)(2,1)}) custom-call(s32[2]{0:T(128)} %pad_add_fusion.table_ref, f32[576,128]{1,0:T(8,128)} %get-tuple-element.203.head_ref, ...), custom_call_target="tpu_custom_call" | custom-call | tf_op jit(solution)/shard_map/finish/pallas_call | solution.py:371
  (187 shorter events, 27.2 us)
Async XLA Ops:
  2.5 14.7 %collective-permute-start.2 = (bf16[576,128]{1,0:T(8,128)(2,1)}, bf16[576,128]{1,0:T(8,128)(2,1)S(1)}, u32[]{:S(2)}, u32[]{:S(2)}) collective-permute-start(bf16[576,128]{1,0:T(8,128)(2,1)} %get-tuple-element.97), channel_id=1, source_target_pairs={{0,8},{1,9},{2,10},{3,11},{4,12},{5,13},{6,14},{7,15},{8,16},{9,17... | collective-permute-start | bytes 442376 | tf_op jit(solution)/shard_map/ppermute | solution.py:75
  5.4 12.6 %collective-permute-start.3 = (bf16[576,128]{1,0:T(8,128)(2,1)}, bf16[576,128]{1,0:T(8,128)(2,1)S(1)}, u32[]{:S(2)}, u32[]{:S(2)}) collective-permute-start(bf16[576,128]{1,0:T(8,128)(2,1)} %get-tuple-element.97), channel_id=1, source_target_pairs={{0,16},{1,17},{2,18},{3,19},{4,20},{5,21},{6,22},{7,23},{8,24},{9,... | collective-permute-start | bytes 442376 | tf_op jit(solution)/shard_map/ppermute | solution.py:75
  8.1 9.9 %collective-permute-start.4 = (bf16[576,128]{1,0:T(8,128)(2,1)}, bf16[576,128]{1,0:T(8,128)(2,1)S(1)}, u32[]{:S(2)}, u32[]{:S(2)}) collective-permute-start(bf16[576,128]{1,0:T(8,128)(2,1)} %get-tuple-element.97), channel_id=1, source_target_pairs={{0,24},{1,25},{2,26},{3,27},{4,28},{5,29},{6,30},{7,31},{8,0},{9,1... | collective-permute-start | bytes 442376 | tf_op jit(solution)/shard_map/ppermute | solution.py:75
  9.4 7.8 %collective-permute-start = (bf16[288,128]{1,0:T(8,128)(2,1)}, bf16[288,128]{1,0:T(8,128)(2,1)S(1)}, u32[]{:S(2)}, u32[]{:S(2)}) collective-permute-start(bf16[288,128]{1,0:T(8,128)(2,1)} %get-tuple-element.101), channel_id=1, source_target_pairs={{0,2},{1,3},{2,0},{3,1},{4,6},{5,7},{6,4},{7,5},{8,10},{9,11},{10,... | collective-permute-start | bytes 221192 | tf_op jit(solution)/shard_map/ppermute | solution.py:75
  13.2 8.4 %collective-permute-start.1 = (bf16[2,128,640]{2,1,0:T(8,128)(2,1)S(1)}, bf16[2,128,640]{2,1,0:T(8,128)(2,1)S(1)}, u32[]{:S(2)}, u32[]{:S(2)}) collective-permute-start(bf16[2,128,640]{2,1,0:T(8,128)(2,1)S(1)} %maximum_maximum_fusion.refs_0_), channel_id=1, source_target_pairs={{0,2},{1,3},{2,0},{3,1},{4,6},{5,7},{6,4},{7,5},{8,10},{9,11},{10,... | collective-permute-start | bytes 983048 | tf_op jit(solution)/shard_map/ppermute | solution.py:80
  21.7 14.1 %collective-permute-start.5 = (bf16[4,576,128]{2,1,0:T(8,128)(2,1)S(1)}, bf16[4,576,128]{2,1,0:T(8,128)(2,1)S(1)}, u32[]{:S(2)}, u32[]{:S(2)}) collective-permute-start(bf16[4,576,128]{2,1,0:T(8,128)(2,1)S(1)} %pad_maximum_fusion.3.refs_1_), channel_id=1, source_target_pairs={{0,4},{1,5},{2,6},{3,7},{4,0},{5,1},{6,2},{7,3},{8,12},{9,13},{10,... | collective-permute-start | bytes 1769480 | tf_op jit(solution)/shard_map/ppermute | solution.py:75
  23.3 12.7 %collective-permute-start.6 = (bf16[4,576,128]{2,1,0:T(8,128)(2,1)S(1)}, bf16[4,576,128]{2,1,0:T(8,128)(2,1)S(1)}, u32[]{:S(2)}, u32[]{:S(2)}) collective-permute-start(bf16[4,576,128]{2,1,0:T(8,128)(2,1)S(1)} %pad_maximum_fusion.3.refs_1_), channel_id=1, source_target_pairs={{0,2},{1,3},{2,0},{3,1},{4,6},{5,7},{6,4},{7,5},{8,10},{9,11},{10,... | collective-permute-start | bytes 1769480 | tf_op jit(solution)/shard_map/ppermute | solution.py:75
  24.1 8.4 %collective-permute-start.7 = (bf16[2,288,128]{2,1,0:T(8,128)(2,1)S(1)}, bf16[2,288,128]{2,1,0:T(8,128)(2,1)S(1)}, u32[]{:S(2)}, u32[]{:S(2)}) collective-permute-start(bf16[2,288,128]{2,1,0:T(8,128)(2,1)S(1)} %pad_maximum_fusion.10), channel_id=1, source_target_pairs={{0,8},{1,9},{2,10},{3,11},{4,12},{5,13},{6,14},{7,15},{8,16},{9,17... | collective-permute-start | bytes 442376 | tf_op jit(solution)/shard_map/ppermute | solution.py:75
  25.0 10.8 %collective-permute-start.8 = (bf16[2,288,128]{2,1,0:T(8,128)(2,1)S(1)}, bf16[2,288,128]{2,1,0:T(8,128)(2,1)S(1)}, u32[]{:S(2)}, u32[]{:S(2)}) collective-permute-start(bf16[2,288,128]{2,1,0:T(8,128)(2,1)S(1)} %pad_maximum_fusion.10), channel_id=1, source_target_pairs={{0,16},{1,17},{2,18},{3,19},{4,20},{5,21},{6,22},{7,23},{8,24},{9,... | collective-permute-start | bytes 442376 | tf_op jit(solution)/shard_map/ppermute | solution.py:75
  26.4 9.4 %collective-permute-start.9 = (bf16[2,288,128]{2,1,0:T(8,128)(2,1)S(1)}, bf16[2,288,128]{2,1,0:T(8,128)(2,1)S(1)}, u32[]{:S(2)}, u32[]{:S(2)}) collective-permute-start(bf16[2,288,128]{2,1,0:T(8,128)(2,1)S(1)} %pad_maximum_fusion.10), channel_id=1, source_target_pairs={{0,24},{1,25},{2,26},{3,27},{4,28},{5,29},{6,30},{7,31},{8,0},{9,1... | collective-permute-start | bytes 442376 | tf_op jit(solution)/shard_map/ppermute | solution.py:75
  36.1 14.8 %collective-permute-start.10 = (bf16[4,576,128]{2,1,0:T(8,128)(2,1)S(1)}, bf16[4,576,128]{2,1,0:T(8,128)(2,1)S(1)}, u32[]{:S(2)}, u32[]{:S(2)}) collective-permute-start(bf16[4,576,128]{2,1,0:T(8,128)(2,1)S(1)} %collective-permute-done.5.refs_2_), channel_id=1, source_target_pairs={{0,2},{1,3},{2,0},{3,1},{4,6},{5,7},{6,4},{7,5},{8,10},{9,11},{10,... | collective-permute-start | bytes 1769480 | tf_op jit(solution)/shard_map/ppermute | solution.py:75
  37.3 14.0 %collective-permute-start.11 = (bf16[8,288,128]{2,1,0:T(8,128)(2,1)S(1)}, bf16[8,288,128]{2,1,0:T(8,128)(2,1)S(1)}, u32[]{:S(2)}, u32[]{:S(2)}) collective-permute-start(bf16[8,288,128]{2,1,0:T(8,128)(2,1)S(1)} %constant_dynamic-update-slice_fusion.refs_9_), channel_id=1, source_target_pairs={{0,4},{1,5},{2,6},{3,7},{4,0},{5,1},{6,2},{7,3},{8,12},{9,13},{10,... | collective-permute-start | bytes 1769480 | tf_op jit(solution)/shard_map/ppermute | solution.py:75
  37.9 13.9 %collective-permute-start.13 = (bf16[4,576,128]{2,1,0:T(8,128)(2,1)S(1)}, bf16[4,576,128]{2,1,0:T(8,128)(2,1)S(1)}, u32[]{:S(2)}, u32[]{:S(2)}) collective-permute-start(bf16[4,576,128]{2,1,0:T(8,128)(2,1)S(1)} %collective-permute-done.5.refs_2_), channel_id=1, source_target_pairs={{0,1},{1,0},{2,3},{3,2},{4,5},{5,4},{6,7},{7,6},{8,9},{9,8},{10,11... | collective-permute-start | bytes 1769480 | tf_op jit(solution)/shard_map/ppermute | solution.py:75
  37.9 15.0 %collective-permute-start.15 = (bf16[8,288,128]{2,1,0:T(8,128)(2,1)S(1)}, bf16[8,288,128]{2,1,0:T(8,128)(2,1)S(1)}, u32[]{:S(2)}, u32[]{:S(2)}) collective-permute-start(bf16[8,288,128]{2,1,0:T(8,128)(2,1)S(1)} %constant_dynamic-update-slice_fusion.refs_9_), channel_id=1, source_target_pairs={{0,1},{1,0},{2,3},{3,2},{4,5},{5,4},{6,7},{7,6},{8,9},{9,8},{10,11... | collective-permute-start | bytes 1769480 | tf_op jit(solution)/shard_map/ppermute | solution.py:75
  38.4 13.4 %collective-permute-start.12 = (bf16[4,576,128]{2,1,0:T(8,128)(2,1)S(1)}, bf16[4,576,128]{2,1,0:T(8,128)(2,1)S(1)}, u32[]{:S(2)}, u32[]{:S(2)}) collective-permute-start(bf16[4,576,128]{2,1,0:T(8,128)(2,1)S(1)} %pad_maximum_fusion.3.refs_1_), channel_id=1, source_target_pairs={{0,1},{1,0},{2,3},{3,2},{4,5},{5,4},{6,7},{7,6},{8,9},{9,8},{10,11... | collective-permute-start | bytes 1769480 | tf_op jit(solution)/shard_map/ppermute | solution.py:75
  84.6 2.9 %collective-permute-start.19 = (bf16[2352,128]{1,0:T(8,128)(2,1)}, bf16[2352,128]{1,0:T(8,128)(2,1)S(1)}, u32[]{:S(2)}, u32[]{:S(2)}) collective-permute-start(bf16[2352,128]{1,0:T(8,128)(2,1)} %get-tuple-element.129), channel_id=1, source_target_pairs={{0,1},{1,0},{2,3},{3,2},{4,5},{5,4},{6,7},{7,6},{8,9},{9,8},{10,11... | collective-permute-start | bytes 1806344 | tf_op jit(solution)/shard_map/ppermute | solution.py:75
  84.8 2.7 %collective-permute-start.20 = (bf16[2304,128]{1,0:T(8,128)(2,1)S(1)}, bf16[2304,128]{1,0:T(8,128)(2,1)S(1)}, u32[]{:S(2)}, u32[]{:S(2)}) collective-permute-start(bf16[2304,128]{1,0:T(8,128)(2,1)S(1)} %get-tuple-element.130), channel_id=1, source_target_pairs={{0,1},{1,0},{2,3},{3,2},{4,5},{5,4},{6,7},{7,6},{8,9},{9,8},{10,11... | collective-permute-start | bytes 1769480 | tf_op jit(solution)/shard_map/ppermute | solution.py:75
  89.7 17.7 %collective-permute-start.21 = (bf16[2352,128]{1,0:T(8,128)(2,1)S(1)}, bf16[2352,128]{1,0:T(8,128)(2,1)S(1)}, u32[]{:S(2)}, u32[]{:S(2)}) collective-permute-start(bf16[2352,128]{1,0:T(8,128)(2,1)S(1)} %pad_maximum_fusion.1), channel_id=1, source_target_pairs={{0,2},{1,3},{2,0},{3,1},{4,6},{5,7},{6,4},{7,5},{8,10},{9,11},{10,... | collective-permute-start | bytes 1806344 | tf_op jit(solution)/shard_map/ppermute | solution.py:75
  90.9 5.4 %collective-permute-start.23 = (bf16[6912,128]{1,0:T(8,128)(2,1)S(1)}, bf16[6912,128]{1,0:T(8,128)(2,1)S(1)}, u32[]{:S(2)}, u32[]{:S(2)}) collective-permute-start(bf16[6912,128]{1,0:T(8,128)(2,1)S(1)} %copy-done.38), channel_id=1, source_target_pairs={{0,1},{1,0},{2,3},{3,2},{4,5},{5,4},{6,7},{7,6},{8,9},{9,8},{10,11... | collective-permute-start | bytes 5308424 | tf_op jit(solution)/shard_map/ppermute | solution.py:75
  90.9 5.2 %collective-permute-start.24 = (bf16[2304,128]{1,0:T(8,128)(2,1)S(1)}, bf16[2304,128]{1,0:T(8,128)(2,1)S(1)}, u32[]{:S(2)}, u32[]{:S(2)}) collective-permute-start(bf16[2304,128]{1,0:T(8,128)(2,1)S(1)} %get-tuple-element.142), channel_id=1, source_target_pairs={{0,1},{1,0},{2,3},{3,2},{4,5},{5,4},{6,7},{7,6},{8,9},{9,8},{10,11... | collective-permute-start | bytes 1769480 | tf_op jit(solution)/shard_map/ppermute | solution.py:75
  91.4 4.6 %collective-permute-start.25 = (bf16[2,2,128,384]{3,2,1,0:T(8,128)(2,1)S(1)}, bf16[2,2,128,384]{3,2,1,0:T(8,128)(2,1)S(1)}, u32[]{:S(2)}, u32[]{:S(2)}) collective-permute-start(bf16[2,2,128,384]{3,2,1,0:T(8,128)(2,1)S(1)} %get-tuple-element.144), channel_id=1, source_target_pairs={{0,1},{1,0},{2,3},{3,2},{4,5},{5,4},{6,7},{7,6},{8,9},{9,8},{10,11... | collective-permute-start | bytes 1179656 | tf_op jit(solution)/shard_map/ppermute | solution.py:80
  91.6 15.8 %collective-permute-start.22 = (bf16[2304,128]{1,0:T(8,128)(2,1)S(1)}, bf16[2304,128]{1,0:T(8,128)(2,1)S(1)}, u32[]{:S(2)}, u32[]{:S(2)}) collective-permute-start(bf16[2304,128]{1,0:T(8,128)(2,1)S(1)} %add_convert_fusion.5), channel_id=1, source_target_pairs={{0,4},{1,5},{2,6},{3,7},{4,0},{5,1},{6,2},{7,3},{8,12},{9,13},{10,... | collective-permute-start | bytes 1769480 | tf_op jit(solution)/shard_map/ppermute | solution.py:75
  108.2 17.0 %collective-permute-start.26 = (bf16[2352,128]{1,0:T(8,128)(2,1)S(1)}, bf16[2352,128]{1,0:T(8,128)(2,1)S(1)}, u32[]{:S(2)}, u32[]{:S(2)}) collective-permute-start(bf16[2352,128]{1,0:T(8,128)(2,1)S(1)} %pad_maximum_fusion.2), channel_id=1, source_target_pairs={{0,4},{1,5},{2,6},{3,7},{4,0},{5,1},{6,2},{7,3},{8,12},{9,13},{10,... | collective-permute-start | bytes 1806344 | tf_op jit(solution)/shard_map/ppermute | solution.py:75
  108.7 16.5 %collective-permute-start.27 = (bf16[2304,128]{1,0:T(8,128)(2,1)}, bf16[2304,128]{1,0:T(8,128)(2,1)S(1)}, u32[]{:S(2)}, u32[]{:S(2)}) collective-permute-start(bf16[2304,128]{1,0:T(8,128)(2,1)} %get-tuple-element.148), channel_id=1, source_target_pairs={{0,2},{1,3},{2,0},{3,1},{4,6},{5,7},{6,4},{7,5},{8,10},{9,11},{10,... | collective-permute-start | bytes 1769480 | tf_op jit(solution)/shard_map/ppermute | solution.py:75
  111.6 8.5 %collective-permute-start.28 = (bf16[576,128]{1,0:T(8,128)(2,1)}, bf16[576,128]{1,0:T(8,128)(2,1)S(1)}, u32[]{:S(2)}, u32[]{:S(2)}) collective-permute-start(bf16[576,128]{1,0:T(8,128)(2,1)} %get-tuple-element.211), channel_id=1, source_target_pairs={{0,8},{1,9},{2,10},{3,11},{4,12},{5,13},{6,14},{7,15},{8,16},{9,17... | collective-permute-start | bytes 442376 | tf_op jit(solution)/shard_map/ppermute | solution.py:75
  115.3 9.8 %collective-permute-start.29 = (bf16[576,128]{1,0:T(8,128)(2,1)}, bf16[576,128]{1,0:T(8,128)(2,1)S(1)}, u32[]{:S(2)}, u32[]{:S(2)}) collective-permute-start(bf16[576,128]{1,0:T(8,128)(2,1)} %get-tuple-element.210), channel_id=1, source_target_pairs={{0,16},{1,17},{2,18},{3,19},{4,20},{5,21},{6,22},{7,23},{8,24},{9,... | collective-permute-start | bytes 442376 | tf_op jit(solution)/shard_map/ppermute | solution.py:75
  115.3 9.8 %collective-permute-start.30 = (bf16[576,128]{1,0:T(8,128)(2,1)}, bf16[576,128]{1,0:T(8,128)(2,1)S(1)}, u32[]{:S(2)}, u32[]{:S(2)}) collective-permute-start(bf16[576,128]{1,0:T(8,128)(2,1)} %get-tuple-element.209), channel_id=1, source_target_pairs={{0,24},{1,25},{2,26},{3,27},{4,28},{5,29},{6,30},{7,31},{8,0},{9,1... | collective-permute-start | bytes 442376 | tf_op jit(solution)/shard_map/ppermute | solution.py:75
  126.2 14.7 %collective-permute-start.31 = (bf16[624,128]{1,0:T(8,128)(2,1)S(1)}, bf16[624,128]{1,0:T(8,128)(2,1)S(1)}, u32[]{:S(2)}, u32[]{:S(2)}) collective-permute-start(bf16[624,128]{1,0:T(8,128)(2,1)S(1)} %get-tuple-element.225), channel_id=1, source_target_pairs={{0,8},{1,9},{2,10},{3,11},{4,12},{5,13},{6,14},{7,15},{8,16},{9,17... | collective-permute-start | bytes 479240 | tf_op jit(solution)/shard_map/ppermute | solution.py:75
  129.9 11.7 %collective-permute-start.32 = (bf16[624,128]{1,0:T(8,128)(2,1)S(1)}, bf16[624,128]{1,0:T(8,128)(2,1)S(1)}, u32[]{:S(2)}, u32[]{:S(2)}) collective-permute-start(bf16[624,128]{1,0:T(8,128)(2,1)S(1)} %get-tuple-element.224), channel_id=1, source_target_pairs={{0,16},{1,17},{2,18},{3,19},{4,20},{5,21},{6,22},{7,23},{8,24},{9,... | collective-permute-start | bytes 479240 | tf_op jit(solution)/shard_map/ppermute | solution.py:75
  132.2 9.4 %collective-permute-start.33 = (bf16[624,128]{1,0:T(8,128)(2,1)S(1)}, bf16[624,128]{1,0:T(8,128)(2,1)S(1)}, u32[]{:S(2)}, u32[]{:S(2)}) collective-permute-start(bf16[624,128]{1,0:T(8,128)(2,1)S(1)} %get-tuple-element.223), channel_id=1, source_target_pairs={{0,24},{1,25},{2,26},{3,27},{4,28},{5,29},{6,30},{7,31},{8,0},{9,1... | collective-permute-start | bytes 479240 | tf_op jit(solution)/shard_map/ppermute | solution.py:75
  133.1 8.5 %collective-permute-start.35 = (bf16[2,128,384]{2,1,0:T(8,128)(2,1)S(1)}, bf16[2,128,384]{2,1,0:T(8,128)(2,1)S(1)}, u32[]{:S(2)}, u32[]{:S(2)}) collective-permute-start(bf16[2,128,384]{2,1,0:T(8,128)(2,1)S(1)} %get-tuple-element.219), channel_id=1, source_target_pairs={{0,2},{1,3},{2,0},{3,1},{4,6},{5,7},{6,4},{7,5},{8,10},{9,11},{10,... | collective-permute-start | bytes 589832 | tf_op jit(solution)/shard_map/ppermute | solution.py:80
  134.9 6.0 %collective-permute-start.34 = (bf16[288,128]{1,0:T(8,128)(2,1)S(1)}, bf16[288,128]{1,0:T(8,128)(2,1)S(1)}, u32[]{:S(2)}, u32[]{:S(2)}) collective-permute-start(bf16[288,128]{1,0:T(8,128)(2,1)S(1)} %get-tuple-element.217), channel_id=1, source_target_pairs={{0,2},{1,3},{2,0},{3,1},{4,6},{5,7},{6,4},{7,5},{8,10},{9,11},{10,... | collective-permute-start | bytes 221192 | tf_op jit(solution)/shard_map/ppermute | solution.py:75
  (44 other events, 241.5 us)

commit v10 on v9

--- a/solution.py
+++ b/solution.py
@@ -152,7 +152,7 @@
             found = coordinates(number)
             slot = fold(order, {n: (found[n] - mine[n]) % SIZES[n] for n in SIZES})
             inside = (found["x"] - mine["x"]) % SIZES["x"]
-            entries.append(start(slot, found["z"], inside))
+            entries.append(start(slot, (found["z"] - mine["z"]) % SIZES["z"], inside))
     entries.append(mine["c"])
     entries.append(mine["z"])
     return jnp.stack([jnp.asarray(entry, jnp.int32) for entry in entries])
@@ -193,10 +193,9 @@
     tail = summed(keep_rest, got_rest_tail).astype(BF16)
     dkv = summed(dkv_keep, got_dkv).astype(BF16)
     got_hx, got_ty, low, mid, far, tail, dkv, vector = together(got_hx, got_ty, low, mid, far, tail, dkv, vector)
-    place = coordinates(device_number() // inner_count())["z"]
 
     def part_for(array, shift):
-        return lax.dynamic_slice_in_dim(array, HEAD_ROWS * ((place + shift) % SIZES["z"]), HEAD_ROWS, 0)
+        return array[HEAD_ROWS * shift : HEAD_ROWS * shift + HEAD_ROWS]
 
     vector = summed_vector(vector, got_hx[PART:])
     hy = jnp.concatenate([summed(mid, got_hx[:PART]).astype(BF16), vector])
@@ -475,11 +474,10 @@
     gain_two = gains_ref[1:2, :]
     low_rows = lower_lanes((ROWS, LANES))
 
-    @pl.loop(0, 2)
-    def _(mb):
+    for mb in range(0, 2):
         lane = lax.broadcasted_iota(jnp.int32, (ROWS, WIDE), 1)
         for slot in range(4):
-            rows = pl.ds(pl.multiple_of(mb * 512 + slot * ROWS, ROWS), ROWS)
+            rows = pl.ds(mb * 512 + slot * ROWS, ROWS)
             x = jnp.where(lane < MODEL_WIDTH, at_slot(tokens_pair, slot)[mb].astype(F32), 0.0)
             normed, _ = normed_rows(x)
             normed_all[rows, :] = normed
@@ -500,9 +498,8 @@
     w_kv[0:288, 256:384] = jnp.where(low, rest_key, half_turn(rest_value)).astype(BF16)
     w_kv[288:576, 256:384] = jnp.where(low, half_turn(rest_key), rest_value).astype(BF16)
 
-    @pl.loop(0, 2)
-    def _(mb):
-        rows = pl.ds(pl.multiple_of(mb * 512, 512), 512)
+    for mb in range(0, 2):
+        rows = pl.ds(mb * 512, 512)
         pair = product(hidden_all[rows, :], w_kv[...]) + bias_kv_ref[...]
         cosines = jnp.concatenate([at_slot(cos_pair, slot)[mb] for slot in range(4)], axis=0)
         sines = jnp.concatenate([at_slot(sin_pair, slot)[mb] for slot in range(4)], axis=0)
@@ -532,12 +529,11 @@
         found = [jnp.where(low_rows, parts[2 * k], parts[2 * k + 1]) for k in range(4)]
         return found + [jnp.where(low_rows, parts[8], 0.0)]
 
-    @pl.loop(0, 2)
-    def _(mb):
-        rows = pl.ds(pl.multiple_of(mb * ROWS, ROWS), ROWS)
-        key_rows = pl.ds(pl.multiple_of(mb * 512, 512), 512)
+    for mb in range(0, 2):
+        rows = pl.ds(mb * ROWS, ROWS)
+        key_rows = pl.ds(mb * 512, 512)
         cosines, sines = cos_pair[0][0, mb], sin_pair[0][0, mb]
-        made = product(hidden_all[pl.ds(pl.multiple_of(mb * 512, 512), ROWS), :], w_q[...]) + bias_q_ref[...]
+        made = product(hidden_all[pl.ds(mb * 512, ROWS), :], w_q[...]) + bias_q_ref[...]
         for k in range(5):
             turned = rope(made[:, LANES * k : LANES * k + LANES], cosines, sines)
             queries[rows, LANES * k : LANES * k + LANES] = (turned * HEAD_SIZE ** (-0.5)).astype(BF16)
@@ -625,30 +621,29 @@
         store_pair(at, even_head, odd_head, TO_HEAD, 0)
         store_pair(at, even_tail, odd_tail, TO_TAIL, 0)
 
-    @pl.loop(0, 4)
-    def _(k):
-        made = rows_product(act_all[:, pl.ds(pl.multiple_of(k * 384, 128), 384)], grad_low)
+    for k in range(0, 4):
+        made = rows_product(act_all[:, pl.ds(k * 384, 384)], grad_low)
         store_rows(12 + k, tiles_of_rows(made[0:192]), tiles_of_rows(made[192:384]))
 
-    def deliveries(first, count, sem):
+    def deliveries(z, sem):
         copies = []
+        inside = pl.multiple_of(HEAD_ROWS * lax.rem(z + 4 - place, 4), HEAD_ROWS)
         for base, outs_of in ((both_all.at[0], parts_out[0:4]), (both_all.at[1], parts_out[4:10])):
             rest = [(outs_of[2], PART * k) for k in range(3)] if len(outs_of) == 4 else [(out, 0) for out in outs_of[2:5]]
             targets = [(outs_of[0], 0, FIRST_AT), (outs_of[1], 0, TAIL_AT)]
             targets += [(out, into, PART * k) for k, (out, into) in enumerate(rest)]
             targets.append((outs_of[-1], 0, 3 * PART))
             for out, into, start in targets:
-                rows = HEAD_ROWS * count
                 copies.append(
                     pltpu.make_async_copy(
-                        base.at[pl.ds(start + HEAD_ROWS * first, rows)],
-                        out.at[pl.ds(into + HEAD_ROWS * first, rows)],
+                        base.at[pl.ds(pl.multiple_of(start + inside, 16), HEAD_ROWS)],
+                        out.at[pl.ds(pl.multiple_of(into + inside, 16), HEAD_ROWS)],
                         out_sems.at[sem + len(copies)],
                     )
                 )
         return copies
 
-    early = deliveries(1, 3, 12)
+    early = deliveries(1, 12) + deliveries(2, 24) + deliveries(3, 36)
     for copy in early:
         copy.start()
 
@@ -663,10 +658,9 @@
     d_attended[...] = times_transposed(d_branch, w_out[...]).astype(BF16)
     grad_out = rows_product(attended[...], d_branch)
 
-    @pl.loop(0, 2)
-    def _(mb):
-        rows = pl.ds(pl.multiple_of(mb * ROWS, ROWS), ROWS)
-        key_rows = pl.ds(pl.multiple_of(mb * 512, 512), 512)
+    for mb in range(0, 2):
+        rows = pl.ds(mb * ROWS, ROWS)
+        key_rows = pl.ds(mb * 512, 512)
         parts = []
         d_keys = []
         d_values = []
@@ -697,7 +691,7 @@
         dkv_all[key_rows, 256:384] = jnp.where(low_keys, key_b, d_values[2]).astype(BF16)
         for slot in range(4):
             target = dkv_send if slot % 2 else dkv_keep
-            target[slot // 2, mb] = dkv_all[pl.ds(pl.multiple_of(mb * 512 + slot * ROWS, ROWS), ROWS), :]
+            target[slot // 2, mb] = dkv_all[pl.ds(mb * 512 + slot * ROWS, ROWS), :]
 
     dkv = dkv_all[...]
     d_q = d_query[...]
@@ -751,9 +745,9 @@
     both = jnp.concatenate([high, vector - high], axis=0).astype(BF16)
     for k in range(2):
         both_all[k, at : at + 2 * VECTOR_ROWS, :] = both
-    last = deliveries(0, 1, 0)
-    last.append(pltpu.make_async_copy(both_all.at[0, pl.ds(at, 2 * VECTOR_ROWS)], parts_out[0].at[pl.ds(PART, 2 * VECTOR_ROWS)], out_sems.at[24]))
-    last.append(pltpu.make_async_copy(both_all.at[1, pl.ds(at, 2 * VECTOR_ROWS)], parts_out[4].at[pl.ds(PART, 2 * VECTOR_ROWS)], out_sems.at[25]))
+    last = deliveries(0, 0)
+    last.append(pltpu.make_async_copy(both_all.at[0, pl.ds(at, 2 * VECTOR_ROWS)], parts_out[0].at[pl.ds(PART, 2 * VECTOR_ROWS)], out_sems.at[48]))
+    last.append(pltpu.make_async_copy(both_all.at[1, pl.ds(at, 2 * VECTOR_ROWS)], parts_out[4].at[pl.ds(PART, 2 * VECTOR_ROWS)], out_sems.at[49]))
     for copy in last:
         copy.start()
     for copy in early + last:
@@ -802,7 +796,7 @@
         in_specs=[pl.BlockSpec(memory_space=pltpu.SMEM)] + [anywhere] * 12 + [vmem] * 12,
         out_specs=(vmem,) + (anywhere,) * 10 + (vmem,) * 4,
         scratch_shapes=[pltpu.VMEM(dims, kind) for dims, kind in scratch]
-        + [pltpu.SemaphoreType.DMA((48,)), pltpu.SemaphoreType.DMA((26,))],
+        + [pltpu.SemaphoreType.DMA((48,)), pltpu.SemaphoreType.DMA((50,))],
         compiler_params=pltpu.CompilerParams(vmem_limit_bytes=50 * 1024 * 1024),
         name="layer",
     )(slots, *heads, *tails, *others)

time: 148 us -> 150 us (1.014)
  waiting for transfers between devices: 54.3 us -> 66.3 us
  starting transfers between devices: 36.4 us -> 32.3 us
  other arithmetic: 12.6 us -> 9.16 us
  local copies, waits for them, and re-layouts: 8.31 us -> 6.47 us
    ppermute x32, waiting for transfers between devices: 45.9 us -> 65.2 us  [moved(): return lax.ppermute(buffer, ('dp', 'ctx'), pairs)]
    ppermute x4, waiting for transfers between devices: 8.36 us -> 1.08 us  [across(): lax.ppermute(buffer, 'ctx', [(i, i ^ distance) for i in range(count)])]
    ppermute x32, starting transfers between devices: 34.7 us -> 30.3 us  [moved(): return lax.ppermute(buffer, ('dp', 'ctx'), pairs)]
    unnamed x82 -> x70, local copies, waits for them, and re-layouts: 3.72 us -> 1.88 us
    convert_element_type x1, other arithmetic: 1.99 us -> 0.16 us  [scatter_blocks(): summed(part_for(tail, s), part_for(got_ty, s)).astype(BF16)]
  transfers between devices with their start and end apart: 36 -> 36, of which waited for: 18 -> 19; matrix products, arithmetic and copies ran while one was open for 10% -> 9% of each run, Pallas kernels for 0% -> 0%
where the time goes in v10:
time: 150 us; the launch traced here: 149 us
  waiting for transfers between devices  66.3 us (44%)
  Pallas kernels  33.7 us (22%)
  starting transfers between devices  32.3 us (22%)
  other arithmetic  9.16 us (6%)
  local copies, waits for them, and re-layouts  6.47 us (4%)
    ppermute x32, waiting for transfers between devices, moved(): return lax.ppermute(buffer, ('dp', 'ctx'), pairs)  65.2 us
    ppermute x32, starting transfers between devices, moved(): return lax.ppermute(buffer, ('dp', 'ctx'), pairs)  30.3 us
    pallas_call x1, Pallas kernels, run_layer(): pl.pallas_call(layer_kernel, out_shape=(shape((2, MODEL_WIDTH, ROWS), BF1...  27 us
    pallas_call x1, Pallas kernels, finish(): pl.pallas_call(finish_kernel, out_shape=shapes, in_specs=[pl.BlockSpec(me...  4.76 us
  transfers between devices with their start and end apart: 36, of which 19 were waited for; matrix products, arithmetic and copies ran while one was open for 9% of the time, Pallas kernels for 0%

profile of v10, /device:TPU:0, one launch (start us, length us, event | category | flops | bytes accessed | tf_op | source)
XLA Modules:
  0.0 149.4 jit_solution(12691912245629199368)
XLA Ops:
  0.7 1.9 %to_tiles.1 = (bf16[576,128]{1,0:T(8,128)(2,1)}, bf16[288,128]{1,0:T(8,128)(2,1)}) custom-call(s32[1]{0:T(128)} %bitcast.kind_ref, f32[864,128]{1,0:T(8,128)} %bitcast.154), custom_call_target="tpu_custom_call" | custom-call | tf_op jit(solution)/shard_map/to_tiles/pallas_call | solution.py:268
  2.5 5.0 %collective-permute-start.4 = (bf16[576,128]{1,0:T(8,128)(2,1)}, bf16[576,128]{1,0:T(8,128)(2,1)S(1)}, u32[]{:S(2)}, u32[]{:S(2)}) collective-permute-start(bf16[576,128]{1,0:T(8,128)(2,1)} %get-tuple-element.97), channel_id=1, source_target_pairs={{0,24},{1,25},{2,26},{3,27},{4,28},{5,29},{6,30},{7,31},{8,0},{9,1... | collective-permute-start | bytes 442376 | tf_op jit(solution)/shard_map/ppermute | solution.py:75
  8.5 1.5 collective-permute-start
  11.0 1.2 copy.39
  15.9 4.3 %collective-permute-done.3 = bf16[576,128]{1,0:T(8,128)(2,1)S(1)} collective-permute-done((bf16[576,128]{1,0:T(8,128)(2,1)}, bf16[576,128]{1,0:T(8,128)(2,1)S(1)}, u32[]{:S(2)}, u32[]{:S(2)}) %collective-permute-start.3) | collective-permute-done | bytes 147488 | tf_op jit(solution)/shard_map/ppermute | solution.py:75
  20.8 3.3 %collective-permute-start.9 = (bf16[2,288,128]{2,1,0:T(8,128)(2,1)S(1)}, bf16[2,288,128]{2,1,0:T(8,128)(2,1)S(1)}, u32[]{:S(2)}, u32[]{:S(2)}) collective-permute-start(bf16[2,288,128]{2,1,0:T(8,128)(2,1)S(1)} %pad_maximum_fusion.10), channel_id=1, source_target_pairs={{0,24},{1,25},{2,26},{3,27},{4,28},{5,29},{6,30},{7,31},{8,0},{9,1... | collective-permute-start | bytes 442376 | tf_op jit(solution)/shard_map/ppermute | solution.py:75
  25.2 1.5 collective-permute-start.6
  26.7 1.5 %collective-permute-start.5 = (bf16[4,576,128]{2,1,0:T(8,128)(2,1)S(1)}, bf16[4,576,128]{2,1,0:T(8,128)(2,1)S(1)}, u32[]{:S(2)}, u32[]{:S(2)}) collective-permute-start(bf16[4,576,128]{2,1,0:T(8,128)(2,1)S(1)} %pad_maximum_fusion.3.refs_1_), channel_id=1, source_target_pairs={{0,4},{1,5},{2,6},{3,7},{4,0},{5,1},{6,2},{7,3},{8,12},{9,13},{10,... | collective-permute-start | bytes 1769480 | tf_op jit(solution)/shard_map/ppermute | solution.py:75
  28.6 1.0 fusion
  29.7 6.7 %collective-permute-done.8 = bf16[2,288,128]{2,1,0:T(8,128)(2,1)S(1)} collective-permute-done((bf16[2,288,128]{2,1,0:T(8,128)(2,1)S(1)}, bf16[2,288,128]{2,1,0:T(8,128)(2,1)S(1)}, u32[]{:S(2)}, u32[]{:S(2)}) %collective-permute-start.8) | collective-permute-done | bytes 147488 | tf_op jit(solution)/shard_map/ppermute | solution.py:75
  36.4 2.3 %collective-permute-done.6.refs_3_ = bf16[4,576,128]{2,1,0:T(8,128)(2,1)S(1)} collective-permute-done((bf16[4,576,128]{2,1,0:T(8,128)(2,1)S(1)}, bf16[4,576,128]{2,1,0:T(8,128)(2,1)S(1)}, u32[]{:S(2)}, u32[]{:S(2)}) %collective-permute-start.6) | collective-permute-done | bytes 589856 | tf_op jit(solution)/shard_map/ppermute | solution.py:75
  38.7 1.2 collective-permute-done.5.refs_2_
  40.1 1.6 %collective-permute-start.11 = (bf16[8,288,128]{2,1,0:T(8,128)(2,1)S(1)}, bf16[8,288,128]{2,1,0:T(8,128)(2,1)S(1)}, u32[]{:S(2)}, u32[]{:S(2)}) collective-permute-start(bf16[8,288,128]{2,1,0:T(8,128)(2,1)S(1)} %constant_dynamic-update-slice_fusion.refs_9_), channel_id=1, source_target_pairs={{0,4},{1,5},{2,6},{3,7},{4,0},{5,1},{6,2},{7,3},{8,12},{9,13},{10,... | collective-permute-start | bytes 1769480 | tf_op jit(solution)/shard_map/ppermute | solution.py:75
  42.9 12.9 %collective-permute-done.11.refs_10_ = bf16[8,288,128]{2,1,0:T(8,128)(2,1)S(1)} collective-permute-done((bf16[8,288,128]{2,1,0:T(8,128)(2,1)S(1)}, bf16[8,288,128]{2,1,0:T(8,128)(2,1)S(1)}, u32[]{:S(2)}, u32[]{:S(2)}) %collective-permute-start.11) | collective-permute-done | bytes 589856 | tf_op jit(solution)/shard_map/ppermute | solution.py:75
  56.3 1.1 collective-permute-done.10.refs_4_
  58.9 1.0 fusion.1
  61.6 27.0 %layer.1 = (bf16[2,576,128]{2,1,0:T(8,128)(2,1)}, bf16[2352,128]{1,0:T(8,128)(2,1)}, bf16[2304,128]{1,0:T(8,128)(2,1)S(1)}, bf16[6912,128]{1,0:T(8,128)(2,1)}, b...) custom-call(s32[98]{0:T(128)S(1)} %stack.448.refs_0_, ...), custom_call_target="tpu_custom_call" | custom-call | tf_op jit(solution)/shard_map/layer/pallas_call | solution.py:786
  89.3 2.4 %collective-permute-done.20 = bf16[2304,128]{1,0:T(8,128)(2,1)S(1)} collective-permute-done((bf16[2304,128]{1,0:T(8,128)(2,1)S(1)}, bf16[2304,128]{1,0:T(8,128)(2,1)S(1)}, u32[]{:S(2)}, u32[]{:S(2)}) %collective-permute-start.20) | collective-permute-done | bytes 589856 | tf_op jit(solution)/shard_map/ppermute | solution.py:75
  91.8 1.2 add_convert_fusion.5
  93.0 1.6 %collective-permute-start.22 = (bf16[2304,128]{1,0:T(8,128)(2,1)S(1)}, bf16[2304,128]{1,0:T(8,128)(2,1)S(1)}, u32[]{:S(2)}, u32[]{:S(2)}) collective-permute-start(bf16[2304,128]{1,0:T(8,128)(2,1)S(1)} %add_convert_fusion.5), channel_id=1, source_target_pairs={{0,4},{1,5},{2,6},{3,7},{4,0},{5,1},{6,2},{7,3},{8,12},{9,13},{10,... | collective-permute-start | bytes 1769480 | tf_op jit(solution)/shard_map/ppermute | solution.py:75
  96.8 2.5 %collective-permute-done.23 = bf16[6912,128]{1,0:T(8,128)(2,1)S(1)} collective-permute-done((bf16[6912,128]{1,0:T(8,128)(2,1)}, bf16[6912,128]{1,0:T(8,128)(2,1)S(1)}, u32[]{:S(2)}, u32[]{:S(2)}) %collective-permute-start.23) | collective-permute-done | bytes 1769504 | tf_op jit(solution)/shard_map/ppermute | solution.py:75
  99.8 8.8 %collective-permute-done.22 = bf16[2304,128]{1,0:T(8,128)(2,1)S(1)} collective-permute-done((bf16[2304,128]{1,0:T(8,128)(2,1)S(1)}, bf16[2304,128]{1,0:T(8,128)(2,1)S(1)}, u32[]{:S(2)}, u32[]{:S(2)}) %collective-permute-start.22) | collective-permute-done | bytes 589856 | tf_op jit(solution)/shard_map/ppermute | solution.py:75
  108.7 2.3 %collective-permute-done.21 = bf16[2352,128]{1,0:T(8,128)(2,1)S(1)} collective-permute-done((bf16[2352,128]{1,0:T(8,128)(2,1)S(1)}, bf16[2352,128]{1,0:T(8,128)(2,1)S(1)}, u32[]{:S(2)}, u32[]{:S(2)}) %collective-permute-start.21) | collective-permute-done | bytes 602144 | tf_op jit(solution)/shard_map/ppermute | solution.py:75
  112.5 2.4 %collective-permute-start.30 = (bf16[576,128]{1,0:T(8,128)(2,1)S(1)}, bf16[576,128]{1,0:T(8,128)(2,1)S(1)}, u32[]{:S(2)}, u32[]{:S(2)}) collective-permute-start(bf16[576,128]{1,0:T(8,128)(2,1)S(1)} %get-tuple-element.209), channel_id=1, source_target_pairs={{0,24},{1,25},{2,26},{3,27},{4,28},{5,29},{6,30},{7,31},{8,0},{9,1... | collective-permute-start | bytes 442376 | tf_op jit(solution)/shard_map/ppermute | solution.py:75
  115.7 3.5 %collective-permute-done.30 = bf16[576,128]{1,0:T(8,128)(2,1)S(1)} collective-permute-done((bf16[576,128]{1,0:T(8,128)(2,1)S(1)}, bf16[576,128]{1,0:T(8,128)(2,1)S(1)}, u32[]{:S(2)}, u32[]{:S(2)}) %collective-permute-start.30) | collective-permute-done | bytes 147488 | tf_op jit(solution)/shard_map/ppermute | solution.py:75
  119.2 8.1 %collective-permute-done.29 = bf16[576,128]{1,0:T(8,128)(2,1)S(1)} collective-permute-done((bf16[576,128]{1,0:T(8,128)(2,1)S(1)}, bf16[576,128]{1,0:T(8,128)(2,1)S(1)}, u32[]{:S(2)}, u32[]{:S(2)}) %collective-permute-start.29) | collective-permute-done | bytes 147488 | tf_op jit(solution)/shard_map/ppermute | solution.py:75
  127.3 1.0 add_convert_fusion.8
  130.1 1.9 %collective-permute-start.31 = (bf16[624,128]{1,0:T(8,128)(2,1)S(1)}, bf16[624,128]{1,0:T(8,128)(2,1)S(1)}, u32[]{:S(2)}, u32[]{:S(2)}) collective-permute-start(bf16[624,128]{1,0:T(8,128)(2,1)S(1)} %get-tuple-element.225), channel_id=1, source_target_pairs={{0,8},{1,9},{2,10},{3,11},{4,12},{5,13},{6,14},{7,15},{8,16},{9,17... | collective-permute-start | bytes 479240 | tf_op jit(solution)/shard_map/ppermute | solution.py:75
  132.8 1.3 collective-permute-start.35
  136.1 3.3 %collective-permute-done.34.other_ref = bf16[288,128]{1,0:T(8,128)(2,1)S(1)} collective-permute-done((bf16[288,128]{1,0:T(8,128)(2,1)S(1)}, bf16[288,128]{1,0:T(8,128)(2,1)S(1)}, u32[]{:S(2)}, u32[]{:S(2)}) %collective-permute-start.34) | collective-permute-done | bytes 73760 | tf_op jit(solution)/shard_map/ppermute | solution.py:75
  139.5 4.2 %collective-permute-done.32.two_ref = bf16[624,128]{1,0:T(8,128)(2,1)S(1)} collective-permute-done((bf16[624,128]{1,0:T(8,128)(2,1)S(1)}, bf16[624,128]{1,0:T(8,128)(2,1)S(1)}, u32[]{:S(2)}, u32[]{:S(2)}) %collective-permute-start.32) | collective-permute-done | bytes 159776 | tf_op jit(solution)/shard_map/ppermute | solution.py:75
  144.5 4.8 %finish.1 = (f32[24,128]{1,0:T(8,128)}, f32[24,128]{1,0:T(8,128)}, f32[24,128]{1,0:T(8,128)}, f32[864,128]{1,0:T(8,128)}, f32[864,128]{1,0:T(8,128)}, /*index=5*/f32[864,128]{1,0:T(8,128)}, bf16[2,576,128]{2,1,0:T(8,128)(2,1)}) custom-call(s32[2]{0:T(128)} %pad_add_fusion.table_ref, f32[576,128]{1,0:T(8,128)} %get-tuple-element.203.head_ref, ...), custom_call_target="tpu_custom_call" | custom-call | tf_op jit(solution)/shard_map/finish/pallas_call | solution.py:370
  (175 shorter events, 23.5 us)
Async XLA Ops:
  2.5 13.4 %collective-permute-start.4 = (bf16[576,128]{1,0:T(8,128)(2,1)}, bf16[576,128]{1,0:T(8,128)(2,1)S(1)}, u32[]{:S(2)}, u32[]{:S(2)}) collective-permute-start(bf16[576,128]{1,0:T(8,128)(2,1)} %get-tuple-element.97), channel_id=1, source_target_pairs={{0,24},{1,25},{2,26},{3,27},{4,28},{5,29},{6,30},{7,31},{8,0},{9,1... | collective-permute-start | bytes 442376 | tf_op jit(solution)/shard_map/ppermute | solution.py:75
  7.6 12.6 %collective-permute-start.3 = (bf16[576,128]{1,0:T(8,128)(2,1)}, bf16[576,128]{1,0:T(8,128)(2,1)S(1)}, u32[]{:S(2)}, u32[]{:S(2)}) collective-permute-start(bf16[576,128]{1,0:T(8,128)(2,1)} %get-tuple-element.97), channel_id=1, source_target_pairs={{0,16},{1,17},{2,18},{3,19},{4,20},{5,21},{6,22},{7,23},{8,24},{9,... | collective-permute-start | bytes 442376 | tf_op jit(solution)/shard_map/ppermute | solution.py:75
  7.6 12.6 %collective-permute-start.2 = (bf16[576,128]{1,0:T(8,128)(2,1)}, bf16[576,128]{1,0:T(8,128)(2,1)S(1)}, u32[]{:S(2)}, u32[]{:S(2)}) collective-permute-start(bf16[576,128]{1,0:T(8,128)(2,1)} %get-tuple-element.97), channel_id=1, source_target_pairs={{0,8},{1,9},{2,10},{3,11},{4,12},{5,13},{6,14},{7,15},{8,16},{9,17... | collective-permute-start | bytes 442376 | tf_op jit(solution)/shard_map/ppermute | solution.py:75
  8.5 7.4 %collective-permute-start = (bf16[288,128]{1,0:T(8,128)(2,1)}, bf16[288,128]{1,0:T(8,128)(2,1)S(1)}, u32[]{:S(2)}, u32[]{:S(2)}) collective-permute-start(bf16[288,128]{1,0:T(8,128)(2,1)} %get-tuple-element.101), channel_id=1, source_target_pairs={{0,2},{1,3},{2,0},{3,1},{4,6},{5,7},{6,4},{7,5},{8,10},{9,11},{10,... | collective-permute-start | bytes 221192 | tf_op jit(solution)/shard_map/ppermute | solution.py:75
  12.3 8.4 %collective-permute-start.1 = (bf16[2,128,640]{2,1,0:T(8,128)(2,1)S(1)}, bf16[2,128,640]{2,1,0:T(8,128)(2,1)S(1)}, u32[]{:S(2)}, u32[]{:S(2)}) collective-permute-start(bf16[2,128,640]{2,1,0:T(8,128)(2,1)S(1)} %maximum_maximum_fusion.refs_0_), channel_id=1, source_target_pairs={{0,2},{1,3},{2,0},{3,1},{4,6},{5,7},{6,4},{7,5},{8,10},{9,11},{10,... | collective-permute-start | bytes 983048 | tf_op jit(solution)/shard_map/ppermute | solution.py:80
  20.8 8.9 %collective-permute-start.9 = (bf16[2,288,128]{2,1,0:T(8,128)(2,1)S(1)}, bf16[2,288,128]{2,1,0:T(8,128)(2,1)S(1)}, u32[]{:S(2)}, u32[]{:S(2)}) collective-permute-start(bf16[2,288,128]{2,1,0:T(8,128)(2,1)S(1)} %pad_maximum_fusion.10), channel_id=1, source_target_pairs={{0,24},{1,25},{2,26},{3,27},{4,28},{5,29},{6,30},{7,31},{8,0},{9,1... | collective-permute-start | bytes 442376 | tf_op jit(solution)/shard_map/ppermute | solution.py:75
  24.0 12.3 %collective-permute-start.8 = (bf16[2,288,128]{2,1,0:T(8,128)(2,1)S(1)}, bf16[2,288,128]{2,1,0:T(8,128)(2,1)S(1)}, u32[]{:S(2)}, u32[]{:S(2)}) collective-permute-start(bf16[2,288,128]{2,1,0:T(8,128)(2,1)S(1)} %pad_maximum_fusion.10), channel_id=1, source_target_pairs={{0,16},{1,17},{2,18},{3,19},{4,20},{5,21},{6,22},{7,23},{8,24},{9,... | collective-permute-start | bytes 442376 | tf_op jit(solution)/shard_map/ppermute | solution.py:75
  24.9 11.5 %collective-permute-start.7 = (bf16[2,288,128]{2,1,0:T(8,128)(2,1)S(1)}, bf16[2,288,128]{2,1,0:T(8,128)(2,1)S(1)}, u32[]{:S(2)}, u32[]{:S(2)}) collective-permute-start(bf16[2,288,128]{2,1,0:T(8,128)(2,1)S(1)} %pad_maximum_fusion.10), channel_id=1, source_target_pairs={{0,8},{1,9},{2,10},{3,11},{4,12},{5,13},{6,14},{7,15},{8,16},{9,17... | collective-permute-start | bytes 442376 | tf_op jit(solution)/shard_map/ppermute | solution.py:75
  25.2 13.5 %collective-permute-start.6 = (bf16[4,576,128]{2,1,0:T(8,128)(2,1)S(1)}, bf16[4,576,128]{2,1,0:T(8,128)(2,1)S(1)}, u32[]{:S(2)}, u32[]{:S(2)}) collective-permute-start(bf16[4,576,128]{2,1,0:T(8,128)(2,1)S(1)} %pad_maximum_fusion.3.refs_1_), channel_id=1, source_target_pairs={{0,2},{1,3},{2,0},{3,1},{4,6},{5,7},{6,4},{7,5},{8,10},{9,11},{10,... | collective-permute-start | bytes 1769480 | tf_op jit(solution)/shard_map/ppermute | solution.py:75
  26.7 13.2 %collective-permute-start.5 = (bf16[4,576,128]{2,1,0:T(8,128)(2,1)S(1)}, bf16[4,576,128]{2,1,0:T(8,128)(2,1)S(1)}, u32[]{:S(2)}, u32[]{:S(2)}) collective-permute-start(bf16[4,576,128]{2,1,0:T(8,128)(2,1)S(1)} %pad_maximum_fusion.3.refs_1_), channel_id=1, source_target_pairs={{0,4},{1,5},{2,6},{3,7},{4,0},{5,1},{6,2},{7,3},{8,12},{9,13},{10,... | collective-permute-start | bytes 1769480 | tf_op jit(solution)/shard_map/ppermute | solution.py:75
  40.1 15.7 %collective-permute-start.11 = (bf16[8,288,128]{2,1,0:T(8,128)(2,1)S(1)}, bf16[8,288,128]{2,1,0:T(8,128)(2,1)S(1)}, u32[]{:S(2)}, u32[]{:S(2)}) collective-permute-start(bf16[8,288,128]{2,1,0:T(8,128)(2,1)S(1)} %constant_dynamic-update-slice_fusion.refs_9_), channel_id=1, source_target_pairs={{0,4},{1,5},{2,6},{3,7},{4,0},{5,1},{6,2},{7,3},{8,12},{9,13},{10,... | collective-permute-start | bytes 1769480 | tf_op jit(solution)/shard_map/ppermute | solution.py:75
  41.7 14.6 %collective-permute-start.13 = (bf16[4,576,128]{2,1,0:T(8,128)(2,1)S(1)}, bf16[4,576,128]{2,1,0:T(8,128)(2,1)S(1)}, u32[]{:S(2)}, u32[]{:S(2)}) collective-permute-start(bf16[4,576,128]{2,1,0:T(8,128)(2,1)S(1)} %collective-permute-done.5.refs_2_), channel_id=1, source_target_pairs={{0,1},{1,0},{2,3},{3,2},{4,5},{5,4},{6,7},{7,6},{8,9},{9,8},{10,11... | collective-permute-start | bytes 1769480 | tf_op jit(solution)/shard_map/ppermute | solution.py:75
  41.9 15.6 %collective-permute-start.10 = (bf16[4,576,128]{2,1,0:T(8,128)(2,1)S(1)}, bf16[4,576,128]{2,1,0:T(8,128)(2,1)S(1)}, u32[]{:S(2)}, u32[]{:S(2)}) collective-permute-start(bf16[4,576,128]{2,1,0:T(8,128)(2,1)S(1)} %collective-permute-done.5.refs_2_), channel_id=1, source_target_pairs={{0,2},{1,3},{2,0},{3,1},{4,6},{5,7},{6,4},{7,5},{8,10},{9,11},{10,... | collective-permute-start | bytes 1769480 | tf_op jit(solution)/shard_map/ppermute | solution.py:75
  42.4 13.9 %collective-permute-start.12 = (bf16[4,576,128]{2,1,0:T(8,128)(2,1)S(1)}, bf16[4,576,128]{2,1,0:T(8,128)(2,1)S(1)}, u32[]{:S(2)}, u32[]{:S(2)}) collective-permute-start(bf16[4,576,128]{2,1,0:T(8,128)(2,1)S(1)} %pad_maximum_fusion.3.refs_1_), channel_id=1, source_target_pairs={{0,1},{1,0},{2,3},{3,2},{4,5},{5,4},{6,7},{7,6},{8,9},{9,8},{10,11... | collective-permute-start | bytes 1769480 | tf_op jit(solution)/shard_map/ppermute | solution.py:75
  42.5 13.8 %collective-permute-start.14 = (bf16[4,576,128]{2,1,0:T(8,128)(2,1)S(1)}, bf16[4,576,128]{2,1,0:T(8,128)(2,1)S(1)}, u32[]{:S(2)}, u32[]{:S(2)}) collective-permute-start(bf16[4,576,128]{2,1,0:T(8,128)(2,1)S(1)} %collective-permute-done.6.refs_3_), channel_id=1, source_target_pairs={{0,1},{1,0},{2,3},{3,2},{4,5},{5,4},{6,7},{7,6},{8,9},{9,8},{10,11... | collective-permute-start | bytes 1769480 | tf_op jit(solution)/shard_map/ppermute | solution.py:75
  58.1 2.7 %collective-permute-start.18 = (bf16[8,288,128]{2,1,0:T(8,128)(2,1)S(1)}, bf16[8,288,128]{2,1,0:T(8,128)(2,1)S(1)}, u32[]{:S(2)}, u32[]{:S(2)}) collective-permute-start(bf16[8,288,128]{2,1,0:T(8,128)(2,1)S(1)} %collective-permute-done.11.refs_10_), channel_id=1, source_target_pairs={{0,1},{1,0},{2,3},{3,2},{4,5},{5,4},{6,7},{7,6},{8,9},{9,8},{10,11... | collective-permute-start | bytes 1769480 | tf_op jit(solution)/shard_map/ppermute | solution.py:75
  88.7 2.9 %collective-permute-start.19 = (bf16[2352,128]{1,0:T(8,128)(2,1)}, bf16[2352,128]{1,0:T(8,128)(2,1)S(1)}, u32[]{:S(2)}, u32[]{:S(2)}) collective-permute-start(bf16[2352,128]{1,0:T(8,128)(2,1)} %get-tuple-element.129), channel_id=1, source_target_pairs={{0,1},{1,0},{2,3},{3,2},{4,5},{5,4},{6,7},{7,6},{8,9},{9,8},{10,11... | collective-permute-start | bytes 1806344 | tf_op jit(solution)/shard_map/ppermute | solution.py:75
  88.9 2.7 %collective-permute-start.20 = (bf16[2304,128]{1,0:T(8,128)(2,1)S(1)}, bf16[2304,128]{1,0:T(8,128)(2,1)S(1)}, u32[]{:S(2)}, u32[]{:S(2)}) collective-permute-start(bf16[2304,128]{1,0:T(8,128)(2,1)S(1)} %get-tuple-element.130), channel_id=1, source_target_pairs={{0,1},{1,0},{2,3},{3,2},{4,5},{5,4},{6,7},{7,6},{8,9},{9,8},{10,11... | collective-permute-start | bytes 1769480 | tf_op jit(solution)/shard_map/ppermute | solution.py:75
  91.6 4.4 %collective-permute-start.25 = (bf16[2,2,128,384]{3,2,1,0:T(8,128)(2,1)S(1)}, bf16[2,2,128,384]{3,2,1,0:T(8,128)(2,1)S(1)}, u32[]{:S(2)}, u32[]{:S(2)}) collective-permute-start(bf16[2,2,128,384]{3,2,1,0:T(8,128)(2,1)S(1)} %get-tuple-element.144), channel_id=1, source_target_pairs={{0,1},{1,0},{2,3},{3,2},{4,5},{5,4},{6,7},{7,6},{8,9},{9,8},{10,11... | collective-permute-start | bytes 1179656 | tf_op jit(solution)/shard_map/ppermute | solution.py:80
  93.0 15.7 %collective-permute-start.22 = (bf16[2304,128]{1,0:T(8,128)(2,1)S(1)}, bf16[2304,128]{1,0:T(8,128)(2,1)S(1)}, u32[]{:S(2)}, u32[]{:S(2)}) collective-permute-start(bf16[2304,128]{1,0:T(8,128)(2,1)S(1)} %add_convert_fusion.5), channel_id=1, source_target_pairs={{0,4},{1,5},{2,6},{3,7},{4,0},{5,1},{6,2},{7,3},{8,12},{9,13},{10,... | collective-permute-start | bytes 1769480 | tf_op jit(solution)/shard_map/ppermute | solution.py:75
  94.7 4.7 %collective-permute-start.23 = (bf16[6912,128]{1,0:T(8,128)(2,1)}, bf16[6912,128]{1,0:T(8,128)(2,1)S(1)}, u32[]{:S(2)}, u32[]{:S(2)}) collective-permute-start(bf16[6912,128]{1,0:T(8,128)(2,1)} %get-tuple-element.138), channel_id=1, source_target_pairs={{0,1},{1,0},{2,3},{3,2},{4,5},{5,4},{6,7},{7,6},{8,9},{9,8},{10,11... | collective-permute-start | bytes 5308424 | tf_op jit(solution)/shard_map/ppermute | solution.py:75
  95.4 15.6 %collective-permute-start.21 = (bf16[2352,128]{1,0:T(8,128)(2,1)S(1)}, bf16[2352,128]{1,0:T(8,128)(2,1)S(1)}, u32[]{:S(2)}, u32[]{:S(2)}) collective-permute-start(bf16[2352,128]{1,0:T(8,128)(2,1)S(1)} %pad_maximum_fusion.1), channel_id=1, source_target_pairs={{0,2},{1,3},{2,0},{3,1},{4,6},{5,7},{6,4},{7,5},{8,10},{9,11},{10,... | collective-permute-start | bytes 1806344 | tf_op jit(solution)/shard_map/ppermute | solution.py:75
  111.2 16.1 %collective-permute-start.26 = (bf16[2352,128]{1,0:T(8,128)(2,1)S(1)}, bf16[2352,128]{1,0:T(8,128)(2,1)S(1)}, u32[]{:S(2)}, u32[]{:S(2)}) collective-permute-start(bf16[2352,128]{1,0:T(8,128)(2,1)S(1)} %pad_maximum_fusion.2), channel_id=1, source_target_pairs={{0,4},{1,5},{2,6},{3,7},{4,0},{5,1},{6,2},{7,3},{8,12},{9,13},{10,... | collective-permute-start | bytes 1806344 | tf_op jit(solution)/shard_map/ppermute | solution.py:75
  111.8 15.5 %collective-permute-start.27 = (bf16[2304,128]{1,0:T(8,128)(2,1)S(1)}, bf16[2304,128]{1,0:T(8,128)(2,1)S(1)}, u32[]{:S(2)}, u32[]{:S(2)}) collective-permute-start(bf16[2304,128]{1,0:T(8,128)(2,1)S(1)} %get-tuple-element.148), channel_id=1, source_target_pairs={{0,2},{1,3},{2,0},{3,1},{4,6},{5,7},{6,4},{7,5},{8,10},{9,11},{10,... | collective-permute-start | bytes 1769480 | tf_op jit(solution)/shard_map/ppermute | solution.py:75
  112.5 6.7 %collective-permute-start.30 = (bf16[576,128]{1,0:T(8,128)(2,1)S(1)}, bf16[576,128]{1,0:T(8,128)(2,1)S(1)}, u32[]{:S(2)}, u32[]{:S(2)}) collective-permute-start(bf16[576,128]{1,0:T(8,128)(2,1)S(1)} %get-tuple-element.209), channel_id=1, source_target_pairs={{0,24},{1,25},{2,26},{3,27},{4,28},{5,29},{6,30},{7,31},{8,0},{9,1... | collective-permute-start | bytes 442376 | tf_op jit(solution)/shard_map/ppermute | solution.py:75
  114.9 12.4 %collective-permute-start.29 = (bf16[576,128]{1,0:T(8,128)(2,1)S(1)}, bf16[576,128]{1,0:T(8,128)(2,1)S(1)}, u32[]{:S(2)}, u32[]{:S(2)}) collective-permute-start(bf16[576,128]{1,0:T(8,128)(2,1)S(1)} %get-tuple-element.210), channel_id=1, source_target_pairs={{0,16},{1,17},{2,18},{3,19},{4,20},{5,21},{6,22},{7,23},{8,24},{9,... | collective-permute-start | bytes 442376 | tf_op jit(solution)/shard_map/ppermute | solution.py:75
  115.4 11.9 %collective-permute-start.28 = (bf16[576,128]{1,0:T(8,128)(2,1)S(1)}, bf16[576,128]{1,0:T(8,128)(2,1)S(1)}, u32[]{:S(2)}, u32[]{:S(2)}) collective-permute-start(bf16[576,128]{1,0:T(8,128)(2,1)S(1)} %get-tuple-element.211), channel_id=1, source_target_pairs={{0,8},{1,9},{2,10},{3,11},{4,12},{5,13},{6,14},{7,15},{8,16},{9,17... | collective-permute-start | bytes 442376 | tf_op jit(solution)/shard_map/ppermute | solution.py:75
  128.3 11.1 %collective-permute-start.33 = (bf16[624,128]{1,0:T(8,128)(2,1)S(1)}, bf16[624,128]{1,0:T(8,128)(2,1)S(1)}, u32[]{:S(2)}, u32[]{:S(2)}) collective-permute-start(bf16[624,128]{1,0:T(8,128)(2,1)S(1)} %get-tuple-element.223), channel_id=1, source_target_pairs={{0,24},{1,25},{2,26},{3,27},{4,28},{5,29},{6,30},{7,31},{8,0},{9,1... | collective-permute-start | bytes 479240 | tf_op jit(solution)/shard_map/ppermute | solution.py:75
  129.3 14.4 %collective-permute-start.32 = (bf16[624,128]{1,0:T(8,128)(2,1)S(1)}, bf16[624,128]{1,0:T(8,128)(2,1)S(1)}, u32[]{:S(2)}, u32[]{:S(2)}) collective-permute-start(bf16[624,128]{1,0:T(8,128)(2,1)S(1)} %get-tuple-element.224), channel_id=1, source_target_pairs={{0,16},{1,17},{2,18},{3,19},{4,20},{5,21},{6,22},{7,23},{8,24},{9,... | collective-permute-start | bytes 479240 | tf_op jit(solution)/shard_map/ppermute | solution.py:75
  130.1 13.6 %collective-permute-start.31 = (bf16[624,128]{1,0:T(8,128)(2,1)S(1)}, bf16[624,128]{1,0:T(8,128)(2,1)S(1)}, u32[]{:S(2)}, u32[]{:S(2)}) collective-permute-start(bf16[624,128]{1,0:T(8,128)(2,1)S(1)} %get-tuple-element.225), channel_id=1, source_target_pairs={{0,8},{1,9},{2,10},{3,11},{4,12},{5,13},{6,14},{7,15},{8,16},{9,17... | collective-permute-start | bytes 479240 | tf_op jit(solution)/shard_map/ppermute | solution.py:75
  132.8 10.9 %collective-permute-start.35 = (bf16[2,128,384]{2,1,0:T(8,128)(2,1)S(1)}, bf16[2,128,384]{2,1,0:T(8,128)(2,1)S(1)}, u32[]{:S(2)}, u32[]{:S(2)}) collective-permute-start(bf16[2,128,384]{2,1,0:T(8,128)(2,1)S(1)} %get-tuple-element.219), channel_id=1, source_target_pairs={{0,2},{1,3},{2,0},{3,1},{4,6},{5,7},{6,4},{7,5},{8,10},{9,11},{10,... | collective-permute-start | bytes 589832 | tf_op jit(solution)/shard_map/ppermute | solution.py:80
  134.8 4.6 %collective-permute-start.34 = (bf16[288,128]{1,0:T(8,128)(2,1)S(1)}, bf16[288,128]{1,0:T(8,128)(2,1)S(1)}, u32[]{:S(2)}, u32[]{:S(2)}) collective-permute-start(bf16[288,128]{1,0:T(8,128)(2,1)S(1)} %get-tuple-element.217), channel_id=1, source_target_pairs={{0,2},{1,3},{2,0},{3,1},{4,6},{5,7},{6,4},{7,5},{8,10},{9,11},{10,... | collective-permute-start | bytes 221192 | tf_op jit(solution)/shard_map/ppermute | solution.py:75
  (38 other events, 271.3 us)

commit v11 on v10

--- a/solution.py
+++ b/solution.py
@@ -93,9 +93,10 @@
     pair = jnp.stack([tail, tx])
     ay = moved(own, "y", 1)
     ax = moved(own, "x", 1)
-    tz = [moved(pair, "z", s) for s in (1, 2, 3)]
     near = jnp.stack([packed, two])
     tables = place_tables(near)
+    pair, *tables = together(pair, *tables)
+    tz = [moved(pair, "z", s) for s in (1, 2, 3)]
     own, pair, ay, ax, near, tables, others, *tz = together(own, pair, ay, ax, near, tables, others, *tz)
     eight = jnp.concatenate([pair] + tz)
     far = across(near, 1)
@@ -105,7 +106,7 @@
     acy = moved(ay, "c", 1)
     acx = moved(ax, "c", 1)
     tc = moved(eight, "c", 1)
-    axy, ty, ac, acy, acx, tc, far = together(axy, ty, ac, acy, acx, tc, far)
+    tc, acx, acy, ac, far, ty, axy = together(tc, acx, acy, ac, far, ty, axy)
     acxy = moved(axy, "c", 1)
     tcy = moved(ty, "c", 1)
     heads = [own, ay, ax, axy, ac, acy, acx, acxy]

time: 150 us -> 151 us (level)
  starting transfers between devices: 32.3 us -> 35.6 us
  waiting for transfers between devices: 66.3 us -> 63.1 us
    ppermute x32, starting transfers between devices: 30.3 us -> 33.5 us  [moved(): return lax.ppermute(buffer, ('dp', 'ctx'), pairs)]
    ppermute x32, waiting for transfers between devices: 65.2 us -> 62.5 us  [moved(): return lax.ppermute(buffer, ('dp', 'ctx'), pairs)]
  transfers between devices with their start and end apart: 36 -> 36, of which waited for: 19 -> 17; matrix products, arithmetic and copies ran while one was open for 9% -> 8% of each run, Pallas kernels for 0% -> 0%
where the time goes in v11:
time: 151 us
  waiting for transfers between devices  63.1 us (42%)
  starting transfers between devices  35.6 us (24%)
  Pallas kernels  33.6 us (22%)
  other arithmetic  9.14 us (6%)
  local copies, waits for them, and re-layouts  7.57 us (5%)
  between operations  1.77 us (1%)
    ppermute x32, waiting for transfers between devices, moved(): return lax.ppermute(buffer, ('dp', 'ctx'), pairs)  62.5 us
    ppermute x32, starting transfers between devices, moved(): return lax.ppermute(buffer, ('dp', 'ctx'), pairs)  33.5 us
    pallas_call x1, Pallas kernels, run_layer(): pl.pallas_call(layer_kernel, out_shape=(shape((2, MODEL_WIDTH, ROWS), BF1...  27 us
    pallas_call x1, Pallas kernels, finish(): pl.pallas_call(finish_kernel, out_shape=shapes, in_specs=[pl.BlockSpec(me...  4.76 us
  transfers between devices with their start and end apart: 36, of which 17 were waited for; matrix products, arithmetic and copies ran while one was open for 8% of the time, Pallas kernels for 0%

profile of v11, /device:TPU:0, one launch (start us, length us, event | category | flops | bytes accessed | tf_op | source)
XLA Modules:
  0.0 150.8 jit_solution(861993392137880183)
XLA Ops:
  0.7 1.9 %to_tiles.1 = (bf16[576,128]{1,0:T(8,128)(2,1)}, bf16[288,128]{1,0:T(8,128)(2,1)}) custom-call(s32[1]{0:T(128)} %bitcast.kind_ref, f32[864,128]{1,0:T(8,128)} %bitcast.154), custom_call_target="tpu_custom_call" | custom-call | tf_op jit(solution)/shard_map/to_tiles/pallas_call | solution.py:269
  2.5 5.0 %collective-permute-start.4 = (bf16[576,128]{1,0:T(8,128)(2,1)}, bf16[576,128]{1,0:T(8,128)(2,1)S(1)}, u32[]{:S(2)}, u32[]{:S(2)}) collective-permute-start(bf16[576,128]{1,0:T(8,128)(2,1)} %get-tuple-element.100), channel_id=1, source_target_pairs={{0,24},{1,25},{2,26},{3,27},{4,28},{5,29},{6,30},{7,31},{8,0},{9,1... | collective-permute-start | bytes 442376 | tf_op jit(solution)/shard_map/ppermute | solution.py:75
  8.5 1.5 collective-permute-start
  10.9 1.2 copy.39
  15.6 4.6 %collective-permute-done.3 = bf16[576,128]{1,0:T(8,128)(2,1)S(1)} collective-permute-done((bf16[576,128]{1,0:T(8,128)(2,1)}, bf16[576,128]{1,0:T(8,128)(2,1)S(1)}, u32[]{:S(2)}, u32[]{:S(2)}) %collective-permute-start.3) | collective-permute-done | bytes 147488 | tf_op jit(solution)/shard_map/ppermute | solution.py:75
  21.8 1.5 %collective-permute-start.5 = (bf16[4,576,128]{2,1,0:T(8,128)(2,1)S(1)}, bf16[4,576,128]{2,1,0:T(8,128)(2,1)}, u32[]{:S(2)}, u32[]{:S(2)}) collective-permute-start(bf16[4,576,128]{2,1,0:T(8,128)(2,1)S(1)} %pad_maximum_fusion.3.refs_1_), channel_id=1, source_target_pairs={{0,4},{1,5},{2,6},{3,7},{4,0},{5,1},{6,2},{7,3},{8,12},{9,13},{10,... | collective-permute-start | bytes 1769480 | tf_op jit(solution)/shard_map/ppermute | solution.py:75
  24.8 2.9 %collective-permute-start.9 = (bf16[2,288,128]{2,1,0:T(8,128)(2,1)S(1)}, bf16[2,288,128]{2,1,0:T(8,128)(2,1)S(1)}, u32[]{:S(2)}, u32[]{:S(2)}) collective-permute-start(bf16[2,288,128]{2,1,0:T(8,128)(2,1)S(1)} %pad_maximum_fusion.10), channel_id=1, source_target_pairs={{0,24},{1,25},{2,26},{3,27},{4,28},{5,29},{6,30},{7,31},{8,0},{9,1... | collective-permute-start | bytes 442376 | tf_op jit(solution)/shard_map/ppermute | solution.py:75
  27.7 1.1 collective-permute-start.8
  30.3 1.4 collective-permute-done.9
  31.7 8.0 %collective-permute-done.8 = bf16[2,288,128]{2,1,0:T(8,128)(2,1)S(1)} collective-permute-done((bf16[2,288,128]{2,1,0:T(8,128)(2,1)S(1)}, bf16[2,288,128]{2,1,0:T(8,128)(2,1)S(1)}, u32[]{:S(2)}, u32[]{:S(2)}) %collective-permute-start.8) | collective-permute-done | bytes 147488 | tf_op jit(solution)/shard_map/ppermute | solution.py:75
  39.7 1.1 constant_dynamic-update-slice_fusion.2
  41.4 1.3 collective-permute-start.16
  43.2 8.4 %collective-permute-done.15.refs_10_ = bf16[8,288,128]{2,1,0:T(8,128)(2,1)S(1)} collective-permute-done((bf16[8,288,128]{2,1,0:T(8,128)(2,1)S(1)}, bf16[8,288,128]{2,1,0:T(8,128)(2,1)S(1)}, u32[]{:S(2)}, u32[]{:S(2)}) %collective-permute-start.15) | collective-permute-done | bytes 589856 | tf_op jit(solution)/shard_map/ppermute | solution.py:75
  53.7 3.7 %collective-permute-done.16.refs_4_ = bf16[4,576,128]{2,1,0:T(8,128)(2,1)S(1)} collective-permute-done((bf16[4,576,128]{2,1,0:T(8,128)(2,1)}, bf16[4,576,128]{2,1,0:T(8,128)(2,1)S(1)}, u32[]{:S(2)}, u32[]{:S(2)}) %collective-permute-start.16) | collective-permute-done | bytes 589856 | tf_op jit(solution)/shard_map/ppermute | solution.py:75
  61.1 27.0 %layer.1 = (bf16[2,576,128]{2,1,0:T(8,128)(2,1)}, bf16[2352,128]{1,0:T(8,128)(2,1)}, bf16[2304,128]{1,0:T(8,128)(2,1)S(1)}, bf16[6912,128]{1,0:T(8,128)(2,1)}, b...) custom-call(s32[98]{0:T(128)S(1)} %stack.448.refs_0_, ...), custom_call_target="tpu_custom_call" | custom-call | tf_op jit(solution)/shard_map/layer/pallas_call | solution.py:787
  88.8 2.4 %collective-permute-done.20 = bf16[2304,128]{1,0:T(8,128)(2,1)S(1)} collective-permute-done((bf16[2304,128]{1,0:T(8,128)(2,1)S(1)}, bf16[2304,128]{1,0:T(8,128)(2,1)S(1)}, u32[]{:S(2)}, u32[]{:S(2)}) %collective-permute-start.20) | collective-permute-done | bytes 589856 | tf_op jit(solution)/shard_map/ppermute | solution.py:75
  91.2 1.2 add_convert_fusion.5
  92.5 1.6 %collective-permute-start.22 = (bf16[2304,128]{1,0:T(8,128)(2,1)S(1)}, bf16[2304,128]{1,0:T(8,128)(2,1)S(1)}, u32[]{:S(2)}, u32[]{:S(2)}) collective-permute-start(bf16[2304,128]{1,0:T(8,128)(2,1)S(1)} %add_convert_fusion.5), channel_id=1, source_target_pairs={{0,4},{1,5},{2,6},{3,7},{4,0},{5,1},{6,2},{7,3},{8,12},{9,13},{10,... | collective-permute-start | bytes 1769480 | tf_op jit(solution)/shard_map/ppermute | solution.py:75
  94.8 1.4 collective-permute-start.21
  96.5 2.3 %collective-permute-done.23 = bf16[6912,128]{1,0:T(8,128)(2,1)S(1)} collective-permute-done((bf16[6912,128]{1,0:T(8,128)(2,1)}, bf16[6912,128]{1,0:T(8,128)(2,1)S(1)}, u32[]{:S(2)}, u32[]{:S(2)}) %collective-permute-start.23) | collective-permute-done | bytes 1769504 | tf_op jit(solution)/shard_map/ppermute | solution.py:75
  99.3 8.8 %collective-permute-done.22 = bf16[2304,128]{1,0:T(8,128)(2,1)S(1)} collective-permute-done((bf16[2304,128]{1,0:T(8,128)(2,1)S(1)}, bf16[2304,128]{1,0:T(8,128)(2,1)S(1)}, u32[]{:S(2)}, u32[]{:S(2)}) %collective-permute-start.22) | collective-permute-done | bytes 589856 | tf_op jit(solution)/shard_map/ppermute | solution.py:75
  108.1 2.3 %collective-permute-done.21 = bf16[2352,128]{1,0:T(8,128)(2,1)S(1)} collective-permute-done((bf16[2352,128]{1,0:T(8,128)(2,1)S(1)}, bf16[2352,128]{1,0:T(8,128)(2,1)S(1)}, u32[]{:S(2)}, u32[]{:S(2)}) %collective-permute-start.21) | collective-permute-done | bytes 602144 | tf_op jit(solution)/shard_map/ppermute | solution.py:75
  111.3 1.3 collective-permute-start.27
  112.7 1.3 collective-permute-start.30
  114.0 2.5 %collective-permute-start.29 = (bf16[576,128]{1,0:T(8,128)(2,1)S(1)}, bf16[576,128]{1,0:T(8,128)(2,1)S(1)}, u32[]{:S(2)}, u32[]{:S(2)}) collective-permute-start(bf16[576,128]{1,0:T(8,128)(2,1)S(1)} %get-tuple-element.216), channel_id=1, source_target_pairs={{0,16},{1,17},{2,18},{3,19},{4,20},{5,21},{6,22},{7,23},{8,24},{9,... | collective-permute-start | bytes 442376 | tf_op jit(solution)/shard_map/ppermute | solution.py:75
  116.5 1.9 %collective-permute-start.28 = (bf16[576,128]{1,0:T(8,128)(2,1)S(1)}, bf16[576,128]{1,0:T(8,128)(2,1)S(1)}, u32[]{:S(2)}, u32[]{:S(2)}) collective-permute-start(bf16[576,128]{1,0:T(8,128)(2,1)S(1)} %get-tuple-element.217), channel_id=1, source_target_pairs={{0,8},{1,9},{2,10},{3,11},{4,12},{5,13},{6,14},{7,15},{8,16},{9,17... | collective-permute-start | bytes 442376 | tf_op jit(solution)/shard_map/ppermute | solution.py:75
  118.8 9.9 %collective-permute-done.29 = bf16[576,128]{1,0:T(8,128)(2,1)S(1)} collective-permute-done((bf16[576,128]{1,0:T(8,128)(2,1)S(1)}, bf16[576,128]{1,0:T(8,128)(2,1)S(1)}, u32[]{:S(2)}, u32[]{:S(2)}) %collective-permute-start.29) | collective-permute-done | bytes 147488 | tf_op jit(solution)/shard_map/ppermute | solution.py:75
  130.7 1.9 %collective-permute-start.31 = (bf16[624,128]{1,0:T(8,128)(2,1)S(1)}, bf16[624,128]{1,0:T(8,128)(2,1)S(1)}, u32[]{:S(2)}, u32[]{:S(2)}) collective-permute-start(bf16[624,128]{1,0:T(8,128)(2,1)S(1)} %get-tuple-element.231), channel_id=1, source_target_pairs={{0,8},{1,9},{2,10},{3,11},{4,12},{5,13},{6,14},{7,15},{8,16},{9,17... | collective-permute-start | bytes 479240 | tf_op jit(solution)/shard_map/ppermute | solution.py:75
  135.0 1.1 collective-permute-start.34
  136.7 4.2 %collective-permute-done.34.other_ref = bf16[288,128]{1,0:T(8,128)(2,1)S(1)} collective-permute-done((bf16[288,128]{1,0:T(8,128)(2,1)S(1)}, bf16[288,128]{1,0:T(8,128)(2,1)S(1)}, u32[]{:S(2)}, u32[]{:S(2)}) %collective-permute-start.34) | collective-permute-done | bytes 73760 | tf_op jit(solution)/shard_map/ppermute | solution.py:75
  140.9 4.2 %collective-permute-done.32.two_ref = bf16[624,128]{1,0:T(8,128)(2,1)S(1)} collective-permute-done((bf16[624,128]{1,0:T(8,128)(2,1)S(1)}, bf16[624,128]{1,0:T(8,128)(2,1)S(1)}, u32[]{:S(2)}, u32[]{:S(2)}) %collective-permute-start.32) | collective-permute-done | bytes 159776 | tf_op jit(solution)/shard_map/ppermute | solution.py:75
  146.0 4.8 %finish.1 = (f32[24,128]{1,0:T(8,128)}, f32[24,128]{1,0:T(8,128)}, f32[24,128]{1,0:T(8,128)}, f32[864,128]{1,0:T(8,128)}, f32[864,128]{1,0:T(8,128)}, /*index=5*/f32[864,128]{1,0:T(8,128)}, bf16[2,576,128]{2,1,0:T(8,128)(2,1)}) custom-call(s32[2]{0:T(128)} %pad_add_fusion.table_ref, f32[576,128]{1,0:T(8,128)} %get-tuple-element.209.head_ref, ...), custom_call_target="tpu_custom_call" | custom-call | tf_op jit(solution)/shard_map/finish/pallas_call | solution.py:371
  (173 shorter events, 25.3 us)
Async XLA Ops:
  2.5 13.0 %collective-permute-start.4 = (bf16[576,128]{1,0:T(8,128)(2,1)}, bf16[576,128]{1,0:T(8,128)(2,1)S(1)}, u32[]{:S(2)}, u32[]{:S(2)}) collective-permute-start(bf16[576,128]{1,0:T(8,128)(2,1)} %get-tuple-element.100), channel_id=1, source_target_pairs={{0,24},{1,25},{2,26},{3,27},{4,28},{5,29},{6,30},{7,31},{8,0},{9,1... | collective-permute-start | bytes 442376 | tf_op jit(solution)/shard_map/ppermute | solution.py:75
  7.6 12.6 %collective-permute-start.3 = (bf16[576,128]{1,0:T(8,128)(2,1)}, bf16[576,128]{1,0:T(8,128)(2,1)S(1)}, u32[]{:S(2)}, u32[]{:S(2)}) collective-permute-start(bf16[576,128]{1,0:T(8,128)(2,1)} %get-tuple-element.100), channel_id=1, source_target_pairs={{0,16},{1,17},{2,18},{3,19},{4,20},{5,21},{6,22},{7,23},{8,24},{9,... | collective-permute-start | bytes 442376 | tf_op jit(solution)/shard_map/ppermute | solution.py:75
  7.6 12.6 %collective-permute-start.2 = (bf16[576,128]{1,0:T(8,128)(2,1)}, bf16[576,128]{1,0:T(8,128)(2,1)S(1)}, u32[]{:S(2)}, u32[]{:S(2)}) collective-permute-start(bf16[576,128]{1,0:T(8,128)(2,1)} %get-tuple-element.100), channel_id=1, source_target_pairs={{0,8},{1,9},{2,10},{3,11},{4,12},{5,13},{6,14},{7,15},{8,16},{9,17... | collective-permute-start | bytes 442376 | tf_op jit(solution)/shard_map/ppermute | solution.py:75
  8.5 7.1 %collective-permute-start = (bf16[288,128]{1,0:T(8,128)(2,1)}, bf16[288,128]{1,0:T(8,128)(2,1)S(1)}, u32[]{:S(2)}, u32[]{:S(2)}) collective-permute-start(bf16[288,128]{1,0:T(8,128)(2,1)} %get-tuple-element.104), channel_id=1, source_target_pairs={{0,2},{1,3},{2,0},{3,1},{4,6},{5,7},{6,4},{7,5},{8,10},{9,11},{10,... | collective-permute-start | bytes 221192 | tf_op jit(solution)/shard_map/ppermute | solution.py:75
  12.3 8.4 %collective-permute-start.1 = (bf16[2,128,640]{2,1,0:T(8,128)(2,1)S(1)}, bf16[2,128,640]{2,1,0:T(8,128)(2,1)S(1)}, u32[]{:S(2)}, u32[]{:S(2)}) collective-permute-start(bf16[2,128,640]{2,1,0:T(8,128)(2,1)S(1)} %maximum_maximum_fusion.refs_0_), channel_id=1, source_target_pairs={{0,2},{1,3},{2,0},{3,1},{4,6},{5,7},{6,4},{7,5},{8,10},{9,11},{10,... | collective-permute-start | bytes 983048 | tf_op jit(solution)/shard_map/ppermute | solution.py:80
  20.8 18.8 %collective-permute-start.6 = (bf16[4,576,128]{2,1,0:T(8,128)(2,1)S(1)}, bf16[4,576,128]{2,1,0:T(8,128)(2,1)S(1)}, u32[]{:S(2)}, u32[]{:S(2)}) collective-permute-start(bf16[4,576,128]{2,1,0:T(8,128)(2,1)S(1)} %pad_maximum_fusion.3.refs_1_), channel_id=1, source_target_pairs={{0,2},{1,3},{2,0},{3,1},{4,6},{5,7},{6,4},{7,5},{8,10},{9,11},{10,... | collective-permute-start | bytes 1769480 | tf_op jit(solution)/shard_map/ppermute | solution.py:75
  21.8 17.8 %collective-permute-start.5 = (bf16[4,576,128]{2,1,0:T(8,128)(2,1)S(1)}, bf16[4,576,128]{2,1,0:T(8,128)(2,1)}, u32[]{:S(2)}, u32[]{:S(2)}) collective-permute-start(bf16[4,576,128]{2,1,0:T(8,128)(2,1)S(1)} %pad_maximum_fusion.3.refs_1_), channel_id=1, source_target_pairs={{0,4},{1,5},{2,6},{3,7},{4,0},{5,1},{6,2},{7,3},{8,12},{9,13},{10,... | collective-permute-start | bytes 1769480 | tf_op jit(solution)/shard_map/ppermute | solution.py:75
  24.8 6.9 %collective-permute-start.9 = (bf16[2,288,128]{2,1,0:T(8,128)(2,1)S(1)}, bf16[2,288,128]{2,1,0:T(8,128)(2,1)S(1)}, u32[]{:S(2)}, u32[]{:S(2)}) collective-permute-start(bf16[2,288,128]{2,1,0:T(8,128)(2,1)S(1)} %pad_maximum_fusion.10), channel_id=1, source_target_pairs={{0,24},{1,25},{2,26},{3,27},{4,28},{5,29},{6,30},{7,31},{8,0},{9,1... | collective-permute-start | bytes 442376 | tf_op jit(solution)/shard_map/ppermute | solution.py:75
  27.7 12.0 %collective-permute-start.8 = (bf16[2,288,128]{2,1,0:T(8,128)(2,1)S(1)}, bf16[2,288,128]{2,1,0:T(8,128)(2,1)S(1)}, u32[]{:S(2)}, u32[]{:S(2)}) collective-permute-start(bf16[2,288,128]{2,1,0:T(8,128)(2,1)S(1)} %pad_maximum_fusion.10), channel_id=1, source_target_pairs={{0,16},{1,17},{2,18},{3,19},{4,20},{5,21},{6,22},{7,23},{8,24},{9,... | collective-permute-start | bytes 442376 | tf_op jit(solution)/shard_map/ppermute | solution.py:75
  28.8 10.9 %collective-permute-start.7 = (bf16[2,288,128]{2,1,0:T(8,128)(2,1)S(1)}, bf16[2,288,128]{2,1,0:T(8,128)(2,1)}, u32[]{:S(2)}, u32[]{:S(2)}) collective-permute-start(bf16[2,288,128]{2,1,0:T(8,128)(2,1)S(1)} %pad_maximum_fusion.10), channel_id=1, source_target_pairs={{0,8},{1,9},{2,10},{3,11},{4,12},{5,13},{6,14},{7,15},{8,16},{9,17... | collective-permute-start | bytes 442376 | tf_op jit(solution)/shard_map/ppermute | solution.py:75
  40.9 10.8 %collective-permute-start.15 = (bf16[8,288,128]{2,1,0:T(8,128)(2,1)S(1)}, bf16[8,288,128]{2,1,0:T(8,128)(2,1)S(1)}, u32[]{:S(2)}, u32[]{:S(2)}) collective-permute-start(bf16[8,288,128]{2,1,0:T(8,128)(2,1)S(1)} %constant_dynamic-update-slice_fusion.refs_9_), channel_id=1, source_target_pairs={{0,4},{1,5},{2,6},{3,7},{4,0},{5,1},{6,2},{7,3},{8,12},{9,13},{10,... | collective-permute-start | bytes 1769480 | tf_op jit(solution)/shard_map/ppermute | solution.py:75
  41.4 10.2 %collective-permute-start.10 = (bf16[8,288,128]{2,1,0:T(8,128)(2,1)S(1)}, bf16[8,288,128]{2,1,0:T(8,128)(2,1)S(1)}, u32[]{:S(2)}, u32[]{:S(2)}) collective-permute-start(bf16[8,288,128]{2,1,0:T(8,128)(2,1)S(1)} %constant_dynamic-update-slice_fusion.refs_9_), channel_id=1, source_target_pairs={{0,1},{1,0},{2,3},{3,2},{4,5},{5,4},{6,7},{7,6},{8,9},{9,8},{10,11... | collective-permute-start | bytes 1769480 | tf_op jit(solution)/shard_map/ppermute | solution.py:75
  41.4 16.0 %collective-permute-start.16 = (bf16[4,576,128]{2,1,0:T(8,128)(2,1)}, bf16[4,576,128]{2,1,0:T(8,128)(2,1)S(1)}, u32[]{:S(2)}, u32[]{:S(2)}) collective-permute-start(bf16[4,576,128]{2,1,0:T(8,128)(2,1)} %collective-permute-done.5.refs_2_), channel_id=1, source_target_pairs={{0,2},{1,3},{2,0},{3,1},{4,6},{5,7},{6,4},{7,5},{8,10},{9,11},{10,... | collective-permute-start | bytes 1769480 | tf_op jit(solution)/shard_map/ppermute | solution.py:75
  42.7 14.7 %collective-permute-start.12 = (bf16[4,576,128]{2,1,0:T(8,128)(2,1)}, bf16[4,576,128]{2,1,0:T(8,128)(2,1)S(1)}, u32[]{:S(2)}, u32[]{:S(2)}) collective-permute-start(bf16[4,576,128]{2,1,0:T(8,128)(2,1)} %collective-permute-done.5.refs_2_), channel_id=1, source_target_pairs={{0,1},{1,0},{2,3},{3,2},{4,5},{5,4},{6,7},{7,6},{8,9},{9,8},{10,11... | collective-permute-start | bytes 1769480 | tf_op jit(solution)/shard_map/ppermute | solution.py:75
  43.0 9.6 %collective-permute-start.13 = (bf16[4,576,128]{2,1,0:T(8,128)(2,1)S(1)}, bf16[4,576,128]{2,1,0:T(8,128)(2,1)S(1)}, u32[]{:S(2)}, u32[]{:S(2)}) collective-permute-start(bf16[4,576,128]{2,1,0:T(8,128)(2,1)S(1)} %pad_maximum_fusion.3.refs_1_), channel_id=1, source_target_pairs={{0,1},{1,0},{2,3},{3,2},{4,5},{5,4},{6,7},{7,6},{8,9},{9,8},{10,11... | collective-permute-start | bytes 1769480 | tf_op jit(solution)/shard_map/ppermute | solution.py:75
  51.7 5.7 %collective-permute-start.14 = (bf16[2,2,128,640]{3,2,1,0:T(8,128)(2,1)S(1)}, bf16[2,2,128,640]{3,2,1,0:T(8,128)(2,1)S(1)}, u32[]{:S(2)}, u32[]{:S(2)}) collective-permute-start(bf16[2,2,128,640]{3,2,1,0:T(8,128)(2,1)S(1)} %pad_maximum_fusion.refs_13_), channel_id=1, source_target_pairs={{0,1},{1,0},{2,3},{3,2},{4,5},{5,4},{6,7},{7,6},{8,9},{9,8},{10,11... | collective-permute-start | bytes 1966088 | tf_op jit(solution)/shard_map/ppermute | solution.py:80
  57.5 2.8 %collective-permute-start.18 = (bf16[8,288,128]{2,1,0:T(8,128)(2,1)S(1)}, bf16[8,288,128]{2,1,0:T(8,128)(2,1)S(1)}, u32[]{:S(2)}, u32[]{:S(2)}) collective-permute-start(bf16[8,288,128]{2,1,0:T(8,128)(2,1)S(1)} %collective-permute-done.15.refs_10_), channel_id=1, source_target_pairs={{0,1},{1,0},{2,3},{3,2},{4,5},{5,4},{6,7},{7,6},{8,9},{9,8},{10,11... | collective-permute-start | bytes 1769480 | tf_op jit(solution)/shard_map/ppermute | solution.py:75
  88.2 2.9 %collective-permute-start.19 = (bf16[2352,128]{1,0:T(8,128)(2,1)}, bf16[2352,128]{1,0:T(8,128)(2,1)S(1)}, u32[]{:S(2)}, u32[]{:S(2)}) collective-permute-start(bf16[2352,128]{1,0:T(8,128)(2,1)} %get-tuple-element.135), channel_id=1, source_target_pairs={{0,1},{1,0},{2,3},{3,2},{4,5},{5,4},{6,7},{7,6},{8,9},{9,8},{10,11... | collective-permute-start | bytes 1806344 | tf_op jit(solution)/shard_map/ppermute | solution.py:75
  91.1 5.1 %collective-permute-start.25 = (bf16[2,2,128,384]{3,2,1,0:T(8,128)(2,1)S(1)}, bf16[2,2,128,384]{3,2,1,0:T(8,128)(2,1)S(1)}, u32[]{:S(2)}, u32[]{:S(2)}) collective-permute-start(bf16[2,2,128,384]{3,2,1,0:T(8,128)(2,1)S(1)} %get-tuple-element.150), channel_id=1, source_target_pairs={{0,1},{1,0},{2,3},{3,2},{4,5},{5,4},{6,7},{7,6},{8,9},{9,8},{10,11... | collective-permute-start | bytes 1179656 | tf_op jit(solution)/shard_map/ppermute | solution.py:80
  92.5 15.7 %collective-permute-start.22 = (bf16[2304,128]{1,0:T(8,128)(2,1)S(1)}, bf16[2304,128]{1,0:T(8,128)(2,1)S(1)}, u32[]{:S(2)}, u32[]{:S(2)}) collective-permute-start(bf16[2304,128]{1,0:T(8,128)(2,1)S(1)} %add_convert_fusion.5), channel_id=1, source_target_pairs={{0,4},{1,5},{2,6},{3,7},{4,0},{5,1},{6,2},{7,3},{8,12},{9,13},{10,... | collective-permute-start | bytes 1769480 | tf_op jit(solution)/shard_map/ppermute | solution.py:75
  94.1 4.7 %collective-permute-start.23 = (bf16[6912,128]{1,0:T(8,128)(2,1)}, bf16[6912,128]{1,0:T(8,128)(2,1)S(1)}, u32[]{:S(2)}, u32[]{:S(2)}) collective-permute-start(bf16[6912,128]{1,0:T(8,128)(2,1)} %get-tuple-element.144), channel_id=1, source_target_pairs={{0,1},{1,0},{2,3},{3,2},{4,5},{5,4},{6,7},{7,6},{8,9},{9,8},{10,11... | collective-permute-start | bytes 5308424 | tf_op jit(solution)/shard_map/ppermute | solution.py:75
  94.8 15.6 %collective-permute-start.21 = (bf16[2352,128]{1,0:T(8,128)(2,1)S(1)}, bf16[2352,128]{1,0:T(8,128)(2,1)S(1)}, u32[]{:S(2)}, u32[]{:S(2)}) collective-permute-start(bf16[2352,128]{1,0:T(8,128)(2,1)S(1)} %pad_maximum_fusion.1), channel_id=1, source_target_pairs={{0,2},{1,3},{2,0},{3,1},{4,6},{5,7},{6,4},{7,5},{8,10},{9,11},{10,... | collective-permute-start | bytes 1806344 | tf_op jit(solution)/shard_map/ppermute | solution.py:75
  110.7 17.9 %collective-permute-start.26 = (bf16[2352,128]{1,0:T(8,128)(2,1)S(1)}, bf16[2352,128]{1,0:T(8,128)(2,1)S(1)}, u32[]{:S(2)}, u32[]{:S(2)}) collective-permute-start(bf16[2352,128]{1,0:T(8,128)(2,1)S(1)} %pad_maximum_fusion.2), channel_id=1, source_target_pairs={{0,4},{1,5},{2,6},{3,7},{4,0},{5,1},{6,2},{7,3},{8,12},{9,13},{10,... | collective-permute-start | bytes 1806344 | tf_op jit(solution)/shard_map/ppermute | solution.py:75
  111.3 17.4 %collective-permute-start.27 = (bf16[2304,128]{1,0:T(8,128)(2,1)S(1)}, bf16[2304,128]{1,0:T(8,128)(2,1)S(1)}, u32[]{:S(2)}, u32[]{:S(2)}) collective-permute-start(bf16[2304,128]{1,0:T(8,128)(2,1)S(1)} %get-tuple-element.154), channel_id=1, source_target_pairs={{0,2},{1,3},{2,0},{3,1},{4,6},{5,7},{6,4},{7,5},{8,10},{9,11},{10,... | collective-permute-start | bytes 1769480 | tf_op jit(solution)/shard_map/ppermute | solution.py:75
  112.7 6.0 %collective-permute-start.30 = (bf16[576,128]{1,0:T(8,128)(2,1)S(1)}, bf16[576,128]{1,0:T(8,128)(2,1)S(1)}, u32[]{:S(2)}, u32[]{:S(2)}) collective-permute-start(bf16[576,128]{1,0:T(8,128)(2,1)S(1)} %get-tuple-element.215), channel_id=1, source_target_pairs={{0,24},{1,25},{2,26},{3,27},{4,28},{5,29},{6,30},{7,31},{8,0},{9,1... | collective-permute-start | bytes 442376 | tf_op jit(solution)/shard_map/ppermute | solution.py:75
  114.0 14.6 %collective-permute-start.29 = (bf16[576,128]{1,0:T(8,128)(2,1)S(1)}, bf16[576,128]{1,0:T(8,128)(2,1)S(1)}, u32[]{:S(2)}, u32[]{:S(2)}) collective-permute-start(bf16[576,128]{1,0:T(8,128)(2,1)S(1)} %get-tuple-element.216), channel_id=1, source_target_pairs={{0,16},{1,17},{2,18},{3,19},{4,20},{5,21},{6,22},{7,23},{8,24},{9,... | collective-permute-start | bytes 442376 | tf_op jit(solution)/shard_map/ppermute | solution.py:75
  116.5 12.1 %collective-permute-start.28 = (bf16[576,128]{1,0:T(8,128)(2,1)S(1)}, bf16[576,128]{1,0:T(8,128)(2,1)S(1)}, u32[]{:S(2)}, u32[]{:S(2)}) collective-permute-start(bf16[576,128]{1,0:T(8,128)(2,1)S(1)} %get-tuple-element.217), channel_id=1, source_target_pairs={{0,8},{1,9},{2,10},{3,11},{4,12},{5,13},{6,14},{7,15},{8,16},{9,17... | collective-permute-start | bytes 442376 | tf_op jit(solution)/shard_map/ppermute | solution.py:75
  129.7 11.3 %collective-permute-start.33 = (bf16[624,128]{1,0:T(8,128)(2,1)S(1)}, bf16[624,128]{1,0:T(8,128)(2,1)S(1)}, u32[]{:S(2)}, u32[]{:S(2)}) collective-permute-start(bf16[624,128]{1,0:T(8,128)(2,1)S(1)} %get-tuple-element.229), channel_id=1, source_target_pairs={{0,24},{1,25},{2,26},{3,27},{4,28},{5,29},{6,30},{7,31},{8,0},{9,1... | collective-permute-start | bytes 479240 | tf_op jit(solution)/shard_map/ppermute | solution.py:75
  129.7 15.5 %collective-permute-start.32 = (bf16[624,128]{1,0:T(8,128)(2,1)S(1)}, bf16[624,128]{1,0:T(8,128)(2,1)S(1)}, u32[]{:S(2)}, u32[]{:S(2)}) collective-permute-start(bf16[624,128]{1,0:T(8,128)(2,1)S(1)} %get-tuple-element.230), channel_id=1, source_target_pairs={{0,16},{1,17},{2,18},{3,19},{4,20},{5,21},{6,22},{7,23},{8,24},{9,... | collective-permute-start | bytes 479240 | tf_op jit(solution)/shard_map/ppermute | solution.py:75
  130.7 14.5 %collective-permute-start.31 = (bf16[624,128]{1,0:T(8,128)(2,1)S(1)}, bf16[624,128]{1,0:T(8,128)(2,1)S(1)}, u32[]{:S(2)}, u32[]{:S(2)}) collective-permute-start(bf16[624,128]{1,0:T(8,128)(2,1)S(1)} %get-tuple-element.231), channel_id=1, source_target_pairs={{0,8},{1,9},{2,10},{3,11},{4,12},{5,13},{6,14},{7,15},{8,16},{9,17... | collective-permute-start | bytes 479240 | tf_op jit(solution)/shard_map/ppermute | solution.py:75
  133.4 11.8 %collective-permute-start.35 = (bf16[2,128,384]{2,1,0:T(8,128)(2,1)S(1)}, bf16[2,128,384]{2,1,0:T(8,128)(2,1)S(1)}, u32[]{:S(2)}, u32[]{:S(2)}) collective-permute-start(bf16[2,128,384]{2,1,0:T(8,128)(2,1)S(1)} %get-tuple-element.225), channel_id=1, source_target_pairs={{0,2},{1,3},{2,0},{3,1},{4,6},{5,7},{6,4},{7,5},{8,10},{9,11},{10,... | collective-permute-start | bytes 589832 | tf_op jit(solution)/shard_map/ppermute | solution.py:80
  135.0 5.9 %collective-permute-start.34 = (bf16[288,128]{1,0:T(8,128)(2,1)S(1)}, bf16[288,128]{1,0:T(8,128)(2,1)S(1)}, u32[]{:S(2)}, u32[]{:S(2)}) collective-permute-start(bf16[288,128]{1,0:T(8,128)(2,1)S(1)} %get-tuple-element.223), channel_id=1, source_target_pairs={{0,2},{1,3},{2,0},{3,1},{4,6},{5,7},{6,4},{7,5},{8,10},{9,11},{10,... | collective-permute-start | bytes 221192 | tf_op jit(solution)/shard_map/ppermute | solution.py:75
  (37 other events, 242.1 us)

commit v12 on v11

--- a/solution.py
+++ b/solution.py
@@ -88,16 +88,18 @@
     hz = [moved(head, "z", s) for s in (1, 2, 3)]
     tx = moved(tail, "x", 1)
     two = across(packed, 2)
-    head, tail, tx, two, *hz = together(head, tail, tx, two, *hz)
+    hz, head, tail, tx, two = together(hz[::-1], head, tail, tx, two)
+    hz = hz[::-1]
     own = jnp.stack([head] + hz)
     pair = jnp.stack([tail, tx])
     ay = moved(own, "y", 1)
     ax = moved(own, "x", 1)
     near = jnp.stack([packed, two])
     tables = place_tables(near)
-    pair, *tables = together(pair, *tables)
+    pair, near = together(pair, near)
     tz = [moved(pair, "z", s) for s in (1, 2, 3)]
-    own, pair, ay, ax, near, tables, others, *tz = together(own, pair, ay, ax, near, tables, others, *tz)
+    own, pair, tz, ax, ay, near, tables, others = together(own, pair, tz[::-1], ax, ay, near, tables, others)
+    tz = tz[::-1]
     eight = jnp.concatenate([pair] + tz)
     far = across(near, 1)
     axy = moved(ay, "x", 1)
@@ -204,7 +206,8 @@
     got_hy = moved(hy, "y", 1)
     got_far = moved(far, "x", 1)
     got_tz = [moved(tz[s], "z", s) for s in (1, 2, 3)]
-    got_hy, got_far, low, own_tail, vector, dkv, *got_tz = together(got_hy, got_far, low, tz[0], vector, dkv, *got_tz)
+    got_tz, got_far, got_hy, low, own_tail, vector, dkv = together(got_tz[::-1], got_far, got_hy, low, tz[0], vector, dkv)
+    got_tz = got_tz[::-1]
     vector = summed_vector(vector, got_hy[PART:])
     head = [summed(part_for(low, s), part_for(got_far, s), part_for(got_hy, s)) for s in range(4)]
     got_hz = [moved(jnp.concatenate([head[s].astype(BF16), vector]), "z", s) for s in (1, 2, 3)]
@@ -212,7 +215,7 @@
     own_tail = summed(own_tail[:TAIL_ROWS], *[part[:TAIL_ROWS] for part in got_tz])
     got_tx = moved(tx, "x", 1)
     got_dkv = across(dkv[1], 2)
-    return (head[0], *got_hz, own_tail, got_tx, vector), (dkv[0], got_dkv)
+    return (head[0], *got_hz[::-1], own_tail, got_tx, vector), (dkv[0], got_dkv)
 
 
 def lower_lanes(shape):
@@ -285,7 +288,7 @@
     )(kind, flat)
 
 
-def finish_kernel(table_ref, head_ref, one_ref, two_ref, three_ref, tail_ref, other_ref, mine_ref, *refs):
+def finish_kernel(table_ref, head_ref, three_ref, two_ref, one_ref, tail_ref, other_ref, mine_ref, *refs):
     kind, place = table_ref[0], table_ref[1]
     tiles, narrow, flat_ref, vector_parts = refs[-4:]
     tokens_ref, gains_ref, w_kv_ref, base_ref, own_dkv, other_dkv = refs[:6]

time: 151 us -> 145 us (0.960)
  waiting for transfers between devices: 63.1 us -> 55.5 us
  starting transfers between devices: 35.6 us -> 37.7 us
    ppermute x32, waiting for transfers between devices: 62.5 us -> 51 us  [moved(): return lax.ppermute(buffer, ('dp', 'ctx'), pairs)]
    ppermute x4, waiting for transfers between devices: 0.57 us -> 4.49 us  [across(): lax.ppermute(buffer, 'ctx', [(i, i ^ distance) for i in range(count)])]
    ppermute x32, starting transfers between devices: 33.5 us -> 35.1 us  [moved(): return lax.ppermute(buffer, ('dp', 'ctx'), pairs)]
  transfers between devices with their start and end apart: 36 -> 36, of which waited for: 17 -> 20; matrix products, arithmetic and copies ran while one was open for 8% -> 9% of each run, Pallas kernels for 0% -> 0%
where the time goes in v12:
time: 145 us; the launch traced here: 144 us
  waiting for transfers between devices  55.5 us (38%)
  starting transfers between devices  37.7 us (26%)
  Pallas kernels  33.7 us (23%)
  other arithmetic  9.16 us (6%)
  local copies, waits for them, and re-layouts  6.49 us (4%)
    ppermute x32, waiting for transfers between devices, moved(): return lax.ppermute(buffer, ('dp', 'ctx'), pairs)  51 us
    ppermute x32, starting transfers between devices, moved(): return lax.ppermute(buffer, ('dp', 'ctx'), pairs)  35.1 us
    pallas_call x1, Pallas kernels, run_layer(): pl.pallas_call(layer_kernel, out_shape=(shape((2, MODEL_WIDTH, ROWS), BF1...  27.1 us
    pallas_call x1, Pallas kernels, finish(): pl.pallas_call(finish_kernel, out_shape=shapes, in_specs=[pl.BlockSpec(me...  4.76 us
    ppermute x4, waiting for transfers between devices, across(): lax.ppermute(buffer, 'ctx', [(i, i ^ distance) for i in range(count)])  4.49 us
  transfers between devices with their start and end apart: 36, of which 20 were waited for; matrix products, arithmetic and copies ran while one was open for 9% of the time, Pallas kernels for 0%

profile of v12, /device:TPU:0, one launch (start us, length us, event | category | flops | bytes accessed | tf_op | source)
XLA Modules:
  0.0 143.9 jit_solution(8897223066052492607)
XLA Ops:
  0.7 1.9 %to_tiles.1 = (bf16[576,128]{1,0:T(8,128)(2,1)}, bf16[288,128]{1,0:T(8,128)(2,1)}) custom-call(s32[1]{0:T(128)} %bitcast.kind_ref, f32[864,128]{1,0:T(8,128)} %bitcast.154), custom_call_target="tpu_custom_call" | custom-call | tf_op jit(solution)/shard_map/to_tiles/pallas_call | solution.py:272
  2.5 2.9 %collective-permute-start.2 = (bf16[576,128]{1,0:T(8,128)(2,1)}, bf16[576,128]{1,0:T(8,128)(2,1)S(1)}, u32[]{:S(2)}, u32[]{:S(2)}) collective-permute-start(bf16[576,128]{1,0:T(8,128)(2,1)} %get-tuple-element.99), channel_id=1, source_target_pairs={{0,8},{1,9},{2,10},{3,11},{4,12},{5,13},{6,14},{7,15},{8,16},{9,17... | collective-permute-start | bytes 442376 | tf_op jit(solution)/shard_map/ppermute | solution.py:75
  5.4 2.7 %collective-permute-start.1 = (bf16[576,128]{1,0:T(8,128)(2,1)}, bf16[576,128]{1,0:T(8,128)(2,1)S(1)}, u32[]{:S(2)}, u32[]{:S(2)}) collective-permute-start(bf16[576,128]{1,0:T(8,128)(2,1)} %get-tuple-element.99), channel_id=1, source_target_pairs={{0,16},{1,17},{2,18},{3,19},{4,20},{5,21},{6,22},{7,23},{8,24},{9,... | collective-permute-start | bytes 442376 | tf_op jit(solution)/shard_map/ppermute | solution.py:75
  8.2 1.2 collective-permute-start
  9.4 1.5 %collective-permute-start.3 = (bf16[288,128]{1,0:T(8,128)(2,1)}, bf16[288,128]{1,0:T(8,128)(2,1)S(1)}, u32[]{:S(2)}, u32[]{:S(2)}) collective-permute-start(bf16[288,128]{1,0:T(8,128)(2,1)} %get-tuple-element.103), channel_id=1, source_target_pairs={{0,2},{1,3},{2,0},{3,1},{4,6},{5,7},{6,4},{7,5},{8,10},{9,11},{10,... | collective-permute-start | bytes 221192 | tf_op jit(solution)/shard_map/ppermute | solution.py:75
  11.8 1.2 copy.39
  16.8 1.2 collective-permute-done.1
  18.1 3.6 %collective-permute-done.4 = bf16[2,128,640]{2,1,0:T(8,128)(2,1)S(1)} collective-permute-done((bf16[2,128,640]{2,1,0:T(8,128)(2,1)S(1)}, bf16[2,128,640]{2,1,0:T(8,128)(2,1)S(1)}, u32[]{:S(2)}, u32[]{:S(2)}) %collective-permute-start.4) | collective-permute-done | bytes 327712 | tf_op jit(solution)/shard_map/ppermute | solution.py:80
  21.7 1.6 %collective-permute-start.9 = (bf16[4,576,128]{2,1,0:T(8,128)(2,1)S(1)}, bf16[4,576,128]{2,1,0:T(8,128)(2,1)S(1)}, u32[]{:S(2)}, u32[]{:S(2)}) collective-permute-start(bf16[4,576,128]{2,1,0:T(8,128)(2,1)S(1)} %pad_maximum_fusion.3.refs_1_), channel_id=1, source_target_pairs={{0,4},{1,5},{2,6},{3,7},{4,0},{5,1},{6,2},{7,3},{8,12},{9,13},{10,... | collective-permute-start | bytes 1769480 | tf_op jit(solution)/shard_map/ppermute | solution.py:75
  25.1 1.5 %collective-permute-start.6 = (bf16[2,288,128]{2,1,0:T(8,128)(2,1)S(1)}, bf16[2,288,128]{2,1,0:T(8,128)(2,1)S(1)}, u32[]{:S(2)}, u32[]{:S(2)}) collective-permute-start(bf16[2,288,128]{2,1,0:T(8,128)(2,1)S(1)} %pad_maximum_fusion.10), channel_id=1, source_target_pairs={{0,16},{1,17},{2,18},{3,19},{4,20},{5,21},{6,22},{7,23},{8,24},{9,... | collective-permute-start | bytes 442376 | tf_op jit(solution)/shard_map/ppermute | solution.py:75
  26.6 1.6 %collective-permute-start.5 = (bf16[2,288,128]{2,1,0:T(8,128)(2,1)S(1)}, bf16[2,288,128]{2,1,0:T(8,128)(2,1)S(1)}, u32[]{:S(2)}, u32[]{:S(2)}) collective-permute-start(bf16[2,288,128]{2,1,0:T(8,128)(2,1)S(1)} %pad_maximum_fusion.10), channel_id=1, source_target_pairs={{0,24},{1,25},{2,26},{3,27},{4,28},{5,29},{6,30},{7,31},{8,0},{9,1... | collective-permute-start | bytes 442376 | tf_op jit(solution)/shard_map/ppermute | solution.py:75
  29.5 3.1 %collective-permute-done.7 = bf16[2,288,128]{2,1,0:T(8,128)(2,1)S(1)} collective-permute-done((bf16[2,288,128]{2,1,0:T(8,128)(2,1)S(1)}, bf16[2,288,128]{2,1,0:T(8,128)(2,1)S(1)}, u32[]{:S(2)}, u32[]{:S(2)}) %collective-permute-start.7) | collective-permute-done | bytes 147488 | tf_op jit(solution)/shard_map/ppermute | solution.py:75
  32.6 3.3 %collective-permute-done.6 = bf16[2,288,128]{2,1,0:T(8,128)(2,1)S(1)} collective-permute-done((bf16[2,288,128]{2,1,0:T(8,128)(2,1)S(1)}, bf16[2,288,128]{2,1,0:T(8,128)(2,1)S(1)}, u32[]{:S(2)}, u32[]{:S(2)}) %collective-permute-start.6) | collective-permute-done | bytes 147488 | tf_op jit(solution)/shard_map/ppermute | solution.py:75
  36.7 1.2 collective-permute-start.16
  38.4 12.7 %collective-permute-done.15.refs_10_ = bf16[8,288,128]{2,1,0:T(8,128)(2,1)S(1)} collective-permute-done((bf16[8,288,128]{2,1,0:T(8,128)(2,1)S(1)}, bf16[8,288,128]{2,1,0:T(8,128)(2,1)S(1)}, u32[]{:S(2)}, u32[]{:S(2)}) %collective-permute-start.15) | collective-permute-done | bytes 589856 | tf_op jit(solution)/shard_map/ppermute | solution.py:75
  52.1 1.1 collective-permute-done.11.refs_7_
  57.7 27.1 %layer.1 = (bf16[2,576,128]{2,1,0:T(8,128)(2,1)}, bf16[2352,128]{1,0:T(8,128)(2,1)}, bf16[2304,128]{1,0:T(8,128)(2,1)S(1)}, bf16[6912,128]{1,0:T(8,128)(2,1)}, b...) custom-call(s32[98]{0:T(128)S(1)} %stack.448.refs_0_, ...), custom_call_target="tpu_custom_call" | custom-call | tf_op jit(solution)/shard_map/layer/pallas_call | solution.py:790
  85.4 2.4 %collective-permute-done.20 = bf16[2304,128]{1,0:T(8,128)(2,1)S(1)} collective-permute-done((bf16[2304,128]{1,0:T(8,128)(2,1)S(1)}, bf16[2304,128]{1,0:T(8,128)(2,1)S(1)}, u32[]{:S(2)}, u32[]{:S(2)}) %collective-permute-start.20) | collective-permute-done | bytes 589856 | tf_op jit(solution)/shard_map/ppermute | solution.py:75
  87.9 1.2 add_convert_fusion.5
  91.9 2.5 %collective-permute-done.23 = bf16[6912,128]{1,0:T(8,128)(2,1)S(1)} collective-permute-done((bf16[6912,128]{1,0:T(8,128)(2,1)}, bf16[6912,128]{1,0:T(8,128)(2,1)S(1)}, u32[]{:S(2)}, u32[]{:S(2)}) %collective-permute-start.23) | collective-permute-done | bytes 1769504 | tf_op jit(solution)/shard_map/ppermute | solution.py:75
  94.9 9.9 %collective-permute-done.22 = bf16[2304,128]{1,0:T(8,128)(2,1)S(1)} collective-permute-done((bf16[2304,128]{1,0:T(8,128)(2,1)S(1)}, bf16[2304,128]{1,0:T(8,128)(2,1)S(1)}, u32[]{:S(2)}, u32[]{:S(2)}) %collective-permute-start.22) | collective-permute-done | bytes 589856 | tf_op jit(solution)/shard_map/ppermute | solution.py:75
  104.8 1.3 collective-permute-done.21
  106.3 1.6 %collective-permute-start.30 = (bf16[2352,128]{1,0:T(8,128)(2,1)S(1)}, bf16[2352,128]{1,0:T(8,128)(2,1)S(1)}, u32[]{:S(2)}, u32[]{:S(2)}) collective-permute-start(bf16[2352,128]{1,0:T(8,128)(2,1)S(1)} %pad_maximum_fusion.2), channel_id=1, source_target_pairs={{0,4},{1,5},{2,6},{3,7},{4,0},{5,1},{6,2},{7,3},{8,12},{9,13},{10,... | collective-permute-start | bytes 1806344 | tf_op jit(solution)/shard_map/ppermute | solution.py:75
  108.6 3.8 %collective-permute-start.28 = (bf16[576,128]{1,0:T(8,128)(2,1)S(1)}, bf16[576,128]{1,0:T(8,128)(2,1)S(1)}, u32[]{:S(2)}, u32[]{:S(2)}) collective-permute-start(bf16[576,128]{1,0:T(8,128)(2,1)S(1)} %get-tuple-element.214), channel_id=1, source_target_pairs={{0,8},{1,9},{2,10},{3,11},{4,12},{5,13},{6,14},{7,15},{8,16},{9,17... | collective-permute-start | bytes 442376 | tf_op jit(solution)/shard_map/ppermute | solution.py:75
  112.4 2.4 %collective-permute-start.26 = (bf16[576,128]{1,0:T(8,128)(2,1)S(1)}, bf16[576,128]{1,0:T(8,128)(2,1)S(1)}, u32[]{:S(2)}, u32[]{:S(2)}) collective-permute-start(bf16[576,128]{1,0:T(8,128)(2,1)S(1)} %get-tuple-element.216), channel_id=1, source_target_pairs={{0,24},{1,25},{2,26},{3,27},{4,28},{5,29},{6,30},{7,31},{8,0},{9,1... | collective-permute-start | bytes 442376 | tf_op jit(solution)/shard_map/ppermute | solution.py:75
  114.8 2.5 %collective-permute-done.28 = bf16[576,128]{1,0:T(8,128)(2,1)S(1)} collective-permute-done((bf16[576,128]{1,0:T(8,128)(2,1)S(1)}, bf16[576,128]{1,0:T(8,128)(2,1)S(1)}, u32[]{:S(2)}, u32[]{:S(2)}) %collective-permute-start.28) | collective-permute-done | bytes 147488 | tf_op jit(solution)/shard_map/ppermute | solution.py:75
  117.3 4.8 %collective-permute-done.27 = bf16[576,128]{1,0:T(8,128)(2,1)S(1)} collective-permute-done((bf16[576,128]{1,0:T(8,128)(2,1)S(1)}, bf16[576,128]{1,0:T(8,128)(2,1)S(1)}, u32[]{:S(2)}, u32[]{:S(2)}) %collective-permute-start.27) | collective-permute-done | bytes 147488 | tf_op jit(solution)/shard_map/ppermute | solution.py:75
  123.1 3.8 %collective-permute-start.33 = (bf16[624,128]{1,0:T(8,128)(2,1)S(1)}, bf16[624,128]{1,0:T(8,128)(2,1)S(1)}, u32[]{:S(2)}, u32[]{:S(2)}) collective-permute-start(bf16[624,128]{1,0:T(8,128)(2,1)S(1)} %get-tuple-element.227), channel_id=1, source_target_pairs={{0,8},{1,9},{2,10},{3,11},{4,12},{5,13},{6,14},{7,15},{8,16},{9,17... | collective-permute-start | bytes 479240 | tf_op jit(solution)/shard_map/ppermute | solution.py:75
  126.9 1.7 %collective-permute-start.32 = (bf16[624,128]{1,0:T(8,128)(2,1)S(1)}, bf16[624,128]{1,0:T(8,128)(2,1)S(1)}, u32[]{:S(2)}, u32[]{:S(2)}) collective-permute-start(bf16[624,128]{1,0:T(8,128)(2,1)S(1)} %get-tuple-element.228), channel_id=1, source_target_pairs={{0,16},{1,17},{2,18},{3,19},{4,20},{5,21},{6,22},{7,23},{8,24},{9,... | collective-permute-start | bytes 479240 | tf_op jit(solution)/shard_map/ppermute | solution.py:75
  130.0 1.3 collective-permute-start.35
  133.4 4.4 %collective-permute-done.34.other_ref = bf16[288,128]{1,0:T(8,128)(2,1)S(1)} collective-permute-done((bf16[288,128]{1,0:T(8,128)(2,1)S(1)}, bf16[288,128]{1,0:T(8,128)(2,1)S(1)}, u32[]{:S(2)}, u32[]{:S(2)}) %collective-permute-start.34) | collective-permute-done | bytes 73760 | tf_op jit(solution)/shard_map/ppermute | solution.py:75
  139.0 4.8 %finish.1 = (f32[24,128]{1,0:T(8,128)}, f32[24,128]{1,0:T(8,128)}, f32[24,128]{1,0:T(8,128)}, f32[864,128]{1,0:T(8,128)}, f32[864,128]{1,0:T(8,128)}, /*index=5*/f32[864,128]{1,0:T(8,128)}, bf16[2,576,128]{2,1,0:T(8,128)(2,1)}) custom-call(s32[2]{0:T(128)} %pad_add_fusion.table_ref, f32[576,128]{1,0:T(8,128)} %get-tuple-element.207.head_ref, ...), custom_call_target="tpu_custom_call" | custom-call | tf_op jit(solution)/shard_map/finish/pallas_call | solution.py:374
  (175 shorter events, 25.1 us)
Async XLA Ops:
  2.5 14.3 %collective-permute-start.2 = (bf16[576,128]{1,0:T(8,128)(2,1)}, bf16[576,128]{1,0:T(8,128)(2,1)S(1)}, u32[]{:S(2)}, u32[]{:S(2)}) collective-permute-start(bf16[576,128]{1,0:T(8,128)(2,1)} %get-tuple-element.99), channel_id=1, source_target_pairs={{0,8},{1,9},{2,10},{3,11},{4,12},{5,13},{6,14},{7,15},{8,16},{9,17... | collective-permute-start | bytes 442376 | tf_op jit(solution)/shard_map/ppermute | solution.py:75
  5.4 12.6 %collective-permute-start.1 = (bf16[576,128]{1,0:T(8,128)(2,1)}, bf16[576,128]{1,0:T(8,128)(2,1)S(1)}, u32[]{:S(2)}, u32[]{:S(2)}) collective-permute-start(bf16[576,128]{1,0:T(8,128)(2,1)} %get-tuple-element.99), channel_id=1, source_target_pairs={{0,16},{1,17},{2,18},{3,19},{4,20},{5,21},{6,22},{7,23},{8,24},{9,... | collective-permute-start | bytes 442376 | tf_op jit(solution)/shard_map/ppermute | solution.py:75
  8.2 9.9 %collective-permute-start = (bf16[576,128]{1,0:T(8,128)(2,1)}, bf16[576,128]{1,0:T(8,128)(2,1)S(1)}, u32[]{:S(2)}, u32[]{:S(2)}) collective-permute-start(bf16[576,128]{1,0:T(8,128)(2,1)} %get-tuple-element.99), channel_id=1, source_target_pairs={{0,24},{1,25},{2,26},{3,27},{4,28},{5,29},{6,30},{7,31},{8,0},{9,1... | collective-permute-start | bytes 442376 | tf_op jit(solution)/shard_map/ppermute | solution.py:75
  9.4 7.4 %collective-permute-start.3 = (bf16[288,128]{1,0:T(8,128)(2,1)}, bf16[288,128]{1,0:T(8,128)(2,1)S(1)}, u32[]{:S(2)}, u32[]{:S(2)}) collective-permute-start(bf16[288,128]{1,0:T(8,128)(2,1)} %get-tuple-element.103), channel_id=1, source_target_pairs={{0,2},{1,3},{2,0},{3,1},{4,6},{5,7},{6,4},{7,5},{8,10},{9,11},{10,... | collective-permute-start | bytes 221192 | tf_op jit(solution)/shard_map/ppermute | solution.py:75
  13.2 8.4 %collective-permute-start.4 = (bf16[2,128,640]{2,1,0:T(8,128)(2,1)S(1)}, bf16[2,128,640]{2,1,0:T(8,128)(2,1)S(1)}, u32[]{:S(2)}, u32[]{:S(2)}) collective-permute-start(bf16[2,128,640]{2,1,0:T(8,128)(2,1)S(1)} %maximum_maximum_fusion.refs_0_), channel_id=1, source_target_pairs={{0,2},{1,3},{2,0},{3,1},{4,6},{5,7},{6,4},{7,5},{8,10},{9,11},{10,... | collective-permute-start | bytes 983048 | tf_op jit(solution)/shard_map/ppermute | solution.py:80
  21.7 14.2 %collective-permute-start.9 = (bf16[4,576,128]{2,1,0:T(8,128)(2,1)S(1)}, bf16[4,576,128]{2,1,0:T(8,128)(2,1)S(1)}, u32[]{:S(2)}, u32[]{:S(2)}) collective-permute-start(bf16[4,576,128]{2,1,0:T(8,128)(2,1)S(1)} %pad_maximum_fusion.3.refs_1_), channel_id=1, source_target_pairs={{0,4},{1,5},{2,6},{3,7},{4,0},{5,1},{6,2},{7,3},{8,12},{9,13},{10,... | collective-permute-start | bytes 1769480 | tf_op jit(solution)/shard_map/ppermute | solution.py:75
  23.3 12.7 %collective-permute-start.8 = (bf16[4,576,128]{2,1,0:T(8,128)(2,1)S(1)}, bf16[4,576,128]{2,1,0:T(8,128)(2,1)S(1)}, u32[]{:S(2)}, u32[]{:S(2)}) collective-permute-start(bf16[4,576,128]{2,1,0:T(8,128)(2,1)S(1)} %pad_maximum_fusion.3.refs_1_), channel_id=1, source_target_pairs={{0,2},{1,3},{2,0},{3,1},{4,6},{5,7},{6,4},{7,5},{8,10},{9,11},{10,... | collective-permute-start | bytes 1769480 | tf_op jit(solution)/shard_map/ppermute | solution.py:75
  24.3 8.4 %collective-permute-start.7 = (bf16[2,288,128]{2,1,0:T(8,128)(2,1)S(1)}, bf16[2,288,128]{2,1,0:T(8,128)(2,1)S(1)}, u32[]{:S(2)}, u32[]{:S(2)}) collective-permute-start(bf16[2,288,128]{2,1,0:T(8,128)(2,1)S(1)} %pad_maximum_fusion.10), channel_id=1, source_target_pairs={{0,8},{1,9},{2,10},{3,11},{4,12},{5,13},{6,14},{7,15},{8,16},{9,17... | collective-permute-start | bytes 442376 | tf_op jit(solution)/shard_map/ppermute | solution.py:75
  25.1 10.8 %collective-permute-start.6 = (bf16[2,288,128]{2,1,0:T(8,128)(2,1)S(1)}, bf16[2,288,128]{2,1,0:T(8,128)(2,1)S(1)}, u32[]{:S(2)}, u32[]{:S(2)}) collective-permute-start(bf16[2,288,128]{2,1,0:T(8,128)(2,1)S(1)} %pad_maximum_fusion.10), channel_id=1, source_target_pairs={{0,16},{1,17},{2,18},{3,19},{4,20},{5,21},{6,22},{7,23},{8,24},{9,... | collective-permute-start | bytes 442376 | tf_op jit(solution)/shard_map/ppermute | solution.py:75
  26.6 9.4 %collective-permute-start.5 = (bf16[2,288,128]{2,1,0:T(8,128)(2,1)S(1)}, bf16[2,288,128]{2,1,0:T(8,128)(2,1)S(1)}, u32[]{:S(2)}, u32[]{:S(2)}) collective-permute-start(bf16[2,288,128]{2,1,0:T(8,128)(2,1)S(1)} %pad_maximum_fusion.10), channel_id=1, source_target_pairs={{0,24},{1,25},{2,26},{3,27},{4,28},{5,29},{6,30},{7,31},{8,0},{9,1... | collective-permute-start | bytes 442376 | tf_op jit(solution)/shard_map/ppermute | solution.py:75
  36.2 14.9 %collective-permute-start.15 = (bf16[8,288,128]{2,1,0:T(8,128)(2,1)S(1)}, bf16[8,288,128]{2,1,0:T(8,128)(2,1)S(1)}, u32[]{:S(2)}, u32[]{:S(2)}) collective-permute-start(bf16[8,288,128]{2,1,0:T(8,128)(2,1)S(1)} %constant_dynamic-update-slice_fusion.refs_9_), channel_id=1, source_target_pairs={{0,4},{1,5},{2,6},{3,7},{4,0},{5,1},{6,2},{7,3},{8,12},{9,13},{10,... | collective-permute-start | bytes 1769480 | tf_op jit(solution)/shard_map/ppermute | solution.py:75
  36.7 14.4 %collective-permute-start.10 = (bf16[8,288,128]{2,1,0:T(8,128)(2,1)S(1)}, bf16[8,288,128]{2,1,0:T(8,128)(2,1)S(1)}, u32[]{:S(2)}, u32[]{:S(2)}) collective-permute-start(bf16[8,288,128]{2,1,0:T(8,128)(2,1)S(1)} %constant_dynamic-update-slice_fusion.refs_9_), channel_id=1, source_target_pairs={{0,1},{1,0},{2,3},{3,2},{4,5},{5,4},{6,7},{7,6},{8,9},{9,8},{10,11... | collective-permute-start | bytes 1769480 | tf_op jit(solution)/shard_map/ppermute | solution.py:75
  36.7 16.4 %collective-permute-start.16 = (bf16[4,576,128]{2,1,0:T(8,128)(2,1)S(1)}, bf16[4,576,128]{2,1,0:T(8,128)(2,1)S(1)}, u32[]{:S(2)}, u32[]{:S(2)}) collective-permute-start(bf16[4,576,128]{2,1,0:T(8,128)(2,1)S(1)} %collective-permute-done.9.refs_2_), channel_id=1, source_target_pairs={{0,2},{1,3},{2,0},{3,1},{4,6},{5,7},{6,4},{7,5},{8,10},{9,11},{10,... | collective-permute-start | bytes 1769480 | tf_op jit(solution)/shard_map/ppermute | solution.py:75
  37.9 15.2 %collective-permute-start.12 = (bf16[4,576,128]{2,1,0:T(8,128)(2,1)S(1)}, bf16[4,576,128]{2,1,0:T(8,128)(2,1)S(1)}, u32[]{:S(2)}, u32[]{:S(2)}) collective-permute-start(bf16[4,576,128]{2,1,0:T(8,128)(2,1)S(1)} %collective-permute-done.9.refs_2_), channel_id=1, source_target_pairs={{0,1},{1,0},{2,3},{3,2},{4,5},{5,4},{6,7},{7,6},{8,9},{9,8},{10,11... | collective-permute-start | bytes 1769480 | tf_op jit(solution)/shard_map/ppermute | solution.py:75
  38.2 13.9 %collective-permute-start.13 = (bf16[4,576,128]{2,1,0:T(8,128)(2,1)S(1)}, bf16[4,576,128]{2,1,0:T(8,128)(2,1)S(1)}, u32[]{:S(2)}, u32[]{:S(2)}) collective-permute-start(bf16[4,576,128]{2,1,0:T(8,128)(2,1)S(1)} %pad_maximum_fusion.3.refs_1_), channel_id=1, source_target_pairs={{0,1},{1,0},{2,3},{3,2},{4,5},{5,4},{6,7},{7,6},{8,9},{9,8},{10,11... | collective-permute-start | bytes 1769480 | tf_op jit(solution)/shard_map/ppermute | solution.py:75
  51.1 2.9 %collective-permute-start.14 = (bf16[2,2,128,640]{3,2,1,0:T(8,128)(2,1)S(1)}, bf16[2,2,128,640]{3,2,1,0:T(8,128)(2,1)S(1)}, u32[]{:S(2)}, u32[]{:S(2)}) collective-permute-start(bf16[2,2,128,640]{3,2,1,0:T(8,128)(2,1)S(1)} %pad_maximum_fusion.refs_13_), channel_id=1, source_target_pairs={{0,1},{1,0},{2,3},{3,2},{4,5},{5,4},{6,7},{7,6},{8,9},{9,8},{10,11... | collective-permute-start | bytes 1966088 | tf_op jit(solution)/shard_map/ppermute | solution.py:80
  84.8 2.9 %collective-permute-start.19 = (bf16[2352,128]{1,0:T(8,128)(2,1)}, bf16[2352,128]{1,0:T(8,128)(2,1)S(1)}, u32[]{:S(2)}, u32[]{:S(2)}) collective-permute-start(bf16[2352,128]{1,0:T(8,128)(2,1)} %get-tuple-element.133), channel_id=1, source_target_pairs={{0,1},{1,0},{2,3},{3,2},{4,5},{5,4},{6,7},{7,6},{8,9},{9,8},{10,11... | collective-permute-start | bytes 1806344 | tf_op jit(solution)/shard_map/ppermute | solution.py:75
  85.0 2.7 %collective-permute-start.20 = (bf16[2304,128]{1,0:T(8,128)(2,1)S(1)}, bf16[2304,128]{1,0:T(8,128)(2,1)S(1)}, u32[]{:S(2)}, u32[]{:S(2)}) collective-permute-start(bf16[2304,128]{1,0:T(8,128)(2,1)S(1)} %get-tuple-element.134), channel_id=1, source_target_pairs={{0,1},{1,0},{2,3},{3,2},{4,5},{5,4},{6,7},{7,6},{8,9},{9,8},{10,11... | collective-permute-start | bytes 1769480 | tf_op jit(solution)/shard_map/ppermute | solution.py:75
  87.7 3.5 %collective-permute-start.25 = (bf16[2,2,128,384]{3,2,1,0:T(8,128)(2,1)S(1)}, bf16[2,2,128,384]{3,2,1,0:T(8,128)(2,1)S(1)}, u32[]{:S(2)}, u32[]{:S(2)}) collective-permute-start(bf16[2,2,128,384]{3,2,1,0:T(8,128)(2,1)S(1)} %get-tuple-element.148), channel_id=1, source_target_pairs={{0,1},{1,0},{2,3},{3,2},{4,5},{5,4},{6,7},{7,6},{8,9},{9,8},{10,11... | collective-permute-start | bytes 1179656 | tf_op jit(solution)/shard_map/ppermute | solution.py:80
  89.1 15.7 %collective-permute-start.22 = (bf16[2304,128]{1,0:T(8,128)(2,1)S(1)}, bf16[2304,128]{1,0:T(8,128)(2,1)S(1)}, u32[]{:S(2)}, u32[]{:S(2)}) collective-permute-start(bf16[2304,128]{1,0:T(8,128)(2,1)S(1)} %add_convert_fusion.5), channel_id=1, source_target_pairs={{0,4},{1,5},{2,6},{3,7},{4,0},{5,1},{6,2},{7,3},{8,12},{9,13},{10,... | collective-permute-start | bytes 1769480 | tf_op jit(solution)/shard_map/ppermute | solution.py:75
  89.8 4.7 %collective-permute-start.23 = (bf16[6912,128]{1,0:T(8,128)(2,1)}, bf16[6912,128]{1,0:T(8,128)(2,1)S(1)}, u32[]{:S(2)}, u32[]{:S(2)}) collective-permute-start(bf16[6912,128]{1,0:T(8,128)(2,1)} %get-tuple-element.142), channel_id=1, source_target_pairs={{0,1},{1,0},{2,3},{3,2},{4,5},{5,4},{6,7},{7,6},{8,9},{9,8},{10,11... | collective-permute-start | bytes 5308424 | tf_op jit(solution)/shard_map/ppermute | solution.py:75
  90.4 15.6 %collective-permute-start.21 = (bf16[2352,128]{1,0:T(8,128)(2,1)S(1)}, bf16[2352,128]{1,0:T(8,128)(2,1)S(1)}, u32[]{:S(2)}, u32[]{:S(2)}) collective-permute-start(bf16[2352,128]{1,0:T(8,128)(2,1)S(1)} %pad_maximum_fusion.1), channel_id=1, source_target_pairs={{0,2},{1,3},{2,0},{3,1},{4,6},{5,7},{6,4},{7,5},{8,10},{9,11},{10,... | collective-permute-start | bytes 1806344 | tf_op jit(solution)/shard_map/ppermute | solution.py:75
  106.3 15.8 %collective-permute-start.30 = (bf16[2352,128]{1,0:T(8,128)(2,1)S(1)}, bf16[2352,128]{1,0:T(8,128)(2,1)S(1)}, u32[]{:S(2)}, u32[]{:S(2)}) collective-permute-start(bf16[2352,128]{1,0:T(8,128)(2,1)S(1)} %pad_maximum_fusion.2), channel_id=1, source_target_pairs={{0,4},{1,5},{2,6},{3,7},{4,0},{5,1},{6,2},{7,3},{8,12},{9,13},{10,... | collective-permute-start | bytes 1806344 | tf_op jit(solution)/shard_map/ppermute | solution.py:75
  107.9 14.2 %collective-permute-start.29 = (bf16[2304,128]{1,0:T(8,128)(2,1)S(1)}, bf16[2304,128]{1,0:T(8,128)(2,1)S(1)}, u32[]{:S(2)}, u32[]{:S(2)}) collective-permute-start(bf16[2304,128]{1,0:T(8,128)(2,1)S(1)} %get-tuple-element.151), channel_id=1, source_target_pairs={{0,2},{1,3},{2,0},{3,1},{4,6},{5,7},{6,4},{7,5},{8,10},{9,11},{10,... | collective-permute-start | bytes 1769480 | tf_op jit(solution)/shard_map/ppermute | solution.py:75
  108.6 8.7 %collective-permute-start.28 = (bf16[576,128]{1,0:T(8,128)(2,1)S(1)}, bf16[576,128]{1,0:T(8,128)(2,1)S(1)}, u32[]{:S(2)}, u32[]{:S(2)}) collective-permute-start(bf16[576,128]{1,0:T(8,128)(2,1)S(1)} %get-tuple-element.214), channel_id=1, source_target_pairs={{0,8},{1,9},{2,10},{3,11},{4,12},{5,13},{6,14},{7,15},{8,16},{9,17... | collective-permute-start | bytes 442376 | tf_op jit(solution)/shard_map/ppermute | solution.py:75
  112.4 9.7 %collective-permute-start.27 = (bf16[576,128]{1,0:T(8,128)(2,1)S(1)}, bf16[576,128]{1,0:T(8,128)(2,1)S(1)}, u32[]{:S(2)}, u32[]{:S(2)}) collective-permute-start(bf16[576,128]{1,0:T(8,128)(2,1)S(1)} %get-tuple-element.215), channel_id=1, source_target_pairs={{0,16},{1,17},{2,18},{3,19},{4,20},{5,21},{6,22},{7,23},{8,24},{9,... | collective-permute-start | bytes 442376 | tf_op jit(solution)/shard_map/ppermute | solution.py:75
  112.4 9.7 %collective-permute-start.26 = (bf16[576,128]{1,0:T(8,128)(2,1)S(1)}, bf16[576,128]{1,0:T(8,128)(2,1)S(1)}, u32[]{:S(2)}, u32[]{:S(2)}) collective-permute-start(bf16[576,128]{1,0:T(8,128)(2,1)S(1)} %get-tuple-element.216), channel_id=1, source_target_pairs={{0,24},{1,25},{2,26},{3,27},{4,28},{5,29},{6,30},{7,31},{8,0},{9,1... | collective-permute-start | bytes 442376 | tf_op jit(solution)/shard_map/ppermute | solution.py:75
  123.1 14.6 %collective-permute-start.33 = (bf16[624,128]{1,0:T(8,128)(2,1)S(1)}, bf16[624,128]{1,0:T(8,128)(2,1)S(1)}, u32[]{:S(2)}, u32[]{:S(2)}) collective-permute-start(bf16[624,128]{1,0:T(8,128)(2,1)S(1)} %get-tuple-element.227), channel_id=1, source_target_pairs={{0,8},{1,9},{2,10},{3,11},{4,12},{5,13},{6,14},{7,15},{8,16},{9,17... | collective-permute-start | bytes 479240 | tf_op jit(solution)/shard_map/ppermute | solution.py:75
  126.9 11.3 %collective-permute-start.32 = (bf16[624,128]{1,0:T(8,128)(2,1)S(1)}, bf16[624,128]{1,0:T(8,128)(2,1)S(1)}, u32[]{:S(2)}, u32[]{:S(2)}) collective-permute-start(bf16[624,128]{1,0:T(8,128)(2,1)S(1)} %get-tuple-element.228), channel_id=1, source_target_pairs={{0,16},{1,17},{2,18},{3,19},{4,20},{5,21},{6,22},{7,23},{8,24},{9,... | collective-permute-start | bytes 479240 | tf_op jit(solution)/shard_map/ppermute | solution.py:75
  128.6 9.6 %collective-permute-start.31 = (bf16[624,128]{1,0:T(8,128)(2,1)S(1)}, bf16[624,128]{1,0:T(8,128)(2,1)S(1)}, u32[]{:S(2)}, u32[]{:S(2)}) collective-permute-start(bf16[624,128]{1,0:T(8,128)(2,1)S(1)} %get-tuple-element.229), channel_id=1, source_target_pairs={{0,24},{1,25},{2,26},{3,27},{4,28},{5,29},{6,30},{7,31},{8,0},{9,1... | collective-permute-start | bytes 479240 | tf_op jit(solution)/shard_map/ppermute | solution.py:75
  130.0 8.2 %collective-permute-start.35 = (bf16[2,128,384]{2,1,0:T(8,128)(2,1)S(1)}, bf16[2,128,384]{2,1,0:T(8,128)(2,1)S(1)}, u32[]{:S(2)}, u32[]{:S(2)}) collective-permute-start(bf16[2,128,384]{2,1,0:T(8,128)(2,1)S(1)} %get-tuple-element.223), channel_id=1, source_target_pairs={{0,2},{1,3},{2,0},{3,1},{4,6},{5,7},{6,4},{7,5},{8,10},{9,11},{10,... | collective-permute-start | bytes 589832 | tf_op jit(solution)/shard_map/ppermute | solution.py:80
  132.1 5.6 %collective-permute-start.34 = (bf16[288,128]{1,0:T(8,128)(2,1)S(1)}, bf16[288,128]{1,0:T(8,128)(2,1)S(1)}, u32[]{:S(2)}, u32[]{:S(2)}) collective-permute-start(bf16[288,128]{1,0:T(8,128)(2,1)S(1)} %get-tuple-element.221), channel_id=1, source_target_pairs={{0,2},{1,3},{2,0},{3,1},{4,6},{5,7},{6,4},{7,5},{8,10},{9,11},{10,... | collective-permute-start | bytes 221192 | tf_op jit(solution)/shard_map/ppermute | solution.py:75
  (38 other events, 234.2 us)

commit v13 on v12

--- a/solution.py
+++ b/solution.py
@@ -85,6 +85,7 @@
 
 
 def gather_all(head, tail, packed, others):
+    head, tail, packed = together(head, tail, packed)
     hz = [moved(head, "z", s) for s in (1, 2, 3)]
     tx = moved(tail, "x", 1)
     two = across(packed, 2)

time: 145 us -> 147 us (1.014)
  waiting for transfers between devices: 55.5 us -> 57.5 us
    ppermute x32, waiting for transfers between devices: 51 us -> 54.5 us  [moved(): return lax.ppermute(buffer, ('dp', 'ctx'), pairs)]
  transfers between devices with their start and end apart: 36 -> 36, of which waited for: 20 -> 19; matrix products, arithmetic and copies ran while one was open for 9% -> 7% of each run, Pallas kernels for 0% -> 0%
where the time goes in v13:
time: 147 us; the launch traced here: 146 us
  waiting for transfers between devices  57.5 us (39%)
  starting transfers between devices  37.7 us (26%)
  Pallas kernels  33.7 us (23%)
  other arithmetic  9.05 us (6%)
  local copies, waits for them, and re-layouts  6.57 us (4%)
    ppermute x32, waiting for transfers between devices, moved(): return lax.ppermute(buffer, ('dp', 'ctx'), pairs)  54.5 us
    ppermute x32, starting transfers between devices, moved(): return lax.ppermute(buffer, ('dp', 'ctx'), pairs)  35.2 us
    pallas_call x1, Pallas kernels, run_layer(): pl.pallas_call(layer_kernel, out_shape=(shape((2, MODEL_WIDTH, ROWS), BF1...  27.1 us
    pallas_call x1, Pallas kernels, finish(): pl.pallas_call(finish_kernel, out_shape=shapes, in_specs=[pl.BlockSpec(me...  4.76 us
    ppermute x4, waiting for transfers between devices, across(): lax.ppermute(buffer, 'ctx', [(i, i ^ distance) for i in range(count)])  3.06 us
  transfers between devices with their start and end apart: 36, of which 19 were waited for; matrix products, arithmetic and copies ran while one was open for 7% of the time, Pallas kernels for 0%

profile of v13, /device:TPU:0, one launch (start us, length us, event | category | flops | bytes accessed | tf_op | source)
XLA Modules:
  0.0 145.9 jit_solution(557372680447003192)
XLA Ops:
  0.7 1.9 %to_tiles.1 = (bf16[576,128]{1,0:T(8,128)(2,1)}, bf16[288,128]{1,0:T(8,128)(2,1)}) custom-call(s32[1]{0:T(128)} %bitcast.kind_ref, f32[864,128]{1,0:T(8,128)} %bitcast.153), custom_call_target="tpu_custom_call" | custom-call | tf_op jit(solution)/shard_map/to_tiles/pallas_call | solution.py:273
  3.6 1.2 copy.39
  5.0 3.0 %collective-permute-start.2 = (bf16[576,128]{1,0:T(8,128)(2,1)S(1)}, bf16[576,128]{1,0:T(8,128)(2,1)S(1)}, u32[]{:S(2)}, u32[]{:S(2)}) collective-permute-start(bf16[576,128]{1,0:T(8,128)(2,1)S(1)} %copy-done.27), channel_id=1, source_target_pairs={{0,8},{1,9},{2,10},{3,11},{4,12},{5,13},{6,14},{7,15},{8,16},{9,17... | collective-permute-start | bytes 442376 | tf_op jit(solution)/shard_map/ppermute | solution.py:75
  8.0 2.7 %collective-permute-start.1 = (bf16[576,128]{1,0:T(8,128)(2,1)S(1)}, bf16[576,128]{1,0:T(8,128)(2,1)S(1)}, u32[]{:S(2)}, u32[]{:S(2)}) collective-permute-start(bf16[576,128]{1,0:T(8,128)(2,1)S(1)} %copy-done.27), channel_id=1, source_target_pairs={{0,16},{1,17},{2,18},{3,19},{4,20},{5,21},{6,22},{7,23},{8,24},{9,... | collective-permute-start | bytes 442376 | tf_op jit(solution)/shard_map/ppermute | solution.py:75
  10.7 1.2 collective-permute-start
  11.9 1.5 %collective-permute-start.3 = (bf16[288,128]{1,0:T(8,128)(2,1)S(1)}, bf16[288,128]{1,0:T(8,128)(2,1)S(1)}, u32[]{:S(2)}, u32[]{:S(2)}) collective-permute-start(bf16[288,128]{1,0:T(8,128)(2,1)S(1)} %copy-done.28), channel_id=1, source_target_pairs={{0,2},{1,3},{2,0},{3,1},{4,6},{5,7},{6,4},{7,5},{8,10},{9,11},{10,... | collective-permute-start | bytes 221192 | tf_op jit(solution)/shard_map/ppermute | solution.py:75
  17.0 3.4 %collective-permute-done.1 = bf16[576,128]{1,0:T(8,128)(2,1)S(1)} collective-permute-done((bf16[576,128]{1,0:T(8,128)(2,1)S(1)}, bf16[576,128]{1,0:T(8,128)(2,1)S(1)}, u32[]{:S(2)}, u32[]{:S(2)}) %collective-permute-start.1) | collective-permute-done | bytes 147488 | tf_op jit(solution)/shard_map/ppermute | solution.py:75
  20.4 2.1 %collective-permute-done.4 = bf16[2,128,640]{2,1,0:T(8,128)(2,1)S(1)} collective-permute-done((bf16[2,128,640]{2,1,0:T(8,128)(2,1)S(1)}, bf16[2,128,640]{2,1,0:T(8,128)(2,1)S(1)}, u32[]{:S(2)}, u32[]{:S(2)}) %collective-permute-start.4) | collective-permute-done | bytes 327712 | tf_op jit(solution)/shard_map/ppermute | solution.py:80
  22.6 1.6 %collective-permute-start.9 = (bf16[4,576,128]{2,1,0:T(8,128)(2,1)S(1)}, bf16[4,576,128]{2,1,0:T(8,128)(2,1)S(1)}, u32[]{:S(2)}, u32[]{:S(2)}) collective-permute-start(bf16[4,576,128]{2,1,0:T(8,128)(2,1)S(1)} %pad_maximum_fusion.3.refs_1_), channel_id=1, source_target_pairs={{0,4},{1,5},{2,6},{3,7},{4,0},{5,1},{6,2},{7,3},{8,12},{9,13},{10,... | collective-permute-start | bytes 1769480 | tf_op jit(solution)/shard_map/ppermute | solution.py:75
  24.2 1.1 collective-permute-start.8
  25.4 2.0 %collective-permute-start.7 = (bf16[2,288,128]{2,1,0:T(8,128)(2,1)S(1)}, bf16[2,288,128]{2,1,0:T(8,128)(2,1)S(1)}, u32[]{:S(2)}, u32[]{:S(2)}) collective-permute-start(bf16[2,288,128]{2,1,0:T(8,128)(2,1)S(1)} %pad_maximum_fusion.10), channel_id=1, source_target_pairs={{0,8},{1,9},{2,10},{3,11},{4,12},{5,13},{6,14},{7,15},{8,16},{9,17... | collective-permute-start | bytes 442376 | tf_op jit(solution)/shard_map/ppermute | solution.py:75
  27.4 1.5 %collective-permute-start.6 = (bf16[2,288,128]{2,1,0:T(8,128)(2,1)S(1)}, bf16[2,288,128]{2,1,0:T(8,128)(2,1)S(1)}, u32[]{:S(2)}, u32[]{:S(2)}) collective-permute-start(bf16[2,288,128]{2,1,0:T(8,128)(2,1)S(1)} %pad_maximum_fusion.10), channel_id=1, source_target_pairs={{0,16},{1,17},{2,18},{3,19},{4,20},{5,21},{6,22},{7,23},{8,24},{9,... | collective-permute-start | bytes 442376 | tf_op jit(solution)/shard_map/ppermute | solution.py:75
  31.2 2.9 %collective-permute-done.7 = bf16[2,288,128]{2,1,0:T(8,128)(2,1)S(1)} collective-permute-done((bf16[2,288,128]{2,1,0:T(8,128)(2,1)S(1)}, bf16[2,288,128]{2,1,0:T(8,128)(2,1)S(1)}, u32[]{:S(2)}, u32[]{:S(2)}) %collective-permute-start.7) | collective-permute-done | bytes 147488 | tf_op jit(solution)/shard_map/ppermute | solution.py:75
  34.1 3.8 %collective-permute-done.6 = bf16[2,288,128]{2,1,0:T(8,128)(2,1)S(1)} collective-permute-done((bf16[2,288,128]{2,1,0:T(8,128)(2,1)S(1)}, bf16[2,288,128]{2,1,0:T(8,128)(2,1)S(1)}, u32[]{:S(2)}, u32[]{:S(2)}) %collective-permute-start.6) | collective-permute-done | bytes 147488 | tf_op jit(solution)/shard_map/ppermute | solution.py:75
  39.6 13.5 %collective-permute-done.15.refs_10_ = bf16[8,288,128]{2,1,0:T(8,128)(2,1)S(1)} collective-permute-done((bf16[8,288,128]{2,1,0:T(8,128)(2,1)S(1)}, bf16[8,288,128]{2,1,0:T(8,128)(2,1)S(1)}, u32[]{:S(2)}, u32[]{:S(2)}) %collective-permute-start.15) | collective-permute-done | bytes 589856 | tf_op jit(solution)/shard_map/ppermute | solution.py:75
  54.1 1.1 collective-permute-done.11.refs_7_
  59.8 27.1 %layer.1 = (bf16[2,576,128]{2,1,0:T(8,128)(2,1)}, bf16[2352,128]{1,0:T(8,128)(2,1)}, bf16[2304,128]{1,0:T(8,128)(2,1)S(1)}, bf16[6912,128]{1,0:T(8,128)(2,1)}, b...) custom-call(s32[98]{0:T(128)S(1)} %stack.448.refs_0_, ...), custom_call_target="tpu_custom_call" | custom-call | tf_op jit(solution)/shard_map/layer/pallas_call | solution.py:791
  87.5 2.4 %collective-permute-done.20 = bf16[2304,128]{1,0:T(8,128)(2,1)S(1)} collective-permute-done((bf16[2304,128]{1,0:T(8,128)(2,1)S(1)}, bf16[2304,128]{1,0:T(8,128)(2,1)S(1)}, u32[]{:S(2)}, u32[]{:S(2)}) %collective-permute-start.20) | collective-permute-done | bytes 589856 | tf_op jit(solution)/shard_map/ppermute | solution.py:75
  90.0 1.2 add_convert_fusion.5
  94.0 2.5 %collective-permute-done.23 = bf16[6912,128]{1,0:T(8,128)(2,1)S(1)} collective-permute-done((bf16[6912,128]{1,0:T(8,128)(2,1)}, bf16[6912,128]{1,0:T(8,128)(2,1)S(1)}, u32[]{:S(2)}, u32[]{:S(2)}) %collective-permute-start.23) | collective-permute-done | bytes 1769504 | tf_op jit(solution)/shard_map/ppermute | solution.py:75
  97.0 9.9 %collective-permute-done.22 = bf16[2304,128]{1,0:T(8,128)(2,1)S(1)} collective-permute-done((bf16[2304,128]{1,0:T(8,128)(2,1)S(1)}, bf16[2304,128]{1,0:T(8,128)(2,1)S(1)}, u32[]{:S(2)}, u32[]{:S(2)}) %collective-permute-start.22) | collective-permute-done | bytes 589856 | tf_op jit(solution)/shard_map/ppermute | solution.py:75
  106.8 1.3 collective-permute-done.21
  108.4 1.6 %collective-permute-start.30 = (bf16[2352,128]{1,0:T(8,128)(2,1)S(1)}, bf16[2352,128]{1,0:T(8,128)(2,1)S(1)}, u32[]{:S(2)}, u32[]{:S(2)}) collective-permute-start(bf16[2352,128]{1,0:T(8,128)(2,1)S(1)} %pad_maximum_fusion.2), channel_id=1, source_target_pairs={{0,4},{1,5},{2,6},{3,7},{4,0},{5,1},{6,2},{7,3},{8,12},{9,13},{10,... | collective-permute-start | bytes 1806344 | tf_op jit(solution)/shard_map/ppermute | solution.py:75
  110.7 3.8 %collective-permute-start.28 = (bf16[576,128]{1,0:T(8,128)(2,1)S(1)}, bf16[576,128]{1,0:T(8,128)(2,1)S(1)}, u32[]{:S(2)}, u32[]{:S(2)}) collective-permute-start(bf16[576,128]{1,0:T(8,128)(2,1)S(1)} %get-tuple-element.220), channel_id=1, source_target_pairs={{0,8},{1,9},{2,10},{3,11},{4,12},{5,13},{6,14},{7,15},{8,16},{9,17... | collective-permute-start | bytes 442376 | tf_op jit(solution)/shard_map/ppermute | solution.py:75
  115.1 1.8 %collective-permute-start.26 = (bf16[576,128]{1,0:T(8,128)(2,1)S(1)}, bf16[576,128]{1,0:T(8,128)(2,1)S(1)}, u32[]{:S(2)}, u32[]{:S(2)}) collective-permute-start(bf16[576,128]{1,0:T(8,128)(2,1)S(1)} %get-tuple-element.222), channel_id=1, source_target_pairs={{0,24},{1,25},{2,26},{3,27},{4,28},{5,29},{6,30},{7,31},{8,0},{9,1... | collective-permute-start | bytes 442376 | tf_op jit(solution)/shard_map/ppermute | solution.py:75
  116.9 2.4 %collective-permute-done.28 = bf16[576,128]{1,0:T(8,128)(2,1)S(1)} collective-permute-done((bf16[576,128]{1,0:T(8,128)(2,1)S(1)}, bf16[576,128]{1,0:T(8,128)(2,1)S(1)}, u32[]{:S(2)}, u32[]{:S(2)}) %collective-permute-start.28) | collective-permute-done | bytes 147488 | tf_op jit(solution)/shard_map/ppermute | solution.py:75
  119.4 4.8 %collective-permute-done.27 = bf16[576,128]{1,0:T(8,128)(2,1)S(1)} collective-permute-done((bf16[576,128]{1,0:T(8,128)(2,1)S(1)}, bf16[576,128]{1,0:T(8,128)(2,1)S(1)}, u32[]{:S(2)}, u32[]{:S(2)}) %collective-permute-start.27) | collective-permute-done | bytes 147488 | tf_op jit(solution)/shard_map/ppermute | solution.py:75
  125.2 3.7 %collective-permute-start.33 = (bf16[624,128]{1,0:T(8,128)(2,1)S(1)}, bf16[624,128]{1,0:T(8,128)(2,1)S(1)}, u32[]{:S(2)}, u32[]{:S(2)}) collective-permute-start(bf16[624,128]{1,0:T(8,128)(2,1)S(1)} %get-tuple-element.233), channel_id=1, source_target_pairs={{0,8},{1,9},{2,10},{3,11},{4,12},{5,13},{6,14},{7,15},{8,16},{9,17... | collective-permute-start | bytes 479240 | tf_op jit(solution)/shard_map/ppermute | solution.py:75
  128.9 1.7 %collective-permute-start.32 = (bf16[624,128]{1,0:T(8,128)(2,1)S(1)}, bf16[624,128]{1,0:T(8,128)(2,1)S(1)}, u32[]{:S(2)}, u32[]{:S(2)}) collective-permute-start(bf16[624,128]{1,0:T(8,128)(2,1)S(1)} %get-tuple-element.234), channel_id=1, source_target_pairs={{0,16},{1,17},{2,18},{3,19},{4,20},{5,21},{6,22},{7,23},{8,24},{9,... | collective-permute-start | bytes 479240 | tf_op jit(solution)/shard_map/ppermute | solution.py:75
  132.1 1.3 collective-permute-start.35
  135.4 4.4 %collective-permute-done.34.other_ref = bf16[288,128]{1,0:T(8,128)(2,1)S(1)} collective-permute-done((bf16[288,128]{1,0:T(8,128)(2,1)S(1)}, bf16[288,128]{1,0:T(8,128)(2,1)S(1)}, u32[]{:S(2)}, u32[]{:S(2)}) %collective-permute-start.34) | collective-permute-done | bytes 73760 | tf_op jit(solution)/shard_map/ppermute | solution.py:75
  141.1 4.8 %finish.1 = (f32[24,128]{1,0:T(8,128)}, f32[24,128]{1,0:T(8,128)}, f32[24,128]{1,0:T(8,128)}, f32[864,128]{1,0:T(8,128)}, f32[864,128]{1,0:T(8,128)}, /*index=5*/f32[864,128]{1,0:T(8,128)}, bf16[2,576,128]{2,1,0:T(8,128)(2,1)}) custom-call(s32[2]{0:T(128)} %pad_add_fusion.table_ref, f32[576,128]{1,0:T(8,128)} %get-tuple-element.213.head_ref, ...), custom_call_target="tpu_custom_call" | custom-call | tf_op jit(solution)/shard_map/finish/pallas_call | solution.py:375
  (174 shorter events, 25.6 us)
Async XLA Ops:
  5.0 12.0 %collective-permute-start.2 = (bf16[576,128]{1,0:T(8,128)(2,1)S(1)}, bf16[576,128]{1,0:T(8,128)(2,1)S(1)}, u32[]{:S(2)}, u32[]{:S(2)}) collective-permute-start(bf16[576,128]{1,0:T(8,128)(2,1)S(1)} %copy-done.27), channel_id=1, source_target_pairs={{0,8},{1,9},{2,10},{3,11},{4,12},{5,13},{6,14},{7,15},{8,16},{9,17... | collective-permute-start | bytes 442376 | tf_op jit(solution)/shard_map/ppermute | solution.py:75
  8.0 12.4 %collective-permute-start.1 = (bf16[576,128]{1,0:T(8,128)(2,1)S(1)}, bf16[576,128]{1,0:T(8,128)(2,1)S(1)}, u32[]{:S(2)}, u32[]{:S(2)}) collective-permute-start(bf16[576,128]{1,0:T(8,128)(2,1)S(1)} %copy-done.27), channel_id=1, source_target_pairs={{0,16},{1,17},{2,18},{3,19},{4,20},{5,21},{6,22},{7,23},{8,24},{9,... | collective-permute-start | bytes 442376 | tf_op jit(solution)/shard_map/ppermute | solution.py:75
  10.7 9.7 %collective-permute-start = (bf16[576,128]{1,0:T(8,128)(2,1)S(1)}, bf16[576,128]{1,0:T(8,128)(2,1)S(1)}, u32[]{:S(2)}, u32[]{:S(2)}) collective-permute-start(bf16[576,128]{1,0:T(8,128)(2,1)S(1)} %copy-done.27), channel_id=1, source_target_pairs={{0,24},{1,25},{2,26},{3,27},{4,28},{5,29},{6,30},{7,31},{8,0},{9,1... | collective-permute-start | bytes 442376 | tf_op jit(solution)/shard_map/ppermute | solution.py:75
  11.9 5.1 %collective-permute-start.3 = (bf16[288,128]{1,0:T(8,128)(2,1)S(1)}, bf16[288,128]{1,0:T(8,128)(2,1)S(1)}, u32[]{:S(2)}, u32[]{:S(2)}) collective-permute-start(bf16[288,128]{1,0:T(8,128)(2,1)S(1)} %copy-done.28), channel_id=1, source_target_pairs={{0,2},{1,3},{2,0},{3,1},{4,6},{5,7},{6,4},{7,5},{8,10},{9,11},{10,... | collective-permute-start | bytes 221192 | tf_op jit(solution)/shard_map/ppermute | solution.py:75
  13.4 9.1 %collective-permute-start.4 = (bf16[2,128,640]{2,1,0:T(8,128)(2,1)S(1)}, bf16[2,128,640]{2,1,0:T(8,128)(2,1)S(1)}, u32[]{:S(2)}, u32[]{:S(2)}) collective-permute-start(bf16[2,128,640]{2,1,0:T(8,128)(2,1)S(1)} %maximum_maximum_fusion.refs_0_), channel_id=1, source_target_pairs={{0,2},{1,3},{2,0},{3,1},{4,6},{5,7},{6,4},{7,5},{8,10},{9,11},{10,... | collective-permute-start | bytes 983048 | tf_op jit(solution)/shard_map/ppermute | solution.py:80
  22.6 15.2 %collective-permute-start.9 = (bf16[4,576,128]{2,1,0:T(8,128)(2,1)S(1)}, bf16[4,576,128]{2,1,0:T(8,128)(2,1)S(1)}, u32[]{:S(2)}, u32[]{:S(2)}) collective-permute-start(bf16[4,576,128]{2,1,0:T(8,128)(2,1)S(1)} %pad_maximum_fusion.3.refs_1_), channel_id=1, source_target_pairs={{0,4},{1,5},{2,6},{3,7},{4,0},{5,1},{6,2},{7,3},{8,12},{9,13},{10,... | collective-permute-start | bytes 1769480 | tf_op jit(solution)/shard_map/ppermute | solution.py:75
  24.2 13.6 %collective-permute-start.8 = (bf16[4,576,128]{2,1,0:T(8,128)(2,1)S(1)}, bf16[4,576,128]{2,1,0:T(8,128)(2,1)S(1)}, u32[]{:S(2)}, u32[]{:S(2)}) collective-permute-start(bf16[4,576,128]{2,1,0:T(8,128)(2,1)S(1)} %pad_maximum_fusion.3.refs_1_), channel_id=1, source_target_pairs={{0,2},{1,3},{2,0},{3,1},{4,6},{5,7},{6,4},{7,5},{8,10},{9,11},{10,... | collective-permute-start | bytes 1769480 | tf_op jit(solution)/shard_map/ppermute | solution.py:75
  25.4 8.7 %collective-permute-start.7 = (bf16[2,288,128]{2,1,0:T(8,128)(2,1)S(1)}, bf16[2,288,128]{2,1,0:T(8,128)(2,1)S(1)}, u32[]{:S(2)}, u32[]{:S(2)}) collective-permute-start(bf16[2,288,128]{2,1,0:T(8,128)(2,1)S(1)} %pad_maximum_fusion.10), channel_id=1, source_target_pairs={{0,8},{1,9},{2,10},{3,11},{4,12},{5,13},{6,14},{7,15},{8,16},{9,17... | collective-permute-start | bytes 442376 | tf_op jit(solution)/shard_map/ppermute | solution.py:75
  27.4 10.5 %collective-permute-start.6 = (bf16[2,288,128]{2,1,0:T(8,128)(2,1)S(1)}, bf16[2,288,128]{2,1,0:T(8,128)(2,1)S(1)}, u32[]{:S(2)}, u32[]{:S(2)}) collective-permute-start(bf16[2,288,128]{2,1,0:T(8,128)(2,1)S(1)} %pad_maximum_fusion.10), channel_id=1, source_target_pairs={{0,16},{1,17},{2,18},{3,19},{4,20},{5,21},{6,22},{7,23},{8,24},{9,... | collective-permute-start | bytes 442376 | tf_op jit(solution)/shard_map/ppermute | solution.py:75
  28.9 9.0 %collective-permute-start.5 = (bf16[2,288,128]{2,1,0:T(8,128)(2,1)S(1)}, bf16[2,288,128]{2,1,0:T(8,128)(2,1)S(1)}, u32[]{:S(2)}, u32[]{:S(2)}) collective-permute-start(bf16[2,288,128]{2,1,0:T(8,128)(2,1)S(1)} %pad_maximum_fusion.10), channel_id=1, source_target_pairs={{0,24},{1,25},{2,26},{3,27},{4,28},{5,29},{6,30},{7,31},{8,0},{9,1... | collective-permute-start | bytes 442376 | tf_op jit(solution)/shard_map/ppermute | solution.py:75
  38.0 15.2 %collective-permute-start.15 = (bf16[8,288,128]{2,1,0:T(8,128)(2,1)S(1)}, bf16[8,288,128]{2,1,0:T(8,128)(2,1)S(1)}, u32[]{:S(2)}, u32[]{:S(2)}) collective-permute-start(bf16[8,288,128]{2,1,0:T(8,128)(2,1)S(1)} %constant_dynamic-update-slice_fusion.refs_9_), channel_id=1, source_target_pairs={{0,4},{1,5},{2,6},{3,7},{4,0},{5,1},{6,2},{7,3},{8,12},{9,13},{10,... | collective-permute-start | bytes 1769480 | tf_op jit(solution)/shard_map/ppermute | solution.py:75
  38.5 14.7 %collective-permute-start.10 = (bf16[8,288,128]{2,1,0:T(8,128)(2,1)S(1)}, bf16[8,288,128]{2,1,0:T(8,128)(2,1)S(1)}, u32[]{:S(2)}, u32[]{:S(2)}) collective-permute-start(bf16[8,288,128]{2,1,0:T(8,128)(2,1)S(1)} %constant_dynamic-update-slice_fusion.refs_9_), channel_id=1, source_target_pairs={{0,1},{1,0},{2,3},{3,2},{4,5},{5,4},{6,7},{7,6},{8,9},{9,8},{10,11... | collective-permute-start | bytes 1769480 | tf_op jit(solution)/shard_map/ppermute | solution.py:75
  38.5 16.7 %collective-permute-start.16 = (bf16[4,576,128]{2,1,0:T(8,128)(2,1)S(1)}, bf16[4,576,128]{2,1,0:T(8,128)(2,1)S(1)}, u32[]{:S(2)}, u32[]{:S(2)}) collective-permute-start(bf16[4,576,128]{2,1,0:T(8,128)(2,1)S(1)} %collective-permute-done.9.refs_2_), channel_id=1, source_target_pairs={{0,2},{1,3},{2,0},{3,1},{4,6},{5,7},{6,4},{7,5},{8,10},{9,11},{10,... | collective-permute-start | bytes 1769480 | tf_op jit(solution)/shard_map/ppermute | solution.py:75
  39.1 16.1 %collective-permute-start.12 = (bf16[4,576,128]{2,1,0:T(8,128)(2,1)S(1)}, bf16[4,576,128]{2,1,0:T(8,128)(2,1)S(1)}, u32[]{:S(2)}, u32[]{:S(2)}) collective-permute-start(bf16[4,576,128]{2,1,0:T(8,128)(2,1)S(1)} %collective-permute-done.9.refs_2_), channel_id=1, source_target_pairs={{0,1},{1,0},{2,3},{3,2},{4,5},{5,4},{6,7},{7,6},{8,9},{9,8},{10,11... | collective-permute-start | bytes 1769480 | tf_op jit(solution)/shard_map/ppermute | solution.py:75
  39.4 14.7 %collective-permute-start.13 = (bf16[4,576,128]{2,1,0:T(8,128)(2,1)S(1)}, bf16[4,576,128]{2,1,0:T(8,128)(2,1)S(1)}, u32[]{:S(2)}, u32[]{:S(2)}) collective-permute-start(bf16[4,576,128]{2,1,0:T(8,128)(2,1)S(1)} %pad_maximum_fusion.3.refs_1_), channel_id=1, source_target_pairs={{0,1},{1,0},{2,3},{3,2},{4,5},{5,4},{6,7},{7,6},{8,9},{9,8},{10,11... | collective-permute-start | bytes 1769480 | tf_op jit(solution)/shard_map/ppermute | solution.py:75
  53.2 2.9 %collective-permute-start.14 = (bf16[2,2,128,640]{3,2,1,0:T(8,128)(2,1)S(1)}, bf16[2,2,128,640]{3,2,1,0:T(8,128)(2,1)S(1)}, u32[]{:S(2)}, u32[]{:S(2)}) collective-permute-start(bf16[2,2,128,640]{3,2,1,0:T(8,128)(2,1)S(1)} %pad_maximum_fusion.refs_13_), channel_id=1, source_target_pairs={{0,1},{1,0},{2,3},{3,2},{4,5},{5,4},{6,7},{7,6},{8,9},{9,8},{10,11... | collective-permute-start | bytes 1966088 | tf_op jit(solution)/shard_map/ppermute | solution.py:80
  86.9 2.9 %collective-permute-start.19 = (bf16[2352,128]{1,0:T(8,128)(2,1)}, bf16[2352,128]{1,0:T(8,128)(2,1)S(1)}, u32[]{:S(2)}, u32[]{:S(2)}) collective-permute-start(bf16[2352,128]{1,0:T(8,128)(2,1)} %get-tuple-element.139), channel_id=1, source_target_pairs={{0,1},{1,0},{2,3},{3,2},{4,5},{5,4},{6,7},{7,6},{8,9},{9,8},{10,11... | collective-permute-start | bytes 1806344 | tf_op jit(solution)/shard_map/ppermute | solution.py:75
  87.1 2.7 %collective-permute-start.20 = (bf16[2304,128]{1,0:T(8,128)(2,1)S(1)}, bf16[2304,128]{1,0:T(8,128)(2,1)S(1)}, u32[]{:S(2)}, u32[]{:S(2)}) collective-permute-start(bf16[2304,128]{1,0:T(8,128)(2,1)S(1)} %get-tuple-element.140), channel_id=1, source_target_pairs={{0,1},{1,0},{2,3},{3,2},{4,5},{5,4},{6,7},{7,6},{8,9},{9,8},{10,11... | collective-permute-start | bytes 1769480 | tf_op jit(solution)/shard_map/ppermute | solution.py:75
  89.8 3.4 %collective-permute-start.25 = (bf16[2,2,128,384]{3,2,1,0:T(8,128)(2,1)S(1)}, bf16[2,2,128,384]{3,2,1,0:T(8,128)(2,1)S(1)}, u32[]{:S(2)}, u32[]{:S(2)}) collective-permute-start(bf16[2,2,128,384]{3,2,1,0:T(8,128)(2,1)S(1)} %get-tuple-element.154), channel_id=1, source_target_pairs={{0,1},{1,0},{2,3},{3,2},{4,5},{5,4},{6,7},{7,6},{8,9},{9,8},{10,11... | collective-permute-start | bytes 1179656 | tf_op jit(solution)/shard_map/ppermute | solution.py:80
  91.2 15.7 %collective-permute-start.22 = (bf16[2304,128]{1,0:T(8,128)(2,1)S(1)}, bf16[2304,128]{1,0:T(8,128)(2,1)S(1)}, u32[]{:S(2)}, u32[]{:S(2)}) collective-permute-start(bf16[2304,128]{1,0:T(8,128)(2,1)S(1)} %add_convert_fusion.5), channel_id=1, source_target_pairs={{0,4},{1,5},{2,6},{3,7},{4,0},{5,1},{6,2},{7,3},{8,12},{9,13},{10,... | collective-permute-start | bytes 1769480 | tf_op jit(solution)/shard_map/ppermute | solution.py:75
  91.8 4.7 %collective-permute-start.23 = (bf16[6912,128]{1,0:T(8,128)(2,1)}, bf16[6912,128]{1,0:T(8,128)(2,1)S(1)}, u32[]{:S(2)}, u32[]{:S(2)}) collective-permute-start(bf16[6912,128]{1,0:T(8,128)(2,1)} %get-tuple-element.148), channel_id=1, source_target_pairs={{0,1},{1,0},{2,3},{3,2},{4,5},{5,4},{6,7},{7,6},{8,9},{9,8},{10,11... | collective-permute-start | bytes 5308424 | tf_op jit(solution)/shard_map/ppermute | solution.py:75
  92.5 15.6 %collective-permute-start.21 = (bf16[2352,128]{1,0:T(8,128)(2,1)S(1)}, bf16[2352,128]{1,0:T(8,128)(2,1)S(1)}, u32[]{:S(2)}, u32[]{:S(2)}) collective-permute-start(bf16[2352,128]{1,0:T(8,128)(2,1)S(1)} %pad_maximum_fusion.1), channel_id=1, source_target_pairs={{0,2},{1,3},{2,0},{3,1},{4,6},{5,7},{6,4},{7,5},{8,10},{9,11},{10,... | collective-permute-start | bytes 1806344 | tf_op jit(solution)/shard_map/ppermute | solution.py:75
  108.4 15.8 %collective-permute-start.30 = (bf16[2352,128]{1,0:T(8,128)(2,1)S(1)}, bf16[2352,128]{1,0:T(8,128)(2,1)S(1)}, u32[]{:S(2)}, u32[]{:S(2)}) collective-permute-start(bf16[2352,128]{1,0:T(8,128)(2,1)S(1)} %pad_maximum_fusion.2), channel_id=1, source_target_pairs={{0,4},{1,5},{2,6},{3,7},{4,0},{5,1},{6,2},{7,3},{8,12},{9,13},{10,... | collective-permute-start | bytes 1806344 | tf_op jit(solution)/shard_map/ppermute | solution.py:75
  110.0 14.2 %collective-permute-start.29 = (bf16[2304,128]{1,0:T(8,128)(2,1)S(1)}, bf16[2304,128]{1,0:T(8,128)(2,1)S(1)}, u32[]{:S(2)}, u32[]{:S(2)}) collective-permute-start(bf16[2304,128]{1,0:T(8,128)(2,1)S(1)} %get-tuple-element.157), channel_id=1, source_target_pairs={{0,2},{1,3},{2,0},{3,1},{4,6},{5,7},{6,4},{7,5},{8,10},{9,11},{10,... | collective-permute-start | bytes 1769480 | tf_op jit(solution)/shard_map/ppermute | solution.py:75
  110.7 8.6 %collective-permute-start.28 = (bf16[576,128]{1,0:T(8,128)(2,1)S(1)}, bf16[576,128]{1,0:T(8,128)(2,1)S(1)}, u32[]{:S(2)}, u32[]{:S(2)}) collective-permute-start(bf16[576,128]{1,0:T(8,128)(2,1)S(1)} %get-tuple-element.220), channel_id=1, source_target_pairs={{0,8},{1,9},{2,10},{3,11},{4,12},{5,13},{6,14},{7,15},{8,16},{9,17... | collective-permute-start | bytes 442376 | tf_op jit(solution)/shard_map/ppermute | solution.py:75
  114.5 9.6 %collective-permute-start.27 = (bf16[576,128]{1,0:T(8,128)(2,1)S(1)}, bf16[576,128]{1,0:T(8,128)(2,1)S(1)}, u32[]{:S(2)}, u32[]{:S(2)}) collective-permute-start(bf16[576,128]{1,0:T(8,128)(2,1)S(1)} %get-tuple-element.221), channel_id=1, source_target_pairs={{0,16},{1,17},{2,18},{3,19},{4,20},{5,21},{6,22},{7,23},{8,24},{9,... | collective-permute-start | bytes 442376 | tf_op jit(solution)/shard_map/ppermute | solution.py:75
  115.1 9.0 %collective-permute-start.26 = (bf16[576,128]{1,0:T(8,128)(2,1)S(1)}, bf16[576,128]{1,0:T(8,128)(2,1)S(1)}, u32[]{:S(2)}, u32[]{:S(2)}) collective-permute-start(bf16[576,128]{1,0:T(8,128)(2,1)S(1)} %get-tuple-element.222), channel_id=1, source_target_pairs={{0,24},{1,25},{2,26},{3,27},{4,28},{5,29},{6,30},{7,31},{8,0},{9,1... | collective-permute-start | bytes 442376 | tf_op jit(solution)/shard_map/ppermute | solution.py:75
  125.2 14.6 %collective-permute-start.33 = (bf16[624,128]{1,0:T(8,128)(2,1)S(1)}, bf16[624,128]{1,0:T(8,128)(2,1)S(1)}, u32[]{:S(2)}, u32[]{:S(2)}) collective-permute-start(bf16[624,128]{1,0:T(8,128)(2,1)S(1)} %get-tuple-element.233), channel_id=1, source_target_pairs={{0,8},{1,9},{2,10},{3,11},{4,12},{5,13},{6,14},{7,15},{8,16},{9,17... | collective-permute-start | bytes 479240 | tf_op jit(solution)/shard_map/ppermute | solution.py:75
  128.9 11.4 %collective-permute-start.32 = (bf16[624,128]{1,0:T(8,128)(2,1)S(1)}, bf16[624,128]{1,0:T(8,128)(2,1)S(1)}, u32[]{:S(2)}, u32[]{:S(2)}) collective-permute-start(bf16[624,128]{1,0:T(8,128)(2,1)S(1)} %get-tuple-element.234), channel_id=1, source_target_pairs={{0,16},{1,17},{2,18},{3,19},{4,20},{5,21},{6,22},{7,23},{8,24},{9,... | collective-permute-start | bytes 479240 | tf_op jit(solution)/shard_map/ppermute | solution.py:75
  130.7 9.6 %collective-permute-start.31 = (bf16[624,128]{1,0:T(8,128)(2,1)S(1)}, bf16[624,128]{1,0:T(8,128)(2,1)S(1)}, u32[]{:S(2)}, u32[]{:S(2)}) collective-permute-start(bf16[624,128]{1,0:T(8,128)(2,1)S(1)} %get-tuple-element.235), channel_id=1, source_target_pairs={{0,24},{1,25},{2,26},{3,27},{4,28},{5,29},{6,30},{7,31},{8,0},{9,1... | collective-permute-start | bytes 479240 | tf_op jit(solution)/shard_map/ppermute | solution.py:75
  132.1 8.2 %collective-permute-start.35 = (bf16[2,128,384]{2,1,0:T(8,128)(2,1)S(1)}, bf16[2,128,384]{2,1,0:T(8,128)(2,1)S(1)}, u32[]{:S(2)}, u32[]{:S(2)}) collective-permute-start(bf16[2,128,384]{2,1,0:T(8,128)(2,1)S(1)} %get-tuple-element.229), channel_id=1, source_target_pairs={{0,2},{1,3},{2,0},{3,1},{4,6},{5,7},{6,4},{7,5},{8,10},{9,11},{10,... | collective-permute-start | bytes 589832 | tf_op jit(solution)/shard_map/ppermute | solution.py:80
  134.2 5.7 %collective-permute-start.34 = (bf16[288,128]{1,0:T(8,128)(2,1)S(1)}, bf16[288,128]{1,0:T(8,128)(2,1)S(1)}, u32[]{:S(2)}, u32[]{:S(2)}) collective-permute-start(bf16[288,128]{1,0:T(8,128)(2,1)S(1)} %get-tuple-element.227), channel_id=1, source_target_pairs={{0,2},{1,3},{2,0},{3,1},{4,6},{5,7},{6,4},{7,5},{8,10},{9,11},{10,... | collective-permute-start | bytes 221192 | tf_op jit(solution)/shard_map/ppermute | solution.py:75
  (38 other events, 305.3 us)

commit v14 on v12

--- a/solution.py
+++ b/solution.py
@@ -551,8 +551,9 @@
             top = jnp.max(scores, axis=-1, keepdims=True)
             powers = jnp.exp(scores - top)
             found = powers * (1.0 / jnp.sum(powers, axis=-1, keepdims=True))
+            found = found.astype(BF16)
             probs[mb, group] = found
-            out = product(found.astype(BF16), values[key_rows, lanes])
+            out = product(found, values[key_rows, lanes])
             outs[mb, group] = out
             parts += [out[ROWS * k : ROWS * k + ROWS] for k in range(3)]
         for k, tile in enumerate(tiles_of_heads(parts)):
@@ -675,11 +676,11 @@
             found = probs[mb, group]
             d_probs = times_transposed(cotangent, values[key_rows, lanes])
             delta = jnp.sum(outs[mb, group] * cotangent.astype(F32), axis=-1, keepdims=True)
-            d_scores = (found * (d_probs - delta)).astype(BF16)
+            d_scores = (found.astype(F32) * (d_probs - delta)).astype(BF16)
             out = product(d_scores, keys[key_rows, lanes]) * HEAD_SIZE ** (-0.5)
             parts += [out[ROWS * k : ROWS * k + ROWS] for k in range(3)]
             d_key = rows_product(d_scores, query_rows)
-            d_value = rows_product(found.astype(BF16), cotangent)
+            d_value = rows_product(found, cotangent)
             d_keys.append(d_key + half_turn(d_key))
             d_values.append(d_value + half_turn(d_value))
         cosines, sines = cos_pair[0][0, mb], sin_pair[0][0, mb]
@@ -775,7 +776,7 @@
         ((1024, 384), BF16),
         ((1024, 384), BF16),
         ((256, WIDE), BF16),
-        ((2, 3, 384, 512), F32),
+        ((2, 3, 384, 512), BF16),
         ((256, WIDE), BF16),
         ((256, FF), BF16),
         ((256, WIDE), F32),

time: 145 us -> 145 us (level)
  transfers between devices with their start and end apart: 36 -> 36, of which waited for: 20 -> 19; matrix products, arithmetic and copies ran while one was open for 9% -> 9% of each run, Pallas kernels for 0% -> 0%
where the time goes in v14:
time: 145 us; the launch traced here: 144 us
  waiting for transfers between devices  55.5 us (38%)
  starting transfers between devices  37.6 us (26%)
  Pallas kernels  33.7 us (23%)
  other arithmetic  9.16 us (6%)
  local copies, waits for them, and re-layouts  6.49 us (4%)
    ppermute x32, waiting for transfers between devices, moved(): return lax.ppermute(buffer, ('dp', 'ctx'), pairs)  51 us
    ppermute x32, starting transfers between devices, moved(): return lax.ppermute(buffer, ('dp', 'ctx'), pairs)  35 us
    pallas_call x1, Pallas kernels, run_layer(): pl.pallas_call(layer_kernel, out_shape=(shape((2, MODEL_WIDTH, ROWS), BF1...  27.1 us
    pallas_call x1, Pallas kernels, finish(): pl.pallas_call(finish_kernel, out_shape=shapes, in_specs=[pl.BlockSpec(me...  4.76 us
    ppermute x4, waiting for transfers between devices, across(): lax.ppermute(buffer, 'ctx', [(i, i ^ distance) for i in range(count)])  4.49 us
  transfers between devices with their start and end apart: 36, of which 19 were waited for; matrix products, arithmetic and copies ran while one was open for 9% of the time, Pallas kernels for 0%

profile of v14, /device:TPU:0, one launch (start us, length us, event | category | flops | bytes accessed | tf_op | source)
XLA Modules:
  0.0 143.9 jit_solution(6282581723939651651)
XLA Ops:
  0.7 1.9 %to_tiles.1 = (bf16[576,128]{1,0:T(8,128)(2,1)}, bf16[288,128]{1,0:T(8,128)(2,1)}) custom-call(s32[1]{0:T(128)} %bitcast.kind_ref, f32[864,128]{1,0:T(8,128)} %bitcast.154), custom_call_target="tpu_custom_call" | custom-call | tf_op jit(solution)/shard_map/to_tiles/pallas_call | solution.py:272
  2.5 2.9 %collective-permute-start.2 = (bf16[576,128]{1,0:T(8,128)(2,1)}, bf16[576,128]{1,0:T(8,128)(2,1)S(1)}, u32[]{:S(2)}, u32[]{:S(2)}) collective-permute-start(bf16[576,128]{1,0:T(8,128)(2,1)} %get-tuple-element.99), channel_id=1, source_target_pairs={{0,8},{1,9},{2,10},{3,11},{4,12},{5,13},{6,14},{7,15},{8,16},{9,17... | collective-permute-start | bytes 442376 | tf_op jit(solution)/shard_map/ppermute | solution.py:75
  5.4 2.7 %collective-permute-start.1 = (bf16[576,128]{1,0:T(8,128)(2,1)}, bf16[576,128]{1,0:T(8,128)(2,1)S(1)}, u32[]{:S(2)}, u32[]{:S(2)}) collective-permute-start(bf16[576,128]{1,0:T(8,128)(2,1)} %get-tuple-element.99), channel_id=1, source_target_pairs={{0,16},{1,17},{2,18},{3,19},{4,20},{5,21},{6,22},{7,23},{8,24},{9,... | collective-permute-start | bytes 442376 | tf_op jit(solution)/shard_map/ppermute | solution.py:75
  8.2 1.2 collective-permute-start
  9.4 1.5 %collective-permute-start.3 = (bf16[288,128]{1,0:T(8,128)(2,1)}, bf16[288,128]{1,0:T(8,128)(2,1)S(1)}, u32[]{:S(2)}, u32[]{:S(2)}) collective-permute-start(bf16[288,128]{1,0:T(8,128)(2,1)} %get-tuple-element.103), channel_id=1, source_target_pairs={{0,2},{1,3},{2,0},{3,1},{4,6},{5,7},{6,4},{7,5},{8,10},{9,11},{10,... | collective-permute-start | bytes 221192 | tf_op jit(solution)/shard_map/ppermute | solution.py:75
  11.8 1.2 copy.39
  16.8 1.2 collective-permute-done.1
  18.1 3.6 %collective-permute-done.4 = bf16[2,128,640]{2,1,0:T(8,128)(2,1)S(1)} collective-permute-done((bf16[2,128,640]{2,1,0:T(8,128)(2,1)S(1)}, bf16[2,128,640]{2,1,0:T(8,128)(2,1)S(1)}, u32[]{:S(2)}, u32[]{:S(2)}) %collective-permute-start.4) | collective-permute-done | bytes 327712 | tf_op jit(solution)/shard_map/ppermute | solution.py:80
  21.7 1.6 %collective-permute-start.9 = (bf16[4,576,128]{2,1,0:T(8,128)(2,1)S(1)}, bf16[4,576,128]{2,1,0:T(8,128)(2,1)S(1)}, u32[]{:S(2)}, u32[]{:S(2)}) collective-permute-start(bf16[4,576,128]{2,1,0:T(8,128)(2,1)S(1)} %pad_maximum_fusion.3.refs_1_), channel_id=1, source_target_pairs={{0,4},{1,5},{2,6},{3,7},{4,0},{5,1},{6,2},{7,3},{8,12},{9,13},{10,... | collective-permute-start | bytes 1769480 | tf_op jit(solution)/shard_map/ppermute | solution.py:75
  25.1 1.5 %collective-permute-start.6 = (bf16[2,288,128]{2,1,0:T(8,128)(2,1)S(1)}, bf16[2,288,128]{2,1,0:T(8,128)(2,1)S(1)}, u32[]{:S(2)}, u32[]{:S(2)}) collective-permute-start(bf16[2,288,128]{2,1,0:T(8,128)(2,1)S(1)} %pad_maximum_fusion.10), channel_id=1, source_target_pairs={{0,16},{1,17},{2,18},{3,19},{4,20},{5,21},{6,22},{7,23},{8,24},{9,... | collective-permute-start | bytes 442376 | tf_op jit(solution)/shard_map/ppermute | solution.py:75
  26.6 1.6 %collective-permute-start.5 = (bf16[2,288,128]{2,1,0:T(8,128)(2,1)S(1)}, bf16[2,288,128]{2,1,0:T(8,128)(2,1)S(1)}, u32[]{:S(2)}, u32[]{:S(2)}) collective-permute-start(bf16[2,288,128]{2,1,0:T(8,128)(2,1)S(1)} %pad_maximum_fusion.10), channel_id=1, source_target_pairs={{0,24},{1,25},{2,26},{3,27},{4,28},{5,29},{6,30},{7,31},{8,0},{9,1... | collective-permute-start | bytes 442376 | tf_op jit(solution)/shard_map/ppermute | solution.py:75
  29.5 3.1 %collective-permute-done.7 = bf16[2,288,128]{2,1,0:T(8,128)(2,1)S(1)} collective-permute-done((bf16[2,288,128]{2,1,0:T(8,128)(2,1)S(1)}, bf16[2,288,128]{2,1,0:T(8,128)(2,1)S(1)}, u32[]{:S(2)}, u32[]{:S(2)}) %collective-permute-start.7) | collective-permute-done | bytes 147488 | tf_op jit(solution)/shard_map/ppermute | solution.py:75
  32.6 3.3 %collective-permute-done.6 = bf16[2,288,128]{2,1,0:T(8,128)(2,1)S(1)} collective-permute-done((bf16[2,288,128]{2,1,0:T(8,128)(2,1)S(1)}, bf16[2,288,128]{2,1,0:T(8,128)(2,1)S(1)}, u32[]{:S(2)}, u32[]{:S(2)}) %collective-permute-start.6) | collective-permute-done | bytes 147488 | tf_op jit(solution)/shard_map/ppermute | solution.py:75
  36.7 1.2 collective-permute-start.16
  38.4 12.7 %collective-permute-done.15.refs_10_ = bf16[8,288,128]{2,1,0:T(8,128)(2,1)S(1)} collective-permute-done((bf16[8,288,128]{2,1,0:T(8,128)(2,1)S(1)}, bf16[8,288,128]{2,1,0:T(8,128)(2,1)S(1)}, u32[]{:S(2)}, u32[]{:S(2)}) %collective-permute-start.15) | collective-permute-done | bytes 589856 | tf_op jit(solution)/shard_map/ppermute | solution.py:75
  52.1 1.1 collective-permute-done.11.refs_7_
  57.7 27.1 %layer.1 = (bf16[2,576,128]{2,1,0:T(8,128)(2,1)}, bf16[2352,128]{1,0:T(8,128)(2,1)}, bf16[2304,128]{1,0:T(8,128)(2,1)S(1)}, bf16[6912,128]{1,0:T(8,128)(2,1)}, b...) custom-call(s32[98]{0:T(128)S(1)} %stack.448.refs_0_, ...), custom_call_target="tpu_custom_call" | custom-call | tf_op jit(solution)/shard_map/layer/pallas_call | solution.py:791
  85.4 2.4 %collective-permute-done.20 = bf16[2304,128]{1,0:T(8,128)(2,1)S(1)} collective-permute-done((bf16[2304,128]{1,0:T(8,128)(2,1)S(1)}, bf16[2304,128]{1,0:T(8,128)(2,1)S(1)}, u32[]{:S(2)}, u32[]{:S(2)}) %collective-permute-start.20) | collective-permute-done | bytes 589856 | tf_op jit(solution)/shard_map/ppermute | solution.py:75
  87.9 1.2 add_convert_fusion.5
  92.0 2.5 %collective-permute-done.23 = bf16[6912,128]{1,0:T(8,128)(2,1)S(1)} collective-permute-done((bf16[6912,128]{1,0:T(8,128)(2,1)}, bf16[6912,128]{1,0:T(8,128)(2,1)S(1)}, u32[]{:S(2)}, u32[]{:S(2)}) %collective-permute-start.23) | collective-permute-done | bytes 1769504 | tf_op jit(solution)/shard_map/ppermute | solution.py:75
  95.0 9.9 %collective-permute-done.22 = bf16[2304,128]{1,0:T(8,128)(2,1)S(1)} collective-permute-done((bf16[2304,128]{1,0:T(8,128)(2,1)S(1)}, bf16[2304,128]{1,0:T(8,128)(2,1)S(1)}, u32[]{:S(2)}, u32[]{:S(2)}) %collective-permute-start.22) | collective-permute-done | bytes 589856 | tf_op jit(solution)/shard_map/ppermute | solution.py:75
  104.8 1.3 collective-permute-done.21
  106.4 1.6 %collective-permute-start.30 = (bf16[2352,128]{1,0:T(8,128)(2,1)S(1)}, bf16[2352,128]{1,0:T(8,128)(2,1)S(1)}, u32[]{:S(2)}, u32[]{:S(2)}) collective-permute-start(bf16[2352,128]{1,0:T(8,128)(2,1)S(1)} %pad_maximum_fusion.2), channel_id=1, source_target_pairs={{0,4},{1,5},{2,6},{3,7},{4,0},{5,1},{6,2},{7,3},{8,12},{9,13},{10,... | collective-permute-start | bytes 1806344 | tf_op jit(solution)/shard_map/ppermute | solution.py:75
  108.7 3.7 %collective-permute-start.28 = (bf16[576,128]{1,0:T(8,128)(2,1)S(1)}, bf16[576,128]{1,0:T(8,128)(2,1)S(1)}, u32[]{:S(2)}, u32[]{:S(2)}) collective-permute-start(bf16[576,128]{1,0:T(8,128)(2,1)S(1)} %get-tuple-element.214), channel_id=1, source_target_pairs={{0,8},{1,9},{2,10},{3,11},{4,12},{5,13},{6,14},{7,15},{8,16},{9,17... | collective-permute-start | bytes 442376 | tf_op jit(solution)/shard_map/ppermute | solution.py:75
  112.4 2.4 %collective-permute-start.26 = (bf16[576,128]{1,0:T(8,128)(2,1)S(1)}, bf16[576,128]{1,0:T(8,128)(2,1)S(1)}, u32[]{:S(2)}, u32[]{:S(2)}) collective-permute-start(bf16[576,128]{1,0:T(8,128)(2,1)S(1)} %get-tuple-element.216), channel_id=1, source_target_pairs={{0,24},{1,25},{2,26},{3,27},{4,28},{5,29},{6,30},{7,31},{8,0},{9,1... | collective-permute-start | bytes 442376 | tf_op jit(solution)/shard_map/ppermute | solution.py:75
  114.9 2.5 %collective-permute-done.28 = bf16[576,128]{1,0:T(8,128)(2,1)S(1)} collective-permute-done((bf16[576,128]{1,0:T(8,128)(2,1)S(1)}, bf16[576,128]{1,0:T(8,128)(2,1)S(1)}, u32[]{:S(2)}, u32[]{:S(2)}) %collective-permute-start.28) | collective-permute-done | bytes 147488 | tf_op jit(solution)/shard_map/ppermute | solution.py:75
  117.4 4.7 %collective-permute-done.27 = bf16[576,128]{1,0:T(8,128)(2,1)S(1)} collective-permute-done((bf16[576,128]{1,0:T(8,128)(2,1)S(1)}, bf16[576,128]{1,0:T(8,128)(2,1)S(1)}, u32[]{:S(2)}, u32[]{:S(2)}) %collective-permute-start.27) | collective-permute-done | bytes 147488 | tf_op jit(solution)/shard_map/ppermute | solution.py:75
  123.2 3.7 %collective-permute-start.33 = (bf16[624,128]{1,0:T(8,128)(2,1)S(1)}, bf16[624,128]{1,0:T(8,128)(2,1)S(1)}, u32[]{:S(2)}, u32[]{:S(2)}) collective-permute-start(bf16[624,128]{1,0:T(8,128)(2,1)S(1)} %get-tuple-element.227), channel_id=1, source_target_pairs={{0,8},{1,9},{2,10},{3,11},{4,12},{5,13},{6,14},{7,15},{8,16},{9,17... | collective-permute-start | bytes 479240 | tf_op jit(solution)/shard_map/ppermute | solution.py:75
  126.9 1.7 %collective-permute-start.32 = (bf16[624,128]{1,0:T(8,128)(2,1)S(1)}, bf16[624,128]{1,0:T(8,128)(2,1)S(1)}, u32[]{:S(2)}, u32[]{:S(2)}) collective-permute-start(bf16[624,128]{1,0:T(8,128)(2,1)S(1)} %get-tuple-element.228), channel_id=1, source_target_pairs={{0,16},{1,17},{2,18},{3,19},{4,20},{5,21},{6,22},{7,23},{8,24},{9,... | collective-permute-start | bytes 479240 | tf_op jit(solution)/shard_map/ppermute | solution.py:75
  130.1 1.4 collective-permute-start.35
  133.4 4.4 %collective-permute-done.34.other_ref = bf16[288,128]{1,0:T(8,128)(2,1)S(1)} collective-permute-done((bf16[288,128]{1,0:T(8,128)(2,1)S(1)}, bf16[288,128]{1,0:T(8,128)(2,1)S(1)}, u32[]{:S(2)}, u32[]{:S(2)}) %collective-permute-start.34) | collective-permute-done | bytes 73760 | tf_op jit(solution)/shard_map/ppermute | solution.py:75
  139.0 4.8 %finish.1 = (f32[24,128]{1,0:T(8,128)}, f32[24,128]{1,0:T(8,128)}, f32[24,128]{1,0:T(8,128)}, f32[864,128]{1,0:T(8,128)}, f32[864,128]{1,0:T(8,128)}, /*index=5*/f32[864,128]{1,0:T(8,128)}, bf16[2,576,128]{2,1,0:T(8,128)(2,1)}) custom-call(s32[2]{0:T(128)} %pad_add_fusion.table_ref, f32[576,128]{1,0:T(8,128)} %get-tuple-element.207.head_ref, ...), custom_call_target="tpu_custom_call" | custom-call | tf_op jit(solution)/shard_map/finish/pallas_call | solution.py:374
  (175 shorter events, 25.0 us)
Async XLA Ops:
  2.5 14.3 %collective-permute-start.2 = (bf16[576,128]{1,0:T(8,128)(2,1)}, bf16[576,128]{1,0:T(8,128)(2,1)S(1)}, u32[]{:S(2)}, u32[]{:S(2)}) collective-permute-start(bf16[576,128]{1,0:T(8,128)(2,1)} %get-tuple-element.99), channel_id=1, source_target_pairs={{0,8},{1,9},{2,10},{3,11},{4,12},{5,13},{6,14},{7,15},{8,16},{9,17... | collective-permute-start | bytes 442376 | tf_op jit(solution)/shard_map/ppermute | solution.py:75
  5.4 12.6 %collective-permute-start.1 = (bf16[576,128]{1,0:T(8,128)(2,1)}, bf16[576,128]{1,0:T(8,128)(2,1)S(1)}, u32[]{:S(2)}, u32[]{:S(2)}) collective-permute-start(bf16[576,128]{1,0:T(8,128)(2,1)} %get-tuple-element.99), channel_id=1, source_target_pairs={{0,16},{1,17},{2,18},{3,19},{4,20},{5,21},{6,22},{7,23},{8,24},{9,... | collective-permute-start | bytes 442376 | tf_op jit(solution)/shard_map/ppermute | solution.py:75
  8.2 9.9 %collective-permute-start = (bf16[576,128]{1,0:T(8,128)(2,1)}, bf16[576,128]{1,0:T(8,128)(2,1)S(1)}, u32[]{:S(2)}, u32[]{:S(2)}) collective-permute-start(bf16[576,128]{1,0:T(8,128)(2,1)} %get-tuple-element.99), channel_id=1, source_target_pairs={{0,24},{1,25},{2,26},{3,27},{4,28},{5,29},{6,30},{7,31},{8,0},{9,1... | collective-permute-start | bytes 442376 | tf_op jit(solution)/shard_map/ppermute | solution.py:75
  9.4 7.4 %collective-permute-start.3 = (bf16[288,128]{1,0:T(8,128)(2,1)}, bf16[288,128]{1,0:T(8,128)(2,1)S(1)}, u32[]{:S(2)}, u32[]{:S(2)}) collective-permute-start(bf16[288,128]{1,0:T(8,128)(2,1)} %get-tuple-element.103), channel_id=1, source_target_pairs={{0,2},{1,3},{2,0},{3,1},{4,6},{5,7},{6,4},{7,5},{8,10},{9,11},{10,... | collective-permute-start | bytes 221192 | tf_op jit(solution)/shard_map/ppermute | solution.py:75
  13.2 8.4 %collective-permute-start.4 = (bf16[2,128,640]{2,1,0:T(8,128)(2,1)S(1)}, bf16[2,128,640]{2,1,0:T(8,128)(2,1)S(1)}, u32[]{:S(2)}, u32[]{:S(2)}) collective-permute-start(bf16[2,128,640]{2,1,0:T(8,128)(2,1)S(1)} %maximum_maximum_fusion.refs_0_), channel_id=1, source_target_pairs={{0,2},{1,3},{2,0},{3,1},{4,6},{5,7},{6,4},{7,5},{8,10},{9,11},{10,... | collective-permute-start | bytes 983048 | tf_op jit(solution)/shard_map/ppermute | solution.py:80
  21.7 14.2 %collective-permute-start.9 = (bf16[4,576,128]{2,1,0:T(8,128)(2,1)S(1)}, bf16[4,576,128]{2,1,0:T(8,128)(2,1)S(1)}, u32[]{:S(2)}, u32[]{:S(2)}) collective-permute-start(bf16[4,576,128]{2,1,0:T(8,128)(2,1)S(1)} %pad_maximum_fusion.3.refs_1_), channel_id=1, source_target_pairs={{0,4},{1,5},{2,6},{3,7},{4,0},{5,1},{6,2},{7,3},{8,12},{9,13},{10,... | collective-permute-start | bytes 1769480 | tf_op jit(solution)/shard_map/ppermute | solution.py:75
  23.3 12.7 %collective-permute-start.8 = (bf16[4,576,128]{2,1,0:T(8,128)(2,1)S(1)}, bf16[4,576,128]{2,1,0:T(8,128)(2,1)S(1)}, u32[]{:S(2)}, u32[]{:S(2)}) collective-permute-start(bf16[4,576,128]{2,1,0:T(8,128)(2,1)S(1)} %pad_maximum_fusion.3.refs_1_), channel_id=1, source_target_pairs={{0,2},{1,3},{2,0},{3,1},{4,6},{5,7},{6,4},{7,5},{8,10},{9,11},{10,... | collective-permute-start | bytes 1769480 | tf_op jit(solution)/shard_map/ppermute | solution.py:75
  24.3 8.4 %collective-permute-start.7 = (bf16[2,288,128]{2,1,0:T(8,128)(2,1)S(1)}, bf16[2,288,128]{2,1,0:T(8,128)(2,1)S(1)}, u32[]{:S(2)}, u32[]{:S(2)}) collective-permute-start(bf16[2,288,128]{2,1,0:T(8,128)(2,1)S(1)} %pad_maximum_fusion.10), channel_id=1, source_target_pairs={{0,8},{1,9},{2,10},{3,11},{4,12},{5,13},{6,14},{7,15},{8,16},{9,17... | collective-permute-start | bytes 442376 | tf_op jit(solution)/shard_map/ppermute | solution.py:75
  25.1 10.8 %collective-permute-start.6 = (bf16[2,288,128]{2,1,0:T(8,128)(2,1)S(1)}, bf16[2,288,128]{2,1,0:T(8,128)(2,1)S(1)}, u32[]{:S(2)}, u32[]{:S(2)}) collective-permute-start(bf16[2,288,128]{2,1,0:T(8,128)(2,1)S(1)} %pad_maximum_fusion.10), channel_id=1, source_target_pairs={{0,16},{1,17},{2,18},{3,19},{4,20},{5,21},{6,22},{7,23},{8,24},{9,... | collective-permute-start | bytes 442376 | tf_op jit(solution)/shard_map/ppermute | solution.py:75
  26.6 9.4 %collective-permute-start.5 = (bf16[2,288,128]{2,1,0:T(8,128)(2,1)S(1)}, bf16[2,288,128]{2,1,0:T(8,128)(2,1)S(1)}, u32[]{:S(2)}, u32[]{:S(2)}) collective-permute-start(bf16[2,288,128]{2,1,0:T(8,128)(2,1)S(1)} %pad_maximum_fusion.10), channel_id=1, source_target_pairs={{0,24},{1,25},{2,26},{3,27},{4,28},{5,29},{6,30},{7,31},{8,0},{9,1... | collective-permute-start | bytes 442376 | tf_op jit(solution)/shard_map/ppermute | solution.py:75
  36.2 14.9 %collective-permute-start.15 = (bf16[8,288,128]{2,1,0:T(8,128)(2,1)S(1)}, bf16[8,288,128]{2,1,0:T(8,128)(2,1)S(1)}, u32[]{:S(2)}, u32[]{:S(2)}) collective-permute-start(bf16[8,288,128]{2,1,0:T(8,128)(2,1)S(1)} %constant_dynamic-update-slice_fusion.refs_9_), channel_id=1, source_target_pairs={{0,4},{1,5},{2,6},{3,7},{4,0},{5,1},{6,2},{7,3},{8,12},{9,13},{10,... | collective-permute-start | bytes 1769480 | tf_op jit(solution)/shard_map/ppermute | solution.py:75
  36.7 14.4 %collective-permute-start.10 = (bf16[8,288,128]{2,1,0:T(8,128)(2,1)S(1)}, bf16[8,288,128]{2,1,0:T(8,128)(2,1)S(1)}, u32[]{:S(2)}, u32[]{:S(2)}) collective-permute-start(bf16[8,288,128]{2,1,0:T(8,128)(2,1)S(1)} %constant_dynamic-update-slice_fusion.refs_9_), channel_id=1, source_target_pairs={{0,1},{1,0},{2,3},{3,2},{4,5},{5,4},{6,7},{7,6},{8,9},{9,8},{10,11... | collective-permute-start | bytes 1769480 | tf_op jit(solution)/shard_map/ppermute | solution.py:75
  36.7 16.4 %collective-permute-start.16 = (bf16[4,576,128]{2,1,0:T(8,128)(2,1)S(1)}, bf16[4,576,128]{2,1,0:T(8,128)(2,1)S(1)}, u32[]{:S(2)}, u32[]{:S(2)}) collective-permute-start(bf16[4,576,128]{2,1,0:T(8,128)(2,1)S(1)} %collective-permute-done.9.refs_2_), channel_id=1, source_target_pairs={{0,2},{1,3},{2,0},{3,1},{4,6},{5,7},{6,4},{7,5},{8,10},{9,11},{10,... | collective-permute-start | bytes 1769480 | tf_op jit(solution)/shard_map/ppermute | solution.py:75
  37.9 15.2 %collective-permute-start.12 = (bf16[4,576,128]{2,1,0:T(8,128)(2,1)S(1)}, bf16[4,576,128]{2,1,0:T(8,128)(2,1)S(1)}, u32[]{:S(2)}, u32[]{:S(2)}) collective-permute-start(bf16[4,576,128]{2,1,0:T(8,128)(2,1)S(1)} %collective-permute-done.9.refs_2_), channel_id=1, source_target_pairs={{0,1},{1,0},{2,3},{3,2},{4,5},{5,4},{6,7},{7,6},{8,9},{9,8},{10,11... | collective-permute-start | bytes 1769480 | tf_op jit(solution)/shard_map/ppermute | solution.py:75
  38.2 13.9 %collective-permute-start.13 = (bf16[4,576,128]{2,1,0:T(8,128)(2,1)S(1)}, bf16[4,576,128]{2,1,0:T(8,128)(2,1)S(1)}, u32[]{:S(2)}, u32[]{:S(2)}) collective-permute-start(bf16[4,576,128]{2,1,0:T(8,128)(2,1)S(1)} %pad_maximum_fusion.3.refs_1_), channel_id=1, source_target_pairs={{0,1},{1,0},{2,3},{3,2},{4,5},{5,4},{6,7},{7,6},{8,9},{9,8},{10,11... | collective-permute-start | bytes 1769480 | tf_op jit(solution)/shard_map/ppermute | solution.py:75
  51.1 2.9 %collective-permute-start.14 = (bf16[2,2,128,640]{3,2,1,0:T(8,128)(2,1)S(1)}, bf16[2,2,128,640]{3,2,1,0:T(8,128)(2,1)S(1)}, u32[]{:S(2)}, u32[]{:S(2)}) collective-permute-start(bf16[2,2,128,640]{3,2,1,0:T(8,128)(2,1)S(1)} %pad_maximum_fusion.refs_13_), channel_id=1, source_target_pairs={{0,1},{1,0},{2,3},{3,2},{4,5},{5,4},{6,7},{7,6},{8,9},{9,8},{10,11... | collective-permute-start | bytes 1966088 | tf_op jit(solution)/shard_map/ppermute | solution.py:80
  84.9 2.9 %collective-permute-start.19 = (bf16[2352,128]{1,0:T(8,128)(2,1)}, bf16[2352,128]{1,0:T(8,128)(2,1)S(1)}, u32[]{:S(2)}, u32[]{:S(2)}) collective-permute-start(bf16[2352,128]{1,0:T(8,128)(2,1)} %get-tuple-element.133), channel_id=1, source_target_pairs={{0,1},{1,0},{2,3},{3,2},{4,5},{5,4},{6,7},{7,6},{8,9},{9,8},{10,11... | collective-permute-start | bytes 1806344 | tf_op jit(solution)/shard_map/ppermute | solution.py:75
  85.1 2.7 %collective-permute-start.20 = (bf16[2304,128]{1,0:T(8,128)(2,1)S(1)}, bf16[2304,128]{1,0:T(8,128)(2,1)S(1)}, u32[]{:S(2)}, u32[]{:S(2)}) collective-permute-start(bf16[2304,128]{1,0:T(8,128)(2,1)S(1)} %get-tuple-element.134), channel_id=1, source_target_pairs={{0,1},{1,0},{2,3},{3,2},{4,5},{5,4},{6,7},{7,6},{8,9},{9,8},{10,11... | collective-permute-start | bytes 1769480 | tf_op jit(solution)/shard_map/ppermute | solution.py:75
  87.8 3.5 %collective-permute-start.25 = (bf16[2,2,128,384]{3,2,1,0:T(8,128)(2,1)S(1)}, bf16[2,2,128,384]{3,2,1,0:T(8,128)(2,1)S(1)}, u32[]{:S(2)}, u32[]{:S(2)}) collective-permute-start(bf16[2,2,128,384]{3,2,1,0:T(8,128)(2,1)S(1)} %get-tuple-element.148), channel_id=1, source_target_pairs={{0,1},{1,0},{2,3},{3,2},{4,5},{5,4},{6,7},{7,6},{8,9},{9,8},{10,11... | collective-permute-start | bytes 1179656 | tf_op jit(solution)/shard_map/ppermute | solution.py:80
  89.2 15.7 %collective-permute-start.22 = (bf16[2304,128]{1,0:T(8,128)(2,1)S(1)}, bf16[2304,128]{1,0:T(8,128)(2,1)S(1)}, u32[]{:S(2)}, u32[]{:S(2)}) collective-permute-start(bf16[2304,128]{1,0:T(8,128)(2,1)S(1)} %add_convert_fusion.5), channel_id=1, source_target_pairs={{0,4},{1,5},{2,6},{3,7},{4,0},{5,1},{6,2},{7,3},{8,12},{9,13},{10,... | collective-permute-start | bytes 1769480 | tf_op jit(solution)/shard_map/ppermute | solution.py:75
  89.8 4.7 %collective-permute-start.23 = (bf16[6912,128]{1,0:T(8,128)(2,1)}, bf16[6912,128]{1,0:T(8,128)(2,1)S(1)}, u32[]{:S(2)}, u32[]{:S(2)}) collective-permute-start(bf16[6912,128]{1,0:T(8,128)(2,1)} %get-tuple-element.142), channel_id=1, source_target_pairs={{0,1},{1,0},{2,3},{3,2},{4,5},{5,4},{6,7},{7,6},{8,9},{9,8},{10,11... | collective-permute-start | bytes 5308424 | tf_op jit(solution)/shard_map/ppermute | solution.py:75
  90.5 15.6 %collective-permute-start.21 = (bf16[2352,128]{1,0:T(8,128)(2,1)S(1)}, bf16[2352,128]{1,0:T(8,128)(2,1)S(1)}, u32[]{:S(2)}, u32[]{:S(2)}) collective-permute-start(bf16[2352,128]{1,0:T(8,128)(2,1)S(1)} %pad_maximum_fusion.1), channel_id=1, source_target_pairs={{0,2},{1,3},{2,0},{3,1},{4,6},{5,7},{6,4},{7,5},{8,10},{9,11},{10,... | collective-permute-start | bytes 1806344 | tf_op jit(solution)/shard_map/ppermute | solution.py:75
  106.4 15.8 %collective-permute-start.30 = (bf16[2352,128]{1,0:T(8,128)(2,1)S(1)}, bf16[2352,128]{1,0:T(8,128)(2,1)S(1)}, u32[]{:S(2)}, u32[]{:S(2)}) collective-permute-start(bf16[2352,128]{1,0:T(8,128)(2,1)S(1)} %pad_maximum_fusion.2), channel_id=1, source_target_pairs={{0,4},{1,5},{2,6},{3,7},{4,0},{5,1},{6,2},{7,3},{8,12},{9,13},{10,... | collective-permute-start | bytes 1806344 | tf_op jit(solution)/shard_map/ppermute | solution.py:75
  108.0 14.2 %collective-permute-start.29 = (bf16[2304,128]{1,0:T(8,128)(2,1)S(1)}, bf16[2304,128]{1,0:T(8,128)(2,1)S(1)}, u32[]{:S(2)}, u32[]{:S(2)}) collective-permute-start(bf16[2304,128]{1,0:T(8,128)(2,1)S(1)} %get-tuple-element.151), channel_id=1, source_target_pairs={{0,2},{1,3},{2,0},{3,1},{4,6},{5,7},{6,4},{7,5},{8,10},{9,11},{10,... | collective-permute-start | bytes 1769480 | tf_op jit(solution)/shard_map/ppermute | solution.py:75
  108.7 8.7 %collective-permute-start.28 = (bf16[576,128]{1,0:T(8,128)(2,1)S(1)}, bf16[576,128]{1,0:T(8,128)(2,1)S(1)}, u32[]{:S(2)}, u32[]{:S(2)}) collective-permute-start(bf16[576,128]{1,0:T(8,128)(2,1)S(1)} %get-tuple-element.214), channel_id=1, source_target_pairs={{0,8},{1,9},{2,10},{3,11},{4,12},{5,13},{6,14},{7,15},{8,16},{9,17... | collective-permute-start | bytes 442376 | tf_op jit(solution)/shard_map/ppermute | solution.py:75
  112.4 9.7 %collective-permute-start.27 = (bf16[576,128]{1,0:T(8,128)(2,1)S(1)}, bf16[576,128]{1,0:T(8,128)(2,1)S(1)}, u32[]{:S(2)}, u32[]{:S(2)}) collective-permute-start(bf16[576,128]{1,0:T(8,128)(2,1)S(1)} %get-tuple-element.215), channel_id=1, source_target_pairs={{0,16},{1,17},{2,18},{3,19},{4,20},{5,21},{6,22},{7,23},{8,24},{9,... | collective-permute-start | bytes 442376 | tf_op jit(solution)/shard_map/ppermute | solution.py:75
  112.4 9.7 %collective-permute-start.26 = (bf16[576,128]{1,0:T(8,128)(2,1)S(1)}, bf16[576,128]{1,0:T(8,128)(2,1)S(1)}, u32[]{:S(2)}, u32[]{:S(2)}) collective-permute-start(bf16[576,128]{1,0:T(8,128)(2,1)S(1)} %get-tuple-element.216), channel_id=1, source_target_pairs={{0,24},{1,25},{2,26},{3,27},{4,28},{5,29},{6,30},{7,31},{8,0},{9,1... | collective-permute-start | bytes 442376 | tf_op jit(solution)/shard_map/ppermute | solution.py:75
  123.2 14.6 %collective-permute-start.33 = (bf16[624,128]{1,0:T(8,128)(2,1)S(1)}, bf16[624,128]{1,0:T(8,128)(2,1)S(1)}, u32[]{:S(2)}, u32[]{:S(2)}) collective-permute-start(bf16[624,128]{1,0:T(8,128)(2,1)S(1)} %get-tuple-element.227), channel_id=1, source_target_pairs={{0,8},{1,9},{2,10},{3,11},{4,12},{5,13},{6,14},{7,15},{8,16},{9,17... | collective-permute-start | bytes 479240 | tf_op jit(solution)/shard_map/ppermute | solution.py:75
  126.9 11.3 %collective-permute-start.32 = (bf16[624,128]{1,0:T(8,128)(2,1)S(1)}, bf16[624,128]{1,0:T(8,128)(2,1)S(1)}, u32[]{:S(2)}, u32[]{:S(2)}) collective-permute-start(bf16[624,128]{1,0:T(8,128)(2,1)S(1)} %get-tuple-element.228), channel_id=1, source_target_pairs={{0,16},{1,17},{2,18},{3,19},{4,20},{5,21},{6,22},{7,23},{8,24},{9,... | collective-permute-start | bytes 479240 | tf_op jit(solution)/shard_map/ppermute | solution.py:75
  128.6 9.6 %collective-permute-start.31 = (bf16[624,128]{1,0:T(8,128)(2,1)S(1)}, bf16[624,128]{1,0:T(8,128)(2,1)S(1)}, u32[]{:S(2)}, u32[]{:S(2)}) collective-permute-start(bf16[624,128]{1,0:T(8,128)(2,1)S(1)} %get-tuple-element.229), channel_id=1, source_target_pairs={{0,24},{1,25},{2,26},{3,27},{4,28},{5,29},{6,30},{7,31},{8,0},{9,1... | collective-permute-start | bytes 479240 | tf_op jit(solution)/shard_map/ppermute | solution.py:75
  130.1 8.2 %collective-permute-start.35 = (bf16[2,128,384]{2,1,0:T(8,128)(2,1)S(1)}, bf16[2,128,384]{2,1,0:T(8,128)(2,1)S(1)}, u32[]{:S(2)}, u32[]{:S(2)}) collective-permute-start(bf16[2,128,384]{2,1,0:T(8,128)(2,1)S(1)} %get-tuple-element.223), channel_id=1, source_target_pairs={{0,2},{1,3},{2,0},{3,1},{4,6},{5,7},{6,4},{7,5},{8,10},{9,11},{10,... | collective-permute-start | bytes 589832 | tf_op jit(solution)/shard_map/ppermute | solution.py:80
  132.2 5.7 %collective-permute-start.34 = (bf16[288,128]{1,0:T(8,128)(2,1)S(1)}, bf16[288,128]{1,0:T(8,128)(2,1)S(1)}, u32[]{:S(2)}, u32[]{:S(2)}) collective-permute-start(bf16[288,128]{1,0:T(8,128)(2,1)S(1)} %get-tuple-element.221), channel_id=1, source_target_pairs={{0,2},{1,3},{2,0},{3,1},{4,6},{5,7},{6,4},{7,5},{8,10},{9,11},{10,... | collective-permute-start | bytes 221192 | tf_op jit(solution)/shard_map/ppermute | solution.py:75
  (38 other events, 234.2 us)
